TPU v7x, 128 devices: a whole 4x4x4 slice. The times are simulated.
128 devices in a mesh: gx: 8 (over y_lo, z), gy: 16 (over x, y_hi, core).
Axes of the slice: x: 4, y: 4 (y_hi: 2, y_lo: 2; y = y_hi * 2 + y_lo), z: 4, core: 2. Of those that a mesh axis runs over, the one named last changes fastest.
Arguments:
- source_now: float32 [256, 128, 512], P('gy', 'gx'), may hold values from -6 to 6
- source_next: float32 [256, 128, 512], P('gy', 'gx'), may hold values from -6 to 6
- receiver_now: float32 [128, 512, 256], P('gx', 'gy'), may hold values from -6 to 6
- receiver_next: float32 [128, 512, 256], P('gx', 'gy'), may hold values from -6 to 6
- velocity: float32 [128, 512, 256], P('gx', 'gy'), may hold values from 0.05 to 0.18
- saved_planes: float32 [4, 2, 256, 512], replicated, may hold values from -6 to 6
- plane_index: int32 [4], replicated, may hold values from 0 to 3
- wavelet: float32 [4], replicated, may hold values from -8 to 8
- source_cell: int32 [3], replicated, may hold values from 4 to 123
- traces: float32 [4, 4096], replicated, may hold values from -6 to 6
- receiver_x: int32 [4096], replicated, may hold values from 0 to 127
- receiver_y: int32 [4096], replicated, may hold values from 0 to 511
Outputs:
- image_sum: float32 [128, 512, 256], P('gx', 'gy')
- receiver_field: float32 [128, 512, 256], P('gx', 'gy')
- source_field: float32 [256, 128, 512], P('gy', 'gx')
Inputs may be any that keep to these rules, and one draw needn't show every extreme that they name: `receiver_x`: receivers may share a cell; their traces add.
All inputs are finite; a program needn't handle non-finite values.
Results may differ from a plain program's by a relative error of at most 0.00055.
The roundings to bfloat16 on the way count: a program that leaves them out, or rounds other values in their place, can miss the bound.
Values may be sent and summed in bfloat16 or wider, within the bound.
No kernel may reach another device: no remote copies, remote signals or barrier semaphores. Data moves between devices by JAX's collectives and lax.ppermute only.
A program may use at most 192 MiB of HBM per device.

v0:
```python
import jax
import jax.numpy as jnp
from jax import lax
from jax.sharding import PartitionSpec as P

STEPS = 4


coeffs = (-205.0 / 72.0, 8.0 / 5.0, -1.0 / 5.0, 8.0 / 315.0, -1.0 / 560.0)
receiver_plane = 2


def padded_2(block, sides, width):
    for axis, dim in sides:
        count = lax.axis_size(axis)
        forward = [(i, i + 1) for i in range(count - 1)]
        backward = [(target, source) for source, target in forward]
        low = lax.ppermute(
            lax.slice_in_dim(block, block.shape[dim] - width, None, axis=dim), axis, forward
        )
        high = lax.ppermute(lax.slice_in_dim(block, 0, width, axis=dim), axis, backward)
        block = jnp.concatenate([low, block, high], axis=dim)
    return block


def shifted(padded, leading, dim_index, offset):
    starts = [0] * padded.ndim
    limits = list(padded.shape)
    for other in range(3):
        position = leading + other
        starts[position] = 4 + (offset if other == dim_index else 0)
        limits[position] = starts[position] + padded.shape[position] - 8
    return lax.slice(padded, starts, limits)


def laplace(padded, leading):
    summed = 3.0 * coeffs[0] * shifted(padded, leading, 0, 0)
    for dim_index in range(3):
        for distance in range(1, 5):
            summed = summed + coeffs[distance] * (
                shifted(padded, leading, dim_index, distance)
                + shifted(padded, leading, dim_index, -distance)
            )
    return summed


def on_device(
    source_now,
    source_next,
    receiver_now,
    receiver_next,
    velocity,
    saved_planes,
    plane_index,
    wavelet,
    source_cell,
    traces,
    receiver_x,
    receiver_y,
):
    width_x, width_y, depth = receiver_now.shape
    slab_depth = source_now.shape[0]
    span_x = lax.axis_size("gx") * width_x
    x_global = lax.axis_index("gx") * width_x + jnp.arange(width_x, dtype=jnp.int32)
    y_global = lax.axis_index("gy") * width_y + jnp.arange(width_y, dtype=jnp.int32)
    onehot_x = (x_global[:, None] == receiver_x[None, :]).astype(jnp.float32)
    onehot_y = (receiver_y[:, None] == y_global[None, :]).astype(jnp.float32)
    image_sum = jnp.zeros(receiver_now.shape, jnp.float32)
    vel_source = lax.all_to_all(
        jnp.transpose(velocity, (2, 0, 1)), "gy", split_axis=0, concat_axis=2, tiled=True
    )
    full_y = source_now.shape[2]
    z_global = lax.axis_index("gy") * slab_depth + jnp.arange(slab_depth, dtype=jnp.int32)
    y_all = jnp.arange(full_y, dtype=jnp.int32)
    point_mask = (
        (z_global == source_cell[2])[:, None, None]
        & (x_global == source_cell[0])[None, :, None]
        & (y_all == source_cell[1])[None, None, :]
    ).astype(jnp.float32)
    for step_index in range(STEPS):
        padded = padded_2(source_now, (("gx", 1), ("gy", 0)), 4)
        padded = jnp.pad(padded, ((0, 0), (0, 0), (4, 4)))
        earlier = 2.0 * source_now - source_next + vel_source * laplace(padded, 0)
        earlier = earlier + point_mask * wavelet[step_index]
        planes = saved_planes[plane_index[step_index]]
        planes = lax.dynamic_slice_in_dim(planes, lax.axis_index("gy") * slab_depth, slab_depth, 1)
        earlier = jnp.where((x_global == 0)[None, :, None], planes[0][:, None, :], earlier)
        earlier = jnp.where((x_global == span_x - 1)[None, :, None], planes[1][:, None, :], earlier)
        source_next, source_now = (source_now, earlier)
        padded_rcv = padded_2(receiver_now, (("gx", 0), ("gy", 1)), 4)
        padded_rcv = jnp.pad(padded_rcv, ((0, 0), (0, 0), (4, 4)))
        later_rcv = 2.0 * receiver_now - receiver_next + velocity * laplace(padded_rcv, 0)
        weighted = traces[step_index][:, None] * onehot_y
        receiver_next, receiver_now = (
            receiver_now,
            later_rcv.at[:, :, receiver_plane].add(
                jnp.dot(
                    onehot_x,
                    weighted,
                    precision=lax.Precision.HIGHEST,
                    preferred_element_type=jnp.float32,
                )
            ),
        )
        if step_index % 2 == 1:
            brick = lax.all_to_all(
                source_now.astype(jnp.bfloat16), "gy", split_axis=2, concat_axis=0, tiled=True
            )
            rounded = jnp.transpose(brick, (1, 2, 0)).astype(jnp.float32)
            image_sum = image_sum + rounded * receiver_now
    return (image_sum, receiver_now, source_now)


def solution(mesh):
    placed = (
        P("gy", "gx", None),
        P("gy", "gx", None),
        P("gx", "gy", None),
        P("gx", "gy", None),
        P("gx", "gy", None),
        P(),
        P(),
        P(),
        P(),
        P(),
        P(),
        P(),
    )
    return jax.shard_map(
        on_device,
        mesh=mesh,
        in_specs=placed,
        out_specs=(P("gx", "gy", None), P("gx", "gy", None), P("gy", "gx", None)),
        check_vma=False,
    )
```

profile of v0, /device:TPU:25, one launch (start us, length us, event | category | flops | bytes accessed | tf_op | source)
XLA Modules:
  0.0 500.0 jit_solution(4983328950037206778)
XLA Ops:
  2.3 3.5 collective-permute-start.9
  5.9 4.2 collective-permute-start.8
  14.2 7.9 %all-to-all-start = ((f32[16,1,8192]{2,1,0:T(1,128)}), f32[16,1,8192]{2,1,0:T(1,128)}, u32[]{:S(2)}, u32[]{:S(2)}) async-start(f32[16,1,8192]{2,1,0:T(1,128)} %reshape.235), calls=%async_computation | async-start | bytes 1048576 | tf_op jit(solution)/shard_map/all_to_all | solution.py:69
  24.9 5.5 %collective-permute-start.1 = (f32[16,4,512]{2,1,0:T(4,128)}, f32[16,4,512]{2,1,0:T(4,128)S(1)}, u32[]{:S(2)}, u32[]{:S(2)}) collective-permute-start(f32[16,4,512]{2,1,0:T(4,128)} %get-tuple-element.128), channel_id=1, source_target_pairs={{16,0},{32,16},{48,32},{64,48},{80,64},{96,80},{112,96},{17,1},{33... | collective-permute-start | bytes 393224 | tf_op jit(solution)/shard_map/ppermute | solution.py:21
  53.3 3.1 copy.215
  57.1 3.9 collective-permute-start.11
  68.8 3.5 copy.257
  74.8 3.6 copy.255
  89.1 4.1 collective-permute-start.2
  93.2 4.4 collective-permute-start.3
  103.7 5.4 %select_maximum_fusion.12 = f32[24,40,264]{1,0,2:T(8,128)S(1)} fusion(f32[24,4,256]{1,0,2:T(8,128)} %copy.216, f32[24,32,256]{1,0,2:T(8,128)} %copy.215, f32[24,4,256]{1,0,2:T(8,128)} %copy.218), kind=kLoop, calls=%fused_computation.50 | loop fusion | flops 2027520 | bytes 1996800 | tf_op jit(solution)/shard_map/concatenate | solution.py:22
  109.2 31.5 %fusion.11 = f32[16,32,256]{1,0,2:T(8,128)S(1)} fusion(f32[16,32,256]{1,0,2:T(8,128)} %copy-done.5, f32[24,4,256]{1,0,2:T(8,128)} %copy.218, f32[24,32,256]{1,0,2:T(8,128)} %copy.215, f32[24,4,256]{1,0,2:T(8,128)} %copy.216, f32[24,40,264]{1,0,2:T(8,128)S(1)} %select_maximum_fusion.12, f32[16,32,256]{1,0,2:T(8,128)} %copy.256, f32[16,32,256]{1,0,2:T(8,128)} %copy.257, ...), kind=kLoop, calls=%fused_computation.86 | loop fusion | flops 6422528 | bytes 11468800 | tf_op jit(solution)/shard_map/add | solution.py:92
  143.4 5.5 %collective-permute-start.12 = (f32[4,32,256]{1,0,2:T(4,128)S(1)}, f32[4,32,256]{1,0,2:T(4,128)S(1)}, u32[]{:S(2)}, u32[]{:S(2)}) collective-permute-start(f32[4,32,256]{1,0,2:T(4,128)S(1)} %get-tuple-element.94), channel_id=1, source_target_pairs={{16,0},{32,16},{48,32},{64,48},{80,64},{96,80},{112,96},{17,1},{33... | collective-permute-start | bytes 393224 | tf_op jit(solution)/shard_map/ppermute | solution.py:21
  150.7 7.4 %collective-permute-done.13 = f32[4,32,256]{1,0,2:T(4,128)S(1)} collective-permute-done((f32[4,32,256]{1,0,2:T(4,128)S(1)}, f32[4,32,256]{1,0,2:T(4,128)S(1)}, u32[]{:S(2)}, u32[]{:S(2)}) %collective-permute-start.13) | collective-permute-done | bytes 131104 | tf_op jit(solution)/shard_map/ppermute | solution.py:18
  160.6 3.6 fusion.342
  170.9 6.2 %collective-permute-start.15 = (f32[24,4,256]{2,0,1:T(8,128)S(1)}, f32[24,4,256]{2,0,1:T(8,128)S(1)}, u32[]{:S(2)}, u32[]{:S(2)}) collective-permute-start(f32[24,4,256]{2,0,1:T(8,128)S(1)} %copy.227), channel_id=1, source_target_pairs={{0,1},{1,2},{2,3},{3,4},{4,5},{5,6},{6,7},{7,8},{8,9},{9,10},{10,1... | collective-permute-start | bytes 294920 | tf_op jit(solution)/shard_map/ppermute | solution.py:18
  183.1 6.2 %select_maximum_fusion.8 = f32[24,40,264]{1,0,2:T(8,128)S(1)} fusion(f32[24,4,256]{1,0,2:T(8,128)} %copy.226, f32[24,4,256]{1,0,2:T(8,128)} %copy.228, f32[4,32,256]{1,0,2:T(4,128)} %copy-done.32, f32[16,32,256]{1,0,2:T(8,128)} %copy-done.3, f32[4,32,256]{1,0,2:T(4,128)} %copy-done.30), kind=kLoop, calls=%fused_computation.46 | loop fusion | flops 3041280 | bytes 1996800 | tf_op jit(solution)/shard_map/concatenate | solution.py:22
  189.5 4.3 pad_maximum_fusion.1
  193.9 27.8 %fusion.89 = f32[16,32,256]{1,0,2:T(8,128)} fusion(f32[16,32,256]{1,0,2:T(8,128)} %copy-done.5, f32[16,32,256]{1,0,2:T(8,128)} %copy-done.3, f32[4,32,256]{1,0,2:T(4,128)} %copy-done.30, f32[4,32,256]{1,0,2:T(4,128)} %copy-done.32, f32[24,40,264]{1,0,2:T(8,128)S(1)} %select_maximum_fusion.8, f32[24,36,256]{1,0,2:T(8,128)} %get-tuple-element.87, ...), kind=kLoop, calls=%fused_computation.164 | loop fusion | flops 6422528 | bytes 10747904 | tf_op jit(solution)/shard_map/add | solution.py:92
  228.1 6.1 %collective-permute-start.24 = (f32[4,32,256]{1,0,2:T(4,128)}, f32[4,32,256]{1,0,2:T(4,128)}, u32[]{:S(2)}, u32[]{:S(2)}) collective-permute-start(f32[4,32,256]{1,0,2:T(4,128)} %get-tuple-element.92), channel_id=1, source_target_pairs={{16,0},{32,16},{48,32},{64,48},{80,64},{96,80},{112,96},{17,1},{33... | collective-permute-start | bytes 393224 | tf_op jit(solution)/shard_map/ppermute | solution.py:21
  243.5 6.1 %fusion.141 = f32[16,16,512]{2,1,0:T(8,128)S(1)} fusion(f32[16,16,512]{2,1,0:T(8,128)S(1)} %all_to_all.30, f32[16,16,512]{2,1,0:T(8,128)S(1)} %copy-done.15, f32[16,4,512]{2,1,0:T(4,128)S(1)} %collective-permute-done, f32[24,24,520]{2,1,0:T(8,128)S(1)} %copy-done.21, f32[16,20,512]{2,1,0:T(8,128)} %copy-done.25, f32[20,24,512]{2,1,0:T(8,128)} %get-tuple-element.109, ...), kind=kLoop, calls=%fused_computation.332 | loop fusion | flops 6553600 | bytes 12780324 | tf_op jit(solution)/shard_map/jit(_where)/select_n | solution.py:88
  249.7 3.4 collective-permute-start.5
  256.8 3.6 fusion.341
  267.1 6.0 %collective-permute-start.27 = (f32[24,4,256]{2,0,1:T(8,128)S(1)}, f32[24,4,256]{2,0,1:T(8,128)S(1)}, u32[]{:S(2)}, u32[]{:S(2)}) collective-permute-start(f32[24,4,256]{2,0,1:T(8,128)S(1)} %copy.236), channel_id=1, source_target_pairs={{0,1},{1,2},{2,3},{3,4},{4,5},{5,6},{6,7},{7,8},{8,9},{9,10},{10,1... | collective-permute-start | bytes 294920 | tf_op jit(solution)/shard_map/ppermute | solution.py:18
  275.9 6.5 %collective-permute-start.7 = (f32[4,24,512]{2,1,0:T(8,128)}, f32[4,24,512]{2,1,0:T(8,128)}, u32[]{:S(2)}, u32[]{:S(2)}) collective-permute-start(f32[4,24,512]{2,1,0:T(8,128)} %get-tuple-element.106), channel_id=1, source_target_pairs={{0,1},{1,2},{2,3},{3,4},{4,5},{5,6},{6,7},{7,8},{8,9},{9,10},{10,1... | collective-permute-start | bytes 589832 | tf_op jit(solution)/shard_map/ppermute | solution.py:18
  286.9 5.3 %select_maximum_fusion.4 = f32[24,40,264]{1,0,2:T(8,128)S(1)} fusion(f32[24,4,256]{1,0,2:T(8,128)} %copy.235, f32[24,4,256]{1,0,2:T(8,128)} %copy.237, f32[4,32,256]{1,0,2:T(4,128)} %collective-permute-done.24, f32[16,32,256]{1,0,2:T(8,128)} %fusion.322, f32[4,32,256]{1,0,2:T(4,128)} %collective-permute-done.25), kind=kLoop, calls=%fused_computation.42 | loop fusion | flops 3041280 | bytes 1996800 | tf_op jit(solution)/shard_map/concatenate | solution.py:22
  293.1 5.8 %pad_maximum_fusion.3 = (f32[24,36,256]{1,0,2:T(8,128)}, f32[24,36,256]{1,0,2:T(8,128)}) fusion(f32[24,4,256]{1,0,2:T(8,128)S(1)} %copy-done.11, f32[4,32,256]{1,0,2:T(4,128)} %collective-permute-done.24, f32[16,32,256]{1,0,2:T(8,128)S(1)} %copy-done.1, f32[4,32,256]{1,0,2:T(4,128)} %collective-permute-done.25, f32[24,4,256]{1,0,2:T(8,128)S(1)} %copy-done.13), kind=kLoop, calls=%fused_computation.57 | loop fusion | flops 1327104 | bytes 2752512 | tf_op jit(solution)/shard_map/concatenate | solution.py:22
  298.9 27.5 %fusion.63 = f32[16,32,256]{1,0,2:T(8,128)} fusion(f32[16,32,256]{1,0,2:T(8,128)} %copy-done.5, f32[16,32,256]{1,0,2:T(8,128)} %fusion.322, f32[4,32,256]{1,0,2:T(4,128)} %collective-permute-done.25, f32[4,32,256]{1,0,2:T(4,128)} %collective-permute-done.24, f32[24,40,264]{1,0,2:T(8,128)S(1)} %select_maximum_fusion.4, f32[24,36,256]{1,0,2:T(8,128)} %get-tuple-element.83, ...), kind=kLoop, calls=%fused_computation.138 | loop fusion | flops 6422528 | bytes 10747904 | tf_op jit(solution)/shard_map/add | solution.py:92
  332.0 5.5 %collective-permute-start.28 = (f32[4,32,256]{1,0,2:T(4,128)S(1)}, f32[4,32,256]{1,0,2:T(4,128)S(1)}, u32[]{:S(2)}, u32[]{:S(2)}) collective-permute-start(f32[4,32,256]{1,0,2:T(4,128)S(1)} %get-tuple-element.90), channel_id=1, source_target_pairs={{16,0},{32,16},{48,32},{64,48},{80,64},{96,80},{112,96},{17,1},{33... | collective-permute-start | bytes 393224 | tf_op jit(solution)/shard_map/ppermute | solution.py:21
  345.7 5.5 %collective-permute-start.17 = (f32[16,4,512]{2,1,0:T(4,128)S(1)}, f32[16,4,512]{2,1,0:T(4,128)S(1)}, u32[]{:S(2)}, u32[]{:S(2)}) collective-permute-start(f32[16,4,512]{2,1,0:T(4,128)S(1)} %get-tuple-element.124), channel_id=1, source_target_pairs={{16,0},{32,16},{48,32},{64,48},{80,64},{96,80},{112,96},{17,1},{33... | collective-permute-start | bytes 393224 | tf_op jit(solution)/shard_map/ppermute | solution.py:21
  355.1 6.2 %collective-permute-start.19 = (f32[4,24,512]{2,1,0:T(8,128)S(1)}, f32[4,24,512]{2,1,0:T(8,128)S(1)}, u32[]{:S(2)}, u32[]{:S(2)}) collective-permute-start(f32[4,24,512]{2,1,0:T(8,128)S(1)} %get-tuple-element.102), channel_id=1, source_target_pairs={{0,1},{1,2},{2,3},{3,4},{4,5},{5,6},{6,7},{7,8},{8,9},{9,10},{10,1... | collective-permute-start | bytes 589832 | tf_op jit(solution)/shard_map/ppermute | solution.py:18
  361.3 3.6 fusion.340
  371.6 6.0 %collective-permute-start.31 = (f32[24,4,256]{2,0,1:T(8,128)S(1)}, f32[24,4,256]{2,0,1:T(8,128)S(1)}, u32[]{:S(2)}, u32[]{:S(2)}) collective-permute-start(f32[24,4,256]{2,0,1:T(8,128)S(1)} %copy.243), channel_id=1, source_target_pairs={{0,1},{1,2},{2,3},{3,4},{4,5},{5,6},{6,7},{7,8},{8,9},{9,10},{10,1... | collective-permute-start | bytes 294920 | tf_op jit(solution)/shard_map/ppermute | solution.py:18
  380.5 4.4 reshape.239
  384.9 7.0 %all-to-all-start.1 = ((bf16[16,2,4096]{2,1,0:T(2,128)(2,1)}), bf16[16,2,4096]{2,1,0:T(2,128)(2,1)}, u32[]{:S(2)}, u32[]{:S(2)}) async-start(bf16[16,2,4096]{2,1,0:T(2,128)(2,1)} %reshape.239), calls=%async_computation.1 | async-start | bytes 524288 | tf_op jit(solution)/shard_map/all_to_all | solution.py:106
  400.9 5.9 %collective-permute-start.21 = (f32[16,4,512]{2,1,0:T(4,128)S(1)}, f32[16,4,512]{2,1,0:T(4,128)S(1)}, u32[]{:S(2)}, u32[]{:S(2)}) collective-permute-start(f32[16,4,512]{2,1,0:T(4,128)S(1)} %get-tuple-element.123), channel_id=1, source_target_pairs={{16,0},{32,16},{48,32},{64,48},{80,64},{96,80},{112,96},{17,1},{33... | collective-permute-start | bytes 393224 | tf_op jit(solution)/shard_map/ppermute | solution.py:21
  411.9 3.3 collective-permute-done.20
  415.3 3.4 collective-permute-start.22
  418.7 4.5 collective-permute-start.23
  423.3 4.4 pad_maximum_fusion.5
  429.5 3.6 fusion.338
  435.9 4.4 reshape.237
  440.3 7.3 %all-to-all-start.2 = ((bf16[16,2,4096]{2,1,0:T(2,128)(2,1)}), bf16[16,2,4096]{2,1,0:T(2,128)(2,1)S(1)}, u32[]{:S(2)}, u32[]{:S(2)}) async-start(bf16[16,2,4096]{2,1,0:T(2,128)(2,1)} %reshape.237), calls=%async_computation.2 | async-start | bytes 524288 | tf_op jit(solution)/shard_map/all_to_all | solution.py:106
  447.6 27.3 %fusion.37 = f32[16,32,256]{1,0,2:T(8,128)} fusion(f32[16,32,256]{1,0,2:T(8,128)} %copy-done.5, f32[16,32,256]{1,0,2:T(8,128)} %fusion.321, f32[4,32,256]{1,0,2:T(4,128)} %copy-done.26, f32[4,32,256]{1,0,2:T(4,128)} %copy-done.28, f32[24,40,264]{1,0,2:T(8,128)S(1)} %select_maximum_fusion, f32[24,36,256]{1,0,2:T(8,128)} %get-tuple-element.79, ...), kind=kLoop, calls=%fused_computation.112 | loop fusion | flops 6422528 | bytes 10747904 | tf_op jit(solution)/shard_map/add | solution.py:92
  476.7 3.3 copy.249
  487.9 3.9 copy.233
  491.8 4.8 fusion.137
  496.5 3.3 copy.248
  (262 shorter events, 160.7 us)
Async XLA Ops:
  2.3 48.0 %collective-permute-start.9 = (f32[4,32,256]{2,1,0:T(8,128)}, f32[4,32,256]{2,1,0:T(8,128)}, u32[]{:S(2)}, u32[]{:S(2)}) collective-permute-start(f32[4,32,256]{2,1,0:T(8,128)} %get-tuple-element.134), channel_id=1, source_target_pairs={{0,16},{16,32},{32,48},{48,64},{64,80},{80,96},{96,112},{1,17},{17... | collective-permute-start | bytes 393224 | tf_op jit(solution)/shard_map/ppermute | solution.py:18
  5.9 45.6 %collective-permute-start.8 = (f32[4,32,256]{2,1,0:T(8,128)}, f32[4,32,256]{2,1,0:T(8,128)}, u32[]{:S(2)}, u32[]{:S(2)}) collective-permute-start(f32[4,32,256]{2,1,0:T(8,128)} %get-tuple-element.133), channel_id=1, source_target_pairs={{16,0},{32,16},{48,32},{64,48},{80,64},{96,80},{112,96},{17,1},{33... | collective-permute-start | bytes 393224 | tf_op jit(solution)/shard_map/ppermute | solution.py:21
  12.5 32.9 %copy-start.34 = (f32[16,32,256]{2,1,0:T(8,128)S(1)}, f32[16,32,256]{2,1,0:T(8,128)}, u32[]{:S(2)}) copy-start(f32[16,32,256]{2,1,0:T(8,128)} %param.22) | copy-start | bytes 1572868
  14.2 220.0 %all-to-all-start = ((f32[16,1,8192]{2,1,0:T(1,128)}), f32[16,1,8192]{2,1,0:T(1,128)}, u32[]{:S(2)}, u32[]{:S(2)}) async-start(f32[16,1,8192]{2,1,0:T(1,128)} %reshape.235), calls=%async_computation | async-start | bytes 1048576 | tf_op jit(solution)/shard_map/all_to_all | solution.py:69
  22.9 65.4 %collective-permute-start = (f32[16,4,512]{2,1,0:T(4,128)}, f32[16,4,512]{2,1,0:T(4,128)S(1)}, u32[]{:S(2)}, u32[]{:S(2)}) collective-permute-start(f32[16,4,512]{2,1,0:T(4,128)} %get-tuple-element.129), channel_id=1, source_target_pairs={{0,16},{16,32},{32,48},{48,64},{64,80},{80,96},{96,112},{1,17},{17... | collective-permute-start | bytes 393224 | tf_op jit(solution)/shard_map/ppermute | solution.py:18
  24.9 63.4 %collective-permute-start.1 = (f32[16,4,512]{2,1,0:T(4,128)}, f32[16,4,512]{2,1,0:T(4,128)S(1)}, u32[]{:S(2)}, u32[]{:S(2)}) collective-permute-start(f32[16,4,512]{2,1,0:T(4,128)} %get-tuple-element.128), channel_id=1, source_target_pairs={{16,0},{32,16},{48,32},{64,48},{80,64},{96,80},{112,96},{17,1},{33... | collective-permute-start | bytes 393224 | tf_op jit(solution)/shard_map/ppermute | solution.py:21
  57.1 40.5 %collective-permute-start.11 = (f32[24,4,256]{2,0,1:T(8,128)}, f32[24,4,256]{2,0,1:T(8,128)}, u32[]{:S(2)}, u32[]{:S(2)}) collective-permute-start(f32[24,4,256]{2,0,1:T(8,128)} %copy.259), channel_id=1, source_target_pairs={{0,1},{1,2},{2,3},{3,4},{4,5},{5,6},{6,7},{7,8},{8,9},{9,10},{10,1... | collective-permute-start | bytes 294920 | tf_op jit(solution)/shard_map/ppermute | solution.py:18
  61.7 39.0 %collective-permute-start.10 = (f32[24,4,256]{2,0,1:T(8,128)}, f32[24,4,256]{2,0,1:T(8,128)}, u32[]{:S(2)}, u32[]{:S(2)}) collective-permute-start(f32[24,4,256]{2,0,1:T(8,128)} %copy.258), channel_id=1, source_target_pairs={{1,0},{2,1},{3,2},{4,3},{5,4},{6,5},{7,6},{8,7},{9,8},{10,9},{11,1... | collective-permute-start | bytes 294920 | tf_op jit(solution)/shard_map/ppermute | solution.py:21
  89.1 59.7 %collective-permute-start.2 = (f32[4,24,512]{2,1,0:T(8,128)}, f32[4,24,512]{2,1,0:T(8,128)S(1)}, u32[]{:S(2)}, u32[]{:S(2)}) collective-permute-start(f32[4,24,512]{2,1,0:T(8,128)} %get-tuple-element.111), channel_id=1, source_target_pairs={{1,0},{2,1},{3,2},{4,3},{5,4},{6,5},{7,6},{8,7},{9,8},{10,9},{11,1... | collective-permute-start | bytes 589832 | tf_op jit(solution)/shard_map/ppermute | solution.py:21
  93.2 55.7 %collective-permute-start.3 = (f32[4,24,512]{2,1,0:T(8,128)}, f32[4,24,512]{2,1,0:T(8,128)S(1)}, u32[]{:S(2)}, u32[]{:S(2)}) collective-permute-start(f32[4,24,512]{2,1,0:T(8,128)} %get-tuple-element.110), channel_id=1, source_target_pairs={{0,1},{1,2},{2,3},{3,4},{4,5},{5,6},{6,7},{7,8},{8,9},{9,10},{10,1... | collective-permute-start | bytes 589832 | tf_op jit(solution)/shard_map/ppermute | solution.py:18
  109.2 31.5 %copy-start.55 = (s32[4096]{0:T(1024)S(1)}, s32[4096]{0:T(1024)}, u32[]{:S(2)}) copy-start(s32[4096]{0:T(1024)} %param.31) | copy-start | bytes 49156
  109.2 31.5 %copy-start.58 = (s32[4096]{0:T(1024)S(1)}, s32[4096]{0:T(1024)}, u32[]{:S(2)}) copy-start(s32[4096]{0:T(1024)} %param.30) | copy-start | bytes 49156
  109.2 31.5 %copy-start.61 = (s32[16]{0:T(128)S(1)}, s32[16]{0:T(128)}, u32[]{:S(2)}) copy-start(s32[16]{0:T(128)} %iota_add_fusion.1) | copy-start | bytes 196
  109.2 31.5 %copy-start.63 = (s32[32]{0:T(128)S(1)}, s32[32]{0:T(128)}, u32[]{:S(2)}) copy-start(s32[32]{0:T(128)} %iota_add_fusion) | copy-start | bytes 388
  141.4 16.6 %collective-permute-start.13 = (f32[4,32,256]{1,0,2:T(4,128)S(1)}, f32[4,32,256]{1,0,2:T(4,128)S(1)}, u32[]{:S(2)}, u32[]{:S(2)}) collective-permute-start(f32[4,32,256]{1,0,2:T(4,128)S(1)} %get-tuple-element.95), channel_id=1, source_target_pairs={{0,16},{16,32},{32,48},{48,64},{64,80},{80,96},{96,112},{1,17},{17... | collective-permute-start | bytes 393224 | tf_op jit(solution)/shard_map/ppermute | solution.py:18
  143.4 16.5 %collective-permute-start.12 = (f32[4,32,256]{1,0,2:T(4,128)S(1)}, f32[4,32,256]{1,0,2:T(4,128)S(1)}, u32[]{:S(2)}, u32[]{:S(2)}) collective-permute-start(f32[4,32,256]{1,0,2:T(4,128)S(1)} %get-tuple-element.94), channel_id=1, source_target_pairs={{16,0},{32,16},{48,32},{64,48},{80,64},{96,80},{112,96},{17,1},{33... | collective-permute-start | bytes 393224 | tf_op jit(solution)/shard_map/ppermute | solution.py:21
  166.6 12.1 %collective-permute-start.14 = (f32[24,4,256]{2,0,1:T(8,128)S(1)}, f32[24,4,256]{2,0,1:T(8,128)S(1)}, u32[]{:S(2)}, u32[]{:S(2)}) collective-permute-start(f32[24,4,256]{2,0,1:T(8,128)S(1)} %copy.225), channel_id=1, source_target_pairs={{1,0},{2,1},{3,2},{4,3},{5,4},{6,5},{7,6},{8,7},{9,8},{10,9},{11,1... | collective-permute-start | bytes 294920 | tf_op jit(solution)/shard_map/ppermute | solution.py:21
  170.9 10.0 %collective-permute-start.15 = (f32[24,4,256]{2,0,1:T(8,128)S(1)}, f32[24,4,256]{2,0,1:T(8,128)S(1)}, u32[]{:S(2)}, u32[]{:S(2)}) collective-permute-start(f32[24,4,256]{2,0,1:T(8,128)S(1)} %copy.227), channel_id=1, source_target_pairs={{0,1},{1,2},{2,3},{3,4},{4,5},{5,6},{6,7},{7,8},{8,9},{9,10},{10,1... | collective-permute-start | bytes 294920 | tf_op jit(solution)/shard_map/ppermute | solution.py:18
  193.8 27.8 %copy-start.51 = (f32[1,4096]{1,0:T(1,128)S(1)}, f32[1,4096]{1,0:T(1,128)}, u32[]{:S(2)}) copy-start(f32[1,4096]{1,0:T(1,128)} %get-tuple-element.140) | copy-start | bytes 49156
  193.8 27.8 %copy-start.56 = (s32[4096]{0:T(1024)S(1)}, s32[4096]{0:T(1024)}, u32[]{:S(2)}) copy-start(s32[4096]{0:T(1024)} %param.31) | copy-start | bytes 49156
  193.9 27.9 %copy-start.59 = (s32[4096]{0:T(1024)S(1)}, s32[4096]{0:T(1024)}, u32[]{:S(2)}) copy-start(s32[4096]{0:T(1024)} %param.30) | copy-start | bytes 49156
  193.9 27.9 %copy-start.62 = (s32[16]{0:T(128)S(1)}, s32[16]{0:T(128)}, u32[]{:S(2)}) copy-start(s32[16]{0:T(128)} %iota_add_fusion.1) | copy-start | bytes 196
  193.9 27.9 %copy-start.64 = (s32[32]{0:T(128)S(1)}, s32[32]{0:T(128)}, u32[]{:S(2)}) copy-start(s32[32]{0:T(128)} %iota_add_fusion) | copy-start | bytes 388
  226.2 28.7 %collective-permute-start.25 = (f32[4,32,256]{1,0,2:T(4,128)}, f32[4,32,256]{1,0,2:T(4,128)}, u32[]{:S(2)}, u32[]{:S(2)}) collective-permute-start(f32[4,32,256]{1,0,2:T(4,128)} %get-tuple-element.93), channel_id=1, source_target_pairs={{0,16},{16,32},{32,48},{48,64},{64,80},{80,96},{96,112},{1,17},{17... | collective-permute-start | bytes 393224 | tf_op jit(solution)/shard_map/ppermute | solution.py:18
  228.1 26.8 %collective-permute-start.24 = (f32[4,32,256]{1,0,2:T(4,128)}, f32[4,32,256]{1,0,2:T(4,128)}, u32[]{:S(2)}, u32[]{:S(2)}) collective-permute-start(f32[4,32,256]{1,0,2:T(4,128)} %get-tuple-element.92), channel_id=1, source_target_pairs={{16,0},{32,16},{48,32},{64,48},{80,64},{96,80},{112,96},{17,1},{33... | collective-permute-start | bytes 393224 | tf_op jit(solution)/shard_map/ppermute | solution.py:21
  249.7 23.5 %collective-permute-start.5 = (f32[16,4,512]{2,1,0:T(4,128)S(1)}, f32[16,4,512]{2,1,0:T(4,128)S(1)}, u32[]{:S(2)}, u32[]{:S(2)}) collective-permute-start(f32[16,4,512]{2,1,0:T(4,128)S(1)} %get-tuple-element.127), channel_id=1, source_target_pairs={{16,0},{32,16},{48,32},{64,48},{80,64},{96,80},{112,96},{17,1},{33... | collective-permute-start | bytes 393224 | tf_op jit(solution)/shard_map/ppermute | solution.py:21
  253.0 20.2 %collective-permute-start.4 = (f32[16,4,512]{2,1,0:T(4,128)S(1)}, f32[16,4,512]{2,1,0:T(4,128)S(1)}, u32[]{:S(2)}, u32[]{:S(2)}) collective-permute-start(f32[16,4,512]{2,1,0:T(4,128)S(1)} %get-tuple-element.126), channel_id=1, source_target_pairs={{0,16},{16,32},{32,48},{48,64},{64,80},{80,96},{96,112},{1,17},{17... | collective-permute-start | bytes 393224 | tf_op jit(solution)/shard_map/ppermute | solution.py:18
  262.8 19.6 %collective-permute-start.26 = (f32[24,4,256]{2,0,1:T(8,128)S(1)}, f32[24,4,256]{2,0,1:T(8,128)S(1)}, u32[]{:S(2)}, u32[]{:S(2)}) collective-permute-start(f32[24,4,256]{2,0,1:T(8,128)S(1)} %copy.234), channel_id=1, source_target_pairs={{1,0},{2,1},{3,2},{4,3},{5,4},{6,5},{7,6},{8,7},{9,8},{10,9},{11,1... | collective-permute-start | bytes 294920 | tf_op jit(solution)/shard_map/ppermute | solution.py:21
  267.1 17.5 %collective-permute-start.27 = (f32[24,4,256]{2,0,1:T(8,128)S(1)}, f32[24,4,256]{2,0,1:T(8,128)S(1)}, u32[]{:S(2)}, u32[]{:S(2)}) collective-permute-start(f32[24,4,256]{2,0,1:T(8,128)S(1)} %copy.236), channel_id=1, source_target_pairs={{0,1},{1,2},{2,3},{3,4},{4,5},{5,6},{6,7},{7,8},{8,9},{9,10},{10,1... | collective-permute-start | bytes 294920 | tf_op jit(solution)/shard_map/ppermute | solution.py:18
  274.0 63.5 %collective-permute-start.6 = (f32[4,24,512]{2,1,0:T(8,128)}, f32[4,24,512]{2,1,0:T(8,128)}, u32[]{:S(2)}, u32[]{:S(2)}) collective-permute-start(f32[4,24,512]{2,1,0:T(8,128)} %get-tuple-element.107), channel_id=1, source_target_pairs={{1,0},{2,1},{3,2},{4,3},{5,4},{6,5},{7,6},{8,7},{9,8},{10,9},{11,1... | collective-permute-start | bytes 589832 | tf_op jit(solution)/shard_map/ppermute | solution.py:21
  275.9 61.5 %collective-permute-start.7 = (f32[4,24,512]{2,1,0:T(8,128)}, f32[4,24,512]{2,1,0:T(8,128)}, u32[]{:S(2)}, u32[]{:S(2)}) collective-permute-start(f32[4,24,512]{2,1,0:T(8,128)} %get-tuple-element.106), channel_id=1, source_target_pairs={{0,1},{1,2},{2,3},{3,4},{4,5},{5,6},{6,7},{7,8},{8,9},{9,10},{10,1... | collective-permute-start | bytes 589832 | tf_op jit(solution)/shard_map/ppermute | solution.py:18
  330.1 21.1 %collective-permute-start.29 = (f32[4,32,256]{1,0,2:T(4,128)S(1)}, f32[4,32,256]{1,0,2:T(4,128)S(1)}, u32[]{:S(2)}, u32[]{:S(2)}) collective-permute-start(f32[4,32,256]{1,0,2:T(4,128)S(1)} %get-tuple-element.91), channel_id=1, source_target_pairs={{0,16},{16,32},{32,48},{48,64},{64,80},{80,96},{96,112},{1,17},{17... | collective-permute-start | bytes 393224 | tf_op jit(solution)/shard_map/ppermute | solution.py:18
  332.0 19.2 %collective-permute-start.28 = (f32[4,32,256]{1,0,2:T(4,128)S(1)}, f32[4,32,256]{1,0,2:T(4,128)S(1)}, u32[]{:S(2)}, u32[]{:S(2)}) collective-permute-start(f32[4,32,256]{1,0,2:T(4,128)S(1)} %get-tuple-element.90), channel_id=1, source_target_pairs={{16,0},{32,16},{48,32},{64,48},{80,64},{96,80},{112,96},{17,1},{33... | collective-permute-start | bytes 393224 | tf_op jit(solution)/shard_map/ppermute | solution.py:21
  343.7 53.5 %copy-start.19 = (f32[16,16,512]{2,1,0:T(8,128)}, f32[16,16,512]{2,1,0:T(8,128)S(1)}, u32[]{:S(2)}) copy-start(f32[16,16,512]{2,1,0:T(8,128)S(1)} %get-tuple-element.67) | copy-start | bytes 1572868
  343.8 8.4 %collective-permute-start.16 = (f32[16,4,512]{2,1,0:T(4,128)S(1)}, f32[16,4,512]{2,1,0:T(4,128)S(1)}, u32[]{:S(2)}, u32[]{:S(2)}) collective-permute-start(f32[16,4,512]{2,1,0:T(4,128)S(1)} %get-tuple-element.125), channel_id=1, source_target_pairs={{0,16},{16,32},{32,48},{48,64},{64,80},{80,96},{96,112},{1,17},{17... | collective-permute-start | bytes 393224 | tf_op jit(solution)/shard_map/ppermute | solution.py:18
  345.7 7.4 %collective-permute-start.17 = (f32[16,4,512]{2,1,0:T(4,128)S(1)}, f32[16,4,512]{2,1,0:T(4,128)S(1)}, u32[]{:S(2)}, u32[]{:S(2)}) collective-permute-start(f32[16,4,512]{2,1,0:T(4,128)S(1)} %get-tuple-element.124), channel_id=1, source_target_pairs={{16,0},{32,16},{48,32},{64,48},{80,64},{96,80},{112,96},{17,1},{33... | collective-permute-start | bytes 393224 | tf_op jit(solution)/shard_map/ppermute | solution.py:21
  353.2 43.1 %collective-permute-start.18 = (f32[4,24,512]{2,1,0:T(8,128)S(1)}, f32[4,24,512]{2,1,0:T(8,128)S(1)}, u32[]{:S(2)}, u32[]{:S(2)}) collective-permute-start(f32[4,24,512]{2,1,0:T(8,128)S(1)} %get-tuple-element.103), channel_id=1, source_target_pairs={{1,0},{2,1},{3,2},{4,3},{5,4},{6,5},{7,6},{8,7},{9,8},{10,9},{11,1... | collective-permute-start | bytes 589832 | tf_op jit(solution)/shard_map/ppermute | solution.py:21
  355.1 41.2 %collective-permute-start.19 = (f32[4,24,512]{2,1,0:T(8,128)S(1)}, f32[4,24,512]{2,1,0:T(8,128)S(1)}, u32[]{:S(2)}, u32[]{:S(2)}) collective-permute-start(f32[4,24,512]{2,1,0:T(8,128)S(1)} %get-tuple-element.102), channel_id=1, source_target_pairs={{0,1},{1,2},{2,3},{3,4},{4,5},{5,6},{6,7},{7,8},{8,9},{9,10},{10,1... | collective-permute-start | bytes 589832 | tf_op jit(solution)/shard_map/ppermute | solution.py:18
  367.3 24.5 %collective-permute-start.30 = (f32[24,4,256]{2,0,1:T(8,128)S(1)}, f32[24,4,256]{2,0,1:T(8,128)S(1)}, u32[]{:S(2)}, u32[]{:S(2)}) collective-permute-start(f32[24,4,256]{2,0,1:T(8,128)S(1)} %copy.241), channel_id=1, source_target_pairs={{1,0},{2,1},{3,2},{4,3},{5,4},{6,5},{7,6},{8,7},{9,8},{10,9},{11,1... | collective-permute-start | bytes 294920 | tf_op jit(solution)/shard_map/ppermute | solution.py:21
  371.6 22.4 %collective-permute-start.31 = (f32[24,4,256]{2,0,1:T(8,128)S(1)}, f32[24,4,256]{2,0,1:T(8,128)S(1)}, u32[]{:S(2)}, u32[]{:S(2)}) collective-permute-start(f32[24,4,256]{2,0,1:T(8,128)S(1)} %copy.243), channel_id=1, source_target_pairs={{0,1},{1,2},{2,3},{3,4},{4,5},{5,6},{6,7},{7,8},{8,9},{9,10},{10,1... | collective-permute-start | bytes 294920 | tf_op jit(solution)/shard_map/ppermute | solution.py:18
  384.9 55.4 %all-to-all-start.1 = ((bf16[16,2,4096]{2,1,0:T(2,128)(2,1)}), bf16[16,2,4096]{2,1,0:T(2,128)(2,1)}, u32[]{:S(2)}, u32[]{:S(2)}) async-start(bf16[16,2,4096]{2,1,0:T(2,128)(2,1)} %reshape.239), calls=%async_computation.1 | async-start | bytes 524288 | tf_op jit(solution)/shard_map/all_to_all | solution.py:106
  400.9 11.0 %collective-permute-start.21 = (f32[16,4,512]{2,1,0:T(4,128)S(1)}, f32[16,4,512]{2,1,0:T(4,128)S(1)}, u32[]{:S(2)}, u32[]{:S(2)}) collective-permute-start(f32[16,4,512]{2,1,0:T(4,128)S(1)} %get-tuple-element.123), channel_id=1, source_target_pairs={{16,0},{32,16},{48,32},{64,48},{80,64},{96,80},{112,96},{17,1},{33... | collective-permute-start | bytes 393224 | tf_op jit(solution)/shard_map/ppermute | solution.py:21
  406.8 8.4 %collective-permute-start.20 = (f32[16,4,512]{2,1,0:T(4,128)S(1)}, f32[16,4,512]{2,1,0:T(4,128)S(1)}, u32[]{:S(2)}, u32[]{:S(2)}) collective-permute-start(f32[16,4,512]{2,1,0:T(4,128)S(1)} %get-tuple-element.122), channel_id=1, source_target_pairs={{0,16},{16,32},{32,48},{48,64},{64,80},{80,96},{96,112},{1,17},{17... | collective-permute-start | bytes 393224 | tf_op jit(solution)/shard_map/ppermute | solution.py:18
  415.3 12.4 %collective-permute-start.22 = (f32[4,24,512]{2,1,0:T(8,128)S(1)}, f32[4,24,512]{2,1,0:T(8,128)S(1)}, u32[]{:S(2)}, u32[]{:S(2)}) collective-permute-start(f32[4,24,512]{2,1,0:T(8,128)S(1)} %get-tuple-element.99), channel_id=1, source_target_pairs={{1,0},{2,1},{3,2},{4,3},{5,4},{6,5},{7,6},{8,7},{9,8},{10,9},{11,1... | collective-permute-start | bytes 589832 | tf_op jit(solution)/shard_map/ppermute | solution.py:21
  418.7 8.9 %collective-permute-start.23 = (f32[4,24,512]{2,1,0:T(8,128)S(1)}, f32[4,24,512]{2,1,0:T(8,128)S(1)}, u32[]{:S(2)}, u32[]{:S(2)}) collective-permute-start(f32[4,24,512]{2,1,0:T(8,128)S(1)} %get-tuple-element.98), channel_id=1, source_target_pairs={{0,1},{1,2},{2,3},{3,4},{4,5},{5,6},{6,7},{7,8},{8,9},{9,10},{10,1... | collective-permute-start | bytes 589832 | tf_op jit(solution)/shard_map/ppermute | solution.py:18
  440.3 45.2 %all-to-all-start.2 = ((bf16[16,2,4096]{2,1,0:T(2,128)(2,1)}), bf16[16,2,4096]{2,1,0:T(2,128)(2,1)S(1)}, u32[]{:S(2)}, u32[]{:S(2)}) async-start(bf16[16,2,4096]{2,1,0:T(2,128)(2,1)} %reshape.237), calls=%async_computation.2 | async-start | bytes 524288 | tf_op jit(solution)/shard_map/all_to_all | solution.py:106
  447.6 27.3 %copy-start.50 = (f32[1,4096]{1,0:T(1,128)S(1)}, f32[1,4096]{1,0:T(1,128)}, u32[]{:S(2)}) copy-start(f32[1,4096]{1,0:T(1,128)} %get-tuple-element.139) | copy-start | bytes 49156
  447.6 27.3 %copy-start.57 = (s32[4096]{0:T(1024)S(1)}, s32[4096]{0:T(1024)}, u32[]{:S(2)}) copy-start(s32[4096]{0:T(1024)} %param.31) | copy-start | bytes 49156
  (52 other events, 409.1 us)
where the time goes:
time: 510 us; the launch traced here: 500 us
  other arithmetic  188 us (37%)
  starting transfers between devices  143 us (28%)
  local copies, waits for them, and re-layouts  139 us (27%)
  waiting for transfers between devices  13.5 us (3%)
  between operations  9.9 us (2%)
  matrix products  6.01 us (1%)
    add x4, other arithmetic, on_device(): 2.0 * receiver_now - receiver_next + velocity * laplace(padded_rcv, 0)  114 us
    ppermute x16, starting transfers between devices, padded_2(): lax.ppermute(lax.slice_in_dim(block, block.shape[dim] - width, None, axis...  60.9 us
    ppermute x16, starting transfers between devices, padded_2(): lax.ppermute(lax.slice_in_dim(block, 0, width, axis=dim), axis, backward)  60.5 us
    unnamed x153, local copies, waits for them, and re-layouts  58.4 us
    concatenate x22, other arithmetic, padded_2(): block = jnp.concatenate([low, block, high], axis=dim)  47.6 us
    slice x8, local copies, waits for them, and re-layouts, padded_2(): lax.slice_in_dim(block, block.shape[dim] - width, None, axis=dim)  18 us
    all_to_all x2, starting transfers between devices, on_device(): lax.all_to_all(source_now.astype(jnp.bfloat16), 'gy', split_axis=2, conca...  14.3 us
    slice x10, local copies, waits for them, and re-layouts, padded_2(): lax.slice_in_dim(block, 0, width, axis=dim)  14.2 us
  transfers between devices with their start and end apart: 35, of which 4 were waited for; matrix products, arithmetic and copies ran while one was open for 62% of the time, Pallas kernels for 0%

commit v1 on v0

v1 whole, which is shorter than its diff:
```python
import jax
import jax.numpy as jnp
from jax import lax
from jax.experimental import pallas as pl
from jax.experimental.pallas import tpu as pltpu
from jax.sharding import PartitionSpec as P

STEPS = 4
C0, C1, C2, C3, C4 = (-205.0 / 72.0, 8.0 / 5.0, -1.0 / 5.0, 8.0 / 315.0, -1.0 / 560.0)
COEFFS = (C0, C1, C2, C3, C4)
RECEIVER_PLANE = 2
PLANES = 5
F32, BF16 = jnp.float32, jnp.bfloat16
VMEM_LIMIT = 48 * 1024 * 1024

RCV = dict(lead=16, rows=32, lanes=256)
SRC = dict(lead=16, rows=16, lanes=512)


def padded_shape(f):
    return (f["lanes"] // 128, f["lead"] + 8, f["rows"] + 16, 128)


def flat(ref):
    return ref.reshape(ref.shape[0], ref.shape[1] * ref.shape[2], 128)


def split(value):
    high = value.astype(BF16)
    return high, (value - high.astype(F32)).astype(BF16)


def planes_of(layers):
    return [*split(layers[0]), *[layer.astype(BF16) for layer in layers[1:]]]


def layers_of(planes):
    planes = [plane.astype(F32) for plane in planes]
    return [planes[0] + planes[1], *planes[2:]]


def pack_halos(src, rcv, gx_low, gx_high, gy_low, gy_high):
    for out_x, out_y, side in ((gx_low, gy_low, 0), (gx_high, gy_high, 1)):
        order = [0, 1, 2, 3] if side == 0 else [15, 14, 13, 12]
        order_y = [0, 1, 2, 3] if side == 0 else [31, 30, 29, 28]
        for t in range(4):
            lanes = slice(t * 128, t * 128 + 128)
            half, col = divmod(t, 2)
            layers = [rcv[col, a * 32 + half * 16 : a * 32 + half * 16 + 16, :] for a in order]
            for p, plane in enumerate(planes_of(layers)):
                out_x[p, :, lanes] = plane
            layers = [src[t, pl.ds(b, 16, stride=16), :] for b in order]
            for p, plane in enumerate(planes_of(layers)):
                out_x[PLANES + p, :, lanes] = plane
            layers = [src[t, a * 16 : a * 16 + 16, :] for a in order]
            for p, plane in enumerate(planes_of(layers)):
                out_y[p, :, lanes] = plane
        for col in range(2):
            layers = [rcv[col, pl.ds(b, 16, stride=32), :] for b in order_y]
            for p, plane in enumerate(planes_of(layers)):
                q, lane = PLANES + p // 2, (p % 2) * 256 + col * 128
                out_y[q, :, lane : lane + 128] = plane


def unpack_halos(psrc, prcv, gx_low, gx_high, gy_low, gy_high):
    ix, iy = lax.axis_index("gx"), lax.axis_index("gy")
    for in_x, in_y, side, live_x, live_y in (
        (gx_low, gy_low, 0, ix > 0, iy > 0),
        (gx_high, gy_high, 1, ix < 7, iy < 15),
    ):
        live_x, live_y = jnp.broadcast_to(live_x, (16, 128)), jnp.broadcast_to(live_y, (16, 128))
        for t in range(4):
            lanes = slice(t * 128, t * 128 + 128)
            half, col = divmod(t, 2)
            for h, layer in enumerate(layers_of([in_x[p, :, lanes] for p in range(PLANES)])):
                row = (3 - h if side == 0 else 20 + h) * 48 + 8 + half * 16
                prcv[col, row : row + 16, :] = jnp.where(live_x, layer, 0.0)
            for h, layer in enumerate(layers_of([in_x[PLANES + p, :, lanes] for p in range(PLANES)])):
                row = 4 * 32 + (7 - h if side == 0 else 24 + h)
                psrc[t, pl.ds(row, 16, stride=32), :] = jnp.where(live_x, layer, 0.0)
            for h, layer in enumerate(layers_of([in_y[p, :, lanes] for p in range(PLANES)])):
                row = (3 - h if side == 0 else 20 + h) * 32 + 8
                psrc[t, row : row + 16, :] = jnp.where(live_y, layer, 0.0)
        for col in range(2):
            planes = []
            for p in range(PLANES):
                lane = (p % 2) * 256 + col * 128
                planes.append(in_y[PLANES + p // 2, :, lane : lane + 128])
            for h, layer in enumerate(layers_of(planes)):
                row = 4 * 48 + (7 - h if side == 0 else 40 + h)
                prcv[col, pl.ds(row, 16, stride=48), :] = jnp.where(live_y, layer, 0.0)


def column(ref, rows, t):
    return ref.at[rows, pl.ds(t * 128, 128)] if len(ref.shape) == 2 else ref.at[t, rows, :]


def step_field(f, padded, nxt, vel, out, inject=None):
    rows, tiles = f["rows"], f["lanes"] // 128
    stride = rows + 16
    lane = lax.broadcasted_iota(jnp.int32, (rows, 128), 1)
    below = {k: lane < k for k in range(1, 5)}
    above = {k: lane >= 128 - k for k in range(1, 5)}

    def layer(a, carry):
        base = pl.multiple_of((a + 4) * stride, 8)
        here = [padded[t, pl.ds(base + 8, rows), :] for t in range(tiles)]
        around = [padded[t, pl.ds(base, stride), :] for t in range(tiles)]
        total = [(3.0 * C0) * c for c in here]
        for k in range(1, 5):
            up = [pltpu.roll(c, k, 1) for c in here]
            down = [pltpu.roll(c, 128 - k, 1) for c in here]
            for t in range(tiles):
                s = padded[t, pl.ds(pl.multiple_of(base + 8 - k * stride, 8), rows), :]
                s = s + padded[t, pl.ds(pl.multiple_of(base + 8 + k * stride, 8), rows), :]
                s = s + around[t][8 - k : 8 - k + rows]
                s = s + around[t][8 + k : 8 + k + rows]
                s = s + jnp.where(below[k], up[t - 1] if t > 0 else 0.0, up[t])
                s = s + jnp.where(above[k], down[t + 1] if t + 1 < tiles else 0.0, down[t])
                total[t] = total[t] + COEFFS[k] * s
        at = pl.ds(pl.multiple_of(a * rows, 8), rows)
        for t in range(tiles):
            value = 2.0 * here[t] - column(nxt, at, t)[...] + column(vel, at, t)[...] * total[t]
            if inject is not None and t == 0:
                value = value + jnp.where(
                    lane == RECEIVER_PLANE, pltpu.roll(inject, RECEIVER_PLANE + 128 - a, 1), 0.0
                )
            column(out, at, t)[...] = value
        return carry

    lax.fori_loop(0, f["lead"], layer, 0)


def pack_brick(src, out):
    group = lax.broadcasted_iota(jnp.int32, (16, 128), 1) // 32
    for t in range(4):
        for xg in range(4):
            rows = [src[t, pl.ds(xg * 4 + xl, 16, stride=16), :] for xl in range(4)]
            for g in range(4):
                piece = None
                for xl in range(4):
                    turned = rows[xl] if xl == g else pltpu.roll(rows[xl], ((xl - g) % 4) * 32, 1)
                    piece = turned if piece is None else jnp.where(group == xl, turned, piece)
                out[t * 4 + g, :, xg * 128 : xg * 128 + 128] = piece.astype(BF16)


def unpack_velocity(pieces, out):
    group = lax.broadcasted_iota(jnp.int32, (16, 128), 1) // 32
    for t in range(4):
        for xg in range(4):
            parts = [pieces[t * 4 + g, :, xg * 128 : xg * 128 + 128] for g in range(4)]
            for xl in range(4):
                row = None
                for g in range(4):
                    turned = parts[g] if xl == g else pltpu.roll(parts[g], ((g - xl) % 4) * 32, 1)
                    row = turned if row is None else jnp.where(group == g, turned, row)
                out[t, pl.ds(xg * 4 + xl, 16, stride=16), :] = row


GX_BUF = jax.ShapeDtypeStruct((2 * PLANES, 16, 512), BF16)
GY_BUF = jax.ShapeDtypeStruct((PLANES + 3, 16, 512), BF16)
SRC_COLS = jax.ShapeDtypeStruct((4, 256, 128), F32)
RCV_COLS = jax.ShapeDtypeStruct((2, 512, 128), F32)
BRICKS = jax.ShapeDtypeStruct((16, 2, 16, 512), BF16)
VM = pl.BlockSpec(memory_space=pltpu.VMEM)
SM = pl.BlockSpec(memory_space=pltpu.SMEM)
HB = pl.BlockSpec(memory_space=pl.ANY)


def params():
    return pltpu.CompilerParams(vmem_limit_bytes=VMEM_LIMIT)


def column_copies(block, cols, sem):
    if len(block.shape) == 4:
        return [pltpu.make_async_copy(block, cols, sem)]
    return [
        pltpu.make_async_copy(block.at[:, :, pl.ds(t * 128, 128)], cols.at[t], sem) for t in range(cols.shape[0])
    ]


def first_halos(src, rcv):
    def kernel(src, rcv, gx_low, gx_high, gy_low, gy_high, src_cols, rcv_cols, sem):
        copies = column_copies(src, src_cols, sem) + column_copies(rcv, rcv_cols, sem)
        for copy in copies:
            copy.start()
        for copy in copies:
            copy.wait()
        pack_halos(flat(src_cols), flat(rcv_cols), gx_low, gx_high, gy_low, gy_high)

    return pl.pallas_call(
        kernel,
        out_shape=[GX_BUF, GX_BUF, GY_BUF, GY_BUF],
        in_specs=[HB] * 2,
        out_specs=[VM] * 4,
        scratch_shapes=[
            pltpu.VMEM((4, 16, 16, 128), F32),
            pltpu.VMEM((2, 16, 32, 128), F32),
            pltpu.SemaphoreType.DMA,
        ],
        compiler_params=params(),
        name="first_halos",
    )(src, rcv)


def turn_velocity(vel):
    def kernel(vel, out):
        for q in range(4):
            out[:, q * 128 : q * 128 + 128] = vel[q * 128 : q * 128 + 128, :].T

    return pl.pallas_call(
        kernel,
        out_shape=jax.ShapeDtypeStruct((256, 512), F32),
        in_specs=[VM],
        out_specs=VM,
        compiler_params=params(),
        name="turn_velocity",
    )(vel)


def injections(traces, receiver_x, receiver_y):
    def kernel(traces, rx, ry, out):
        x0, y0 = lax.axis_index("gx") * 16, lax.axis_index("gy") * 32
        xs = x0 + lax.broadcasted_iota(jnp.int32, (128, 512), 0)
        ys = y0 + lax.broadcasted_iota(jnp.int32, (32, 512), 0)
        total = jnp.zeros((128, 128), F32)
        for c in range(8):
            cols = slice(c * 512, c * 512 + 512)
            at_x = jnp.where(rx[:, cols] == xs, 1.0, 0.0)
            at_y = ry[:, cols] == ys
            weighted = jnp.concatenate(
                [jnp.where(at_y, traces[s : s + 1, cols], 0.0) for s in range(STEPS)], axis=0
            )
            total = total + lax.dot_general(
                weighted,
                at_x,
                (((1,), (1,)), ((), ())),
                precision=lax.Precision.HIGHEST,
                preferred_element_type=F32,
            )
        out[...] = total

    return pl.pallas_call(
        kernel,
        out_shape=jax.ShapeDtypeStruct((128, 128), F32),
        in_specs=[VM] * 3,
        out_specs=VM,
        compiler_params=params(),
        name="injections",
    )(traces, receiver_x.reshape(1, -1), receiver_y.reshape(1, -1))


def one_step(step, src, src_next, rcv, rcv_next, vel_src, vel, halos, saved, plane_index, wavelet, cell, inject):
    first, last = step == 0, step == STEPS - 1

    def kernel(*refs):
        (src, src_next, rcv, rcv_next, vel_src, vel, gxl, gxh, gyl, gyh, saved, plane_index, wavelet, cell, inject) = (
            refs[:15]
        )
        outs = refs[15:]
        src_out, rcv_out = outs[:2]
        padded_src, padded_rcv, plane, sems = outs[-5:-1]
        src_cols = outs[-1] if last else src_out
        ix, iy = lax.axis_index("gx"), lax.axis_index("gy")
        copies = column_copies(src, padded_src.at[:, pl.ds(4, 16), pl.ds(8, 16), :], sems.at[0])
        copies += column_copies(rcv, padded_rcv.at[:, pl.ds(4, 16), pl.ds(8, 32), :], sems.at[0])
        for copy in copies:
            copy.start()
        edge = (ix == 0) | (ix == 7)
        side = jnp.where(ix == 0, 0, 1)
        restores = [
            pltpu.make_async_copy(
                saved.at[plane_index[step], side, pl.ds(pl.multiple_of(iy * 16, 16), 16), pl.ds(t * 128, 128)],
                plane.at[t],
                sems.at[1],
            )
            for t in range(4)
        ]

        @pl.when(edge)
        def _():
            for copy in restores:
                copy.start()

        psrc, prcv = flat(padded_src), flat(padded_rcv)
        if first:
            velocity_src = outs[2]
            unpack_velocity(vel_src, velocity_src)
        else:
            velocity_src = vel_src
        unpack_halos(psrc, prcv, gxl, gxh, gyl, gyh)
        for copy in copies:
            copy.wait()
        step_field(SRC, psrc, src_next, velocity_src, src_cols)
        z, x, y = cell[2] - iy * 16, cell[0] - ix * 16, cell[1]

        @pl.when((z >= 0) & (z < 16) & (x >= 0) & (x < 16))
        def _():
            at = pl.ds(z * 16 + x, 1)
            lanes = lax.broadcasted_iota(jnp.int32, (1, 128), 1)
            for t in range(4):
                src_cols[t, at, :] = src_cols[t, at, :] + jnp.where(lanes + t * 128 == y, wavelet[step], 0.0)

        @pl.when(edge)
        def _():
            for copy in restores:
                copy.wait()

        @pl.when(ix == 0)
        def _():
            for t in range(4):
                src_cols[t, pl.ds(0, 16, stride=16), :] = plane[t]

        @pl.when(ix == 7)
        def _():
            for t in range(4):
                src_cols[t, pl.ds(15, 16, stride=16), :] = plane[t]

        step_field(RCV, prcv, rcv_next, vel, rcv_out, inject[step * 32 : step * 32 + 32, :])
        if last:
            bricks = outs[2]
            result = [
                pltpu.make_async_copy(src_cols.at[t], src_out.at[:, pl.ds(t * 128, 128)], sems.at[0])
                for t in range(4)
            ]
            for copy in result:
                copy.start()
            pack_brick(src_next, bricks.at[:, 0])
            pack_brick(src_cols, bricks.at[:, 1])
            for copy in result:
                copy.wait()
        else:
            pack_halos(src_out, rcv_out, *(outs[3:7] if first else outs[2:6]))

    out_shape = [SRC_COLS, RCV_COLS]
    if first:
        out_shape.append(SRC_COLS)
    if last:
        out_shape = [jax.ShapeDtypeStruct((256, 512), F32), jax.ShapeDtypeStruct((512, 256), F32), BRICKS]
    else:
        out_shape += [GX_BUF, GX_BUF, GY_BUF, GY_BUF]
    return pl.pallas_call(
        kernel,
        out_shape=out_shape,
        in_specs=[HB, VM, HB, VM, VM, VM, VM, VM, VM, VM, HB, SM, SM, SM, VM],
        out_specs=[HB if last else VM] + [VM] * (len(out_shape) - 1),
        scratch_shapes=[
            pltpu.VMEM(padded_shape(SRC), F32),
            pltpu.VMEM(padded_shape(RCV), F32),
            pltpu.VMEM((4, 16, 128), F32),
            pltpu.SemaphoreType.DMA((2,)),
        ]
        + ([pltpu.VMEM((4, 256, 128), F32)] if last else [pltpu.VMEM((8, 128), F32)]),
        compiler_params=params(),
        name=f"step{step}",
    )(src, src_next, rcv, rcv_next, vel_src, vel, *halos, saved, plane_index, wavelet, cell, inject)


def make_image(bricks, rcv_early, rcv_late):
    def kernel(bricks, rcv_early, rcv_late, out):
        for q in range(4):
            rows, cols = slice(q * 128, q * 128 + 128), slice(q * 128, q * 128 + 128)
            early = bricks[:, 0, :, cols].reshape(256, 128).astype(F32).T
            late = bricks[:, 1, :, cols].reshape(256, 128).astype(F32).T
            for t in range(2):
                lanes = slice(t * 128, t * 128 + 128)
                out[rows, lanes] = early[:, lanes] * rcv_early[t, rows, :] + late[:, lanes] * rcv_late[rows, lanes]

    return pl.pallas_call(
        kernel,
        out_shape=jax.ShapeDtypeStruct((512, 256), F32),
        in_specs=[VM] * 3,
        out_specs=VM,
        compiler_params=params(),
        name="make_image",
    )(bricks, rcv_early, rcv_late)


def exchange(buffers):
    gx_low, gx_high, gy_low, gy_high = buffers
    ring = lambda n, by: [(i, (i + by) % n) for i in range(n)]
    return (
        lax.ppermute(gx_high, "gx", ring(8, 1)),
        lax.ppermute(gx_low, "gx", ring(8, -1)),
        lax.ppermute(gy_high, "gy", ring(16, 1)),
        lax.ppermute(gy_low, "gy", ring(16, -1)),
    )


def on_device(
    source_now,
    source_next,
    receiver_now,
    receiver_next,
    velocity,
    saved_planes,
    plane_index,
    wavelet,
    source_cell,
    traces,
    receiver_x,
    receiver_y,
):
    src, src_next = source_now, source_next.reshape(256, 512)
    rcv, rcv_next = receiver_now, receiver_next.reshape(512, 256)
    vel = velocity.reshape(512, 256)
    halos = exchange(first_halos(src, rcv))
    turned = turn_velocity(vel).reshape(16, 16, 512)
    vel_src = lax.all_to_all(turned, "gy", split_axis=0, concat_axis=0, tiled=True)
    inject = injections(traces, receiver_x, receiver_y)
    for step in range(STEPS):
        outs = one_step(
            step, src, src_next, rcv, rcv_next, vel_src, vel, halos, saved_planes, plane_index, wavelet, source_cell, inject
        )
        if step == 0:
            vel_src = outs[2]
            src_next, rcv_next = source_now.reshape(256, 512), receiver_now.reshape(512, 256)
        else:
            src_next, rcv_next = src.reshape(4, 256, 128), rcv.reshape(2, 512, 128)
        if step == STEPS - 1:
            bricks = outs[2]
        else:
            halos = exchange(outs[-4:])
            if step == 1:
                rcv_early = outs[1]
            src, rcv = outs[0].reshape(4, 16, 16, 128), outs[1].reshape(2, 16, 32, 128)
    src, rcv = outs[:2]
    bricks = lax.all_to_all(bricks, "gy", split_axis=0, concat_axis=0, tiled=True)
    image = make_image(bricks, rcv_early, rcv)
    return (image.reshape(16, 32, 256), rcv.reshape(16, 32, 256), src.reshape(16, 16, 512))


def solution(mesh):
    field, turned = P("gx", "gy", None), P("gy", "gx", None)
    return jax.shard_map(
        on_device,
        mesh=mesh,
        in_specs=(turned, turned, field, field, field, P(), P(), P(), P(), P(), P(), P()),
        out_specs=(field, field, turned),
        check_vma=False,
    )
```

time: 510 us -> 119 us (0.23)
  the two profiles are of different devices: /device:TPU:25 before, /device:TPU:1 now
where the time goes in v1:
time: 119 us; the launch traced here: 118 us
  starting transfers between devices  35.4 us (30%)
  Pallas kernels  30.1 us (25%)
  waiting for transfers between devices  21.4 us (18%)
  blocking collectives  16.7 us (14%)
  local copies, waits for them, and re-layouts  13.6 us (11%)
    pallas_call x4, Pallas kernels, one_step(): pl.pallas_call(kernel, out_shape=out_shape, in_specs=[HB, VM, HB, VM, VM,...  25.7 us
    all_to_all x1, blocking collectives, on_device(): lax.all_to_all(bricks, 'gy', split_axis=0, concat_axis=0, tiled=True)  16.7 us
    unnamed x36, local copies, waits for them, and re-layouts  13.6 us
    ppermute x4, starting transfers between devices, exchange(): lax.ppermute(gx_low, 'gx', ring(8, -1))  13 us
    ppermute x4, waiting for transfers between devices, exchange(): lax.ppermute(gy_high, 'gy', ring(16, 1))  12.3 us
    ppermute x4, starting transfers between devices, exchange(): lax.ppermute(gy_high, 'gy', ring(16, 1))  12 us
    ppermute x4, waiting for transfers between devices, exchange(): lax.ppermute(gy_low, 'gy', ring(16, -1))  9.1 us
    all_to_all x1, starting transfers between devices, on_device(): lax.all_to_all(turned, 'gy', split_axis=0, concat_axis=0, tiled=True)  8.45 us
  transfers between devices with their start and end apart: 17, of which 7 were waited for; matrix products, arithmetic and copies ran while one was open for 0% of the time, Pallas kernels for 2%

profile of v1, /device:TPU:1, one launch (start us, length us, event | category | flops | bytes accessed | tf_op | source)
XLA Modules:
  0.0 118.0 jit_solution(16657373793193581306)
XLA Ops:
  0.6 0.0 copy-start
  0.6 1.0 copy-done
  1.7 1.0 turn_velocity.1
  2.7 8.4 %all-to-all-start = ((f32[16,16,512]{2,1,0:T(8,128)}), f32[16,16,512]{2,1,0:T(8,128)S(1)}, u32[]{:S(2)}, u32[]{:S(2)}) async-start(f32[16,16,512]{2,1,0:T(8,128)} %bitcast.3), calls=%async_computation | async-start | bytes 1048576 | tf_op jit(solution)/shard_map/all_to_all | solution.py:409
  11.1 1.0 copy-done.2
  12.2 1.0 copy-done.4
  13.2 0.3 first_halos.1
  13.5 0.0 copy-start.13
  13.6 0.0 copy-start.15
  13.6 0.0 copy-start.17
  13.6 1.7 %collective-permute-start = (bf16[10,16,512]{2,1,0:T(8,128)(2,1)S(1)}, bf16[10,16,512]{2,1,0:T(8,128)(2,1)S(1)}, u32[]{:S(2)}, u32[]{:S(2)}) collective-permute-start(bf16[10,16,512]{2,1,0:T(8,128)(2,1)S(1)} %get-tuple-element.29), channel_id=1, source_target_pairs={{0,16},{16,32},{32,48},{48,64},{64,80},{80,96},{96,112},{112,0},{1... | collective-permute-start | bytes 491528 | tf_op jit(solution)/shard_map/ppermute | solution.py:383
  15.3 2.3 %collective-permute-start.1 = (bf16[10,16,512]{2,1,0:T(8,128)(2,1)S(1)}, bf16[10,16,512]{2,1,0:T(8,128)(2,1)S(1)}, u32[]{:S(2)}, u32[]{:S(2)}) collective-permute-start(bf16[10,16,512]{2,1,0:T(8,128)(2,1)S(1)} %get-tuple-element.30), channel_id=1, source_target_pairs={{0,112},{16,0},{32,16},{48,32},{64,48},{80,64},{96,80},{112,96},{1... | collective-permute-start | bytes 491528 | tf_op jit(solution)/shard_map/ppermute | solution.py:384
  17.6 4.0 %collective-permute-start.2 = (bf16[8,16,512]{2,1,0:T(8,128)(2,1)S(1)}, bf16[8,16,512]{2,1,0:T(8,128)(2,1)S(1)}, u32[]{:S(2)}, u32[]{:S(2)}) collective-permute-start(bf16[8,16,512]{2,1,0:T(8,128)(2,1)S(1)} %get-tuple-element.31), channel_id=1, source_target_pairs={{0,1},{1,2},{2,3},{3,4},{4,5},{5,6},{6,7},{7,8},{8,9},{9,10},{10,1... | collective-permute-start | bytes 393224 | tf_op jit(solution)/shard_map/ppermute | solution.py:385
  21.6 0.8 copy-done.9
  22.5 0.7 copy-done.10
  23.2 0.7 copy-done.11
  23.9 2.0 %injections.1.refs_14_ = f32[128,128]{1,0:T(8,128)S(1)} custom-call(f32[4,4096]{1,0:T(4,128)S(1)} %copy-done.9, s32[1,4096]{1,0:T(1,128)S(1)} %bitcast.33, s32[1,4096]{1,0:T(1,128)S(1)} %bitcast.34), custom_call_target="tpu_custom_call" | custom-call | tf_op jit(solution)/shard_map/injections/pallas_call | solution.py:243
  25.9 2.9 %collective-permute-done.3.refs_9_ = bf16[8,16,512]{2,1,0:T(8,128)(2,1)S(1)} collective-permute-done((bf16[8,16,512]{2,1,0:T(8,128)(2,1)S(1)}, bf16[8,16,512]{2,1,0:T(8,128)(2,1)S(1)}, u32[]{:S(2)}, u32[]{:S(2)}) %collective-permute-start.3) | collective-permute-done | bytes 131104 | tf_op jit(solution)/shard_map/ppermute | solution.py:386
  28.9 1.0 copy-done.1
  29.9 1.0 copy-done.3
  30.9 1.0 copy-done.5
  32.0 1.0 copy-done.6
  33.0 1.0 copy-done.7
  34.1 0.7 copy-done.12
  34.7 0.7 copy-done.14
  35.4 0.7 copy-done.16
  36.0 6.3 %step0.1 = (f32[4,256,128]{2,1,0:T(8,128)S(1)}, f32[2,512,128]{2,1,0:T(8,128)S(1)}, f32[4,256,128]{2,1,0:T(8,128)S(1)}, bf16[10,16,512]{2,1,0:T(8,128)(2,1)S(1)}...) custom-call(f32[16,16,512]{2,1,0:T(8,128)S(1)} %copy-done.3, ...), custom_call_target="tpu_custom_call" | custom-call | tf_op jit(solution)/shard_map/step0/pallas_call | solution.py:342
  42.4 0.1 collective-permute-start.4
  42.4 3.6 %collective-permute-start.5 = (bf16[10,16,512]{2,1,0:T(8,128)(2,1)S(1)}, bf16[10,16,512]{2,1,0:T(8,128)(2,1)S(1)}, u32[]{:S(2)}, u32[]{:S(2)}) collective-permute-start(bf16[10,16,512]{2,1,0:T(8,128)(2,1)S(1)} %get-tuple-element.37), channel_id=1, source_target_pairs={{0,112},{16,0},{32,16},{48,32},{64,48},{80,64},{96,80},{112,96},{1... | collective-permute-start | bytes 491528 | tf_op jit(solution)/shard_map/ppermute | solution.py:384
  46.0 3.1 %collective-permute-start.6 = (bf16[8,16,512]{2,1,0:T(8,128)(2,1)S(1)}, bf16[8,16,512]{2,1,0:T(8,128)(2,1)S(1)}, u32[]{:S(2)}, u32[]{:S(2)}) collective-permute-start(bf16[8,16,512]{2,1,0:T(8,128)(2,1)S(1)} %get-tuple-element.38), channel_id=1, source_target_pairs={{0,1},{1,2},{2,3},{3,4},{4,5},{5,6},{6,7},{7,8},{8,9},{9,10},{10,1... | collective-permute-start | bytes 393224 | tf_op jit(solution)/shard_map/ppermute | solution.py:385
  49.1 3.7 %collective-permute-done.6.refs_8_ = bf16[8,16,512]{2,1,0:T(8,128)(2,1)S(1)} collective-permute-done((bf16[8,16,512]{2,1,0:T(8,128)(2,1)S(1)}, bf16[8,16,512]{2,1,0:T(8,128)(2,1)S(1)}, u32[]{:S(2)}, u32[]{:S(2)}) %collective-permute-start.6) | collective-permute-done | bytes 131104 | tf_op jit(solution)/shard_map/ppermute | solution.py:385
  52.8 2.6 %collective-permute-done.7.refs_9_ = bf16[8,16,512]{2,1,0:T(8,128)(2,1)S(1)} collective-permute-done((bf16[8,16,512]{2,1,0:T(8,128)(2,1)S(1)}, bf16[8,16,512]{2,1,0:T(8,128)(2,1)S(1)}, u32[]{:S(2)}, u32[]{:S(2)}) %collective-permute-start.7) | collective-permute-done | bytes 131104 | tf_op jit(solution)/shard_map/ppermute | solution.py:386
  55.4 5.9 %step1.1 = (f32[4,256,128]{2,1,0:T(8,128)S(1)}, f32[2,512,128]{2,1,0:T(8,128)S(1)}, bf16[10,16,512]{2,1,0:T(8,128)(2,1)S(1)}, bf16[10,16,512]{2,1,0:T(8,128)(2,1...) custom-call(f32[4,16,16,128]{3,2,1,0:T(8,128)S(1)} %bitcast.25, f32[256,512]{1,0:T(8,128)S(1)} %bitcast.22, ...), custom_call_target="tpu_custom_call" | custom-call | tf_op jit(solution)/shard_map/step1/pallas_call | solution.py:342
  61.3 0.1 collective-permute-start.8
  61.4 3.6 %collective-permute-start.9 = (bf16[10,16,512]{2,1,0:T(8,128)(2,1)S(1)}, bf16[10,16,512]{2,1,0:T(8,128)(2,1)S(1)}, u32[]{:S(2)}, u32[]{:S(2)}) collective-permute-start(bf16[10,16,512]{2,1,0:T(8,128)(2,1)S(1)} %get-tuple-element.43), channel_id=1, source_target_pairs={{0,112},{16,0},{32,16},{48,32},{64,48},{80,64},{96,80},{112,96},{1... | collective-permute-start | bytes 491528 | tf_op jit(solution)/shard_map/ppermute | solution.py:384
  65.0 2.0 %collective-permute-start.10 = (bf16[8,16,512]{2,1,0:T(8,128)(2,1)S(1)}, bf16[8,16,512]{2,1,0:T(8,128)(2,1)S(1)}, u32[]{:S(2)}, u32[]{:S(2)}) collective-permute-start(bf16[8,16,512]{2,1,0:T(8,128)(2,1)S(1)} %get-tuple-element.44), channel_id=1, source_target_pairs={{0,1},{1,2},{2,3},{3,4},{4,5},{5,6},{6,7},{7,8},{8,9},{9,10},{10,1... | collective-permute-start | bytes 393224 | tf_op jit(solution)/shard_map/ppermute | solution.py:385
  67.0 4.6 %collective-permute-done.10.refs_8_ = bf16[8,16,512]{2,1,0:T(8,128)(2,1)S(1)} collective-permute-done((bf16[8,16,512]{2,1,0:T(8,128)(2,1)S(1)}, bf16[8,16,512]{2,1,0:T(8,128)(2,1)S(1)}, u32[]{:S(2)}, u32[]{:S(2)}) %collective-permute-start.10) | collective-permute-done | bytes 131104 | tf_op jit(solution)/shard_map/ppermute | solution.py:385
  71.5 1.7 %collective-permute-done.11.refs_9_ = bf16[8,16,512]{2,1,0:T(8,128)(2,1)S(1)} collective-permute-done((bf16[8,16,512]{2,1,0:T(8,128)(2,1)S(1)}, bf16[8,16,512]{2,1,0:T(8,128)(2,1)S(1)}, u32[]{:S(2)}, u32[]{:S(2)}) %collective-permute-start.11) | collective-permute-done | bytes 131104 | tf_op jit(solution)/shard_map/ppermute | solution.py:386
  73.3 5.9 %step2.1 = (f32[4,256,128]{2,1,0:T(8,128)S(1)}, f32[2,512,128]{2,1,0:T(8,128)S(1)}, bf16[10,16,512]{2,1,0:T(8,128)(2,1)S(1)}, bf16[10,16,512]{2,1,0:T(8,128)(2,1...) custom-call(f32[4,16,16,128]{3,2,1,0:T(8,128)S(1)} %bitcast.27, ...), custom_call_target="tpu_custom_call" | custom-call | tf_op jit(solution)/shard_map/step2/pallas_call | solution.py:342
  79.2 0.1 collective-permute-start.12
  79.2 3.6 %collective-permute-start.13 = (bf16[10,16,512]{2,1,0:T(8,128)(2,1)S(1)}, bf16[10,16,512]{2,1,0:T(8,128)(2,1)S(1)}, u32[]{:S(2)}, u32[]{:S(2)}) collective-permute-start(bf16[10,16,512]{2,1,0:T(8,128)(2,1)S(1)} %get-tuple-element.49), channel_id=1, source_target_pairs={{0,112},{16,0},{32,16},{48,32},{64,48},{80,64},{96,80},{112,96},{1... | collective-permute-start | bytes 491528 | tf_op jit(solution)/shard_map/ppermute | solution.py:384
  82.8 2.8 %collective-permute-start.14 = (bf16[8,16,512]{2,1,0:T(8,128)(2,1)S(1)}, bf16[8,16,512]{2,1,0:T(8,128)(2,1)S(1)}, u32[]{:S(2)}, u32[]{:S(2)}) collective-permute-start(bf16[8,16,512]{2,1,0:T(8,128)(2,1)S(1)} %get-tuple-element.50), channel_id=1, source_target_pairs={{0,1},{1,2},{2,3},{3,4},{4,5},{5,6},{6,7},{7,8},{8,9},{9,10},{10,1... | collective-permute-start | bytes 393224 | tf_op jit(solution)/shard_map/ppermute | solution.py:385
  85.6 4.0 %collective-permute-done.14.refs_8_ = bf16[8,16,512]{2,1,0:T(8,128)(2,1)S(1)} collective-permute-done((bf16[8,16,512]{2,1,0:T(8,128)(2,1)S(1)}, bf16[8,16,512]{2,1,0:T(8,128)(2,1)S(1)}, u32[]{:S(2)}, u32[]{:S(2)}) %collective-permute-start.14) | collective-permute-done | bytes 131104 | tf_op jit(solution)/shard_map/ppermute | solution.py:385
  89.6 1.9 %collective-permute-done.15.refs_9_ = bf16[8,16,512]{2,1,0:T(8,128)(2,1)S(1)} collective-permute-done((bf16[8,16,512]{2,1,0:T(8,128)(2,1)S(1)}, bf16[8,16,512]{2,1,0:T(8,128)(2,1)S(1)}, u32[]{:S(2)}, u32[]{:S(2)}) %collective-permute-start.15) | collective-permute-done | bytes 131104 | tf_op jit(solution)/shard_map/ppermute | solution.py:386
  91.5 7.6 %step3.1 = (f32[256,512]{1,0:T(8,128)}, f32[512,256]{1,0:T(8,128)}, bf16[16,2,16,512]{3,2,1,0:T(8,128)(2,1)S(1)}) custom-call(f32[4,16,16,128]{3,2,1,0:T(8,128)S(1)} %bitcast.30, f32[4,256,128]{2,1,0:T(8,128)S(1)} %get-tuple-element.40.refs_1_, f32[2,16,32,128]{3,2,1,0:T(8,128)S(1)} %bitcast.31, f32[2,512,128]{2,1,0:T(8,128)S(1)} %get-tuple-element.41.refs_3_.rcv_early, ...), custom_call_target="tpu_custom_call" | custom-call | tf_op jit(solution)/shard_map/step3/pallas_call | solution.py:342
  99.2 16.7 %all_to_all.10.bricks = bf16[16,2,16,512]{3,2,1,0:T(8,128)(2,1)S(1)} all-to-all(bf16[16,2,16,512]{3,2,1,0:T(8,128)(2,1)S(1)} %get-tuple-element.52), channel_id=1, replica_groups=mesh['gx'=8,'gy'=16] {'gy'}, dimensions={0} | all-to-all | bytes 1048576 | tf_op jit(solution)/shard_map/all_to_all | solution.py:428
  115.9 1.0 copy-done.8
  117.0 1.0 make_image.1
  (31 shorter events, 0.1 us)
Async XLA Ops:
  0.6 1.0 copy-start
  2.7 26.2 %all-to-all-start = ((f32[16,16,512]{2,1,0:T(8,128)}), f32[16,16,512]{2,1,0:T(8,128)S(1)}, u32[]{:S(2)}, u32[]{:S(2)}) async-start(f32[16,16,512]{2,1,0:T(8,128)} %bitcast.3), calls=%async_computation | async-start | bytes 1048576 | tf_op jit(solution)/shard_map/all_to_all | solution.py:409
  11.1 1.0 copy-start.2
  12.2 1.0 copy-start.4
  13.5 41.9 %copy-start.13 = (s32[4]{0:T(128)S(1)}, s32[4]{0:T(128)}, u32[]{:S(2)}) copy-start(s32[4]{0:T(128)} %refs_11_.7) | copy-start | bytes 52
  13.6 41.9 %copy-start.15 = (f32[4]{0:T(128)S(1)}, f32[4]{0:T(128)}, u32[]{:S(2)}) copy-start(f32[4]{0:T(128)} %refs_12_.7) | copy-start | bytes 52
  13.6 41.9 %copy-start.17 = (s32[3]{0:T(128)S(1)}, s32[3]{0:T(128)}, u32[]{:S(2)}) copy-start(s32[3]{0:T(128)} %refs_13_.7) | copy-start | bytes 40
  13.6 15.3 %collective-permute-start = (bf16[10,16,512]{2,1,0:T(8,128)(2,1)S(1)}, bf16[10,16,512]{2,1,0:T(8,128)(2,1)S(1)}, u32[]{:S(2)}, u32[]{:S(2)}) collective-permute-start(bf16[10,16,512]{2,1,0:T(8,128)(2,1)S(1)} %get-tuple-element.29), channel_id=1, source_target_pairs={{0,16},{16,32},{32,48},{48,64},{64,80},{80,96},{96,112},{112,0},{1... | collective-permute-start | bytes 491528 | tf_op jit(solution)/shard_map/ppermute | solution.py:383
  15.3 13.5 %collective-permute-start.1 = (bf16[10,16,512]{2,1,0:T(8,128)(2,1)S(1)}, bf16[10,16,512]{2,1,0:T(8,128)(2,1)S(1)}, u32[]{:S(2)}, u32[]{:S(2)}) collective-permute-start(bf16[10,16,512]{2,1,0:T(8,128)(2,1)S(1)} %get-tuple-element.30), channel_id=1, source_target_pairs={{0,112},{16,0},{32,16},{48,32},{64,48},{80,64},{96,80},{112,96},{1... | collective-permute-start | bytes 491528 | tf_op jit(solution)/shard_map/ppermute | solution.py:384
  17.6 8.3 %collective-permute-start.2 = (bf16[8,16,512]{2,1,0:T(8,128)(2,1)S(1)}, bf16[8,16,512]{2,1,0:T(8,128)(2,1)S(1)}, u32[]{:S(2)}, u32[]{:S(2)}) collective-permute-start(bf16[8,16,512]{2,1,0:T(8,128)(2,1)S(1)} %get-tuple-element.31), channel_id=1, source_target_pairs={{0,1},{1,2},{2,3},{3,4},{4,5},{5,6},{6,7},{7,8},{8,9},{9,10},{10,1... | collective-permute-start | bytes 393224 | tf_op jit(solution)/shard_map/ppermute | solution.py:385
  21.6 7.2 %collective-permute-start.3 = (bf16[8,16,512]{2,1,0:T(8,128)(2,1)S(1)}, bf16[8,16,512]{2,1,0:T(8,128)(2,1)S(1)}, u32[]{:S(2)}, u32[]{:S(2)}) collective-permute-start(bf16[8,16,512]{2,1,0:T(8,128)(2,1)S(1)} %get-tuple-element.32), channel_id=1, source_target_pairs={{0,15},{1,0},{2,1},{3,2},{4,3},{5,4},{6,5},{7,6},{8,7},{9,8},{10,9... | collective-permute-start | bytes 393224 | tf_op jit(solution)/shard_map/ppermute | solution.py:386
  21.6 0.8 copy-start.9
  22.5 0.7 copy-start.10
  23.2 0.7 copy-start.11
  28.9 1.0 copy-start.1
  29.9 1.0 copy-start.3
  30.9 1.0 copy-start.5
  32.0 1.0 copy-start.6
  33.0 1.0 copy-start.7
  34.1 0.7 copy-start.12
  34.7 0.7 copy-start.14
  35.4 0.7 copy-start.16
  42.4 13.0 %collective-permute-start.4 = (bf16[10,16,512]{2,1,0:T(8,128)(2,1)S(1)}, bf16[10,16,512]{2,1,0:T(8,128)(2,1)S(1)}, u32[]{:S(2)}, u32[]{:S(2)}) collective-permute-start(bf16[10,16,512]{2,1,0:T(8,128)(2,1)S(1)} %get-tuple-element.36), channel_id=1, source_target_pairs={{0,16},{16,32},{32,48},{48,64},{64,80},{80,96},{96,112},{112,0},{1... | collective-permute-start | bytes 491528 | tf_op jit(solution)/shard_map/ppermute | solution.py:383
  42.4 13.0 %collective-permute-start.5 = (bf16[10,16,512]{2,1,0:T(8,128)(2,1)S(1)}, bf16[10,16,512]{2,1,0:T(8,128)(2,1)S(1)}, u32[]{:S(2)}, u32[]{:S(2)}) collective-permute-start(bf16[10,16,512]{2,1,0:T(8,128)(2,1)S(1)} %get-tuple-element.37), channel_id=1, source_target_pairs={{0,112},{16,0},{32,16},{48,32},{64,48},{80,64},{96,80},{112,96},{1... | collective-permute-start | bytes 491528 | tf_op jit(solution)/shard_map/ppermute | solution.py:384
  46.0 6.8 %collective-permute-start.6 = (bf16[8,16,512]{2,1,0:T(8,128)(2,1)S(1)}, bf16[8,16,512]{2,1,0:T(8,128)(2,1)S(1)}, u32[]{:S(2)}, u32[]{:S(2)}) collective-permute-start(bf16[8,16,512]{2,1,0:T(8,128)(2,1)S(1)} %get-tuple-element.38), channel_id=1, source_target_pairs={{0,1},{1,2},{2,3},{3,4},{4,5},{5,6},{6,7},{7,8},{8,9},{9,10},{10,1... | collective-permute-start | bytes 393224 | tf_op jit(solution)/shard_map/ppermute | solution.py:385
  49.1 6.3 %collective-permute-start.7 = (bf16[8,16,512]{2,1,0:T(8,128)(2,1)S(1)}, bf16[8,16,512]{2,1,0:T(8,128)(2,1)S(1)}, u32[]{:S(2)}, u32[]{:S(2)}) collective-permute-start(bf16[8,16,512]{2,1,0:T(8,128)(2,1)S(1)} %get-tuple-element.39), channel_id=1, source_target_pairs={{0,15},{1,0},{2,1},{3,2},{4,3},{5,4},{6,5},{7,6},{8,7},{9,8},{10,9... | collective-permute-start | bytes 393224 | tf_op jit(solution)/shard_map/ppermute | solution.py:386
  61.3 11.9 %collective-permute-start.8 = (bf16[10,16,512]{2,1,0:T(8,128)(2,1)S(1)}, bf16[10,16,512]{2,1,0:T(8,128)(2,1)S(1)}, u32[]{:S(2)}, u32[]{:S(2)}) collective-permute-start(bf16[10,16,512]{2,1,0:T(8,128)(2,1)S(1)} %get-tuple-element.42), channel_id=1, source_target_pairs={{0,16},{16,32},{32,48},{48,64},{64,80},{80,96},{96,112},{112,0},{1... | collective-permute-start | bytes 491528 | tf_op jit(solution)/shard_map/ppermute | solution.py:383
  61.4 11.9 %collective-permute-start.9 = (bf16[10,16,512]{2,1,0:T(8,128)(2,1)S(1)}, bf16[10,16,512]{2,1,0:T(8,128)(2,1)S(1)}, u32[]{:S(2)}, u32[]{:S(2)}) collective-permute-start(bf16[10,16,512]{2,1,0:T(8,128)(2,1)S(1)} %get-tuple-element.43), channel_id=1, source_target_pairs={{0,112},{16,0},{32,16},{48,32},{64,48},{80,64},{96,80},{112,96},{1... | collective-permute-start | bytes 491528 | tf_op jit(solution)/shard_map/ppermute | solution.py:384
  65.0 6.6 %collective-permute-start.10 = (bf16[8,16,512]{2,1,0:T(8,128)(2,1)S(1)}, bf16[8,16,512]{2,1,0:T(8,128)(2,1)S(1)}, u32[]{:S(2)}, u32[]{:S(2)}) collective-permute-start(bf16[8,16,512]{2,1,0:T(8,128)(2,1)S(1)} %get-tuple-element.44), channel_id=1, source_target_pairs={{0,1},{1,2},{2,3},{3,4},{4,5},{5,6},{6,7},{7,8},{8,9},{9,10},{10,1... | collective-permute-start | bytes 393224 | tf_op jit(solution)/shard_map/ppermute | solution.py:385
  67.0 6.3 %collective-permute-start.11 = (bf16[8,16,512]{2,1,0:T(8,128)(2,1)S(1)}, bf16[8,16,512]{2,1,0:T(8,128)(2,1)S(1)}, u32[]{:S(2)}, u32[]{:S(2)}) collective-permute-start(bf16[8,16,512]{2,1,0:T(8,128)(2,1)S(1)} %get-tuple-element.45), channel_id=1, source_target_pairs={{0,15},{1,0},{2,1},{3,2},{4,3},{5,4},{6,5},{7,6},{8,7},{9,8},{10,9... | collective-permute-start | bytes 393224 | tf_op jit(solution)/shard_map/ppermute | solution.py:386
  79.2 12.4 %collective-permute-start.12 = (bf16[10,16,512]{2,1,0:T(8,128)(2,1)S(1)}, bf16[10,16,512]{2,1,0:T(8,128)(2,1)S(1)}, u32[]{:S(2)}, u32[]{:S(2)}) collective-permute-start(bf16[10,16,512]{2,1,0:T(8,128)(2,1)S(1)} %get-tuple-element.48), channel_id=1, source_target_pairs={{0,16},{16,32},{32,48},{48,64},{64,80},{80,96},{96,112},{112,0},{1... | collective-permute-start | bytes 491528 | tf_op jit(solution)/shard_map/ppermute | solution.py:383
  79.2 12.3 %collective-permute-start.13 = (bf16[10,16,512]{2,1,0:T(8,128)(2,1)S(1)}, bf16[10,16,512]{2,1,0:T(8,128)(2,1)S(1)}, u32[]{:S(2)}, u32[]{:S(2)}) collective-permute-start(bf16[10,16,512]{2,1,0:T(8,128)(2,1)S(1)} %get-tuple-element.49), channel_id=1, source_target_pairs={{0,112},{16,0},{32,16},{48,32},{64,48},{80,64},{96,80},{112,96},{1... | collective-permute-start | bytes 491528 | tf_op jit(solution)/shard_map/ppermute | solution.py:384
  82.8 6.8 %collective-permute-start.14 = (bf16[8,16,512]{2,1,0:T(8,128)(2,1)S(1)}, bf16[8,16,512]{2,1,0:T(8,128)(2,1)S(1)}, u32[]{:S(2)}, u32[]{:S(2)}) collective-permute-start(bf16[8,16,512]{2,1,0:T(8,128)(2,1)S(1)} %get-tuple-element.50), channel_id=1, source_target_pairs={{0,1},{1,2},{2,3},{3,4},{4,5},{5,6},{6,7},{7,8},{8,9},{9,10},{10,1... | collective-permute-start | bytes 393224 | tf_op jit(solution)/shard_map/ppermute | solution.py:385
  85.6 5.9 %collective-permute-start.15 = (bf16[8,16,512]{2,1,0:T(8,128)(2,1)S(1)}, bf16[8,16,512]{2,1,0:T(8,128)(2,1)S(1)}, u32[]{:S(2)}, u32[]{:S(2)}) collective-permute-start(bf16[8,16,512]{2,1,0:T(8,128)(2,1)S(1)} %get-tuple-element.51), channel_id=1, source_target_pairs={{0,15},{1,0},{2,1},{3,2},{4,3},{5,4},{6,5},{7,6},{8,7},{9,8},{10,9... | collective-permute-start | bytes 393224 | tf_op jit(solution)/shard_map/ppermute | solution.py:386
  115.9 1.0 copy-start.8

commit v2 on v1

v2 whole, which is shorter than its diff:
```python
import jax
import jax.numpy as jnp
from jax import lax
from jax.experimental import pallas as pl
from jax.experimental.pallas import tpu as pltpu
from jax.sharding import PartitionSpec as P

STEPS = 4
C0, C1, C2, C3, C4 = (-205.0 / 72.0, 8.0 / 5.0, -1.0 / 5.0, 8.0 / 315.0, -1.0 / 560.0)
COEFFS = (C0, C1, C2, C3, C4)
RECEIVER_PLANE = 2
PLANES = 5
F32, BF16 = jnp.float32, jnp.bfloat16
VMEM_LIMIT = 24 * 1024 * 1024

RCV = dict(lead=16, rows=32, lanes=256)
SRC = dict(lead=16, rows=16, lanes=512)


def flat(ref):
    return ref.reshape(ref.shape[0], ref.shape[1] * ref.shape[2], 128)


def split(value):
    high = value.astype(BF16)
    return high, (value - high.astype(F32)).astype(BF16)


def planes_of(layers):
    return [*split(layers[0]), *[layer.astype(BF16) for layer in layers[1:]]]


def layers_of(planes):
    planes = [plane.astype(F32) for plane in planes]
    return [planes[0] + planes[1], *planes[2:]]


def pack_halos(src, rcv, gx_low, gx_high, gy_low, gy_high):
    for out_x, out_y, side in ((gx_low, gy_low, 0), (gx_high, gy_high, 1)):
        order = [0, 1, 2, 3] if side == 0 else [15, 14, 13, 12]
        order_y = [0, 1, 2, 3] if side == 0 else [31, 30, 29, 28]
        for t in range(4):
            lanes = slice(t * 128, t * 128 + 128)
            half, col = divmod(t, 2)
            layers = [rcv[col, a * 32 + half * 16 : a * 32 + half * 16 + 16, :] for a in order]
            for p, plane in enumerate(planes_of(layers)):
                out_x[p, :, lanes] = plane
            layers = [src[t, pl.ds(b, 16, stride=16), :] for b in order]
            for p, plane in enumerate(planes_of(layers)):
                out_x[PLANES + p, :, lanes] = plane
            layers = [src[t, a * 16 : a * 16 + 16, :] for a in order]
            for p, plane in enumerate(planes_of(layers)):
                out_y[p, :, lanes] = plane
        for col in range(2):
            layers = [rcv[col, pl.ds(b, 16, stride=32), :] for b in order_y]
            for p, plane in enumerate(planes_of(layers)):
                q, lane = PLANES + p // 2, (p % 2) * 256 + col * 128
                out_y[q, :, lane : lane + 128] = plane


def add_halos(out_src, out_rcv, vel_src, vel_rcv, gx_low, gx_high, gy_low, gy_high):
    ix, iy = lax.axis_index("gx"), lax.axis_index("gy")

    def add(out, vel, t, rows_of, layers, live):
        layers = [jnp.where(live, layer, 0.0) for layer in layers]
        for d in range(4):
            term = COEFFS[d + 1] * layers[0]
            for h in range(1, 4 - d):
                term = term + COEFFS[d + h + 1] * layers[h]
            rows = rows_of(d)
            out[t, rows, :] = out[t, rows, :] + vel[t, rows, :] * term

    for in_x, in_y, high, live_x, live_y in (
        (gx_low, gy_low, False, ix > 0, iy > 0),
        (gx_high, gy_high, True, ix < 7, iy < 15),
    ):
        live_x, live_y = jnp.broadcast_to(live_x, (16, 128)), jnp.broadcast_to(live_y, (16, 128))
        for t in range(4):
            lanes = slice(t * 128, t * 128 + 128)
            half, col = divmod(t, 2)
            add(
                out_rcv,
                vel_rcv,
                col,
                lambda d: pl.ds((15 - d if high else d) * 32 + half * 16, 16),
                layers_of([in_x[p, :, lanes] for p in range(PLANES)]),
                live_x,
            )
            add(
                out_src,
                vel_src,
                t,
                lambda d: pl.ds((15 - d if high else d) * 16, 16),
                layers_of([in_y[p, :, lanes] for p in range(PLANES)]),
                live_y,
            )
            add(
                out_src,
                vel_src,
                t,
                lambda d: pl.ds(15 - d if high else d, 16, stride=16),
                layers_of([in_x[PLANES + p, :, lanes] for p in range(PLANES)]),
                live_x,
            )
        for col in range(2):
            planes = []
            for p in range(PLANES):
                lane = (p % 2) * 256 + col * 128
                planes.append(in_y[PLANES + p // 2, :, lane : lane + 128])
            add(
                out_rcv,
                vel_rcv,
                col,
                lambda d: pl.ds(31 - d if high else d, 16, stride=32),
                layers_of(planes),
                live_y,
            )


def column(ref, rows, t):
    return ref.at[rows, pl.ds(t * 128, 128)] if len(ref.shape) == 2 else ref.at[t, rows, :]


def local_laplacian(f, now, store):
    lead, rows, tiles = f["lead"], f["rows"], f["lanes"] // 128
    lane = lax.broadcasted_iota(jnp.int32, (rows, 128), 1)
    below = {k: lane < k for k in range(1, 5)}
    above = {k: lane >= 128 - k for k in range(1, 5)}
    none = jnp.zeros((8, 128), F32)
    for a in range(lead):
        here = [now[t, a * rows : a * rows + rows, :] for t in range(tiles)]
        around = [jnp.concatenate([none, c, none], axis=0) for c in here]
        total = [(3.0 * C0) * c for c in here]
        for k in range(1, 5):
            up = [pltpu.roll(c, k, 1) for c in here]
            down = [pltpu.roll(c, 128 - k, 1) for c in here]
            for t in range(tiles):
                s = around[t][8 - k : 8 - k + rows] + around[t][8 + k : 8 + k + rows]
                for other in (a - k, a + k):
                    if 0 <= other < lead:
                        s = s + now[t, other * rows : other * rows + rows, :]
                s = s + jnp.where(below[k], up[t - 1] if t > 0 else 0.0, up[t])
                s = s + jnp.where(above[k], down[t + 1] if t + 1 < tiles else 0.0, down[t])
                total[t] = total[t] + COEFFS[k] * s
        for t in range(tiles):
            store(t, a, slice(a * rows, a * rows + rows), here[t], total[t])


def pack_brick(src, out):
    group = lax.broadcasted_iota(jnp.int32, (16, 128), 1) // 32
    for t in range(4):
        for xg in range(4):
            rows = [src[t, pl.ds(xg * 4 + xl, 16, stride=16), :] for xl in range(4)]
            for g in range(4):
                piece = None
                for xl in range(4):
                    turned = rows[xl] if xl == g else pltpu.roll(rows[xl], ((xl - g) % 4) * 32, 1)
                    piece = turned if piece is None else jnp.where(group == xl, turned, piece)
                out[t * 4 + g, :, xg * 128 : xg * 128 + 128] = piece.astype(BF16)


def unpack_velocity(pieces, out):
    group = lax.broadcasted_iota(jnp.int32, (16, 128), 1) // 32
    for t in range(4):
        for xg in range(4):
            parts = [pieces[t * 4 + g, :, xg * 128 : xg * 128 + 128] for g in range(4)]
            for xl in range(4):
                row = None
                for g in range(4):
                    turned = parts[g] if xl == g else pltpu.roll(parts[g], ((g - xl) % 4) * 32, 1)
                    row = turned if row is None else jnp.where(group == g, turned, row)
                out[t, pl.ds(xg * 4 + xl, 16, stride=16), :] = row


GX_BUF = jax.ShapeDtypeStruct((2 * PLANES, 16, 512), BF16)
GY_BUF = jax.ShapeDtypeStruct((PLANES + 3, 16, 512), BF16)
SRC_COLS = jax.ShapeDtypeStruct((4, 256, 128), F32)
RCV_COLS = jax.ShapeDtypeStruct((2, 512, 128), F32)
BRICKS = jax.ShapeDtypeStruct((16, 2, 16, 512), BF16)
VM = pl.BlockSpec(memory_space=pltpu.VMEM)
SM = pl.BlockSpec(memory_space=pltpu.SMEM)
HB = pl.BlockSpec(memory_space=pltpu.HBM)


def in_hbm(*arrays):
    return [pltpu.with_memory_space_constraint(x, pltpu.HBM) for x in arrays]


def params():
    return pltpu.CompilerParams(vmem_limit_bytes=VMEM_LIMIT)


def hint(microseconds):
    return pl.CostEstimate(flops=0, bytes_accessed=int(microseconds * 3.6e6), transcendentals=0)


def column_copies(block, cols, sem):
    return [
        pltpu.make_async_copy(
            block.at[pl.ds(a, 8), :, pl.ds(t * 128, 128)], cols.at[t, pl.ds(a, 8), :, :], sem
        )
        for a in (0, 8)
        for t in range(cols.shape[0])
    ]


def start(copies):
    for copy in copies:
        copy.start()


def wait(copies):
    for copy in copies:
        copy.wait()


def prologue(vel, src, rcv):
    def kernel(vel, src, rcv, vel_cols, src_cols, rcv_cols, turned, gx_low, gx_high, gy_low, gy_high, sems):
        vel_copies = column_copies(vel, vel_cols, sems.at[0])
        copies = column_copies(src, src_cols, sems.at[1]) + column_copies(rcv, rcv_cols, sems.at[1])
        start(vel_copies)
        start(copies)
        wait(vel_copies)
        flat_cols = flat(vel_cols)
        for t in range(2):
            for q in range(4):
                turned[t * 128 : t * 128 + 128, q * 128 : q * 128 + 128] = flat_cols[t, q * 128 : q * 128 + 128, :].T
        wait(copies)
        pack_halos(flat(src_cols), flat(rcv_cols), gx_low, gx_high, gy_low, gy_high)

    rcv_cols = jax.ShapeDtypeStruct((2, 16, 32, 128), F32)
    return pl.pallas_call(
        kernel,
        out_shape=[
            rcv_cols,
            jax.ShapeDtypeStruct((4, 16, 16, 128), F32),
            rcv_cols,
            jax.ShapeDtypeStruct((256, 512), F32),
            GX_BUF,
            GX_BUF,
            GY_BUF,
            GY_BUF,
        ],
        in_specs=[HB] * 3,
        out_specs=[VM] * 8,
        scratch_shapes=[pltpu.SemaphoreType.DMA((2,))],
        compiler_params=params(),
        name="prologue",
    )(*in_hbm(vel, src, rcv))


def source_velocity(pieces):
    return pl.pallas_call(
        unpack_velocity,
        out_shape=SRC_COLS,
        in_specs=[VM],
        out_specs=VM,
        compiler_params=params(),
        name="source_velocity",
    )(pieces)


def prepare(traces, receiver_x, receiver_y, saved, plane_index):
    def kernel(traces_hbm, rx_hbm, ry_hbm, saved, index_hbm, out, planes, traces, rx, ry, index, sems):
        ix, iy = lax.axis_index("gx"), lax.axis_index("gy")
        inputs = [
            pltpu.make_async_copy(traces_hbm, traces, sems.at[0]),
            pltpu.make_async_copy(rx_hbm, rx, sems.at[0]),
            pltpu.make_async_copy(ry_hbm, ry, sems.at[0]),
        ]
        start(inputs)
        get_index = pltpu.make_async_copy(index_hbm, index, sems.at[1])
        get_index.start()
        get_index.wait()
        edge = (ix == 0) | (ix == 7)
        side = jnp.where(ix == 0, 0, 1)
        restores = [
            pltpu.make_async_copy(
                saved.at[index[step], side, pl.ds(pl.multiple_of(iy * 16, 16), 16), pl.ds(t * 128, 128)],
                planes.at[step, t],
                sems.at[2],
            )
            for step in range(STEPS)
            for t in range(4)
        ]

        @pl.when(edge)
        def _():
            start(restores)

        wait(inputs)
        xs = ix * 16 + lax.broadcasted_iota(jnp.int32, (16, 512), 0)
        ys = iy * 32 + lax.broadcasted_iota(jnp.int32, (32, 512), 0)
        total = jnp.zeros((32, 128), F32)
        for c in range(8):
            cols = slice(c * 512, c * 512 + 512)
            at_x = rx[:, cols] == xs
            at_y = jnp.where(ry[:, cols] == ys, 1.0, 0.0)
            weighted = [jnp.where(at_x, traces[s : s + 1, cols], 0.0) for s in range(STEPS)]
            total = total + lax.dot_general(
                at_y,
                jnp.concatenate(weighted + [jnp.zeros((64, 512), F32)], axis=0),
                (((1,), (1,)), ((), ())),
                precision=lax.Precision.HIGHEST,
                preferred_element_type=F32,
            )
        out[...] = total

        @pl.when(edge)
        def _():
            wait(restores)

    return pl.pallas_call(
        kernel,
        out_shape=[jax.ShapeDtypeStruct((32, 128), F32), jax.ShapeDtypeStruct((STEPS, 4, 16, 128), F32)],
        in_specs=[HB] * 5,
        out_specs=[VM] * 2,
        scratch_shapes=[
            pltpu.VMEM((4, 4096), F32),
            pltpu.VMEM((1, 4096), jnp.int32),
            pltpu.VMEM((1, 4096), jnp.int32),
            pltpu.SMEM((4,), jnp.int32),
            pltpu.SemaphoreType.DMA((3,)),
        ],
        compiler_params=params(),
        cost_estimate=hint(2),
        name="prepare",
    )(*in_hbm(traces, receiver_x.reshape(1, -1), receiver_y.reshape(1, -1), saved, plane_index))


def local_step(step, src, src_next, rcv, rcv_next, vel_src, vel, inject, wavelet, cell):
    def kernel(src, src_next, rcv, rcv_next, vel_src, vel, inject, wavelet_hbm, cell_hbm, *refs):
        src_out, rcv_out, wavelet, cell, sems = refs
        scalars = [
            pltpu.make_async_copy(wavelet_hbm, wavelet, sems.at[0]),
            pltpu.make_async_copy(cell_hbm, cell, sems.at[1]),
        ]
        start(scalars)
        lane = lax.broadcasted_iota(jnp.int32, (32, 128), 1)

        def store_src(t, a, rows, here, lap):
            src_out[t, rows, :] = 2.0 * here - column(src_next, rows, t)[...] + vel_src[t, rows, :] * lap

        def store_rcv(t, a, rows, here, lap):
            value = 2.0 * here - column(rcv_next, rows, t)[...] + vel[t, rows, :] * lap
            if t == 0:
                turn = (RECEIVER_PLANE - step * 16 - a) % 128
                value = value + jnp.where(lane == RECEIVER_PLANE, pltpu.roll(inject[...], turn, 1), 0.0)
            rcv_out[t, rows, :] = value

        local_laplacian(SRC, src, store_src)
        local_laplacian(RCV, rcv, store_rcv)
        wait(scalars)
        z = cell[2] - lax.axis_index("gy") * 16
        x = cell[0] - lax.axis_index("gx") * 16

        @pl.when((z >= 0) & (z < 16) & (x >= 0) & (x < 16))
        def _():
            at = pl.ds(z * 16 + x, 1)
            lanes = lax.broadcasted_iota(jnp.int32, (1, 128), 1)
            for t in range(4):
                src_out[t, at, :] = src_out[t, at, :] + jnp.where(lanes + t * 128 == cell[1], wavelet[step], 0.0)

    return pl.pallas_call(
        kernel,
        out_shape=[SRC_COLS, RCV_COLS],
        in_specs=[VM] * 7 + [HB] * 2,
        out_specs=[VM] * 2,
        scratch_shapes=[
            pltpu.SMEM((4,), F32),
            pltpu.SMEM((3,), jnp.int32),
            pltpu.SemaphoreType.DMA((2,)),
        ],
        compiler_params=params(),
        cost_estimate=hint(3),
        name=f"local_step{step}",
    )(src, src_next, rcv, rcv_next, vel_src, vel, inject, *in_hbm(wavelet, cell))


def halo_step(step, local, vel_src, vel, halos, planes, src_early=None):
    last = step == STEPS - 1

    def kernel(local_src, local_rcv, vel_src, vel, gxl, gxh, gyl, gyh, planes, *refs):
        src_early, refs = (refs[0], refs[1:]) if last else (None, refs)
        src, rcv = refs[:2]
        ix = lax.axis_index("gx")
        src[...] = local_src[...]
        rcv[...] = local_rcv[...]
        add_halos(src, rcv, vel_src, vel, gxl, gxh, gyl, gyh)

        @pl.when(ix == 0)
        def _():
            for t in range(4):
                src[t, pl.ds(0, 16, stride=16), :] = planes[step, t]

        @pl.when(ix == 7)
        def _():
            for t in range(4):
                src[t, pl.ds(15, 16, stride=16), :] = planes[step, t]

        if last:
            bricks = refs[2]
            pack_brick(src_early, bricks.at[:, 0])
            pack_brick(src, bricks.at[:, 1])
        else:
            pack_halos(src, rcv, *refs[2:6])

    args = [*local, vel_src, vel, *halos, planes] + ([src_early] if last else [])
    out_shape = [SRC_COLS, RCV_COLS] + ([BRICKS] if last else [GX_BUF, GX_BUF, GY_BUF, GY_BUF])
    return pl.pallas_call(
        kernel,
        out_shape=out_shape,
        in_specs=[VM] * len(args),
        out_specs=[VM] * len(out_shape),
        compiler_params=params(),
        name=f"halo_step{step}",
    )(*args)


def write_fields(src, rcv):
    def kernel(src, rcv, src_out, rcv_out, sem):
        copies = [
            pltpu.make_async_copy(cols.at[t], out.at[:, pl.ds(t * 128, 128)], sem)
            for cols, out in ((src, src_out), (rcv, rcv_out))
            for t in range(cols.shape[0])
        ]
        start(copies)
        wait(copies)

    return pl.pallas_call(
        kernel,
        out_shape=[jax.ShapeDtypeStruct((256, 512), F32), jax.ShapeDtypeStruct((512, 256), F32)],
        in_specs=[VM] * 2,
        out_specs=[HB] * 2,
        scratch_shapes=[pltpu.SemaphoreType.DMA],
        compiler_params=params(),
        cost_estimate=hint(2),
        name="write_fields",
    )(src, rcv)


def make_image(bricks, rcv_early, rcv_late):
    def kernel(bricks, rcv_early, rcv_late, out, held, sem):
        copies = []
        for q in range(4):
            rows = slice(q * 128, q * 128 + 128)
            early = bricks[:, 0, :, rows].reshape(256, 128).astype(F32).T
            late = bricks[:, 1, :, rows].reshape(256, 128).astype(F32).T
            for t in range(2):
                lanes = slice(t * 128, t * 128 + 128)
                held[rows, lanes] = early[:, lanes] * rcv_early[t, rows, :] + late[:, lanes] * rcv_late[t, rows, :]
            copies.append(pltpu.make_async_copy(held.at[rows, :], out.at[rows, :], sem))
            copies[-1].start()
        wait(copies)

    return pl.pallas_call(
        kernel,
        out_shape=jax.ShapeDtypeStruct((512, 256), F32),
        in_specs=[VM] * 3,
        out_specs=HB,
        scratch_shapes=[pltpu.VMEM((512, 256), F32), pltpu.SemaphoreType.DMA],
        compiler_params=params(),
        name="make_image",
    )(bricks, rcv_early, rcv_late)


def exchange(buffers):
    gx_low, gx_high, gy_low, gy_high = buffers
    ring = lambda n, by: [(i, (i + by) % n) for i in range(n)]
    return (
        lax.ppermute(gx_high, "gx", ring(8, 1)),
        lax.ppermute(gx_low, "gx", ring(8, -1)),
        lax.ppermute(gy_high, "gy", ring(16, 1)),
        lax.ppermute(gy_low, "gy", ring(16, -1)),
    )


def on_device(
    source_now,
    source_next,
    receiver_now,
    receiver_next,
    velocity,
    saved_planes,
    plane_index,
    wavelet,
    source_cell,
    traces,
    receiver_x,
    receiver_y,
):
    vel, src, rcv, turned, *first = prologue(velocity, source_now, receiver_now)
    halos = exchange(first)
    vel_src = source_velocity(
        lax.all_to_all(turned.reshape(16, 16, 512), "gy", split_axis=0, concat_axis=0, tiled=True)
    )
    src, rcv, vel = (x.reshape(x.shape[0], -1, 128) for x in (src, rcv, vel))
    inject, planes = prepare(traces, receiver_x, receiver_y, saved_planes, plane_index)
    src_next, rcv_next = source_next.reshape(256, 512), receiver_next.reshape(512, 256)
    for step in range(STEPS):
        local = local_step(step, src, src_next, rcv, rcv_next, vel_src, vel, inject, wavelet, source_cell)
        if step < STEPS - 1:
            src_new, rcv_new, *to_send = halo_step(step, local, vel_src, vel, halos, planes)
            halos = exchange(to_send)
        else:
            src_new, rcv_new, bricks = halo_step(step, local, vel_src, vel, halos, planes, src_next)
        if step == 1:
            rcv_early = rcv_new
        src_next, rcv_next, src, rcv = src, rcv, src_new, rcv_new
    bricks = lax.all_to_all(bricks, "gy", split_axis=0, concat_axis=0, tiled=True)
    source_field, receiver_field = write_fields(src, rcv)
    image = make_image(bricks, rcv_early, rcv)
    return (image.reshape(16, 32, 256), receiver_field.reshape(16, 32, 256), source_field.reshape(16, 16, 512))


def solution(mesh):
    field, turned = P("gx", "gy", None), P("gy", "gx", None)
    return jax.shard_map(
        on_device,
        mesh=mesh,
        in_specs=(turned, turned, field, field, field, P(), P(), P(), P(), P(), P(), P()),
        out_specs=(field, field, turned),
        check_vma=False,
    )
```

time: 119 us -> 93.7 us (0.79)
  blocking collectives: 16.7 us -> 0 us
  local copies, waits for them, and re-layouts: 13.6 us -> 1.33 us
  starting transfers between devices: 35.4 us -> 40.2 us
  Pallas kernels: 30.1 us -> 26.6 us
  waiting for transfers between devices: 21.4 us -> 24.2 us
    all_to_all x1 -> x0, blocking collectives: 16.7 us -> none  [on_device(): lax.all_to_all(bricks, 'gy', split_axis=0, concat_axis=0, tiled=True)]
    unnamed x36 -> x8, local copies, waits for them, and re-layouts: 13.6 us -> 1.33 us
    all_to_all x1 -> x2, waiting for transfers between devices: 0.01 us -> 11.5 us  [the longest x1 10.2 us: on_device(): lax.all_to_all(bricks, 'gy', split_axis=0, concat_axis=0, tiled=True)]
    ppermute x4, waiting for transfers between devices: 12.3 us -> 2.74 us  [exchange(): lax.ppermute(gy_high, 'gy', ring(16, 1))]
    all_to_all x1 -> x2, starting transfers between devices: 8.45 us -> 14.7 us  [the longest x1 8.45 us: on_device(): lax.all_to_all(turned.reshape(16, 16, 512), 'gy', split_axis=0, concat_ax...]
    pallas_call x7 -> x12, Pallas kernels: 29.1 us -> 25.7 us  [the longest x4 14.2 us: local_step(): pl.pallas_call(kernel, out_shape=[SRC_COLS, RCV_COLS], in_specs=[VM] * 7...]
    ppermute x4, starting transfers between devices: 12 us -> 10.6 us  [exchange(): lax.ppermute(gy_high, 'gy', ring(16, 1))]
  transfers between devices with their start and end apart: 17 -> 18, of which waited for: 7 -> 8; matrix products, arithmetic and copies ran while one was open for 0% -> 0% of each run, Pallas kernels for 2% -> 19%
where the time goes in v2:
time: 93.7 us; the launch traced here: 93.3 us
  starting transfers between devices  40.2 us (43%)
  Pallas kernels  26.6 us (28%)
  waiting for transfers between devices  24.2 us (26%)
  local copies, waits for them, and re-layouts  1.33 us (1%)
  between operations  0.99 us (1%)
    pallas_call x4, Pallas kernels, local_step(): pl.pallas_call(kernel, out_shape=[SRC_COLS, RCV_COLS], in_specs=[VM] * 7...  14.2 us
    ppermute x4, starting transfers between devices, exchange(): lax.ppermute(gx_low, 'gx', ring(8, -1))  13 us
    ppermute x4, starting transfers between devices, exchange(): lax.ppermute(gy_high, 'gy', ring(16, 1))  10.6 us
    all_to_all x1, waiting for transfers between devices, on_device(): lax.all_to_all(bricks, 'gy', split_axis=0, concat_axis=0, tiled=True)  10.2 us
    ppermute x4, waiting for transfers between devices, exchange(): lax.ppermute(gy_low, 'gy', ring(16, -1))  9.94 us
    all_to_all x1, starting transfers between devices, on_device(): lax.all_to_all(turned.reshape(16, 16, 512), 'gy', split_axis=0, concat_ax...  8.45 us
    all_to_all x1, starting transfers between devices, on_device(): lax.all_to_all(bricks, 'gy', split_axis=0, concat_axis=0, tiled=True)  6.26 us
    pallas_call x4, Pallas kernels, halo_step(): pl.pallas_call(kernel, out_shape=out_shape, in_specs=[VM] * len(args), ou...  5.86 us
  transfers between devices with their start and end apart: 18, of which 8 were waited for; matrix products, arithmetic and copies ran while one was open for 0% of the time, Pallas kernels for 19%

profile of v2, /device:TPU:1, one launch (start us, length us, event | category | flops | bytes accessed | tf_op | source)
XLA Modules:
  0.0 93.3 jit_solution(8998641850442056655)
XLA Ops:
  0.7 2.4 %prologue.1 = (f32[2,16,32,128]{3,2,1,0:T(8,128)S(1)}, f32[4,16,16,128]{3,2,1,0:T(8,128)S(1)}, f32[2,16,32,128]{3,2,1,0:T(8,128)S(1)}, f32[256,512]{1,0:T(8,128)...) custom-call(f32[16,32,256]{2,1,0:T(8,128)} %vel.1, ...), custom_call_target="tpu_custom_call" | custom-call | tf_op jit(solution)/shard_map/prologue/pallas_call | solution.py:232
  3.1 0.0 copy-start.2
  3.1 0.7 copy-done.2
  3.7 0.7 copy-done.3
  4.4 8.4 %all-to-all-start = ((f32[16,16,512]{2,1,0:T(8,128)}), f32[16,16,512]{2,1,0:T(8,128)S(1)}, u32[]{:S(2)}, u32[]{:S(2)}) async-start(f32[16,16,512]{2,1,0:T(8,128)} %bitcast.4), calls=%async_computation | async-start | bytes 1048576 | tf_op jit(solution)/shard_map/all_to_all | solution.py:495
  12.9 1.6 %collective-permute-start = (bf16[10,16,512]{2,1,0:T(8,128)(2,1)}, bf16[10,16,512]{2,1,0:T(8,128)(2,1)S(1)}, u32[]{:S(2)}, u32[]{:S(2)}) collective-permute-start(bf16[10,16,512]{2,1,0:T(8,128)(2,1)} %copy-done.3), channel_id=1, source_target_pairs={{0,16},{16,32},{32,48},{48,64},{64,80},{80,96},{96,112},{112,0},{1... | collective-permute-start | bytes 491528 | tf_op jit(solution)/shard_map/ppermute | solution.py:471
  14.5 2.3 %collective-permute-start.1 = (bf16[10,16,512]{2,1,0:T(8,128)(2,1)}, bf16[10,16,512]{2,1,0:T(8,128)(2,1)}, u32[]{:S(2)}, u32[]{:S(2)}) collective-permute-start(bf16[10,16,512]{2,1,0:T(8,128)(2,1)} %copy-done.2), channel_id=1, source_target_pairs={{0,112},{16,0},{32,16},{48,32},{64,48},{80,64},{96,80},{112,96},{1... | collective-permute-start | bytes 491528 | tf_op jit(solution)/shard_map/ppermute | solution.py:472
  16.8 4.0 %collective-permute-start.2 = (bf16[8,16,512]{2,1,0:T(8,128)(2,1)}, bf16[8,16,512]{2,1,0:T(8,128)(2,1)}, u32[]{:S(2)}, u32[]{:S(2)}) collective-permute-start(bf16[8,16,512]{2,1,0:T(8,128)(2,1)} %get-tuple-element.53), channel_id=1, source_target_pairs={{0,1},{1,2},{2,3},{3,4},{4,5},{5,6},{6,7},{7,8},{8,9},{9,10},{10,1... | collective-permute-start | bytes 393224 | tf_op jit(solution)/shard_map/ppermute | solution.py:473
  20.8 0.0 collective-permute-start.3
  20.8 1.8 %prepare.1 = (f32[32,128]{1,0:T(8,128)S(1)}, f32[4,4,16,128]{3,2,1,0:T(8,128)S(1)}) custom-call(f32[4,4096]{1,0:T(4,128)} %traces_hbm.1, s32[1,4096]{1,0:T(1,128)} %bitcast.26, s32[1,4096]{1,0:T(1,128)} %bitcast.27, f32[4,2,256,512]{3,2,1,0:T(8,128)} %saved.1, s32[4]{0:T(128)} %index_hbm.1), custom_call_target="tpu_custom_call" | custom-call | bytes 7200000 | tf_op jit(solution)/shard_map/prepare/pallas_call | solution.py:313
  22.7 1.3 %all-to-all-done.pieces = f32[16,16,512]{2,1,0:T(8,128)S(1)} async-done(((f32[16,16,512]{2,1,0:T(8,128)}), f32[16,16,512]{2,1,0:T(8,128)S(1)}, u32[]{:S(2)}, u32[]{:S(2)}) %all-to-all-start) | async-done | bytes 524320 | tf_op jit(solution)/shard_map/all_to_all | solution.py:495
  24.0 0.5 source_velocity.1.vel_src
  24.5 3.5 %local_step0.1 = (f32[4,256,128]{2,1,0:T(8,128)S(1)}, f32[2,512,128]{2,1,0:T(8,128)S(1)}) custom-call(f32[4,256,128]{2,1,0:T(8,128)S(1)} %bitcast.19, f32[256,512]{1,0:T(8,128)S(1)} %bitcast.23, f32[2,512,128]{2,1,0:T(8,128)S(1)} %bitcast.21, f32[512,256]{1,0:T(8,128)S(1)} %bitcast.24, f32[4,256,128]{2,1,0:T(8,128)S(1)} %source_velocity.1.vel_src, ...), custom_call_target="tpu_custom_call" | custom-call | bytes 10800000 | tf_op jit(solution)/shard_map/local_step0/pallas_call | solution.py:364
  28.0 0.0 collective-permute-done.2.gyl
  28.1 2.2 %collective-permute-done.3.gyh = bf16[8,16,512]{2,1,0:T(8,128)(2,1)} collective-permute-done((bf16[8,16,512]{2,1,0:T(8,128)(2,1)}, bf16[8,16,512]{2,1,0:T(8,128)(2,1)}, u32[]{:S(2)}, u32[]{:S(2)}) %collective-permute-start.3) | collective-permute-done | bytes 131104 | tf_op jit(solution)/shard_map/ppermute | solution.py:474
  30.3 0.0 collective-permute-done.gxl
  30.3 0.0 collective-permute-done.1.gxh
  30.3 2.0 %halo_step0.1 = (f32[4,256,128]{2,1,0:T(8,128)S(1)}, f32[2,512,128]{2,1,0:T(8,128)S(1)}, bf16[10,16,512]{2,1,0:T(8,128)(2,1)S(1)}, bf16[10,16,512]{2,1,0:T(8,128...) custom-call(f32[4,256,128]{2,1,0:T(8,128)S(1)} %get-tuple-element.49.local_src, ...), custom_call_target="tpu_custom_call" | custom-call | tf_op jit(solution)/shard_map/halo_step0/pallas_call | solution.py:410
  32.3 0.1 collective-permute-start.4
  32.4 3.6 %collective-permute-start.5 = (bf16[10,16,512]{2,1,0:T(8,128)(2,1)S(1)}, bf16[10,16,512]{2,1,0:T(8,128)(2,1)S(1)}, u32[]{:S(2)}, u32[]{:S(2)}) collective-permute-start(bf16[10,16,512]{2,1,0:T(8,128)(2,1)S(1)} %get-tuple-element.61), channel_id=1, source_target_pairs={{0,112},{16,0},{32,16},{48,32},{64,48},{80,64},{96,80},{112,96},{1... | collective-permute-start | bytes 491528 | tf_op jit(solution)/shard_map/ppermute | solution.py:472
  35.9 2.7 %collective-permute-start.6 = (bf16[8,16,512]{2,1,0:T(8,128)(2,1)S(1)}, bf16[8,16,512]{2,1,0:T(8,128)(2,1)S(1)}, u32[]{:S(2)}, u32[]{:S(2)}) collective-permute-start(bf16[8,16,512]{2,1,0:T(8,128)(2,1)S(1)} %get-tuple-element.62), channel_id=1, source_target_pairs={{0,1},{1,2},{2,3},{3,4},{4,5},{5,6},{6,7},{7,8},{8,9},{9,10},{10,1... | collective-permute-start | bytes 393224 | tf_op jit(solution)/shard_map/ppermute | solution.py:473
  38.7 0.0 collective-permute-start.7
  38.7 3.5 %local_step1.1 = (f32[4,256,128]{2,1,0:T(8,128)S(1)}, f32[2,512,128]{2,1,0:T(8,128)S(1)}) custom-call(f32[4,256,128]{2,1,0:T(8,128)S(1)} %get-tuple-element.56.src.src_next, f32[4,256,128]{2,1,0:T(8,128)S(1)} %bitcast.20, f32[2,512,128]{2,1,0:T(8,128)S(1)} %get-tuple-element.57.rcv.rcv_next, f32[2,512,128]{2,1,0:T(8,128)S(1)} %bitcast.22, ...), custom_call_target="tpu_custom_call" | custom-call | bytes 10800000 | tf_op jit(solution)/shard_map/local_step1/pallas_call | solution.py:364
  42.2 0.0 collective-permute-done.6.gyl
  42.2 2.7 %collective-permute-done.7.gyh = bf16[8,16,512]{2,1,0:T(8,128)(2,1)S(1)} collective-permute-done((bf16[8,16,512]{2,1,0:T(8,128)(2,1)S(1)}, bf16[8,16,512]{2,1,0:T(8,128)(2,1)S(1)}, u32[]{:S(2)}, u32[]{:S(2)}) %collective-permute-start.7) | collective-permute-done | bytes 131104 | tf_op jit(solution)/shard_map/ppermute | solution.py:474
  44.9 0.0 collective-permute-done.4.gxl
  44.9 0.0 collective-permute-done.5.gxh
  44.9 0.9 %halo_step1.1 = (f32[4,256,128]{2,1,0:T(8,128)S(1)}, f32[2,512,128]{2,1,0:T(8,128)S(1)}, bf16[10,16,512]{2,1,0:T(8,128)(2,1)S(1)}, bf16[10,16,512]{2,1,0:T(8,128...) custom-call(f32[4,256,128]{2,1,0:T(8,128)S(1)} %get-tuple-element.58.local_src, ...), custom_call_target="tpu_custom_call" | custom-call | tf_op jit(solution)/shard_map/halo_step1/pallas_call | solution.py:410
  45.9 0.1 collective-permute-start.8
  45.9 3.6 %collective-permute-start.9 = (bf16[10,16,512]{2,1,0:T(8,128)(2,1)S(1)}, bf16[10,16,512]{2,1,0:T(8,128)(2,1)S(1)}, u32[]{:S(2)}, u32[]{:S(2)}) collective-permute-start(bf16[10,16,512]{2,1,0:T(8,128)(2,1)S(1)} %get-tuple-element.69), channel_id=1, source_target_pairs={{0,112},{16,0},{32,16},{48,32},{64,48},{80,64},{96,80},{112,96},{1... | collective-permute-start | bytes 491528 | tf_op jit(solution)/shard_map/ppermute | solution.py:472
  49.5 1.2 %collective-permute-start.10 = (bf16[8,16,512]{2,1,0:T(8,128)(2,1)S(1)}, bf16[8,16,512]{2,1,0:T(8,128)(2,1)S(1)}, u32[]{:S(2)}, u32[]{:S(2)}) collective-permute-start(bf16[8,16,512]{2,1,0:T(8,128)(2,1)S(1)} %get-tuple-element.70), channel_id=1, source_target_pairs={{0,1},{1,2},{2,3},{3,4},{4,5},{5,6},{6,7},{7,8},{8,9},{9,10},{10,1... | collective-permute-start | bytes 393224 | tf_op jit(solution)/shard_map/ppermute | solution.py:473
  50.7 0.0 collective-permute-start.11
  50.7 3.5 %local_step2.1 = (f32[4,256,128]{2,1,0:T(8,128)S(1)}, f32[2,512,128]{2,1,0:T(8,128)S(1)}) custom-call(f32[4,256,128]{2,1,0:T(8,128)S(1)} %get-tuple-element.64.src.src_next.refs_0_, f32[4,256,128]{2,1,0:T(8,128)S(1)} %get-tuple-element.56.src.src_next, f32[2,512,128]{2,1,0:T(8,128)S(1)} %get-tuple-element.65.rcv.rcv_next.rcv_early, ...), custom_call_target="tpu_custom_call" | custom-call | bytes 10800000 | tf_op jit(solution)/shard_map/local_step2/pallas_call | solution.py:364
  54.2 2.1 %collective-permute-done.10.gyl = bf16[8,16,512]{2,1,0:T(8,128)(2,1)S(1)} collective-permute-done((bf16[8,16,512]{2,1,0:T(8,128)(2,1)S(1)}, bf16[8,16,512]{2,1,0:T(8,128)(2,1)S(1)}, u32[]{:S(2)}, u32[]{:S(2)}) %collective-permute-start.10) | collective-permute-done | bytes 131104 | tf_op jit(solution)/shard_map/ppermute | solution.py:473
  56.3 1.9 %collective-permute-done.11.gyh = bf16[8,16,512]{2,1,0:T(8,128)(2,1)S(1)} collective-permute-done((bf16[8,16,512]{2,1,0:T(8,128)(2,1)S(1)}, bf16[8,16,512]{2,1,0:T(8,128)(2,1)S(1)}, u32[]{:S(2)}, u32[]{:S(2)}) %collective-permute-start.11) | collective-permute-done | bytes 131104 | tf_op jit(solution)/shard_map/ppermute | solution.py:474
  58.2 0.9 %halo_step2.1 = (f32[4,256,128]{2,1,0:T(8,128)S(1)}, f32[2,512,128]{2,1,0:T(8,128)S(1)}, bf16[10,16,512]{2,1,0:T(8,128)(2,1)S(1)}, bf16[10,16,512]{2,1,0:T(8,128...) custom-call(f32[4,256,128]{2,1,0:T(8,128)S(1)} %get-tuple-element.66.local_src, ...), custom_call_target="tpu_custom_call" | custom-call | tf_op jit(solution)/shard_map/halo_step2/pallas_call | solution.py:410
  59.2 0.1 collective-permute-start.12
  59.3 3.6 %collective-permute-start.13 = (bf16[10,16,512]{2,1,0:T(8,128)(2,1)S(1)}, bf16[10,16,512]{2,1,0:T(8,128)(2,1)S(1)}, u32[]{:S(2)}, u32[]{:S(2)}) collective-permute-start(bf16[10,16,512]{2,1,0:T(8,128)(2,1)S(1)} %get-tuple-element.77), channel_id=1, source_target_pairs={{0,112},{16,0},{32,16},{48,32},{64,48},{80,64},{96,80},{112,96},{1... | collective-permute-start | bytes 491528 | tf_op jit(solution)/shard_map/ppermute | solution.py:472
  62.8 2.7 %collective-permute-start.14 = (bf16[8,16,512]{2,1,0:T(8,128)(2,1)S(1)}, bf16[8,16,512]{2,1,0:T(8,128)(2,1)S(1)}, u32[]{:S(2)}, u32[]{:S(2)}) collective-permute-start(bf16[8,16,512]{2,1,0:T(8,128)(2,1)S(1)} %get-tuple-element.78), channel_id=1, source_target_pairs={{0,1},{1,2},{2,3},{3,4},{4,5},{5,6},{6,7},{7,8},{8,9},{9,10},{10,1... | collective-permute-start | bytes 393224 | tf_op jit(solution)/shard_map/ppermute | solution.py:473
  65.5 0.0 collective-permute-start.15
  65.5 3.5 %local_step3.1 = (f32[4,256,128]{2,1,0:T(8,128)S(1)}, f32[2,512,128]{2,1,0:T(8,128)S(1)}) custom-call(f32[4,256,128]{2,1,0:T(8,128)S(1)} %get-tuple-element.72.src, f32[4,256,128]{2,1,0:T(8,128)S(1)} %get-tuple-element.64.src.src_next.refs_0_, f32[2,512,128]{2,1,0:T(8,128)S(1)} %get-tuple-element.73.rcv, ...), custom_call_target="tpu_custom_call" | custom-call | bytes 10800000 | tf_op jit(solution)/shard_map/local_step3/pallas_call | solution.py:364
  69.0 0.6 collective-permute-done.14.gyl
  69.7 3.1 %collective-permute-done.15.gyh = bf16[8,16,512]{2,1,0:T(8,128)(2,1)S(1)} collective-permute-done((bf16[8,16,512]{2,1,0:T(8,128)(2,1)S(1)}, bf16[8,16,512]{2,1,0:T(8,128)(2,1)S(1)}, u32[]{:S(2)}, u32[]{:S(2)}) %collective-permute-start.15) | collective-permute-done | bytes 131104 | tf_op jit(solution)/shard_map/ppermute | solution.py:474
  72.8 2.0 %halo_step3.1 = (f32[4,256,128]{2,1,0:T(8,128)S(1)}, f32[2,512,128]{2,1,0:T(8,128)S(1)}, bf16[16,2,16,512]{3,2,1,0:T(8,128)(2,1)}) custom-call(f32[4,256,128]{2,1,0:T(8,128)S(1)} %get-tuple-element.74.local_src, f32[2,512,128]{2,1,0:T(8,128)S(1)} %get-tuple-element.75.local_rcv, f32[4,256,128]{2,1,0:T(8,128)S(1)} %source_velocity.1.vel_src, ...), custom_call_target="tpu_custom_call" | custom-call | tf_op jit(solution)/shard_map/halo_step3/pallas_call | solution.py:410
  74.8 6.3 %all-to-all-start.1 = ((bf16[16,2,16,512]{3,2,1,0:T(8,128)(2,1)}), bf16[16,2,16,512]{3,2,1,0:T(8,128)(2,1)S(1)}, u32[]{:S(2)}, u32[]{:S(2)}) async-start(bf16[16,2,16,512]{3,2,1,0:T(8,128)(2,1)} %get-tuple-element.80), calls=%async_computation.1 | async-start | bytes 1048576 | tf_op jit(solution)/shard_map/all_to_all | solution.py:510
  81.1 1.0 %write_fields.1 = (f32[256,512]{1,0:T(8,128)}, f32[512,256]{1,0:T(8,128)}) custom-call(f32[4,256,128]{2,1,0:T(8,128)S(1)} %get-tuple-element.82.src, f32[2,512,128]{2,1,0:T(8,128)S(1)} %get-tuple-element.81.rcv_late.rcv), custom_call_target="tpu_custom_call" | custom-call | bytes 7200000 | tf_op jit(solution)/shard_map/write_fields/pallas_call | solution.py:430
  82.0 10.2 %all-to-all-done.1.bricks = bf16[16,2,16,512]{3,2,1,0:T(8,128)(2,1)S(1)} async-done(((bf16[16,2,16,512]{3,2,1,0:T(8,128)(2,1)}), bf16[16,2,16,512]{3,2,1,0:T(8,128)(2,1)S(1)}, u32[]{:S(2)}, u32[]{:S(2)}) %all-to-all-start.1) | async-done | bytes 524320 | tf_op jit(solution)/shard_map/all_to_all | solution.py:510
  92.2 0.9 make_image.1
  (9 shorter events, 0.0 us)
Async XLA Ops:
  0.6 23.8 %copy-start.1 = (f32[16,32,256]{2,1,0:T(8,128)S(1)}, f32[16,32,256]{2,1,0:T(8,128)}, u32[]{:S(2)}) copy-start(f32[16,32,256]{2,1,0:T(8,128)} %param.15) | copy-start | bytes 1572868
  0.6 23.8 %copy-start = (f32[16,16,512]{2,1,0:T(8,128)S(1)}, f32[16,16,512]{2,1,0:T(8,128)}, u32[]{:S(2)}) copy-start(f32[16,16,512]{2,1,0:T(8,128)} %param.13) | copy-start | bytes 1572868
  3.1 0.7 copy-start.2
  3.7 0.7 copy-start.3
  4.4 19.6 %all-to-all-start = ((f32[16,16,512]{2,1,0:T(8,128)}), f32[16,16,512]{2,1,0:T(8,128)S(1)}, u32[]{:S(2)}, u32[]{:S(2)}) async-start(f32[16,16,512]{2,1,0:T(8,128)} %bitcast.4), calls=%async_computation | async-start | bytes 1048576 | tf_op jit(solution)/shard_map/all_to_all | solution.py:495
  12.9 17.4 %collective-permute-start = (bf16[10,16,512]{2,1,0:T(8,128)(2,1)}, bf16[10,16,512]{2,1,0:T(8,128)(2,1)S(1)}, u32[]{:S(2)}, u32[]{:S(2)}) collective-permute-start(bf16[10,16,512]{2,1,0:T(8,128)(2,1)} %copy-done.3), channel_id=1, source_target_pairs={{0,16},{16,32},{32,48},{48,64},{64,80},{80,96},{96,112},{112,0},{1... | collective-permute-start | bytes 491528 | tf_op jit(solution)/shard_map/ppermute | solution.py:471
  14.5 15.8 %collective-permute-start.1 = (bf16[10,16,512]{2,1,0:T(8,128)(2,1)}, bf16[10,16,512]{2,1,0:T(8,128)(2,1)}, u32[]{:S(2)}, u32[]{:S(2)}) collective-permute-start(bf16[10,16,512]{2,1,0:T(8,128)(2,1)} %copy-done.2), channel_id=1, source_target_pairs={{0,112},{16,0},{32,16},{48,32},{64,48},{80,64},{96,80},{112,96},{1... | collective-permute-start | bytes 491528 | tf_op jit(solution)/shard_map/ppermute | solution.py:472
  16.8 11.2 %collective-permute-start.2 = (bf16[8,16,512]{2,1,0:T(8,128)(2,1)}, bf16[8,16,512]{2,1,0:T(8,128)(2,1)}, u32[]{:S(2)}, u32[]{:S(2)}) collective-permute-start(bf16[8,16,512]{2,1,0:T(8,128)(2,1)} %get-tuple-element.53), channel_id=1, source_target_pairs={{0,1},{1,2},{2,3},{3,4},{4,5},{5,6},{6,7},{7,8},{8,9},{9,10},{10,1... | collective-permute-start | bytes 393224 | tf_op jit(solution)/shard_map/ppermute | solution.py:473
  20.8 9.5 %collective-permute-start.3 = (bf16[8,16,512]{2,1,0:T(8,128)(2,1)}, bf16[8,16,512]{2,1,0:T(8,128)(2,1)}, u32[]{:S(2)}, u32[]{:S(2)}) collective-permute-start(bf16[8,16,512]{2,1,0:T(8,128)(2,1)} %get-tuple-element.54), channel_id=1, source_target_pairs={{0,15},{1,0},{2,1},{3,2},{4,3},{5,4},{6,5},{7,6},{8,7},{9,8},{10,9... | collective-permute-start | bytes 393224 | tf_op jit(solution)/shard_map/ppermute | solution.py:474
  32.3 12.6 %collective-permute-start.4 = (bf16[10,16,512]{2,1,0:T(8,128)(2,1)S(1)}, bf16[10,16,512]{2,1,0:T(8,128)(2,1)S(1)}, u32[]{:S(2)}, u32[]{:S(2)}) collective-permute-start(bf16[10,16,512]{2,1,0:T(8,128)(2,1)S(1)} %get-tuple-element.60), channel_id=1, source_target_pairs={{0,16},{16,32},{32,48},{48,64},{64,80},{80,96},{96,112},{112,0},{1... | collective-permute-start | bytes 491528 | tf_op jit(solution)/shard_map/ppermute | solution.py:471
  32.4 12.5 %collective-permute-start.5 = (bf16[10,16,512]{2,1,0:T(8,128)(2,1)S(1)}, bf16[10,16,512]{2,1,0:T(8,128)(2,1)S(1)}, u32[]{:S(2)}, u32[]{:S(2)}) collective-permute-start(bf16[10,16,512]{2,1,0:T(8,128)(2,1)S(1)} %get-tuple-element.61), channel_id=1, source_target_pairs={{0,112},{16,0},{32,16},{48,32},{64,48},{80,64},{96,80},{112,96},{1... | collective-permute-start | bytes 491528 | tf_op jit(solution)/shard_map/ppermute | solution.py:472
  35.9 6.3 %collective-permute-start.6 = (bf16[8,16,512]{2,1,0:T(8,128)(2,1)S(1)}, bf16[8,16,512]{2,1,0:T(8,128)(2,1)S(1)}, u32[]{:S(2)}, u32[]{:S(2)}) collective-permute-start(bf16[8,16,512]{2,1,0:T(8,128)(2,1)S(1)} %get-tuple-element.62), channel_id=1, source_target_pairs={{0,1},{1,2},{2,3},{3,4},{4,5},{5,6},{6,7},{7,8},{8,9},{9,10},{10,1... | collective-permute-start | bytes 393224 | tf_op jit(solution)/shard_map/ppermute | solution.py:473
  38.7 6.2 %collective-permute-start.7 = (bf16[8,16,512]{2,1,0:T(8,128)(2,1)S(1)}, bf16[8,16,512]{2,1,0:T(8,128)(2,1)S(1)}, u32[]{:S(2)}, u32[]{:S(2)}) collective-permute-start(bf16[8,16,512]{2,1,0:T(8,128)(2,1)S(1)} %get-tuple-element.63), channel_id=1, source_target_pairs={{0,15},{1,0},{2,1},{3,2},{4,3},{5,4},{6,5},{7,6},{8,7},{9,8},{10,9... | collective-permute-start | bytes 393224 | tf_op jit(solution)/shard_map/ppermute | solution.py:474
  45.9 12.4 %collective-permute-start.8 = (bf16[10,16,512]{2,1,0:T(8,128)(2,1)S(1)}, bf16[10,16,512]{2,1,0:T(8,128)(2,1)S(1)}, u32[]{:S(2)}, u32[]{:S(2)}) collective-permute-start(bf16[10,16,512]{2,1,0:T(8,128)(2,1)S(1)} %get-tuple-element.68), channel_id=1, source_target_pairs={{0,16},{16,32},{32,48},{48,64},{64,80},{80,96},{96,112},{112,0},{1... | collective-permute-start | bytes 491528 | tf_op jit(solution)/shard_map/ppermute | solution.py:471
  45.9 12.3 %collective-permute-start.9 = (bf16[10,16,512]{2,1,0:T(8,128)(2,1)S(1)}, bf16[10,16,512]{2,1,0:T(8,128)(2,1)S(1)}, u32[]{:S(2)}, u32[]{:S(2)}) collective-permute-start(bf16[10,16,512]{2,1,0:T(8,128)(2,1)S(1)} %get-tuple-element.69), channel_id=1, source_target_pairs={{0,112},{16,0},{32,16},{48,32},{64,48},{80,64},{96,80},{112,96},{1... | collective-permute-start | bytes 491528 | tf_op jit(solution)/shard_map/ppermute | solution.py:472
  49.5 6.8 %collective-permute-start.10 = (bf16[8,16,512]{2,1,0:T(8,128)(2,1)S(1)}, bf16[8,16,512]{2,1,0:T(8,128)(2,1)S(1)}, u32[]{:S(2)}, u32[]{:S(2)}) collective-permute-start(bf16[8,16,512]{2,1,0:T(8,128)(2,1)S(1)} %get-tuple-element.70), channel_id=1, source_target_pairs={{0,1},{1,2},{2,3},{3,4},{4,5},{5,6},{6,7},{7,8},{8,9},{9,10},{10,1... | collective-permute-start | bytes 393224 | tf_op jit(solution)/shard_map/ppermute | solution.py:473
  50.7 7.6 %collective-permute-start.11 = (bf16[8,16,512]{2,1,0:T(8,128)(2,1)S(1)}, bf16[8,16,512]{2,1,0:T(8,128)(2,1)S(1)}, u32[]{:S(2)}, u32[]{:S(2)}) collective-permute-start(bf16[8,16,512]{2,1,0:T(8,128)(2,1)S(1)} %get-tuple-element.71), channel_id=1, source_target_pairs={{0,15},{1,0},{2,1},{3,2},{4,3},{5,4},{6,5},{7,6},{8,7},{9,8},{10,9... | collective-permute-start | bytes 393224 | tf_op jit(solution)/shard_map/ppermute | solution.py:474
  59.2 13.6 %collective-permute-start.12 = (bf16[10,16,512]{2,1,0:T(8,128)(2,1)S(1)}, bf16[10,16,512]{2,1,0:T(8,128)(2,1)S(1)}, u32[]{:S(2)}, u32[]{:S(2)}) collective-permute-start(bf16[10,16,512]{2,1,0:T(8,128)(2,1)S(1)} %get-tuple-element.76), channel_id=1, source_target_pairs={{0,16},{16,32},{32,48},{48,64},{64,80},{80,96},{96,112},{112,0},{1... | collective-permute-start | bytes 491528 | tf_op jit(solution)/shard_map/ppermute | solution.py:471
  59.3 13.5 %collective-permute-start.13 = (bf16[10,16,512]{2,1,0:T(8,128)(2,1)S(1)}, bf16[10,16,512]{2,1,0:T(8,128)(2,1)S(1)}, u32[]{:S(2)}, u32[]{:S(2)}) collective-permute-start(bf16[10,16,512]{2,1,0:T(8,128)(2,1)S(1)} %get-tuple-element.77), channel_id=1, source_target_pairs={{0,112},{16,0},{32,16},{48,32},{64,48},{80,64},{96,80},{112,96},{1... | collective-permute-start | bytes 491528 | tf_op jit(solution)/shard_map/ppermute | solution.py:472
  62.8 6.8 %collective-permute-start.14 = (bf16[8,16,512]{2,1,0:T(8,128)(2,1)S(1)}, bf16[8,16,512]{2,1,0:T(8,128)(2,1)S(1)}, u32[]{:S(2)}, u32[]{:S(2)}) collective-permute-start(bf16[8,16,512]{2,1,0:T(8,128)(2,1)S(1)} %get-tuple-element.78), channel_id=1, source_target_pairs={{0,1},{1,2},{2,3},{3,4},{4,5},{5,6},{6,7},{7,8},{8,9},{9,10},{10,1... | collective-permute-start | bytes 393224 | tf_op jit(solution)/shard_map/ppermute | solution.py:473
  65.5 7.3 %collective-permute-start.15 = (bf16[8,16,512]{2,1,0:T(8,128)(2,1)S(1)}, bf16[8,16,512]{2,1,0:T(8,128)(2,1)S(1)}, u32[]{:S(2)}, u32[]{:S(2)}) collective-permute-start(bf16[8,16,512]{2,1,0:T(8,128)(2,1)S(1)} %get-tuple-element.79), channel_id=1, source_target_pairs={{0,15},{1,0},{2,1},{3,2},{4,3},{5,4},{6,5},{7,6},{8,7},{9,8},{10,9... | collective-permute-start | bytes 393224 | tf_op jit(solution)/shard_map/ppermute | solution.py:474
  74.8 17.4 %all-to-all-start.1 = ((bf16[16,2,16,512]{3,2,1,0:T(8,128)(2,1)}), bf16[16,2,16,512]{3,2,1,0:T(8,128)(2,1)S(1)}, u32[]{:S(2)}, u32[]{:S(2)}) async-start(bf16[16,2,16,512]{3,2,1,0:T(8,128)(2,1)} %get-tuple-element.80), calls=%async_computation.1 | async-start | bytes 1048576 | tf_op jit(solution)/shard_map/all_to_all | solution.py:510

commit v3 on v2

--- a/solution.py
+++ b/solution.py
@@ -35,34 +35,46 @@
     return [planes[0] + planes[1], *planes[2:]]
 
 
-def pack_halos(src, rcv, gx_low, gx_high, gy_low, gy_high):
-    for out_x, out_y, side in ((gx_low, gy_low, 0), (gx_high, gy_high, 1)):
-        order = [0, 1, 2, 3] if side == 0 else [15, 14, 13, 12]
-        order_y = [0, 1, 2, 3] if side == 0 else [31, 30, 29, 28]
+def sides():
+    return lax.axis_index("gx") % 2 == 0, lax.axis_index("gy") % 2 == 0
+
+
+def layer_at(high, count, h):
+    return jnp.where(high, count - 1 - h, h)
+
+
+def pack_halos(src, rcv, gx_first, gx_second, gy_first, gy_second):
+    up_x, up_y = sides()
+    for out_x, out_y, high_x, high_y in (
+        (gx_second, gy_second, ~up_x, ~up_y),
+        (gx_first, gy_first, up_x, up_y),
+    ):
         for t in range(4):
             lanes = slice(t * 128, t * 128 + 128)
             half, col = divmod(t, 2)
-            layers = [rcv[col, a * 32 + half * 16 : a * 32 + half * 16 + 16, :] for a in order]
-            for p, plane in enumerate(planes_of(layers)):
+            rows = [pl.multiple_of(layer_at(high_x, 16, h) * 32 + half * 16, 16) for h in range(4)]
+            for p, plane in enumerate(planes_of([rcv[col, pl.ds(row, 16), :] for row in rows])):
                 out_x[p, :, lanes] = plane
-            layers = [src[t, pl.ds(b, 16, stride=16), :] for b in order]
+            layers = [src[t, pl.ds(layer_at(high_x, 16, h), 16, stride=16), :] for h in range(4)]
             for p, plane in enumerate(planes_of(layers)):
                 out_x[PLANES + p, :, lanes] = plane
-            layers = [src[t, a * 16 : a * 16 + 16, :] for a in order]
-            for p, plane in enumerate(planes_of(layers)):
+            rows = [pl.multiple_of(layer_at(high_y, 16, h) * 16, 16) for h in range(4)]
+            for p, plane in enumerate(planes_of([src[t, pl.ds(row, 16), :] for row in rows])):
                 out_y[p, :, lanes] = plane
         for col in range(2):
-            layers = [rcv[col, pl.ds(b, 16, stride=32), :] for b in order_y]
+            layers = [rcv[col, pl.ds(layer_at(high_y, 32, h), 16, stride=32), :] for h in range(4)]
             for p, plane in enumerate(planes_of(layers)):
                 q, lane = PLANES + p // 2, (p % 2) * 256 + col * 128
                 out_y[q, :, lane : lane + 128] = plane
 
 
-def add_halos(out_src, out_rcv, vel_src, vel_rcv, gx_low, gx_high, gy_low, gy_high):
+def add_halos(out_src, out_rcv, vel_src, vel_rcv, gx_first, gx_second, gy_first, gy_second):
     ix, iy = lax.axis_index("gx"), lax.axis_index("gy")
+    up_x, up_y = sides()
 
     def add(out, vel, t, rows_of, layers, live):
-        layers = [jnp.where(live, layer, 0.0) for layer in layers]
+        if live is not None:
+            layers = [jnp.where(live, layer, 0.0) for layer in layers]
         for d in range(4):
             term = COEFFS[d + 1] * layers[0]
             for h in range(1, 4 - d):
@@ -70,11 +82,12 @@
             rows = rows_of(d)
             out[t, rows, :] = out[t, rows, :] + vel[t, rows, :] * term
 
-    for in_x, in_y, high, live_x, live_y in (
-        (gx_low, gy_low, False, ix > 0, iy > 0),
-        (gx_high, gy_high, True, ix < 7, iy < 15),
+    live_x = jnp.broadcast_to((ix != 0) & (ix != 7), (16, 128))
+    live_y = jnp.broadcast_to((iy != 0) & (iy != 15), (16, 128))
+    for in_x, in_y, high_x, high_y, live_x, live_y in (
+        (gx_first, gy_first, up_x, up_y, None, None),
+        (gx_second, gy_second, ~up_x, ~up_y, live_x, live_y),
     ):
-        live_x, live_y = jnp.broadcast_to(live_x, (16, 128)), jnp.broadcast_to(live_y, (16, 128))
         for t in range(4):
             lanes = slice(t * 128, t * 128 + 128)
             half, col = divmod(t, 2)
@@ -82,7 +95,7 @@
                 out_rcv,
                 vel_rcv,
                 col,
-                lambda d: pl.ds((15 - d if high else d) * 32 + half * 16, 16),
+                lambda d: pl.ds(pl.multiple_of(layer_at(high_x, 16, d) * 32 + half * 16, 16), 16),
                 layers_of([in_x[p, :, lanes] for p in range(PLANES)]),
                 live_x,
             )
@@ -90,7 +103,7 @@
                 out_src,
                 vel_src,
                 t,
-                lambda d: pl.ds((15 - d if high else d) * 16, 16),
+                lambda d: pl.ds(pl.multiple_of(layer_at(high_y, 16, d) * 16, 16), 16),
                 layers_of([in_y[p, :, lanes] for p in range(PLANES)]),
                 live_y,
             )
@@ -98,7 +111,7 @@
                 out_src,
                 vel_src,
                 t,
-                lambda d: pl.ds(15 - d if high else d, 16, stride=16),
+                lambda d: pl.ds(layer_at(high_x, 16, d), 16, stride=16),
                 layers_of([in_x[PLANES + p, :, lanes] for p in range(PLANES)]),
                 live_x,
             )
@@ -111,14 +124,10 @@
                 out_rcv,
                 vel_rcv,
                 col,
-                lambda d: pl.ds(31 - d if high else d, 16, stride=32),
+                lambda d: pl.ds(layer_at(high_y, 32, d), 16, stride=32),
                 layers_of(planes),
                 live_y,
             )
-
-
-def column(ref, rows, t):
-    return ref.at[rows, pl.ds(t * 128, 128)] if len(ref.shape) == 2 else ref.at[t, rows, :]
 
 
 def local_laplacian(f, now, store):
@@ -146,9 +155,9 @@
             store(t, a, slice(a * rows, a * rows + rows), here[t], total[t])
 
 
-def pack_brick(src, out):
+def pack_brick(src, out, columns=range(4)):
     group = lax.broadcasted_iota(jnp.int32, (16, 128), 1) // 32
-    for t in range(4):
+    for t in columns:
         for xg in range(4):
             rows = [src[t, pl.ds(xg * 4 + xl, 16, stride=16), :] for xl in range(4)]
             for g in range(4):
@@ -176,7 +185,7 @@
 GY_BUF = jax.ShapeDtypeStruct((PLANES + 3, 16, 512), BF16)
 SRC_COLS = jax.ShapeDtypeStruct((4, 256, 128), F32)
 RCV_COLS = jax.ShapeDtypeStruct((2, 512, 128), F32)
-BRICKS = jax.ShapeDtypeStruct((16, 2, 16, 512), BF16)
+BRICK = jax.ShapeDtypeStruct((16, 16, 512), BF16)
 VM = pl.BlockSpec(memory_space=pltpu.VMEM)
 SM = pl.BlockSpec(memory_space=pltpu.SMEM)
 HB = pl.BlockSpec(memory_space=pltpu.HBM)
@@ -215,35 +224,45 @@
 
 
 def prologue(vel, src, rcv):
-    def kernel(vel, src, rcv, vel_cols, src_cols, rcv_cols, turned, gx_low, gx_high, gy_low, gy_high, sems):
-        vel_copies = column_copies(vel, vel_cols, sems.at[0])
-        copies = column_copies(src, src_cols, sems.at[1]) + column_copies(rcv, rcv_cols, sems.at[1])
-        start(vel_copies)
+    def kernel(vel, src, rcv, vel_cols, src_cols, rcv_cols, *refs):
+        results, (turned, *packed), sems = refs[:5], refs[5:10], refs[10]
+        pieces = [
+            pltpu.make_async_copy(
+                vel.at[pl.ds(q * 4, 4), :, pl.ds(t * 128, 128)], vel_cols.at[t, pl.ds(q * 4, 4), :, :], sems.at[q]
+            )
+            for q in range(4)
+            for t in range(2)
+        ]
+        start(pieces)
+        copies = column_copies(src, src_cols, sems.at[4]) + column_copies(rcv, rcv_cols, sems.at[4])
         start(copies)
-        wait(vel_copies)
         flat_cols = flat(vel_cols)
-        for t in range(2):
-            for q in range(4):
-                turned[t * 128 : t * 128 + 128, q * 128 : q * 128 + 128] = flat_cols[t, q * 128 : q * 128 + 128, :].T
+        outs = []
+        for q in range(4):
+            wait(pieces[2 * q : 2 * q + 2])
+            lanes = pl.ds(q * 128, 128)
+            for t in range(2):
+                turned[t * 128 : t * 128 + 128, lanes] = flat_cols[t, q * 128 : q * 128 + 128, :].T
+            outs.append(pltpu.make_async_copy(turned.at[:, lanes], results[0].at[:, lanes], sems.at[5]))
+            outs[-1].start()
         wait(copies)
-        pack_halos(flat(src_cols), flat(rcv_cols), gx_low, gx_high, gy_low, gy_high)
+        pack_halos(flat(src_cols), flat(rcv_cols), *packed)
+        sends = [pltpu.make_async_copy(held, out, sems.at[6]) for held, out in zip(packed, results[1:])]
+        start(sends)
+        wait(outs)
+        wait(sends)
 
     rcv_cols = jax.ShapeDtypeStruct((2, 16, 32, 128), F32)
+    halo_shapes = [GX_BUF.shape, GX_BUF.shape, GY_BUF.shape, GY_BUF.shape]
     return pl.pallas_call(
         kernel,
-        out_shape=[
-            rcv_cols,
-            jax.ShapeDtypeStruct((4, 16, 16, 128), F32),
-            rcv_cols,
-            jax.ShapeDtypeStruct((256, 512), F32),
-            GX_BUF,
-            GX_BUF,
-            GY_BUF,
-            GY_BUF,
-        ],
+        out_shape=[rcv_cols, jax.ShapeDtypeStruct((4, 16, 16, 128), F32), rcv_cols, pltpu.HBM((256, 512), F32)]
+        + [pltpu.HBM(shape, BF16) for shape in halo_shapes],
         in_specs=[HB] * 3,
-        out_specs=[VM] * 8,
-        scratch_shapes=[pltpu.SemaphoreType.DMA((2,))],
+        out_specs=[VM] * 3 + [HB] * 5,
+        scratch_shapes=[pltpu.VMEM((256, 512), F32)]
+        + [pltpu.VMEM(shape, BF16) for shape in halo_shapes]
+        + [pltpu.SemaphoreType.DMA((7,))],
         compiler_params=params(),
         name="prologue",
     )(*in_hbm(vel, src, rcv))
@@ -329,8 +348,20 @@
 
 
 def local_step(step, src, src_next, rcv, rcv_next, vel_src, vel, inject, wavelet, cell):
-    def kernel(src, src_next, rcv, rcv_next, vel_src, vel, inject, wavelet_hbm, cell_hbm, *refs):
-        src_out, rcv_out, wavelet, cell, sems = refs
+    first, last = step == 0, step == STEPS - 1
+    from_hbm = step < 2
+
+    def kernel(*refs):
+        refs = list(refs)
+        if from_hbm:
+            later = [pltpu.make_async_copy(refs[i], refs[-j], refs[-3].at[2]) for i, j in ((1, 2), (3, 1))]
+            start(later)
+            next_src, next_rcv = refs[-2:]
+            refs = refs[:-2]
+        src, src_next, rcv, rcv_next = refs[:4]
+        vel_src = None if first else refs.pop(4)
+        vel, inject, wavelet_hbm, cell_hbm, src_out, rcv_out = refs[4:10]
+        more, (wavelet, cell, sems) = refs[10:-3], refs[-3:]
         scalars = [
             pltpu.make_async_copy(wavelet_hbm, wavelet, sems.at[0]),
             pltpu.make_async_copy(cell_hbm, cell, sems.at[1]),
@@ -339,10 +370,20 @@
         lane = lax.broadcasted_iota(jnp.int32, (32, 128), 1)
 
         def store_src(t, a, rows, here, lap):
-            src_out[t, rows, :] = 2.0 * here - column(src_next, rows, t)[...] + vel_src[t, rows, :] * lap
+            value = 2.0 * here
+            if not from_hbm:
+                value = value - src_next[t, rows, :]
+            if first:
+                more[0][t, rows, :] = lap
+            else:
+                value = value + vel_src[t, rows, :] * lap
+            src_out[t, rows, :] = value
 
         def store_rcv(t, a, rows, here, lap):
-            value = 2.0 * here - column(rcv_next, rows, t)[...] + vel[t, rows, :] * lap
+            value = 2.0 * here
+            if not from_hbm:
+                value = value - rcv_next[t, rows, :]
+            value = value + vel[t, rows, :] * lap
             if t == 0:
                 turn = (RECEIVER_PLANE - step * 16 - a) % 128
                 value = value + jnp.where(lane == RECEIVER_PLANE, pltpu.roll(inject[...], turn, 1), 0.0)
@@ -350,6 +391,13 @@
 
         local_laplacian(SRC, src, store_src)
         local_laplacian(RCV, rcv, store_rcv)
+        if last:
+            pack_brick(src_next, more[0])
+        if from_hbm:
+            wait(later)
+            for cols, block in ((src_out, next_src), (rcv_out, next_rcv)):
+                for t in range(cols.shape[0]):
+                    cols[t] = cols[t] - block[:, t * 128 : t * 128 + 128]
         wait(scalars)
         z = cell[2] - lax.axis_index("gy") * 16
         x = cell[0] - lax.axis_index("gx") * 16
@@ -361,31 +409,51 @@
             for t in range(4):
                 src_out[t, at, :] = src_out[t, at, :] + jnp.where(lanes + t * 128 == cell[1], wavelet[step], 0.0)
 
+    if from_hbm:
+        src_next, rcv_next = in_hbm(src_next, rcv_next)
+    next_spec = HB if from_hbm else VM
+    args = [src, src_next, rcv, rcv_next] + ([] if first else [vel_src]) + [vel, inject]
+    out_shape = [SRC_COLS, RCV_COLS]
+    if first:
+        out_shape.append(SRC_COLS)
+    if last:
+        out_shape.append(BRICK)
     return pl.pallas_call(
         kernel,
-        out_shape=[SRC_COLS, RCV_COLS],
-        in_specs=[VM] * 7 + [HB] * 2,
-        out_specs=[VM] * 2,
+        out_shape=out_shape,
+        in_specs=[VM, next_spec, VM, next_spec] + [VM] * (len(args) - 4) + [HB] * 2,
+        out_specs=[VM] * len(out_shape),
         scratch_shapes=[
             pltpu.SMEM((4,), F32),
             pltpu.SMEM((3,), jnp.int32),
-            pltpu.SemaphoreType.DMA((2,)),
-        ],
+            pltpu.SemaphoreType.DMA((3,)),
+        ]
+        + ([pltpu.VMEM((256, 512), F32), pltpu.VMEM((512, 256), F32)] if from_hbm else []),
         compiler_params=params(),
         cost_estimate=hint(3),
         name=f"local_step{step}",
-    )(src, src_next, rcv, rcv_next, vel_src, vel, inject, *in_hbm(wavelet, cell))
-
-
-def halo_step(step, local, vel_src, vel, halos, planes, src_early=None):
-    last = step == STEPS - 1
-
-    def kernel(local_src, local_rcv, vel_src, vel, gxl, gxh, gyl, gyh, planes, *refs):
-        src_early, refs = (refs[0], refs[1:]) if last else (None, refs)
-        src, rcv = refs[:2]
+    )(*args, *in_hbm(wavelet, cell))
+
+
+def halo_step(step, local, vel_src, vel, halos, planes):
+    first, last = step == 0, step == STEPS - 1
+
+    def kernel(*refs):
+        refs = list(refs)
+        local_src, local_rcv = refs[:2]
+        extra = refs.pop(2) if first or last else None
+        vel_src, vel, gxl, gxh, gyl, gyh, planes, src, rcv = refs[2:11]
+        refs = refs[11:]
         ix = lax.axis_index("gx")
-        src[...] = local_src[...]
         rcv[...] = local_rcv[...]
+        if last:
+            bricks, late, sems = refs
+            early_copy = pltpu.make_async_copy(extra, bricks.at[:, 0], sems.at[0])
+            early_copy.start()
+        if first:
+            src[...] = local_src[...] + vel_src[...] * extra[...]
+        else:
+            src[...] = local_src[...]
         add_halos(src, rcv, vel_src, vel, gxl, gxh, gyl, gyh)
 
         @pl.when(ix == 0)
@@ -399,19 +467,25 @@
                 src[t, pl.ds(15, 16, stride=16), :] = planes[step, t]
 
         if last:
-            bricks = refs[2]
-            pack_brick(src_early, bricks.at[:, 0])
-            pack_brick(src, bricks.at[:, 1])
+            copies = [early_copy]
+            for t in range(4):
+                pack_brick(src, late, (t,))
+                part = pl.ds(t * 4, 4)
+                copies.append(pltpu.make_async_copy(late.at[part], bricks.at[part, 1], sems.at[1]))
+                copies[-1].start()
+            wait(copies)
         else:
-            pack_halos(src, rcv, *refs[2:6])
-
-    args = [*local, vel_src, vel, *halos, planes] + ([src_early] if last else [])
-    out_shape = [SRC_COLS, RCV_COLS] + ([BRICKS] if last else [GX_BUF, GX_BUF, GY_BUF, GY_BUF])
+            pack_halos(src, rcv, *refs)
+
+    args = [*local, vel_src, vel, *halos, planes]
+    out_shape = [SRC_COLS, RCV_COLS]
+    out_shape += [pltpu.HBM((16, 2, 16, 512), BF16)] if last else [GX_BUF, GX_BUF, GY_BUF, GY_BUF]
     return pl.pallas_call(
         kernel,
         out_shape=out_shape,
         in_specs=[VM] * len(args),
-        out_specs=[VM] * len(out_shape),
+        out_specs=[VM, VM, HB] if last else [VM] * len(out_shape),
+        scratch_shapes=[pltpu.VMEM((16, 16, 512), BF16), pltpu.SemaphoreType.DMA((2,))] if last else [],
         compiler_params=params(),
         name=f"halo_step{step}",
     )(*args)
@@ -465,14 +539,14 @@
 
 
 def exchange(buffers):
-    gx_low, gx_high, gy_low, gy_high = buffers
-    ring = lambda n, by: [(i, (i + by) % n) for i in range(n)]
-    return (
-        lax.ppermute(gx_high, "gx", ring(8, 1)),
-        lax.ppermute(gx_low, "gx", ring(8, -1)),
-        lax.ppermute(gy_high, "gy", ring(16, 1)),
-        lax.ppermute(gy_low, "gy", ring(16, -1)),
-    )
+    gx_first, gx_second, gy_first, gy_second = buffers
+    inner = lambda n: [(i, i ^ 1) for i in range(n)]
+    outer = lambda n: [(i, (((i + 1) ^ 1) - 1) % n) for i in range(n)]
+    from_gx_second = lax.ppermute(gx_second, "gx", outer(8))
+    from_gx_first = lax.ppermute(gx_first, "gx", inner(8))
+    from_gy_second = lax.ppermute(gy_second, "gy", outer(16))
+    from_gy_first = lax.ppermute(gy_first, "gy", inner(16))
+    return from_gx_first, from_gx_second, from_gy_first, from_gy_second
 
 
 def on_device(
@@ -503,10 +577,12 @@
             src_new, rcv_new, *to_send = halo_step(step, local, vel_src, vel, halos, planes)
             halos = exchange(to_send)
         else:
-            src_new, rcv_new, bricks = halo_step(step, local, vel_src, vel, halos, planes, src_next)
+            src_new, rcv_new, bricks = halo_step(step, local, vel_src, vel, halos, planes)
         if step == 1:
             rcv_early = rcv_new
         src_next, rcv_next, src, rcv = src, rcv, src_new, rcv_new
+        if step == 0:
+            src_next, rcv_next = source_now.reshape(256, 512), receiver_now.reshape(512, 256)
     bricks = lax.all_to_all(bricks, "gy", split_axis=0, concat_axis=0, tiled=True)
     source_field, receiver_field = write_fields(src, rcv)
     image = make_image(bricks, rcv_early, rcv)

time: 93.7 us -> 87.2 us (0.931)
  waiting for transfers between devices: 24.2 us -> 17.7 us
  Pallas kernels: 26.6 us -> 28.5 us
  starting transfers between devices: 40.2 us -> 38.7 us
    ppermute x16, waiting for transfers between devices: 12.7 us -> 7.53 us  [the longest x4 7.5 us: exchange(): from_gy_second = lax.ppermute(gy_second, 'gy', outer(16))]
    ppermute x16, starting transfers between devices: 25.4 us -> 23.2 us  [the longest x4 8.5 us: exchange(): from_gy_second = lax.ppermute(gy_second, 'gy', outer(16))]
    all_to_all x1, waiting for transfers between devices: 1.33 us -> 0.01 us  [on_device(): lax.all_to_all(turned.reshape(16, 16, 512), 'gy', split_axis=0, concat_ax...]
    pallas_call x4, Pallas kernels: 14.2 us -> 15.3 us  [local_step(): pl.pallas_call(kernel, out_shape=out_shape, in_specs=[VM, next_spec, VM,...]
  transfers between devices with their start and end apart: 18 -> 18, of which waited for: 8 -> 5; matrix products, arithmetic and copies ran while one was open for 0% -> 0% of each run, Pallas kernels for 19% -> 21%
where the time goes in v3:
time: 87.2 us; the launch traced here: 86.8 us
  starting transfers between devices  38.7 us (44%)
  Pallas kernels  28.5 us (33%)
  waiting for transfers between devices  17.7 us (20%)
  between operations  0.99 us (1%)
    pallas_call x4, Pallas kernels, local_step(): pl.pallas_call(kernel, out_shape=out_shape, in_specs=[VM, next_spec, VM,...  15.3 us
    all_to_all x1, waiting for transfers between devices, on_device(): lax.all_to_all(bricks, 'gy', split_axis=0, concat_axis=0, tiled=True)  10.2 us
    ppermute x4, starting transfers between devices, exchange(): from_gy_second = lax.ppermute(gy_second, 'gy', outer(16))  8.5 us
    all_to_all x1, starting transfers between devices, on_device(): lax.all_to_all(turned.reshape(16, 16, 512), 'gy', split_axis=0, concat_ax...  8.45 us
    ppermute x4, starting transfers between devices, exchange(): from_gx_second = lax.ppermute(gx_second, 'gx', outer(8))  7.95 us
    ppermute x4, waiting for transfers between devices, exchange(): from_gy_second = lax.ppermute(gy_second, 'gy', outer(16))  7.5 us
    all_to_all x1, starting transfers between devices, on_device(): lax.all_to_all(bricks, 'gy', split_axis=0, concat_axis=0, tiled=True)  7.12 us
    pallas_call x4, Pallas kernels, halo_step(): pl.pallas_call(kernel, out_shape=out_shape, in_specs=[VM] * len(args), ou...  6.53 us
  transfers between devices with their start and end apart: 18, of which 5 were waited for; matrix products, arithmetic and copies ran while one was open for 0% of the time, Pallas kernels for 21%

profile of v3, /device:TPU:1, one launch (start us, length us, event | category | flops | bytes accessed | tf_op | source)
XLA Modules:
  0.0 86.8 jit_solution(1139732114754634578)
XLA Ops:
  0.6 2.5 %prologue.1 = (f32[2,16,32,128]{3,2,1,0:T(8,128)S(1)}, f32[4,16,16,128]{3,2,1,0:T(8,128)S(1)}, f32[2,16,32,128]{3,2,1,0:T(8,128)S(1)}, f32[256,512]{1,0:T(8,128)...) custom-call(f32[16,32,256]{2,1,0:T(8,128)} %vel.1, ...), custom_call_target="tpu_custom_call" | custom-call | tf_op jit(solution)/shard_map/prologue/pallas_call | solution.py:257
  3.1 0.0 copy-start
  3.1 0.8 copy-done
  3.9 8.4 %all-to-all-start = ((f32[16,16,512]{2,1,0:T(8,128)}), f32[16,16,512]{2,1,0:T(8,128)S(1)}, u32[]{:S(2)}, u32[]{:S(2)}) async-start(f32[16,16,512]{2,1,0:T(8,128)} %bitcast.27), calls=%async_computation | async-start | bytes 1048576 | tf_op jit(solution)/shard_map/all_to_all | solution.py:569
  12.4 1.7 %collective-permute-start = (bf16[10,16,512]{2,1,0:T(8,128)(2,1)}, bf16[10,16,512]{2,1,0:T(8,128)(2,1)S(1)}, u32[]{:S(2)}, u32[]{:S(2)}) collective-permute-start(bf16[10,16,512]{2,1,0:T(8,128)(2,1)} %get-tuple-element.54), channel_id=1, source_target_pairs={{0,16},{16,0},{32,48},{48,32},{64,80},{80,64},{96,112},{112,96},{1... | collective-permute-start | bytes 491528 | tf_op jit(solution)/shard_map/ppermute | solution.py:546
  14.1 2.4 %collective-permute-start.1 = (bf16[10,16,512]{2,1,0:T(8,128)(2,1)}, bf16[10,16,512]{2,1,0:T(8,128)(2,1)}, u32[]{:S(2)}, u32[]{:S(2)}) collective-permute-start(bf16[10,16,512]{2,1,0:T(8,128)(2,1)} %get-tuple-element.55), channel_id=1, source_target_pairs={{0,112},{16,32},{32,16},{48,64},{64,48},{80,96},{96,80},{112,0},{1... | collective-permute-start | bytes 491528 | tf_op jit(solution)/shard_map/ppermute | solution.py:545
  16.5 0.6 collective-permute-start.2
  17.1 3.6 %collective-permute-start.3 = (bf16[8,16,512]{2,1,0:T(8,128)(2,1)}, bf16[8,16,512]{2,1,0:T(8,128)(2,1)}, u32[]{:S(2)}, u32[]{:S(2)}) collective-permute-start(bf16[8,16,512]{2,1,0:T(8,128)(2,1)} %get-tuple-element.57), channel_id=1, source_target_pairs={{0,15},{1,2},{2,1},{3,4},{4,3},{5,6},{6,5},{7,8},{8,7},{9,10},{10,... | collective-permute-start | bytes 393224 | tf_op jit(solution)/shard_map/ppermute | solution.py:547
  20.8 1.8 %prepare.1 = (f32[32,128]{1,0:T(8,128)S(1)}, f32[4,4,16,128]{3,2,1,0:T(8,128)S(1)}) custom-call(f32[4,4096]{1,0:T(4,128)} %traces_hbm.1, s32[1,4096]{1,0:T(1,128)} %bitcast.29, s32[1,4096]{1,0:T(1,128)} %bitcast.30, f32[4,2,256,512]{3,2,1,0:T(8,128)} %saved.1, s32[4]{0:T(128)} %index_hbm.1), custom_call_target="tpu_custom_call" | custom-call | bytes 7200000 | tf_op jit(solution)/shard_map/prepare/pallas_call | solution.py:332
  22.6 3.9 %local_step0.1 = (f32[4,256,128]{2,1,0:T(8,128)S(1)}, f32[2,512,128]{2,1,0:T(8,128)S(1)}, f32[4,256,128]{2,1,0:T(8,128)S(1)}) custom-call(f32[4,256,128]{2,1,0:T(8,128)S(1)} %bitcast.21, f32[256,512]{1,0:T(8,128)} %bitcast.25, f32[2,512,128]{2,1,0:T(8,128)S(1)} %bitcast.22, f32[512,256]{1,0:T(8,128)} %bitcast.26, f32[2,512,128]{2,1,0:T(8,128)S(1)} %bitcast.13, ...), custom_call_target="tpu_custom_call" | custom-call | bytes 10800000 | tf_op jit(solution)/shard_map/local_step0/pallas_call | solution.py:421
  26.6 0.0 all-to-all-done.pieces
  26.6 0.5 source_velocity.1.refs_3_.refs_4_.refs_2_
  27.0 0.0 collective-permute-done.2.refs_7_
  27.1 2.8 %collective-permute-done.3.refs_8_ = bf16[8,16,512]{2,1,0:T(8,128)(2,1)} collective-permute-done((bf16[8,16,512]{2,1,0:T(8,128)(2,1)}, bf16[8,16,512]{2,1,0:T(8,128)(2,1)}, u32[]{:S(2)}, u32[]{:S(2)}) %collective-permute-start.3) | collective-permute-done | bytes 131104 | tf_op jit(solution)/shard_map/ppermute | solution.py:547
  29.9 0.0 collective-permute-done.refs_5_
  29.9 0.0 collective-permute-done.1.refs_6_
  29.9 2.3 %halo_step0.1 = (f32[4,256,128]{2,1,0:T(8,128)S(1)}, f32[2,512,128]{2,1,0:T(8,128)S(1)}, bf16[10,16,512]{2,1,0:T(8,128)(2,1)S(1)}, bf16[10,16,512]{2,1,0:T(8,128...) custom-call(f32[4,256,128]{2,1,0:T(8,128)S(1)} %get-tuple-element.50.refs_0_, ...), custom_call_target="tpu_custom_call" | custom-call | tf_op jit(solution)/shard_map/halo_step0/pallas_call | solution.py:483
  32.2 0.1 collective-permute-start.4
  32.3 2.5 %collective-permute-start.5 = (bf16[10,16,512]{2,1,0:T(8,128)(2,1)S(1)}, bf16[10,16,512]{2,1,0:T(8,128)(2,1)S(1)}, u32[]{:S(2)}, u32[]{:S(2)}) collective-permute-start(bf16[10,16,512]{2,1,0:T(8,128)(2,1)S(1)} %get-tuple-element.64), channel_id=1, source_target_pairs={{0,112},{16,32},{32,16},{48,64},{64,48},{80,96},{96,80},{112,0},{1... | collective-permute-start | bytes 491528 | tf_op jit(solution)/shard_map/ppermute | solution.py:545
  34.8 0.0 collective-permute-start.6
  34.8 1.6 %collective-permute-start.7 = (bf16[8,16,512]{2,1,0:T(8,128)(2,1)S(1)}, bf16[8,16,512]{2,1,0:T(8,128)(2,1)S(1)}, u32[]{:S(2)}, u32[]{:S(2)}) collective-permute-start(bf16[8,16,512]{2,1,0:T(8,128)(2,1)S(1)} %get-tuple-element.66), channel_id=1, source_target_pairs={{0,15},{1,2},{2,1},{3,4},{4,3},{5,6},{6,5},{7,8},{8,7},{9,10},{10,... | collective-permute-start | bytes 393224 | tf_op jit(solution)/shard_map/ppermute | solution.py:547
  36.4 4.0 %local_step1.1 = (f32[4,256,128]{2,1,0:T(8,128)S(1)}, f32[2,512,128]{2,1,0:T(8,128)S(1)}) custom-call(f32[4,256,128]{2,1,0:T(8,128)S(1)} %get-tuple-element.59.refs_0_.refs_1_, f32[256,512]{1,0:T(8,128)} %bitcast.23, f32[2,512,128]{2,1,0:T(8,128)S(1)} %get-tuple-element.60.refs_2_.refs_3_, f32[512,256]{1,0:T(8,128)} %bitcast.24, ...), custom_call_target="tpu_custom_call" | custom-call | bytes 10800000 | tf_op jit(solution)/shard_map/local_step1/pallas_call | solution.py:421
  40.4 0.0 collective-permute-done.6.refs_6_
  40.4 0.7 collective-permute-done.7.refs_7_
  41.1 0.0 collective-permute-done.4.refs_4_
  41.1 0.0 collective-permute-done.5.refs_5_
  41.1 1.2 %halo_step1.1 = (f32[4,256,128]{2,1,0:T(8,128)S(1)}, f32[2,512,128]{2,1,0:T(8,128)S(1)}, bf16[10,16,512]{2,1,0:T(8,128)(2,1)S(1)}, bf16[10,16,512]{2,1,0:T(8,128...) custom-call(f32[4,256,128]{2,1,0:T(8,128)S(1)} %get-tuple-element.61.refs_0_, ...), custom_call_target="tpu_custom_call" | custom-call | tf_op jit(solution)/shard_map/halo_step1/pallas_call | solution.py:483
  42.3 0.3 collective-permute-start.8
  42.7 2.8 %collective-permute-start.9 = (bf16[10,16,512]{2,1,0:T(8,128)(2,1)S(1)}, bf16[10,16,512]{2,1,0:T(8,128)(2,1)S(1)}, u32[]{:S(2)}, u32[]{:S(2)}) collective-permute-start(bf16[10,16,512]{2,1,0:T(8,128)(2,1)S(1)} %get-tuple-element.72), channel_id=1, source_target_pairs={{0,112},{16,32},{32,16},{48,64},{64,48},{80,96},{96,80},{112,0},{1... | collective-permute-start | bytes 491528 | tf_op jit(solution)/shard_map/ppermute | solution.py:545
  45.5 1.2 %collective-permute-start.10 = (bf16[8,16,512]{2,1,0:T(8,128)(2,1)S(1)}, bf16[8,16,512]{2,1,0:T(8,128)(2,1)S(1)}, u32[]{:S(2)}, u32[]{:S(2)}) collective-permute-start(bf16[8,16,512]{2,1,0:T(8,128)(2,1)S(1)} %get-tuple-element.73), channel_id=1, source_target_pairs={{0,1},{1,0},{2,3},{3,2},{4,5},{5,4},{6,7},{7,6},{8,9},{9,8},{10,11... | collective-permute-start | bytes 393224 | tf_op jit(solution)/shard_map/ppermute | solution.py:548
  46.7 2.4 %collective-permute-start.11 = (bf16[8,16,512]{2,1,0:T(8,128)(2,1)S(1)}, bf16[8,16,512]{2,1,0:T(8,128)(2,1)S(1)}, u32[]{:S(2)}, u32[]{:S(2)}) collective-permute-start(bf16[8,16,512]{2,1,0:T(8,128)(2,1)S(1)} %get-tuple-element.74), channel_id=1, source_target_pairs={{0,15},{1,2},{2,1},{3,4},{4,3},{5,6},{6,5},{7,8},{8,7},{9,10},{10,... | collective-permute-start | bytes 393224 | tf_op jit(solution)/shard_map/ppermute | solution.py:547
  49.1 3.5 %local_step2.1 = (f32[4,256,128]{2,1,0:T(8,128)S(1)}, f32[2,512,128]{2,1,0:T(8,128)S(1)}) custom-call(f32[4,256,128]{2,1,0:T(8,128)S(1)} %get-tuple-element.67.refs_0_.refs_1_, f32[4,256,128]{2,1,0:T(8,128)S(1)} %get-tuple-element.59.refs_0_.refs_1_, f32[2,512,128]{2,1,0:T(8,128)S(1)} %get-tuple-element.68.refs_2_.refs_3_.rcv_early, ...), custom_call_target="tpu_custom_call" | custom-call | bytes 10800000 | tf_op jit(solution)/shard_map/local_step2/pallas_call | solution.py:421
  52.6 0.0 collective-permute-done.10.refs_6_
  52.6 2.5 %collective-permute-done.11.refs_7_ = bf16[8,16,512]{2,1,0:T(8,128)(2,1)S(1)} collective-permute-done((bf16[8,16,512]{2,1,0:T(8,128)(2,1)S(1)}, bf16[8,16,512]{2,1,0:T(8,128)(2,1)S(1)}, u32[]{:S(2)}, u32[]{:S(2)}) %collective-permute-start.11) | collective-permute-done | bytes 131104 | tf_op jit(solution)/shard_map/ppermute | solution.py:547
  55.2 0.0 collective-permute-done.9.refs_5_
  55.2 1.2 %halo_step2.1 = (f32[4,256,128]{2,1,0:T(8,128)S(1)}, f32[2,512,128]{2,1,0:T(8,128)S(1)}, bf16[10,16,512]{2,1,0:T(8,128)(2,1)S(1)}, bf16[10,16,512]{2,1,0:T(8,128...) custom-call(f32[4,256,128]{2,1,0:T(8,128)S(1)} %get-tuple-element.69.refs_0_, ...), custom_call_target="tpu_custom_call" | custom-call | tf_op jit(solution)/shard_map/halo_step2/pallas_call | solution.py:483
  56.4 0.1 collective-permute-start.12
  56.5 0.2 collective-permute-start.13
  56.7 2.7 %collective-permute-start.14 = (bf16[8,16,512]{2,1,0:T(8,128)(2,1)S(1)}, bf16[8,16,512]{2,1,0:T(8,128)(2,1)S(1)}, u32[]{:S(2)}, u32[]{:S(2)}) collective-permute-start(bf16[8,16,512]{2,1,0:T(8,128)(2,1)S(1)} %get-tuple-element.82), channel_id=1, source_target_pairs={{0,1},{1,0},{2,3},{3,2},{4,5},{5,4},{6,7},{7,6},{8,9},{9,8},{10,11... | collective-permute-start | bytes 393224 | tf_op jit(solution)/shard_map/ppermute | solution.py:548
  59.4 0.9 collective-permute-start.15
  60.2 3.9 %local_step3.1 = (f32[4,256,128]{2,1,0:T(8,128)S(1)}, f32[2,512,128]{2,1,0:T(8,128)S(1)}, bf16[16,16,512]{2,1,0:T(8,128)(2,1)S(1)}) custom-call(f32[4,256,128]{2,1,0:T(8,128)S(1)} %get-tuple-element.75.refs_0_, f32[4,256,128]{2,1,0:T(8,128)S(1)} %get-tuple-element.67.refs_0_.refs_1_, f32[2,512,128]{2,1,0:T(8,128)S(1)} %get-tuple-element.76.refs_2_, ...), custom_call_target="tpu_custom_call" | custom-call | bytes 10800000 | tf_op jit(solution)/shard_map/local_step3/pallas_call | solution.py:421
  64.2 1.4 %collective-permute-done.15.refs_8_ = bf16[8,16,512]{2,1,0:T(8,128)(2,1)S(1)} collective-permute-done((bf16[8,16,512]{2,1,0:T(8,128)(2,1)S(1)}, bf16[8,16,512]{2,1,0:T(8,128)(2,1)S(1)}, u32[]{:S(2)}, u32[]{:S(2)}) %collective-permute-start.15) | collective-permute-done | bytes 131104 | tf_op jit(solution)/shard_map/ppermute | solution.py:547
  65.6 0.0 collective-permute-done.12.refs_5_
  65.6 1.8 %halo_step3.1 = (f32[4,256,128]{2,1,0:T(8,128)S(1)}, f32[2,512,128]{2,1,0:T(8,128)S(1)}, bf16[16,2,16,512]{3,2,1,0:T(8,128)(2,1)}) custom-call(f32[4,256,128]{2,1,0:T(8,128)S(1)} %get-tuple-element.77.refs_0_, f32[2,512,128]{2,1,0:T(8,128)S(1)} %get-tuple-element.78.refs_1_, bf16[16,16,512]{2,1,0:T(8,128)(2,1)S(1)} %get-tuple-element.79.refs_2_, ...), custom_call_target="tpu_custom_call" | custom-call | tf_op jit(solution)/shard_map/halo_step3/pallas_call | solution.py:483
  67.4 7.1 %all-to-all-start.1 = ((bf16[16,2,16,512]{3,2,1,0:T(8,128)(2,1)}), bf16[16,2,16,512]{3,2,1,0:T(8,128)(2,1)S(1)}, u32[]{:S(2)}, u32[]{:S(2)}) async-start(bf16[16,2,16,512]{3,2,1,0:T(8,128)(2,1)} %get-tuple-element.84), calls=%async_computation.1 | async-start | bytes 1048576 | tf_op jit(solution)/shard_map/all_to_all | solution.py:586
  74.5 1.0 %write_fields.1 = (f32[256,512]{1,0:T(8,128)}, f32[512,256]{1,0:T(8,128)}) custom-call(f32[4,256,128]{2,1,0:T(8,128)S(1)} %get-tuple-element.86.src, f32[2,512,128]{2,1,0:T(8,128)S(1)} %get-tuple-element.85.rcv_late.rcv), custom_call_target="tpu_custom_call" | custom-call | bytes 7200000 | tf_op jit(solution)/shard_map/write_fields/pallas_call | solution.py:504
  75.5 10.2 %all-to-all-done.1.bricks = bf16[16,2,16,512]{3,2,1,0:T(8,128)(2,1)S(1)} async-done(((bf16[16,2,16,512]{3,2,1,0:T(8,128)(2,1)}), bf16[16,2,16,512]{3,2,1,0:T(8,128)(2,1)S(1)}, u32[]{:S(2)}, u32[]{:S(2)}) %all-to-all-start.1) | async-done | bytes 524320 | tf_op jit(solution)/shard_map/all_to_all | solution.py:586
  85.7 0.9 %make_image.1 = f32[512,256]{1,0:T(8,128)} custom-call(bf16[16,2,16,512]{3,2,1,0:T(8,128)(2,1)S(1)} %all-to-all-done.1.bricks, f32[2,512,128]{2,1,0:T(8,128)S(1)} %get-tuple-element.68.refs_2_.refs_3_.rcv_early, f32[2,512,128]{2,1,0:T(8,128)S(1)} %get-tuple-element.85.rcv_late.rcv), custom_call_target="tpu_custom_call" | custom-call | tf_op jit(solution)/shard_map/make_image/pallas_call | solution.py:530
  (5 shorter events, 0.0 us)
Async XLA Ops:
  3.1 0.8 copy-start
  3.9 22.6 %all-to-all-start = ((f32[16,16,512]{2,1,0:T(8,128)}), f32[16,16,512]{2,1,0:T(8,128)S(1)}, u32[]{:S(2)}, u32[]{:S(2)}) async-start(f32[16,16,512]{2,1,0:T(8,128)} %bitcast.27), calls=%async_computation | async-start | bytes 1048576 | tf_op jit(solution)/shard_map/all_to_all | solution.py:569
  12.4 10.2 %copy-start.1 = (f32[2,16,32,128]{3,2,1,0:T(8,128)S(1)}, f32[2,16,32,128]{3,2,1,0:T(8,128)}, u32[]{:S(2)}) copy-start(f32[2,16,32,128]{3,2,1,0:T(8,128)} %copy-done) | copy-start | bytes 1572868
  12.4 17.5 %collective-permute-start = (bf16[10,16,512]{2,1,0:T(8,128)(2,1)}, bf16[10,16,512]{2,1,0:T(8,128)(2,1)S(1)}, u32[]{:S(2)}, u32[]{:S(2)}) collective-permute-start(bf16[10,16,512]{2,1,0:T(8,128)(2,1)} %get-tuple-element.54), channel_id=1, source_target_pairs={{0,16},{16,0},{32,48},{48,32},{64,80},{80,64},{96,112},{112,96},{1... | collective-permute-start | bytes 491528 | tf_op jit(solution)/shard_map/ppermute | solution.py:546
  14.1 15.8 %collective-permute-start.1 = (bf16[10,16,512]{2,1,0:T(8,128)(2,1)}, bf16[10,16,512]{2,1,0:T(8,128)(2,1)}, u32[]{:S(2)}, u32[]{:S(2)}) collective-permute-start(bf16[10,16,512]{2,1,0:T(8,128)(2,1)} %get-tuple-element.55), channel_id=1, source_target_pairs={{0,112},{16,32},{32,16},{48,64},{64,48},{80,96},{96,80},{112,0},{1... | collective-permute-start | bytes 491528 | tf_op jit(solution)/shard_map/ppermute | solution.py:545
  16.5 10.6 %collective-permute-start.2 = (bf16[8,16,512]{2,1,0:T(8,128)(2,1)}, bf16[8,16,512]{2,1,0:T(8,128)(2,1)}, u32[]{:S(2)}, u32[]{:S(2)}) collective-permute-start(bf16[8,16,512]{2,1,0:T(8,128)(2,1)} %get-tuple-element.56), channel_id=1, source_target_pairs={{0,1},{1,0},{2,3},{3,2},{4,5},{5,4},{6,7},{7,6},{8,9},{9,8},{10,11... | collective-permute-start | bytes 393224 | tf_op jit(solution)/shard_map/ppermute | solution.py:548
  17.1 12.8 %collective-permute-start.3 = (bf16[8,16,512]{2,1,0:T(8,128)(2,1)}, bf16[8,16,512]{2,1,0:T(8,128)(2,1)}, u32[]{:S(2)}, u32[]{:S(2)}) collective-permute-start(bf16[8,16,512]{2,1,0:T(8,128)(2,1)} %get-tuple-element.57), channel_id=1, source_target_pairs={{0,15},{1,2},{2,1},{3,4},{4,3},{5,6},{6,5},{7,8},{8,7},{9,10},{10,... | collective-permute-start | bytes 393224 | tf_op jit(solution)/shard_map/ppermute | solution.py:547
  32.2 8.9 %collective-permute-start.4 = (bf16[10,16,512]{2,1,0:T(8,128)(2,1)S(1)}, bf16[10,16,512]{2,1,0:T(8,128)(2,1)S(1)}, u32[]{:S(2)}, u32[]{:S(2)}) collective-permute-start(bf16[10,16,512]{2,1,0:T(8,128)(2,1)S(1)} %get-tuple-element.63), channel_id=1, source_target_pairs={{0,16},{16,0},{32,48},{48,32},{64,80},{80,64},{96,112},{112,96},{1... | collective-permute-start | bytes 491528 | tf_op jit(solution)/shard_map/ppermute | solution.py:546
  32.3 8.8 %collective-permute-start.5 = (bf16[10,16,512]{2,1,0:T(8,128)(2,1)S(1)}, bf16[10,16,512]{2,1,0:T(8,128)(2,1)S(1)}, u32[]{:S(2)}, u32[]{:S(2)}) collective-permute-start(bf16[10,16,512]{2,1,0:T(8,128)(2,1)S(1)} %get-tuple-element.64), channel_id=1, source_target_pairs={{0,112},{16,32},{32,16},{48,64},{64,48},{80,96},{96,80},{112,0},{1... | collective-permute-start | bytes 491528 | tf_op jit(solution)/shard_map/ppermute | solution.py:545
  34.8 5.6 %collective-permute-start.6 = (bf16[8,16,512]{2,1,0:T(8,128)(2,1)S(1)}, bf16[8,16,512]{2,1,0:T(8,128)(2,1)S(1)}, u32[]{:S(2)}, u32[]{:S(2)}) collective-permute-start(bf16[8,16,512]{2,1,0:T(8,128)(2,1)S(1)} %get-tuple-element.65), channel_id=1, source_target_pairs={{0,1},{1,0},{2,3},{3,2},{4,5},{5,4},{6,7},{7,6},{8,9},{9,8},{10,11... | collective-permute-start | bytes 393224 | tf_op jit(solution)/shard_map/ppermute | solution.py:548
  34.8 6.3 %collective-permute-start.7 = (bf16[8,16,512]{2,1,0:T(8,128)(2,1)S(1)}, bf16[8,16,512]{2,1,0:T(8,128)(2,1)S(1)}, u32[]{:S(2)}, u32[]{:S(2)}) collective-permute-start(bf16[8,16,512]{2,1,0:T(8,128)(2,1)S(1)} %get-tuple-element.66), channel_id=1, source_target_pairs={{0,15},{1,2},{2,1},{3,4},{4,3},{5,6},{6,5},{7,8},{8,7},{9,10},{10,... | collective-permute-start | bytes 393224 | tf_op jit(solution)/shard_map/ppermute | solution.py:547
  42.3 12.8 %collective-permute-start.8 = (bf16[10,16,512]{2,1,0:T(8,128)(2,1)S(1)}, bf16[10,16,512]{2,1,0:T(8,128)(2,1)S(1)}, u32[]{:S(2)}, u32[]{:S(2)}) collective-permute-start(bf16[10,16,512]{2,1,0:T(8,128)(2,1)S(1)} %get-tuple-element.71), channel_id=1, source_target_pairs={{0,16},{16,0},{32,48},{48,32},{64,80},{80,64},{96,112},{112,96},{1... | collective-permute-start | bytes 491528 | tf_op jit(solution)/shard_map/ppermute | solution.py:546
  42.7 12.5 %collective-permute-start.9 = (bf16[10,16,512]{2,1,0:T(8,128)(2,1)S(1)}, bf16[10,16,512]{2,1,0:T(8,128)(2,1)S(1)}, u32[]{:S(2)}, u32[]{:S(2)}) collective-permute-start(bf16[10,16,512]{2,1,0:T(8,128)(2,1)S(1)} %get-tuple-element.72), channel_id=1, source_target_pairs={{0,112},{16,32},{32,16},{48,64},{64,48},{80,96},{96,80},{112,0},{1... | collective-permute-start | bytes 491528 | tf_op jit(solution)/shard_map/ppermute | solution.py:545
  45.5 7.1 %collective-permute-start.10 = (bf16[8,16,512]{2,1,0:T(8,128)(2,1)S(1)}, bf16[8,16,512]{2,1,0:T(8,128)(2,1)S(1)}, u32[]{:S(2)}, u32[]{:S(2)}) collective-permute-start(bf16[8,16,512]{2,1,0:T(8,128)(2,1)S(1)} %get-tuple-element.73), channel_id=1, source_target_pairs={{0,1},{1,0},{2,3},{3,2},{4,5},{5,4},{6,7},{7,6},{8,9},{9,8},{10,11... | collective-permute-start | bytes 393224 | tf_op jit(solution)/shard_map/ppermute | solution.py:548
  46.7 8.5 %collective-permute-start.11 = (bf16[8,16,512]{2,1,0:T(8,128)(2,1)S(1)}, bf16[8,16,512]{2,1,0:T(8,128)(2,1)S(1)}, u32[]{:S(2)}, u32[]{:S(2)}) collective-permute-start(bf16[8,16,512]{2,1,0:T(8,128)(2,1)S(1)} %get-tuple-element.74), channel_id=1, source_target_pairs={{0,15},{1,2},{2,1},{3,4},{4,3},{5,6},{6,5},{7,8},{8,7},{9,10},{10,... | collective-permute-start | bytes 393224 | tf_op jit(solution)/shard_map/ppermute | solution.py:547
  56.4 9.2 %collective-permute-start.12 = (bf16[10,16,512]{2,1,0:T(8,128)(2,1)S(1)}, bf16[10,16,512]{2,1,0:T(8,128)(2,1)S(1)}, u32[]{:S(2)}, u32[]{:S(2)}) collective-permute-start(bf16[10,16,512]{2,1,0:T(8,128)(2,1)S(1)} %get-tuple-element.80), channel_id=1, source_target_pairs={{0,16},{16,0},{32,48},{48,32},{64,80},{80,64},{96,112},{112,96},{1... | collective-permute-start | bytes 491528 | tf_op jit(solution)/shard_map/ppermute | solution.py:546
  56.5 9.1 %collective-permute-start.13 = (bf16[10,16,512]{2,1,0:T(8,128)(2,1)S(1)}, bf16[10,16,512]{2,1,0:T(8,128)(2,1)S(1)}, u32[]{:S(2)}, u32[]{:S(2)}) collective-permute-start(bf16[10,16,512]{2,1,0:T(8,128)(2,1)S(1)} %get-tuple-element.81), channel_id=1, source_target_pairs={{0,112},{16,32},{32,16},{48,64},{64,48},{80,96},{96,80},{112,0},{1... | collective-permute-start | bytes 491528 | tf_op jit(solution)/shard_map/ppermute | solution.py:545
  56.7 7.4 %collective-permute-start.14 = (bf16[8,16,512]{2,1,0:T(8,128)(2,1)S(1)}, bf16[8,16,512]{2,1,0:T(8,128)(2,1)S(1)}, u32[]{:S(2)}, u32[]{:S(2)}) collective-permute-start(bf16[8,16,512]{2,1,0:T(8,128)(2,1)S(1)} %get-tuple-element.82), channel_id=1, source_target_pairs={{0,1},{1,0},{2,3},{3,2},{4,5},{5,4},{6,7},{7,6},{8,9},{9,8},{10,11... | collective-permute-start | bytes 393224 | tf_op jit(solution)/shard_map/ppermute | solution.py:548
  59.4 6.2 %collective-permute-start.15 = (bf16[8,16,512]{2,1,0:T(8,128)(2,1)S(1)}, bf16[8,16,512]{2,1,0:T(8,128)(2,1)S(1)}, u32[]{:S(2)}, u32[]{:S(2)}) collective-permute-start(bf16[8,16,512]{2,1,0:T(8,128)(2,1)S(1)} %get-tuple-element.83), channel_id=1, source_target_pairs={{0,15},{1,2},{2,1},{3,4},{4,3},{5,6},{6,5},{7,8},{8,7},{9,10},{10,... | collective-permute-start | bytes 393224 | tf_op jit(solution)/shard_map/ppermute | solution.py:547
  67.4 18.3 %all-to-all-start.1 = ((bf16[16,2,16,512]{3,2,1,0:T(8,128)(2,1)}), bf16[16,2,16,512]{3,2,1,0:T(8,128)(2,1)S(1)}, u32[]{:S(2)}, u32[]{:S(2)}) async-start(bf16[16,2,16,512]{3,2,1,0:T(8,128)(2,1)} %get-tuple-element.84), calls=%async_computation.1 | async-start | bytes 1048576 | tf_op jit(solution)/shard_map/all_to_all | solution.py:586

commit v4 on v3

v4 whole, which is shorter than its diff:
```python
import jax
import jax.numpy as jnp
from jax import lax
from jax.experimental import pallas as pl
from jax.experimental.pallas import tpu as pltpu
from jax.sharding import PartitionSpec as P

STEPS = 4
C0, C1, C2, C3, C4 = (-205.0 / 72.0, 8.0 / 5.0, -1.0 / 5.0, 8.0 / 315.0, -1.0 / 560.0)
COEFFS = (C0, C1, C2, C3, C4)
RECEIVER_PLANE = 2
PLANES = 5
F32, BF16 = jnp.float32, jnp.bfloat16
VMEM_LIMIT = 24 * 1024 * 1024

RCV = dict(lead=16, rows=32, lanes=256)
SRC = dict(lead=16, rows=16, lanes=512)


def flat(ref):
    return ref.reshape(ref.shape[0], ref.shape[1] * ref.shape[2], 128)


def split(value):
    high = value.astype(BF16)
    return high, (value - high.astype(F32)).astype(BF16)


def planes_of(layers):
    return [*split(layers[0]), *[layer.astype(BF16) for layer in layers[1:]]]


def layers_of(planes):
    planes = [plane.astype(F32) for plane in planes]
    return [planes[0] + planes[1], *planes[2:]]


def sides():
    return lax.axis_index("gx") % 2 == 0, lax.axis_index("gy") % 2 == 0


def layer_at(high, count, h):
    return jnp.where(high, count - 1 - h, h)


def pack_source(src, gx_first, gx_second, gy_first, gy_second):
    up_x, up_y = sides()
    for out_x, out_y, high_x, high_y in (
        (gx_second, gy_second, ~up_x, ~up_y),
        (gx_first, gy_first, up_x, up_y),
    ):
        for t in range(4):
            lanes = slice(t * 128, t * 128 + 128)
            layers = [src[t, pl.ds(layer_at(high_x, 16, h), 16, stride=16), :] for h in range(4)]
            for p, plane in enumerate(planes_of(layers)):
                out_x[p, :, lanes] = plane
            rows = [pl.multiple_of(layer_at(high_y, 16, h) * 16, 16) for h in range(4)]
            for p, plane in enumerate(planes_of([src[t, pl.ds(row, 16), :] for row in rows])):
                out_y[p, :, lanes] = plane


def pack_receiver(rcv, at, gx_first, gx_second, gy_first, gy_second):
    up_x, up_y = sides()
    for out_x, out_y, high_x, high_y in (
        (gx_second, gy_second, ~up_x, ~up_y),
        (gx_first, gy_first, up_x, up_y),
    ):
        for t in range(4):
            lanes = slice(t * 128, t * 128 + 128)
            half, col = divmod(t, 2)
            rows = [pl.multiple_of(layer_at(high_x, 16, h) * 32 + half * 16, 16) for h in range(4)]
            for p, plane in enumerate(planes_of([rcv[col, pl.ds(row, 16), :] for row in rows])):
                out_x[at + p, :, lanes] = plane
        for col in range(2):
            layers = [rcv[col, pl.ds(layer_at(high_y, 32, h), 16, stride=32), :] for h in range(4)]
            for p, plane in enumerate(planes_of(layers)):
                lane = (p % 2) * 256 + col * 128
                out_y[at + p // 2, :, lane : lane + 128] = plane


def add_layers(out, vel, t, rows_of, layers, live):
    if live is not None:
        layers = [jnp.where(live, layer, 0.0) for layer in layers]
    for d in range(4):
        term = COEFFS[d + 1] * layers[0]
        for h in range(1, 4 - d):
            term = term + COEFFS[d + h + 1] * layers[h]
        rows = rows_of(d)
        out[t, rows, :] = out[t, rows, :] + vel[t, rows, :] * term


def received(gx_first, gx_second, gy_first, gy_second):
    ix, iy = lax.axis_index("gx"), lax.axis_index("gy")
    up_x, up_y = sides()
    live_x = jnp.broadcast_to((ix != 0) & (ix != 7), (16, 128))
    live_y = jnp.broadcast_to((iy != 0) & (iy != 15), (16, 128))
    return (
        (gx_first, gy_first, up_x, up_y, None, None),
        (gx_second, gy_second, ~up_x, ~up_y, live_x, live_y),
    )


def add_source(out, vel, *buffers):
    for in_x, in_y, high_x, high_y, live_x, live_y in received(*buffers):
        for t in range(4):
            lanes = slice(t * 128, t * 128 + 128)
            add_layers(
                out,
                vel,
                t,
                lambda d: pl.ds(pl.multiple_of(layer_at(high_y, 16, d) * 16, 16), 16),
                layers_of([in_y[p, :, lanes] for p in range(PLANES)]),
                live_y,
            )
            add_layers(
                out,
                vel,
                t,
                lambda d: pl.ds(layer_at(high_x, 16, d), 16, stride=16),
                layers_of([in_x[p, :, lanes] for p in range(PLANES)]),
                live_x,
            )


def add_receiver(out, vel, at, *buffers):
    for in_x, in_y, high_x, high_y, live_x, live_y in received(*buffers):
        for t in range(4):
            lanes = slice(t * 128, t * 128 + 128)
            half, col = divmod(t, 2)
            add_layers(
                out,
                vel,
                col,
                lambda d: pl.ds(pl.multiple_of(layer_at(high_x, 16, d) * 32 + half * 16, 16), 16),
                layers_of([in_x[at + p, :, lanes] for p in range(PLANES)]),
                live_x,
            )
        for col in range(2):
            planes = []
            for p in range(PLANES):
                lane = (p % 2) * 256 + col * 128
                planes.append(in_y[at + p // 2, :, lane : lane + 128])
            add_layers(
                out,
                vel,
                col,
                lambda d: pl.ds(layer_at(high_y, 32, d), 16, stride=32),
                layers_of(planes),
                live_y,
            )


def local_laplacian(f, now, store):
    lead, rows, tiles = f["lead"], f["rows"], f["lanes"] // 128
    lane = lax.broadcasted_iota(jnp.int32, (rows, 128), 1)
    below = {k: lane < k for k in range(1, 5)}
    above = {k: lane >= 128 - k for k in range(1, 5)}
    none = jnp.zeros((8, 128), F32)
    for a in range(lead):
        here = [now[t, a * rows : a * rows + rows, :] for t in range(tiles)]
        around = [jnp.concatenate([none, c, none], axis=0) for c in here]
        total = [(3.0 * C0) * c for c in here]
        for k in range(1, 5):
            up = [pltpu.roll(c, k, 1) for c in here]
            down = [pltpu.roll(c, 128 - k, 1) for c in here]
            for t in range(tiles):
                s = around[t][8 - k : 8 - k + rows] + around[t][8 + k : 8 + k + rows]
                for other in (a - k, a + k):
                    if 0 <= other < lead:
                        s = s + now[t, other * rows : other * rows + rows, :]
                s = s + jnp.where(below[k], up[t - 1] if t > 0 else 0.0, up[t])
                s = s + jnp.where(above[k], down[t + 1] if t + 1 < tiles else 0.0, down[t])
                total[t] = total[t] + COEFFS[k] * s
        for t in range(tiles):
            store(t, a, slice(a * rows, a * rows + rows), here[t], total[t])


def pack_brick(src, out, columns=range(4)):
    group = lax.broadcasted_iota(jnp.int32, (16, 128), 1) // 32
    for t in columns:
        for xg in range(4):
            rows = [src[t, pl.ds(xg * 4 + xl, 16, stride=16), :] for xl in range(4)]
            for g in range(4):
                piece = None
                for xl in range(4):
                    turned = rows[xl] if xl == g else pltpu.roll(rows[xl], ((xl - g) % 4) * 32, 1)
                    piece = turned if piece is None else jnp.where(group == xl, turned, piece)
                out[t * 4 + g, :, xg * 128 : xg * 128 + 128] = piece.astype(BF16)


def unpack_velocity(pieces, out):
    group = lax.broadcasted_iota(jnp.int32, (16, 128), 1) // 32
    for t in range(4):
        for xg in range(4):
            parts = [pieces[t * 4 + g, :, xg * 128 : xg * 128 + 128] for g in range(4)]
            for xl in range(4):
                row = None
                for g in range(4):
                    turned = parts[g] if xl == g else pltpu.roll(parts[g], ((g - xl) % 4) * 32, 1)
                    row = turned if row is None else jnp.where(group == g, turned, row)
                out[t, pl.ds(xg * 4 + xl, 16, stride=16), :] = row


SRC_PLANES, RCV_PLANES = (PLANES, PLANES), (PLANES, 3)


def halo_buffers(*fields):
    shapes = [(sum(f[axis] for f in fields), 16, 512) for axis in (0, 0, 1, 1)]
    return [jax.ShapeDtypeStruct(shape, BF16) for shape in shapes]


SRC_COLS = jax.ShapeDtypeStruct((4, 256, 128), F32)
RCV_COLS = jax.ShapeDtypeStruct((2, 512, 128), F32)
BRICK = jax.ShapeDtypeStruct((16, 16, 512), BF16)
VM = pl.BlockSpec(memory_space=pltpu.VMEM)
SM = pl.BlockSpec(memory_space=pltpu.SMEM)
HB = pl.BlockSpec(memory_space=pltpu.HBM)


def in_hbm(*arrays):
    return [pltpu.with_memory_space_constraint(x, pltpu.HBM) for x in arrays]


def params():
    return pltpu.CompilerParams(vmem_limit_bytes=VMEM_LIMIT)


def hint(microseconds):
    return pl.CostEstimate(flops=0, bytes_accessed=int(microseconds * 3.6e6), transcendentals=0)


def column_copies(block, cols, sem):
    return [
        pltpu.make_async_copy(
            block.at[pl.ds(a, 8), :, pl.ds(t * 128, 128)], cols.at[t, pl.ds(a, 8), :, :], sem
        )
        for a in (0, 8)
        for t in range(cols.shape[0])
    ]


def start(copies):
    for copy in copies:
        copy.start()


def wait(copies):
    for copy in copies:
        copy.wait()


def turn_velocity(vel):
    def kernel(vel, turned_out, cols, turned, sems):
        pieces = [
            pltpu.make_async_copy(
                vel.at[pl.ds(q * 4, 4), :, pl.ds(t * 128, 128)], cols.at[t, pl.ds(q * 4, 4), :, :], sems.at[q]
            )
            for q in range(4)
            for t in range(2)
        ]
        start(pieces)
        flat_cols = flat(cols)
        outs = []
        for q in range(4):
            wait(pieces[2 * q : 2 * q + 2])
            lanes = pl.ds(q * 128, 128)
            for t in range(2):
                turned[t * 128 : t * 128 + 128, lanes] = flat_cols[t, q * 128 : q * 128 + 128, :].T
            outs.append(pltpu.make_async_copy(turned.at[:, lanes], turned_out.at[:, lanes], sems.at[4]))
            outs[-1].start()
        wait(outs)

    return pl.pallas_call(
        kernel,
        out_shape=pltpu.HBM((256, 512), F32),
        in_specs=[HB],
        out_specs=HB,
        scratch_shapes=[
            pltpu.VMEM((2, 16, 32, 128), F32),
            pltpu.VMEM((256, 512), F32),
            pltpu.SemaphoreType.DMA((5,)),
        ],
        compiler_params=params(),
        name="turn_velocity",
    )(*in_hbm(vel))


def first_halos(src):
    def kernel(src, cols, *refs):
        copies = column_copies(src, cols, refs[-1])
        start(copies)
        wait(copies)
        pack_source(flat(cols), *refs[:4])

    return pl.pallas_call(
        kernel,
        out_shape=[jax.ShapeDtypeStruct((4, 16, 16, 128), F32), *halo_buffers(SRC_PLANES)],
        in_specs=[HB],
        out_specs=[VM] * 5,
        scratch_shapes=[pltpu.SemaphoreType.DMA],
        compiler_params=params(),
        name="first_halos",
    )(*in_hbm(src))


def source_velocity(pieces):
    return pl.pallas_call(
        unpack_velocity,
        out_shape=SRC_COLS,
        in_specs=[VM],
        out_specs=VM,
        compiler_params=params(),
        name="source_velocity",
    )(pieces)


def injections(traces, receiver_x, receiver_y):
    def kernel(traces_hbm, rx_hbm, ry_hbm, out, traces, rx, ry, sem):
        inputs = [
            pltpu.make_async_copy(traces_hbm, traces, sem),
            pltpu.make_async_copy(rx_hbm, rx, sem),
            pltpu.make_async_copy(ry_hbm, ry, sem),
        ]
        start(inputs)
        wait(inputs)
        xs = lax.axis_index("gx") * 16 + lax.broadcasted_iota(jnp.int32, (16, 512), 0)
        ys = lax.axis_index("gy") * 32 + lax.broadcasted_iota(jnp.int32, (32, 512), 0)
        total = jnp.zeros((32, 128), F32)
        for c in range(8):
            cols = slice(c * 512, c * 512 + 512)
            at_x = rx[:, cols] == xs
            at_y = jnp.where(ry[:, cols] == ys, 1.0, 0.0)
            weighted = [jnp.where(at_x, traces[s : s + 1, cols], 0.0) for s in range(STEPS)]
            total = total + lax.dot_general(
                at_y,
                jnp.concatenate(weighted + [jnp.zeros((64, 512), F32)], axis=0),
                (((1,), (1,)), ((), ())),
                precision=lax.Precision.HIGHEST,
                preferred_element_type=F32,
            )
        out[...] = total

    return pl.pallas_call(
        kernel,
        out_shape=jax.ShapeDtypeStruct((32, 128), F32),
        in_specs=[HB] * 3,
        out_specs=VM,
        scratch_shapes=[
            pltpu.VMEM((4, 4096), F32),
            pltpu.VMEM((1, 4096), jnp.int32),
            pltpu.VMEM((1, 4096), jnp.int32),
            pltpu.SemaphoreType.DMA,
        ],
        compiler_params=params(),
        cost_estimate=hint(2),
        name="injections",
    )(*in_hbm(traces, receiver_x.reshape(1, -1), receiver_y.reshape(1, -1)))


def subtract(cols, block):
    for t in range(cols.shape[0]):
        cols[t] = cols[t] - block[:, t * 128 : t * 128 + 128]


def local_source(now, nxt, vel, out, lap_out=None):
    def store(t, a, rows, here, lap):
        value = 2.0 * here
        if nxt is not None:
            value = value - nxt[t, rows, :]
        if vel is None:
            lap_out[t, rows, :] = lap
        else:
            value = value + vel[t, rows, :] * lap
        out[t, rows, :] = value

    local_laplacian(SRC, now, store)


def local_receiver(step, now, nxt, vel, inject, out):
    lane = lax.broadcasted_iota(jnp.int32, (32, 128), 1)

    def store(t, a, rows, here, lap):
        value = 2.0 * here + vel[t, rows, :] * lap
        if nxt is not None:
            value = value - nxt[t, rows, :]
        if t == 0:
            turn = (RECEIVER_PLANE - step * 16 - a) % 128
            value = value + jnp.where(lane == RECEIVER_PLANE, pltpu.roll(inject[...], turn, 1), 0.0)
        out[t, rows, :] = value

    local_laplacian(RCV, now, store)


def add_wavelet(step, cell, wavelet, out):
    z = cell[2] - lax.axis_index("gy") * 16
    x = cell[0] - lax.axis_index("gx") * 16

    @pl.when((z >= 0) & (z < 16) & (x >= 0) & (x < 16))
    def _():
        at = pl.ds(z * 16 + x, 1)
        lanes = lax.broadcasted_iota(jnp.int32, (1, 128), 1)
        for t in range(4):
            out[t, at, :] = out[t, at, :] + jnp.where(lanes + t * 128 == cell[1], wavelet[step], 0.0)


def local_first(src, src_next, rcv, wavelet, cell, saved, plane_index):
    def kernel(src, src_next, rcv, wavelet_hbm, cell_hbm, saved, index_hbm, base, lap, planes, *refs):
        packed, (next_src, rcv_cols, wavelet, cell, index, sems) = refs[:4], refs[4:]
        ix, iy = lax.axis_index("gx"), lax.axis_index("gy")
        get_index = pltpu.make_async_copy(index_hbm, index, sems.at[0])
        get_index.start()
        scalars = [
            pltpu.make_async_copy(wavelet_hbm, wavelet, sems.at[1]),
            pltpu.make_async_copy(cell_hbm, cell, sems.at[2]),
        ]
        get_next = pltpu.make_async_copy(src_next, next_src, sems.at[3])
        get_rcv = column_copies(rcv, rcv_cols, sems.at[4])
        start([*scalars, get_next, *get_rcv])
        local_source(src, None, None, base, lap)
        get_index.wait()
        edge = (ix == 0) | (ix == 7)
        side = jnp.where(ix == 0, 0, 1)
        restores = [
            pltpu.make_async_copy(
                saved.at[index[step], side, pl.ds(pl.multiple_of(iy * 16, 16), 16), pl.ds(t * 128, 128)],
                planes.at[step, t],
                sems.at[5],
            )
            for step in range(STEPS)
            for t in range(4)
        ]

        @pl.when(edge)
        def _():
            start(restores)

        wait(get_rcv)
        pack_receiver(flat(rcv_cols), 0, *packed)
        get_next.wait()
        subtract(base, next_src)
        wait(scalars)
        add_wavelet(0, cell, wavelet, base)

        @pl.when(edge)
        def _():
            wait(restores)

    return pl.pallas_call(
        kernel,
        out_shape=[
            SRC_COLS,
            SRC_COLS,
            jax.ShapeDtypeStruct((STEPS, 4, 16, 128), F32),
            *halo_buffers(RCV_PLANES),
        ],
        in_specs=[VM] + [HB] * 6,
        out_specs=[VM] * 7,
        scratch_shapes=[
            pltpu.VMEM((256, 512), F32),
            pltpu.VMEM((2, 16, 32, 128), F32),
            pltpu.SMEM((4,), F32),
            pltpu.SMEM((3,), jnp.int32),
            pltpu.SMEM((4,), jnp.int32),
            pltpu.SemaphoreType.DMA((6,)),
        ],
        compiler_params=params(),
        cost_estimate=hint(3),
        name="local_first",
    )(src, *in_hbm(src_next, rcv, wavelet, cell, saved, plane_index))


def local_second(src, src_next, rcv, rcv_next, vel, vel_src, inject, wavelet, cell):
    def kernel(src, src_next, rcv, rcv_next, vel, vel_src, inject, wavelet_hbm, cell_hbm, *refs):
        src_out, rcv_out, vel_cols, next_src, rcv_cols, next_rcv, wavelet, cell, sems = refs
        scalars = [
            pltpu.make_async_copy(wavelet_hbm, wavelet, sems.at[0]),
            pltpu.make_async_copy(cell_hbm, cell, sems.at[1]),
        ]
        get_rcv = column_copies(rcv, rcv_cols, sems.at[2]) + column_copies(vel, vel_cols, sems.at[2])
        nexts = [
            pltpu.make_async_copy(src_next, next_src, sems.at[3]),
            pltpu.make_async_copy(rcv_next, next_rcv, sems.at[3]),
        ]
        start([*scalars, *get_rcv, *nexts])
        local_source(src, None, vel_src, src_out)
        wait(get_rcv)
        local_receiver(0, flat(rcv_cols), None, flat(vel_cols), inject, rcv_out)
        wait(nexts)
        subtract(src_out, next_src)
        subtract(rcv_out, next_rcv)
        wait(scalars)
        add_wavelet(1, cell, wavelet, src_out)

    return pl.pallas_call(
        kernel,
        out_shape=[SRC_COLS, RCV_COLS, jax.ShapeDtypeStruct((2, 16, 32, 128), F32)],
        in_specs=[VM] + [HB] * 4 + [VM] * 2 + [HB] * 2,
        out_specs=[VM] * 3,
        scratch_shapes=[
            pltpu.VMEM((256, 512), F32),
            pltpu.VMEM((2, 16, 32, 128), F32),
            pltpu.VMEM((512, 256), F32),
            pltpu.SMEM((4,), F32),
            pltpu.SMEM((3,), jnp.int32),
            pltpu.SemaphoreType.DMA((4,)),
        ],
        compiler_params=params(),
        cost_estimate=hint(4),
        name="local_second",
    )(src, *in_hbm(src_next, rcv, rcv_next, vel), vel_src, inject, *in_hbm(wavelet, cell))


def local_later(step, src, src_next, rcv, rcv_next, vel_src, vel, inject, wavelet, cell):
    from_hbm, last = step == 2, step == STEPS - 1

    def kernel(src, src_next, rcv, rcv_next, vel_src, vel, inject, wavelet_hbm, cell_hbm, src_out, rcv_out, *refs):
        brick = refs[0] if last else None
        wavelet, cell, next_rcv, sems = refs[-4:]
        copies = [
            pltpu.make_async_copy(wavelet_hbm, wavelet, sems.at[0]),
            pltpu.make_async_copy(cell_hbm, cell, sems.at[1]),
        ]
        if from_hbm:
            copies.append(pltpu.make_async_copy(rcv_next, next_rcv, sems.at[2]))
        start(copies)
        local_source(src, src_next, vel_src, src_out)
        local_receiver(step - 1, rcv, None if from_hbm else rcv_next, vel, inject, rcv_out)
        if last:
            pack_brick(src_next, brick)
        wait(copies)
        if from_hbm:
            subtract(rcv_out, next_rcv)
        add_wavelet(step, cell, wavelet, src_out)

    if from_hbm:
        (rcv_next,) = in_hbm(rcv_next)
    out_shape = [SRC_COLS, RCV_COLS] + ([BRICK] if last else [])
    return pl.pallas_call(
        kernel,
        out_shape=out_shape,
        in_specs=[VM] * 3 + [HB if from_hbm else VM] + [VM] * 3 + [HB] * 2,
        out_specs=[VM] * len(out_shape),
        scratch_shapes=[
            pltpu.SMEM((4,), F32),
            pltpu.SMEM((3,), jnp.int32),
            pltpu.VMEM((512, 256) if from_hbm else (8, 128), F32),
            pltpu.SemaphoreType.DMA((3,)),
        ],
        compiler_params=params(),
        cost_estimate=hint(3),
        name=f"local_step{step}",
    )(src, src_next, rcv, rcv_next, vel_src, vel, inject, *in_hbm(wavelet, cell))


def local_last(rcv, rcv_next, vel, inject):
    def kernel(rcv, rcv_next, vel, inject, out):
        local_receiver(STEPS - 1, rcv, rcv_next, vel, inject, out)

    return pl.pallas_call(
        kernel,
        out_shape=RCV_COLS,
        in_specs=[VM] * 4,
        out_specs=VM,
        compiler_params=params(),
        cost_estimate=hint(2),
        name="local_last",
    )(rcv, rcv_next, vel, inject)


def restore_planes(step, src, planes):
    ix = lax.axis_index("gx")

    @pl.when(ix == 0)
    def _():
        for t in range(4):
            src[t, pl.ds(0, 16, stride=16), :] = planes[step, t]

    @pl.when(ix == 7)
    def _():
        for t in range(4):
            src[t, pl.ds(15, 16, stride=16), :] = planes[step, t]


def halo_first(base, lap, vel_src, halos, planes, rcv_packed):
    def kernel(base, lap, vel_src, gx1, gx2, gy1, gy2, planes, *refs):
        rcv_packed, src, packed = refs[:4], refs[4], refs[5:]
        src[...] = base[...] + vel_src[...] * lap[...]
        add_source(src, vel_src, gx1, gx2, gy1, gy2)
        restore_planes(0, src, planes)
        pack_source(src, *packed)
        for half, whole in zip(rcv_packed, packed):
            whole[PLANES:] = half[...]

    args = [base, lap, vel_src, *halos, planes, *rcv_packed]
    return pl.pallas_call(
        kernel,
        out_shape=[SRC_COLS, *halo_buffers(SRC_PLANES, RCV_PLANES)],
        in_specs=[VM] * len(args),
        out_specs=[VM] * 5,
        compiler_params=params(),
        name="halo_first",
    )(*args)


def halo_step(step, local, vel_src, vel, halos, planes):
    last = step == STEPS - 1

    def kernel(*refs):
        refs = list(refs)
        local_src, local_rcv = refs[:2]
        early = refs.pop(2) if last else None
        vel_src, vel, gx1, gx2, gy1, gy2, planes, src, rcv = refs[2:11]
        packed, refs = refs[11:15], refs[15:]
        if last:
            bricks, late, sems = refs
            copies = [pltpu.make_async_copy(early, bricks.at[:, 0], sems.at[0])]
            copies[0].start()
        src[...] = local_src[...]
        add_source(src, vel_src, gx1, gx2, gy1, gy2)
        restore_planes(step, src, planes)
        if last:
            for t in range(4):
                pack_brick(src, late, (t,))
                part = pl.ds(t * 4, 4)
                copies.append(pltpu.make_async_copy(late.at[part], bricks.at[part, 1], sems.at[1]))
                copies[-1].start()
        else:
            pack_source(src, *packed)
        rcv[...] = local_rcv[...]
        add_receiver(rcv, vel, PLANES, gx1, gx2, gy1, gy2)
        pack_receiver(rcv, 0 if last else PLANES, *packed)
        if last:
            wait(copies)

    args = [*local, vel_src, vel, *halos, planes]
    out_shape = [SRC_COLS, RCV_COLS]
    out_shape += halo_buffers(RCV_PLANES) if last else halo_buffers(SRC_PLANES, RCV_PLANES)
    out_shape += [pltpu.HBM((16, 2, 16, 512), BF16)] if last else []
    return pl.pallas_call(
        kernel,
        out_shape=out_shape,
        in_specs=[VM] * len(args),
        out_specs=[VM] * 6 + ([HB] if last else []),
        scratch_shapes=[pltpu.VMEM((16, 16, 512), BF16), pltpu.SemaphoreType.DMA((2,))] if last else [],
        compiler_params=params(),
        name=f"halo_step{step}",
    )(*args)


def halo_last(local, vel, halos):
    def kernel(local, vel, gx1, gx2, gy1, gy2, rcv):
        rcv[...] = local[...]
        add_receiver(rcv, vel, 0, gx1, gx2, gy1, gy2)

    return pl.pallas_call(
        kernel,
        out_shape=RCV_COLS,
        in_specs=[VM] * 6,
        out_specs=VM,
        compiler_params=params(),
        name="halo_last",
    )(local, vel, *halos)


def write_source(src):
    def kernel(src, out, sem):
        copies = [pltpu.make_async_copy(src.at[t], out.at[:, pl.ds(t * 128, 128)], sem) for t in range(4)]
        start(copies)
        wait(copies)

    return pl.pallas_call(
        kernel,
        out_shape=jax.ShapeDtypeStruct((256, 512), F32),
        in_specs=[VM],
        out_specs=HB,
        scratch_shapes=[pltpu.SemaphoreType.DMA],
        compiler_params=params(),
        cost_estimate=hint(1),
        name="write_source",
    )(src)


def make_image(bricks, rcv_early, rcv_late):
    def kernel(bricks, rcv_early, rcv_late, out, rcv_out, held, sems):
        copies = [
            pltpu.make_async_copy(rcv_late.at[t], rcv_out.at[:, pl.ds(t * 128, 128)], sems.at[0]) for t in range(2)
        ]
        start(copies)
        for q in range(4):
            rows = slice(q * 128, q * 128 + 128)
            early = bricks[:, 0, :, rows].reshape(256, 128).astype(F32).T
            late = bricks[:, 1, :, rows].reshape(256, 128).astype(F32).T
            for t in range(2):
                lanes = slice(t * 128, t * 128 + 128)
                held[rows, lanes] = early[:, lanes] * rcv_early[t, rows, :] + late[:, lanes] * rcv_late[t, rows, :]
            copies.append(pltpu.make_async_copy(held.at[rows, :], out.at[rows, :], sems.at[1]))
            copies[-1].start()
        wait(copies)

    return pl.pallas_call(
        kernel,
        out_shape=[jax.ShapeDtypeStruct((512, 256), F32)] * 2,
        in_specs=[VM] * 3,
        out_specs=[HB] * 2,
        scratch_shapes=[pltpu.VMEM((512, 256), F32), pltpu.SemaphoreType.DMA((2,))],
        compiler_params=params(),
        name="make_image",
    )(bricks, rcv_early, rcv_late)


def exchange(buffers):
    gx_first, gx_second, gy_first, gy_second = buffers
    inner = lambda n: [(i, i ^ 1) for i in range(n)]
    outer = lambda n: [(i, (((i + 1) ^ 1) - 1) % n) for i in range(n)]
    from_gx_second = lax.ppermute(gx_second, "gx", outer(8))
    from_gx_first = lax.ppermute(gx_first, "gx", inner(8))
    from_gy_second = lax.ppermute(gy_second, "gy", outer(16))
    from_gy_first = lax.ppermute(gy_first, "gy", inner(16))
    return from_gx_first, from_gx_second, from_gy_first, from_gy_second


def on_device(
    source_now,
    source_next,
    receiver_now,
    receiver_next,
    velocity,
    saved_planes,
    plane_index,
    wavelet,
    source_cell,
    traces,
    receiver_x,
    receiver_y,
):
    turned = turn_velocity(velocity)
    pieces = lax.all_to_all(turned.reshape(16, 16, 512), "gy", split_axis=0, concat_axis=0, tiled=True)
    src, *to_send = first_halos(source_now)
    halos = exchange(to_send)
    src = src.reshape(4, 256, 128)
    base, lap, planes, *rcv_packed = local_first(
        src, source_next.reshape(256, 512), receiver_now, wavelet, source_cell, saved_planes, plane_index
    )
    vel_src = source_velocity(pieces)
    src_0, *to_send = halo_first(base, lap, vel_src, halos, planes, rcv_packed)
    halos = exchange(to_send)
    inject = injections(traces, receiver_x, receiver_y)
    rcv_now = receiver_now.reshape(512, 256)
    *local, vel = local_second(
        src_0,
        source_now.reshape(256, 512),
        receiver_now,
        receiver_next.reshape(512, 256),
        velocity,
        vel_src,
        inject,
        wavelet,
        source_cell,
    )
    vel = vel.reshape(2, 512, 128)
    src_1, rcv_0, *to_send = halo_step(1, local, vel_src, vel, halos, planes)
    halos = exchange(to_send)
    local = local_later(2, src_1, src_0, rcv_0, rcv_now, vel_src, vel, inject, wavelet, source_cell)
    src_2, rcv_1, *to_send = halo_step(2, local, vel_src, vel, halos, planes)
    halos = exchange(to_send)
    local = local_later(3, src_2, src_1, rcv_1, rcv_0, vel_src, vel, inject, wavelet, source_cell)
    src_3, rcv_2, *to_send, bricks = halo_step(3, local, vel_src, vel, halos, planes)
    bricks = lax.all_to_all(bricks, "gy", split_axis=0, concat_axis=0, tiled=True)
    halos = exchange(to_send)
    local = local_last(rcv_2, rcv_1, vel, inject)
    source_field = write_source(src_3)
    rcv_3 = halo_last(local, vel, halos)
    image, receiver_field = make_image(bricks, rcv_1, rcv_3)
    return (image.reshape(16, 32, 256), receiver_field.reshape(16, 32, 256), source_field.reshape(16, 16, 512))


def solution(mesh):
    field, turned = P("gx", "gy", None), P("gy", "gx", None)
    return jax.shard_map(
        on_device,
        mesh=mesh,
        in_specs=(turned, turned, field, field, field, P(), P(), P(), P(), P(), P(), P()),
        out_specs=(field, field, turned),
        check_vma=False,
    )
```

time: 87.2 us -> 84.4 us (0.968)
  waiting for transfers between devices: 17.7 us -> 10.8 us
  starting transfers between devices: 38.7 us -> 44.2 us
    all_to_all x1, waiting for transfers between devices: 10.2 us -> 0.01 us  [on_device(): lax.all_to_all(bricks, 'gy', split_axis=0, concat_axis=0, tiled=True)]
    ppermute x4 -> x5, starting transfers between devices: 8.5 us -> 11.7 us  [exchange(): from_gy_second = lax.ppermute(gy_second, 'gy', outer(16))]
    ppermute x4 -> x5, starting transfers between devices: 7.95 us -> 10.7 us  [exchange(): from_gx_second = lax.ppermute(gx_second, 'gx', outer(8))]
    pallas_call x4 -> x3, Pallas kernels: 6.53 us -> 3.95 us  [halo_step(): pl.pallas_call(kernel, out_shape=out_shape, in_specs=[VM] * len(args), ou...]
    all_to_all x1, starting transfers between devices: 7.12 us -> 4.64 us  [on_device(): lax.all_to_all(bricks, 'gy', split_axis=0, concat_axis=0, tiled=True)]
    ppermute x4 -> x5, starting transfers between devices: 4.47 us -> 6.56 us  [exchange(): from_gy_first = lax.ppermute(gy_first, 'gy', inner(16))]
    ppermute x4 -> x5, waiting for transfers between devices: 7.5 us -> 9.39 us  [exchange(): from_gy_second = lax.ppermute(gy_second, 'gy', outer(16))]
    pallas_call x8 -> x12, Pallas kernels: 21.5 us -> 23.4 us  [the longest x2 7.82 us: local_later(): pl.pallas_call(kernel, out_shape=out_shape, in_specs=[VM] * 3 + [HB if fr...]
  transfers between devices with their start and end apart: 18 -> 22, of which waited for: 5 -> 6; matrix products, arithmetic and copies ran while one was open for 0% -> 0% of each run, Pallas kernels for 21% -> 24%
where the time goes in v4:
time: 84.4 us; the launch traced here: 83.8 us
  starting transfers between devices  44.2 us (52%)
  Pallas kernels  27.8 us (33%)
  waiting for transfers between devices  10.8 us (13%)
  between operations  1 us (1%)
    ppermute x5, starting transfers between devices, exchange(): from_gy_second = lax.ppermute(gy_second, 'gy', outer(16))  11.7 us
    ppermute x5, starting transfers between devices, exchange(): from_gx_second = lax.ppermute(gx_second, 'gx', outer(8))  10.7 us
    ppermute x5, waiting for transfers between devices, exchange(): from_gy_second = lax.ppermute(gy_second, 'gy', outer(16))  9.39 us
    all_to_all x1, starting transfers between devices, on_device(): lax.all_to_all(turned.reshape(16, 16, 512), 'gy', split_axis=0, concat_ax...  8.46 us
    pallas_call x2, Pallas kernels, local_later(): pl.pallas_call(kernel, out_shape=out_shape, in_specs=[VM] * 3 + [HB if fr...  7.82 us
    ppermute x5, starting transfers between devices, exchange(): from_gy_first = lax.ppermute(gy_first, 'gy', inner(16))  6.56 us
    all_to_all x1, starting transfers between devices, on_device(): lax.all_to_all(bricks, 'gy', split_axis=0, concat_axis=0, tiled=True)  4.64 us
    pallas_call x3, Pallas kernels, halo_step(): pl.pallas_call(kernel, out_shape=out_shape, in_specs=[VM] * len(args), ou...  3.95 us
  transfers between devices with their start and end apart: 22, of which 6 were waited for; matrix products, arithmetic and copies ran while one was open for 0% of the time, Pallas kernels for 24%

profile of v4, /device:TPU:1, one launch (start us, length us, event | category | flops | bytes accessed | tf_op | source)
XLA Modules:
  0.0 83.8 jit_solution(16722124806717051689)
XLA Ops:
  0.6 2.0 %turn_velocity.1 = f32[256,512]{1,0:T(8,128)} custom-call(f32[16,32,256]{2,1,0:T(8,128)} %vel.3), custom_call_target="tpu_custom_call" | custom-call | tf_op jit(solution)/shard_map/turn_velocity/pallas_call | solution.py:273
  2.6 8.5 %all-to-all-start = ((f32[16,16,512]{2,1,0:T(8,128)}), f32[16,16,512]{2,1,0:T(8,128)S(1)}, u32[]{:S(2)}, u32[]{:S(2)}) async-start(f32[16,16,512]{2,1,0:T(8,128)} %bitcast.21), calls=%async_computation | async-start | bytes 1048576 | tf_op jit(solution)/shard_map/all_to_all | solution.py:737
  11.1 1.2 %first_halos.1 = (f32[4,16,16,128]{3,2,1,0:T(8,128)S(1)}, bf16[5,16,512]{2,1,0:T(8,128)(2,1)S(1)}, bf16[5,16,512]{2,1,0:T(8,128)(2,1)S(1)}, bf16[5,16,512]{2,1,0:T(8,128)(2,1)S(1)}, bf16[5,16,512]{2,1,0:T(8,128)(2,1)S(1)}) custom-call(f32[16,16,512]{2,1,0:T(8,128)} %src.1), custom_call_target="tpu_custom_call" | custom-call | tf_op jit(solution)/shard_map/first_halos/pallas_call | solution.py:295
  12.3 1.7 %collective-permute-start = (bf16[5,16,512]{2,1,0:T(8,128)(2,1)S(1)}, bf16[5,16,512]{2,1,0:T(8,128)(2,1)S(1)}, u32[]{:S(2)}, u32[]{:S(2)}) collective-permute-start(bf16[5,16,512]{2,1,0:T(8,128)(2,1)S(1)} %get-tuple-element.52), channel_id=1, source_target_pairs={{0,16},{16,0},{32,48},{48,32},{64,80},{80,64},{96,112},{112,96},{1... | collective-permute-start | bytes 245768 | tf_op jit(solution)/shard_map/ppermute | solution.py:716
  14.1 2.4 %collective-permute-start.1 = (bf16[5,16,512]{2,1,0:T(8,128)(2,1)S(1)}, bf16[5,16,512]{2,1,0:T(8,128)(2,1)S(1)}, u32[]{:S(2)}, u32[]{:S(2)}) collective-permute-start(bf16[5,16,512]{2,1,0:T(8,128)(2,1)S(1)} %get-tuple-element.53), channel_id=1, source_target_pairs={{0,112},{16,32},{32,16},{48,64},{64,48},{80,96},{96,80},{112,0},{1... | collective-permute-start | bytes 245768 | tf_op jit(solution)/shard_map/ppermute | solution.py:715
  16.4 0.6 collective-permute-start.2
  17.1 3.6 %collective-permute-start.3 = (bf16[5,16,512]{2,1,0:T(8,128)(2,1)S(1)}, bf16[5,16,512]{2,1,0:T(8,128)(2,1)S(1)}, u32[]{:S(2)}, u32[]{:S(2)}) collective-permute-start(bf16[5,16,512]{2,1,0:T(8,128)(2,1)S(1)} %get-tuple-element.55), channel_id=1, source_target_pairs={{0,15},{1,2},{2,1},{3,4},{4,3},{5,6},{6,5},{7,8},{8,7},{9,10},{10,... | collective-permute-start | bytes 245768 | tf_op jit(solution)/shard_map/ppermute | solution.py:717
  20.7 2.9 %local_first.1 = (f32[4,256,128]{2,1,0:T(8,128)S(1)}, f32[4,256,128]{2,1,0:T(8,128)S(1)}, f32[4,4,16,128]{3,2,1,0:T(8,128)S(1)}, bf16[5,16,512]{2,1,0:T(8,128)(2...) custom-call(f32[4,256,128]{2,1,0:T(8,128)S(1)} %bitcast.19, ...), custom_call_target="tpu_custom_call" | custom-call | bytes 10800000 | tf_op jit(solution)/shard_map/local_first/pallas_call | solution.py:448
  23.6 0.0 all-to-all-done.pieces
  23.6 0.5 source_velocity.1.vel_src.refs_2_.refs_3_
  24.1 1.3 %collective-permute-done.1.gx2 = bf16[5,16,512]{2,1,0:T(8,128)(2,1)S(1)} collective-permute-done((bf16[5,16,512]{2,1,0:T(8,128)(2,1)S(1)}, bf16[5,16,512]{2,1,0:T(8,128)(2,1)S(1)}, u32[]{:S(2)}, u32[]{:S(2)}) %collective-permute-start.1) | collective-permute-done | bytes 81952 | tf_op jit(solution)/shard_map/ppermute | solution.py:715
  25.4 0.0 collective-permute-done.2.gy1
  25.4 0.6 collective-permute-done.3.gy2
  26.0 0.7 halo_first.1
  26.7 0.1 collective-permute-start.4
  26.8 2.6 %collective-permute-start.5 = (bf16[10,16,512]{2,1,0:T(8,128)(2,1)S(1)}, bf16[10,16,512]{2,1,0:T(8,128)(2,1)S(1)}, u32[]{:S(2)}, u32[]{:S(2)}) collective-permute-start(bf16[10,16,512]{2,1,0:T(8,128)(2,1)S(1)} %get-tuple-element.66), channel_id=1, source_target_pairs={{0,112},{16,32},{32,16},{48,64},{64,48},{80,96},{96,80},{112,0},{1... | collective-permute-start | bytes 491528 | tf_op jit(solution)/shard_map/ppermute | solution.py:715
  29.4 0.4 collective-permute-start.6
  29.9 1.7 %collective-permute-start.7 = (bf16[8,16,512]{2,1,0:T(8,128)(2,1)S(1)}, bf16[8,16,512]{2,1,0:T(8,128)(2,1)S(1)}, u32[]{:S(2)}, u32[]{:S(2)}) collective-permute-start(bf16[8,16,512]{2,1,0:T(8,128)(2,1)S(1)} %get-tuple-element.68), channel_id=1, source_target_pairs={{0,15},{1,2},{2,1},{3,4},{4,3},{5,6},{6,5},{7,8},{8,7},{9,10},{10,... | collective-permute-start | bytes 393224 | tf_op jit(solution)/shard_map/ppermute | solution.py:717
  31.6 1.8 %injections.1.inject = f32[32,128]{1,0:T(8,128)S(1)} custom-call(f32[4,4096]{1,0:T(4,128)} %traces_hbm.1, s32[1,4096]{1,0:T(1,128)} %bitcast.26, s32[1,4096]{1,0:T(1,128)} %bitcast.27), custom_call_target="tpu_custom_call" | custom-call | bytes 7200000 | tf_op jit(solution)/shard_map/injections/pallas_call | solution.py:343
  33.4 3.2 %local_second.1 = (f32[4,256,128]{2,1,0:T(8,128)S(1)}, f32[2,512,128]{2,1,0:T(8,128)S(1)}, f32[2,16,32,128]{3,2,1,0:T(8,128)S(1)}) custom-call(f32[4,256,128]{2,1,0:T(8,128)S(1)} %get-tuple-element.61.src.src_next, f32[256,512]{1,0:T(8,128)} %bitcast.22, f32[16,32,256]{2,1,0:T(8,128)} %rcv.3, f32[512,256]{1,0:T(8,128)} %bitcast.25, f32[16,32,256]{2,1,0:T(8,128)} %vel.3, ...), custom_call_target="tpu_custom_call" | custom-call | bytes 14400000 | tf_op jit(solution)/shard_map/local_second/pallas_call | solution.py:494
  36.7 0.0 collective-permute-done.6.refs_6_
  36.7 0.9 %collective-permute-done.7.refs_7_ = bf16[8,16,512]{2,1,0:T(8,128)(2,1)S(1)} collective-permute-done((bf16[8,16,512]{2,1,0:T(8,128)(2,1)S(1)}, bf16[8,16,512]{2,1,0:T(8,128)(2,1)S(1)}, u32[]{:S(2)}, u32[]{:S(2)}) %collective-permute-start.7) | collective-permute-done | bytes 131104 | tf_op jit(solution)/shard_map/ppermute | solution.py:717
  37.5 0.0 collective-permute-done.4.refs_4_
  37.6 0.0 collective-permute-done.5.refs_5_
  37.6 1.2 %halo_step1.1 = (f32[4,256,128]{2,1,0:T(8,128)S(1)}, f32[2,512,128]{2,1,0:T(8,128)S(1)}, bf16[10,16,512]{2,1,0:T(8,128)(2,1)S(1)}, bf16[10,16,512]{2,1,0:T(8,128...) custom-call(f32[4,256,128]{2,1,0:T(8,128)S(1)} %get-tuple-element.62.refs_0_, ...), custom_call_target="tpu_custom_call" | custom-call | tf_op jit(solution)/shard_map/halo_step1/pallas_call | solution.py:639
  38.8 0.1 collective-permute-start.8
  38.9 1.1 %collective-permute-start.9 = (bf16[10,16,512]{2,1,0:T(8,128)(2,1)S(1)}, bf16[10,16,512]{2,1,0:T(8,128)(2,1)S(1)}, u32[]{:S(2)}, u32[]{:S(2)}) collective-permute-start(bf16[10,16,512]{2,1,0:T(8,128)(2,1)S(1)} %get-tuple-element.74), channel_id=1, source_target_pairs={{0,112},{16,32},{32,16},{48,64},{64,48},{80,96},{96,80},{112,0},{1... | collective-permute-start | bytes 491528 | tf_op jit(solution)/shard_map/ppermute | solution.py:715
  40.0 2.5 %collective-permute-start.10 = (bf16[8,16,512]{2,1,0:T(8,128)(2,1)S(1)}, bf16[8,16,512]{2,1,0:T(8,128)(2,1)S(1)}, u32[]{:S(2)}, u32[]{:S(2)}) collective-permute-start(bf16[8,16,512]{2,1,0:T(8,128)(2,1)S(1)} %get-tuple-element.75), channel_id=1, source_target_pairs={{0,1},{1,0},{2,3},{3,2},{4,5},{5,4},{6,7},{7,6},{8,9},{9,8},{10,11... | collective-permute-start | bytes 393224 | tf_op jit(solution)/shard_map/ppermute | solution.py:718
  42.4 1.1 %collective-permute-start.11 = (bf16[8,16,512]{2,1,0:T(8,128)(2,1)S(1)}, bf16[8,16,512]{2,1,0:T(8,128)(2,1)S(1)}, u32[]{:S(2)}, u32[]{:S(2)}) collective-permute-start(bf16[8,16,512]{2,1,0:T(8,128)(2,1)S(1)} %get-tuple-element.76), channel_id=1, source_target_pairs={{0,15},{1,2},{2,1},{3,4},{4,3},{5,6},{6,5},{7,8},{8,7},{9,10},{10,... | collective-permute-start | bytes 393224 | tf_op jit(solution)/shard_map/ppermute | solution.py:717
  43.6 3.9 %local_step2.1 = (f32[4,256,128]{2,1,0:T(8,128)S(1)}, f32[2,512,128]{2,1,0:T(8,128)S(1)}) custom-call(f32[4,256,128]{2,1,0:T(8,128)S(1)} %get-tuple-element.69.src.src_next, f32[4,256,128]{2,1,0:T(8,128)S(1)} %get-tuple-element.61.src.src_next, f32[2,512,128]{2,1,0:T(8,128)S(1)} %get-tuple-element.70.rcv.rcv_next, f32[512,256]{1,0:T(8,128)} %bitcast.20, ...), custom_call_target="tpu_custom_call" | custom-call | bytes 10800000 | tf_op jit(solution)/shard_map/local_step2/pallas_call | solution.py:538
  47.5 1.1 %collective-permute-done.11.refs_7_ = bf16[8,16,512]{2,1,0:T(8,128)(2,1)S(1)} collective-permute-done((bf16[8,16,512]{2,1,0:T(8,128)(2,1)S(1)}, bf16[8,16,512]{2,1,0:T(8,128)(2,1)S(1)}, u32[]{:S(2)}, u32[]{:S(2)}) %collective-permute-start.11) | collective-permute-done | bytes 131104 | tf_op jit(solution)/shard_map/ppermute | solution.py:717
  48.6 1.2 %halo_step2.1 = (f32[4,256,128]{2,1,0:T(8,128)S(1)}, f32[2,512,128]{2,1,0:T(8,128)S(1)}, bf16[10,16,512]{2,1,0:T(8,128)(2,1)S(1)}, bf16[10,16,512]{2,1,0:T(8,128...) custom-call(f32[4,256,128]{2,1,0:T(8,128)S(1)} %get-tuple-element.71.refs_0_, ...), custom_call_target="tpu_custom_call" | custom-call | tf_op jit(solution)/shard_map/halo_step2/pallas_call | solution.py:639
  49.9 0.2 collective-permute-start.12
  50.1 1.9 %collective-permute-start.13 = (bf16[10,16,512]{2,1,0:T(8,128)(2,1)S(1)}, bf16[10,16,512]{2,1,0:T(8,128)(2,1)S(1)}, u32[]{:S(2)}, u32[]{:S(2)}) collective-permute-start(bf16[10,16,512]{2,1,0:T(8,128)(2,1)S(1)} %get-tuple-element.83), channel_id=1, source_target_pairs={{0,112},{16,32},{32,16},{48,64},{64,48},{80,96},{96,80},{112,0},{1... | collective-permute-start | bytes 491528 | tf_op jit(solution)/shard_map/ppermute | solution.py:715
  52.0 2.3 %collective-permute-start.14 = (bf16[8,16,512]{2,1,0:T(8,128)(2,1)S(1)}, bf16[8,16,512]{2,1,0:T(8,128)(2,1)S(1)}, u32[]{:S(2)}, u32[]{:S(2)}) collective-permute-start(bf16[8,16,512]{2,1,0:T(8,128)(2,1)S(1)} %get-tuple-element.84), channel_id=1, source_target_pairs={{0,1},{1,0},{2,3},{3,2},{4,5},{5,4},{6,7},{7,6},{8,9},{9,8},{10,11... | collective-permute-start | bytes 393224 | tf_op jit(solution)/shard_map/ppermute | solution.py:718
  54.3 1.6 %collective-permute-start.15 = (bf16[8,16,512]{2,1,0:T(8,128)(2,1)S(1)}, bf16[8,16,512]{2,1,0:T(8,128)(2,1)S(1)}, u32[]{:S(2)}, u32[]{:S(2)}) collective-permute-start(bf16[8,16,512]{2,1,0:T(8,128)(2,1)S(1)} %get-tuple-element.85), channel_id=1, source_target_pairs={{0,15},{1,2},{2,1},{3,4},{4,3},{5,6},{6,5},{7,8},{8,7},{9,10},{10,... | collective-permute-start | bytes 393224 | tf_op jit(solution)/shard_map/ppermute | solution.py:717
  55.9 3.9 %local_step3.1 = (f32[4,256,128]{2,1,0:T(8,128)S(1)}, f32[2,512,128]{2,1,0:T(8,128)S(1)}, bf16[16,16,512]{2,1,0:T(8,128)(2,1)S(1)}) custom-call(f32[4,256,128]{2,1,0:T(8,128)S(1)} %get-tuple-element.77.src, f32[4,256,128]{2,1,0:T(8,128)S(1)} %get-tuple-element.69.src.src_next, f32[2,512,128]{2,1,0:T(8,128)S(1)} %get-tuple-element.78.rcv.rcv_next.rcv_early, ...), custom_call_target="tpu_custom_call" | custom-call | bytes 10800000 | tf_op jit(solution)/shard_map/local_step3/pallas_call | solution.py:538
  59.8 3.0 %collective-permute-done.15.refs_8_ = bf16[8,16,512]{2,1,0:T(8,128)(2,1)S(1)} collective-permute-done((bf16[8,16,512]{2,1,0:T(8,128)(2,1)S(1)}, bf16[8,16,512]{2,1,0:T(8,128)(2,1)S(1)}, u32[]{:S(2)}, u32[]{:S(2)}) %collective-permute-start.15) | collective-permute-done | bytes 131104 | tf_op jit(solution)/shard_map/ppermute | solution.py:717
  62.8 1.5 %halo_step3.1 = (f32[4,256,128]{2,1,0:T(8,128)S(1)}, f32[2,512,128]{2,1,0:T(8,128)S(1)}, bf16[5,16,512]{2,1,0:T(8,128)(2,1)S(1)}, bf16[5,16,512]{2,1,0:T(8,128)(...) custom-call(f32[4,256,128]{2,1,0:T(8,128)S(1)} %get-tuple-element.79.re, ...), custom_call_target="tpu_custom_call" | custom-call | tf_op jit(solution)/shard_map/halo_step3/pallas_call | solution.py:639
  64.3 4.6 %all-to-all-start.1 = ((bf16[16,2,16,512]{3,2,1,0:T(8,128)(2,1)}), bf16[16,2,16,512]{3,2,1,0:T(8,128)(2,1)S(1)}, u32[]{:S(2)}, u32[]{:S(2)}) async-start(bf16[16,2,16,512]{3,2,1,0:T(8,128)(2,1)} %get-tuple-element.86), calls=%async_computation.1 | async-start | bytes 1048576 | tf_op jit(solution)/shard_map/all_to_all | solution.py:768
  68.9 2.7 %collective-permute-start.17 = (bf16[5,16,512]{2,1,0:T(8,128)(2,1)S(1)}, bf16[5,16,512]{2,1,0:T(8,128)(2,1)S(1)}, u32[]{:S(2)}, u32[]{:S(2)}) collective-permute-start(bf16[5,16,512]{2,1,0:T(8,128)(2,1)S(1)} %get-tuple-element.89), channel_id=1, source_target_pairs={{0,112},{16,32},{32,16},{48,64},{64,48},{80,96},{96,80},{112,0},{1... | collective-permute-start | bytes 245768 | tf_op jit(solution)/shard_map/ppermute | solution.py:715
  71.7 0.7 collective-permute-start.18
  72.4 3.6 %collective-permute-start.19 = (bf16[3,16,512]{2,1,0:T(8,128)(2,1)S(1)}, bf16[3,16,512]{2,1,0:T(8,128)(2,1)S(1)}, u32[]{:S(2)}, u32[]{:S(2)}) collective-permute-start(bf16[3,16,512]{2,1,0:T(8,128)(2,1)S(1)} %get-tuple-element.91), channel_id=1, source_target_pairs={{0,15},{1,2},{2,1},{3,4},{4,3},{5,6},{6,5},{7,8},{8,7},{9,10},{10,... | collective-permute-start | bytes 147464 | tf_op jit(solution)/shard_map/ppermute | solution.py:717
  76.0 1.5 %local_last.1.local = f32[2,512,128]{2,1,0:T(8,128)S(1)} custom-call(f32[2,512,128]{2,1,0:T(8,128)S(1)} %get-tuple-element.87.rcv, f32[2,512,128]{2,1,0:T(8,128)S(1)} %get-tuple-element.78.rcv.rcv_next.rcv_early, f32[2,512,128]{2,1,0:T(8,128)S(1)} %bitcast.17, f32[32,128]{1,0:T(8,128)S(1)} %injections.1.inject), custom_call_target="tpu_custom_call" | custom-call | bytes 7200000 | tf_op jit(solution)/shard_map/local_last/pallas_call | solution.py:559
  77.5 0.8 write_source.1
  78.3 3.9 %collective-permute-done.19.gy2 = bf16[3,16,512]{2,1,0:T(8,128)(2,1)S(1)} collective-permute-done((bf16[3,16,512]{2,1,0:T(8,128)(2,1)S(1)}, bf16[3,16,512]{2,1,0:T(8,128)(2,1)S(1)}, u32[]{:S(2)}, u32[]{:S(2)}) %collective-permute-start.19) | collective-permute-done | bytes 49184 | tf_op jit(solution)/shard_map/ppermute | solution.py:717
  82.2 0.4 halo_last.1.rcv_late
  82.7 1.0 %make_image.1 = (f32[512,256]{1,0:T(8,128)}, f32[512,256]{1,0:T(8,128)}) custom-call(bf16[16,2,16,512]{3,2,1,0:T(8,128)(2,1)S(1)} %all-to-all-done.1.bricks, f32[2,512,128]{2,1,0:T(8,128)S(1)} %get-tuple-element.78.rcv.rcv_next.rcv_early, f32[2,512,128]{2,1,0:T(8,128)S(1)} %halo_last.1.rcv_late), custom_call_target="tpu_custom_call" | custom-call | tf_op jit(solution)/shard_map/make_image/pallas_call | solution.py:700
  (12 shorter events, 0.0 us)
Async XLA Ops:
  2.6 21.0 %all-to-all-start = ((f32[16,16,512]{2,1,0:T(8,128)}), f32[16,16,512]{2,1,0:T(8,128)S(1)}, u32[]{:S(2)}, u32[]{:S(2)}) async-start(f32[16,16,512]{2,1,0:T(8,128)} %bitcast.21), calls=%async_computation | async-start | bytes 1048576 | tf_op jit(solution)/shard_map/all_to_all | solution.py:737
  12.3 11.8 %collective-permute-start = (bf16[5,16,512]{2,1,0:T(8,128)(2,1)S(1)}, bf16[5,16,512]{2,1,0:T(8,128)(2,1)S(1)}, u32[]{:S(2)}, u32[]{:S(2)}) collective-permute-start(bf16[5,16,512]{2,1,0:T(8,128)(2,1)S(1)} %get-tuple-element.52), channel_id=1, source_target_pairs={{0,16},{16,0},{32,48},{48,32},{64,80},{80,64},{96,112},{112,96},{1... | collective-permute-start | bytes 245768 | tf_op jit(solution)/shard_map/ppermute | solution.py:716
  14.1 11.4 %collective-permute-start.1 = (bf16[5,16,512]{2,1,0:T(8,128)(2,1)S(1)}, bf16[5,16,512]{2,1,0:T(8,128)(2,1)S(1)}, u32[]{:S(2)}, u32[]{:S(2)}) collective-permute-start(bf16[5,16,512]{2,1,0:T(8,128)(2,1)S(1)} %get-tuple-element.53), channel_id=1, source_target_pairs={{0,112},{16,32},{32,16},{48,64},{64,48},{80,96},{96,80},{112,0},{1... | collective-permute-start | bytes 245768 | tf_op jit(solution)/shard_map/ppermute | solution.py:715
  16.4 9.0 %collective-permute-start.2 = (bf16[5,16,512]{2,1,0:T(8,128)(2,1)S(1)}, bf16[5,16,512]{2,1,0:T(8,128)(2,1)S(1)}, u32[]{:S(2)}, u32[]{:S(2)}) collective-permute-start(bf16[5,16,512]{2,1,0:T(8,128)(2,1)S(1)} %get-tuple-element.54), channel_id=1, source_target_pairs={{0,1},{1,0},{2,3},{3,2},{4,5},{5,4},{6,7},{7,6},{8,9},{9,8},{10,11... | collective-permute-start | bytes 245768 | tf_op jit(solution)/shard_map/ppermute | solution.py:718
  17.1 8.9 %collective-permute-start.3 = (bf16[5,16,512]{2,1,0:T(8,128)(2,1)S(1)}, bf16[5,16,512]{2,1,0:T(8,128)(2,1)S(1)}, u32[]{:S(2)}, u32[]{:S(2)}) collective-permute-start(bf16[5,16,512]{2,1,0:T(8,128)(2,1)S(1)} %get-tuple-element.55), channel_id=1, source_target_pairs={{0,15},{1,2},{2,1},{3,4},{4,3},{5,6},{6,5},{7,8},{8,7},{9,10},{10,... | collective-permute-start | bytes 245768 | tf_op jit(solution)/shard_map/ppermute | solution.py:717
  26.7 10.8 %collective-permute-start.4 = (bf16[10,16,512]{2,1,0:T(8,128)(2,1)S(1)}, bf16[10,16,512]{2,1,0:T(8,128)(2,1)S(1)}, u32[]{:S(2)}, u32[]{:S(2)}) collective-permute-start(bf16[10,16,512]{2,1,0:T(8,128)(2,1)S(1)} %get-tuple-element.65), channel_id=1, source_target_pairs={{0,16},{16,0},{32,48},{48,32},{64,80},{80,64},{96,112},{112,96},{1... | collective-permute-start | bytes 491528 | tf_op jit(solution)/shard_map/ppermute | solution.py:716
  26.8 10.8 %collective-permute-start.5 = (bf16[10,16,512]{2,1,0:T(8,128)(2,1)S(1)}, bf16[10,16,512]{2,1,0:T(8,128)(2,1)S(1)}, u32[]{:S(2)}, u32[]{:S(2)}) collective-permute-start(bf16[10,16,512]{2,1,0:T(8,128)(2,1)S(1)} %get-tuple-element.66), channel_id=1, source_target_pairs={{0,112},{16,32},{32,16},{48,64},{64,48},{80,96},{96,80},{112,0},{1... | collective-permute-start | bytes 491528 | tf_op jit(solution)/shard_map/ppermute | solution.py:715
  29.4 7.2 %collective-permute-start.6 = (bf16[8,16,512]{2,1,0:T(8,128)(2,1)S(1)}, bf16[8,16,512]{2,1,0:T(8,128)(2,1)S(1)}, u32[]{:S(2)}, u32[]{:S(2)}) collective-permute-start(bf16[8,16,512]{2,1,0:T(8,128)(2,1)S(1)} %get-tuple-element.67), channel_id=1, source_target_pairs={{0,1},{1,0},{2,3},{3,2},{4,5},{5,4},{6,7},{7,6},{8,9},{9,8},{10,11... | collective-permute-start | bytes 393224 | tf_op jit(solution)/shard_map/ppermute | solution.py:718
  29.9 7.7 %collective-permute-start.7 = (bf16[8,16,512]{2,1,0:T(8,128)(2,1)S(1)}, bf16[8,16,512]{2,1,0:T(8,128)(2,1)S(1)}, u32[]{:S(2)}, u32[]{:S(2)}) collective-permute-start(bf16[8,16,512]{2,1,0:T(8,128)(2,1)S(1)} %get-tuple-element.68), channel_id=1, source_target_pairs={{0,15},{1,2},{2,1},{3,4},{4,3},{5,6},{6,5},{7,8},{8,7},{9,10},{10,... | collective-permute-start | bytes 393224 | tf_op jit(solution)/shard_map/ppermute | solution.py:717
  38.8 9.8 %collective-permute-start.8 = (bf16[10,16,512]{2,1,0:T(8,128)(2,1)S(1)}, bf16[10,16,512]{2,1,0:T(8,128)(2,1)S(1)}, u32[]{:S(2)}, u32[]{:S(2)}) collective-permute-start(bf16[10,16,512]{2,1,0:T(8,128)(2,1)S(1)} %get-tuple-element.73), channel_id=1, source_target_pairs={{0,16},{16,0},{32,48},{48,32},{64,80},{80,64},{96,112},{112,96},{1... | collective-permute-start | bytes 491528 | tf_op jit(solution)/shard_map/ppermute | solution.py:716
  38.9 9.8 %collective-permute-start.9 = (bf16[10,16,512]{2,1,0:T(8,128)(2,1)S(1)}, bf16[10,16,512]{2,1,0:T(8,128)(2,1)S(1)}, u32[]{:S(2)}, u32[]{:S(2)}) collective-permute-start(bf16[10,16,512]{2,1,0:T(8,128)(2,1)S(1)} %get-tuple-element.74), channel_id=1, source_target_pairs={{0,112},{16,32},{32,16},{48,64},{64,48},{80,96},{96,80},{112,0},{1... | collective-permute-start | bytes 491528 | tf_op jit(solution)/shard_map/ppermute | solution.py:715
  40.0 7.5 %collective-permute-start.10 = (bf16[8,16,512]{2,1,0:T(8,128)(2,1)S(1)}, bf16[8,16,512]{2,1,0:T(8,128)(2,1)S(1)}, u32[]{:S(2)}, u32[]{:S(2)}) collective-permute-start(bf16[8,16,512]{2,1,0:T(8,128)(2,1)S(1)} %get-tuple-element.75), channel_id=1, source_target_pairs={{0,1},{1,0},{2,3},{3,2},{4,5},{5,4},{6,7},{7,6},{8,9},{9,8},{10,11... | collective-permute-start | bytes 393224 | tf_op jit(solution)/shard_map/ppermute | solution.py:718
  42.4 6.2 %collective-permute-start.11 = (bf16[8,16,512]{2,1,0:T(8,128)(2,1)S(1)}, bf16[8,16,512]{2,1,0:T(8,128)(2,1)S(1)}, u32[]{:S(2)}, u32[]{:S(2)}) collective-permute-start(bf16[8,16,512]{2,1,0:T(8,128)(2,1)S(1)} %get-tuple-element.76), channel_id=1, source_target_pairs={{0,15},{1,2},{2,1},{3,4},{4,3},{5,6},{6,5},{7,8},{8,7},{9,10},{10,... | collective-permute-start | bytes 393224 | tf_op jit(solution)/shard_map/ppermute | solution.py:717
  49.9 12.9 %collective-permute-start.12 = (bf16[10,16,512]{2,1,0:T(8,128)(2,1)S(1)}, bf16[10,16,512]{2,1,0:T(8,128)(2,1)S(1)}, u32[]{:S(2)}, u32[]{:S(2)}) collective-permute-start(bf16[10,16,512]{2,1,0:T(8,128)(2,1)S(1)} %get-tuple-element.82), channel_id=1, source_target_pairs={{0,16},{16,0},{32,48},{48,32},{64,80},{80,64},{96,112},{112,96},{1... | collective-permute-start | bytes 491528 | tf_op jit(solution)/shard_map/ppermute | solution.py:716
  50.1 12.7 %collective-permute-start.13 = (bf16[10,16,512]{2,1,0:T(8,128)(2,1)S(1)}, bf16[10,16,512]{2,1,0:T(8,128)(2,1)S(1)}, u32[]{:S(2)}, u32[]{:S(2)}) collective-permute-start(bf16[10,16,512]{2,1,0:T(8,128)(2,1)S(1)} %get-tuple-element.83), channel_id=1, source_target_pairs={{0,112},{16,32},{32,16},{48,64},{64,48},{80,96},{96,80},{112,0},{1... | collective-permute-start | bytes 491528 | tf_op jit(solution)/shard_map/ppermute | solution.py:715
  52.0 7.8 %collective-permute-start.14 = (bf16[8,16,512]{2,1,0:T(8,128)(2,1)S(1)}, bf16[8,16,512]{2,1,0:T(8,128)(2,1)S(1)}, u32[]{:S(2)}, u32[]{:S(2)}) collective-permute-start(bf16[8,16,512]{2,1,0:T(8,128)(2,1)S(1)} %get-tuple-element.84), channel_id=1, source_target_pairs={{0,1},{1,0},{2,3},{3,2},{4,5},{5,4},{6,7},{7,6},{8,9},{9,8},{10,11... | collective-permute-start | bytes 393224 | tf_op jit(solution)/shard_map/ppermute | solution.py:718
  54.3 8.5 %collective-permute-start.15 = (bf16[8,16,512]{2,1,0:T(8,128)(2,1)S(1)}, bf16[8,16,512]{2,1,0:T(8,128)(2,1)S(1)}, u32[]{:S(2)}, u32[]{:S(2)}) collective-permute-start(bf16[8,16,512]{2,1,0:T(8,128)(2,1)S(1)} %get-tuple-element.85), channel_id=1, source_target_pairs={{0,15},{1,2},{2,1},{3,4},{4,3},{5,6},{6,5},{7,8},{8,7},{9,10},{10,... | collective-permute-start | bytes 393224 | tf_op jit(solution)/shard_map/ppermute | solution.py:717
  64.3 18.4 %all-to-all-start.1 = ((bf16[16,2,16,512]{3,2,1,0:T(8,128)(2,1)}), bf16[16,2,16,512]{3,2,1,0:T(8,128)(2,1)S(1)}, u32[]{:S(2)}, u32[]{:S(2)}) async-start(bf16[16,2,16,512]{3,2,1,0:T(8,128)(2,1)} %get-tuple-element.86), calls=%async_computation.1 | async-start | bytes 1048576 | tf_op jit(solution)/shard_map/all_to_all | solution.py:768
  68.9 13.3 %collective-permute-start.16 = (bf16[5,16,512]{2,1,0:T(8,128)(2,1)S(1)}, bf16[5,16,512]{2,1,0:T(8,128)(2,1)S(1)}, u32[]{:S(2)}, u32[]{:S(2)}) collective-permute-start(bf16[5,16,512]{2,1,0:T(8,128)(2,1)S(1)} %get-tuple-element.88), channel_id=1, source_target_pairs={{0,16},{16,0},{32,48},{48,32},{64,80},{80,64},{96,112},{112,96},{1... | collective-permute-start | bytes 245768 | tf_op jit(solution)/shard_map/ppermute | solution.py:716
  68.9 13.3 %collective-permute-start.17 = (bf16[5,16,512]{2,1,0:T(8,128)(2,1)S(1)}, bf16[5,16,512]{2,1,0:T(8,128)(2,1)S(1)}, u32[]{:S(2)}, u32[]{:S(2)}) collective-permute-start(bf16[5,16,512]{2,1,0:T(8,128)(2,1)S(1)} %get-tuple-element.89), channel_id=1, source_target_pairs={{0,112},{16,32},{32,16},{48,64},{64,48},{80,96},{96,80},{112,0},{1... | collective-permute-start | bytes 245768 | tf_op jit(solution)/shard_map/ppermute | solution.py:715
  71.7 6.6 %collective-permute-start.18 = (bf16[3,16,512]{2,1,0:T(8,128)(2,1)S(1)}, bf16[3,16,512]{2,1,0:T(8,128)(2,1)S(1)}, u32[]{:S(2)}, u32[]{:S(2)}) collective-permute-start(bf16[3,16,512]{2,1,0:T(8,128)(2,1)S(1)} %get-tuple-element.90), channel_id=1, source_target_pairs={{0,1},{1,0},{2,3},{3,2},{4,5},{5,4},{6,7},{7,6},{8,9},{9,8},{10,11... | collective-permute-start | bytes 147464 | tf_op jit(solution)/shard_map/ppermute | solution.py:718
  72.4 9.8 %collective-permute-start.19 = (bf16[3,16,512]{2,1,0:T(8,128)(2,1)S(1)}, bf16[3,16,512]{2,1,0:T(8,128)(2,1)S(1)}, u32[]{:S(2)}, u32[]{:S(2)}) collective-permute-start(bf16[3,16,512]{2,1,0:T(8,128)(2,1)S(1)} %get-tuple-element.91), channel_id=1, source_target_pairs={{0,15},{1,2},{2,1},{3,4},{4,3},{5,6},{6,5},{7,8},{8,7},{9,10},{10,... | collective-permute-start | bytes 147464 | tf_op jit(solution)/shard_map/ppermute | solution.py:717

commit v5 on v4

v5 whole, which is shorter than its diff:
```python
import jax
import jax.numpy as jnp
from jax import lax
from jax.experimental import pallas as pl
from jax.experimental.pallas import tpu as pltpu
from jax.sharding import PartitionSpec as P

STEPS = 4
C0, C1, C2, C3, C4 = (-205.0 / 72.0, 8.0 / 5.0, -1.0 / 5.0, 8.0 / 315.0, -1.0 / 560.0)
COEFFS = (C0, C1, C2, C3, C4)
RECEIVER_PLANE = 2
PLANES = 5
F32, BF16 = jnp.float32, jnp.bfloat16
VMEM_LIMIT = 24 * 1024 * 1024

RCV = dict(lead=16, rows=32, lanes=256)
SRC = dict(lead=16, rows=16, lanes=512)


def flat(ref):
    return ref.reshape(ref.shape[0], ref.shape[1] * ref.shape[2], 128)


def split(value):
    high = value.astype(BF16)
    return high, (value - high.astype(F32)).astype(BF16)


def planes_of(layers):
    return [*split(layers[0]), *[layer.astype(BF16) for layer in layers[1:]]]


def layers_of(planes):
    planes = [plane.astype(F32) for plane in planes]
    return [planes[0] + planes[1], *planes[2:]]


def sides():
    return lax.axis_index("gx") % 2 == 0, lax.axis_index("gy") % 2 == 0


def chosen(up, one, other):
    up = jnp.broadcast_to(up, one[0].shape)
    return [jnp.where(up, x, y) for x, y in zip(one, other)]


def pack_source(src, gx_second, gy_second, gx_first, gy_first):
    up_x, up_y = sides()
    for t in range(4):
        lanes = slice(t * 128, t * 128 + 128)
        low = [src[t, pl.ds(h, 16, stride=16), :] for h in range(4)]
        high = [src[t, pl.ds(15 - h, 16, stride=16), :] for h in range(4)]
        for out, layers in ((gx_second, chosen(up_x, low, high)), (gx_first, chosen(up_x, high, low))):
            for p, plane in enumerate(planes_of(layers)):
                out[p, :, lanes] = plane
        low = [src[t, h * 16 : h * 16 + 16, :] for h in range(4)]
        high = [src[t, (15 - h) * 16 : (15 - h) * 16 + 16, :] for h in range(4)]
        for out, layers in ((gy_second, chosen(up_y, low, high)), (gy_first, chosen(up_y, high, low))):
            for p, plane in enumerate(planes_of(layers)):
                out[p, :, lanes] = plane


def pack_receiver(rcv, at, gx_second, gy_second, gx_first, gy_first):
    up_x, up_y = sides()
    for t in range(4):
        lanes = slice(t * 128, t * 128 + 128)
        half, col = divmod(t, 2)
        low = [rcv[col, h * 32 + half * 16 : h * 32 + half * 16 + 16, :] for h in range(4)]
        high = [rcv[col, (15 - h) * 32 + half * 16 : (15 - h) * 32 + half * 16 + 16, :] for h in range(4)]
        for out, layers in ((gx_second, chosen(up_x, low, high)), (gx_first, chosen(up_x, high, low))):
            for p, plane in enumerate(planes_of(layers)):
                out[at + p, :, lanes] = plane
    for col in range(2):
        low = [rcv[col, pl.ds(h, 16, stride=32), :] for h in range(4)]
        high = [rcv[col, pl.ds(31 - h, 16, stride=32), :] for h in range(4)]
        for out, layers in ((gy_second, chosen(up_y, low, high)), (gy_first, chosen(up_y, high, low))):
            for p, plane in enumerate(planes_of(layers)):
                lane = (p % 2) * 256 + col * 128
                out[at + p // 2, :, lane : lane + 128] = plane


def add_layers(out, vel, t, low_rows, high_rows, first, second, up, ends):
    live = jnp.broadcast_to(~ends, first[0].shape)
    second = [jnp.where(live, layer, 0.0) for layer in second]
    for rows_of, layers in ((low_rows, chosen(up, second, first)), (high_rows, chosen(up, first, second))):
        for d in range(4):
            term = COEFFS[d + 1] * layers[0]
            for h in range(1, 4 - d):
                term = term + COEFFS[d + h + 1] * layers[h]
            rows = rows_of(d)
            out[t, rows, :] = out[t, rows, :] + vel[t, rows, :] * term


def add_source(out, vel, gx_second, gy_second, gx_first, gy_first):
    ix, iy = lax.axis_index("gx"), lax.axis_index("gy")
    up_x, up_y = sides()
    for t in range(4):
        lanes = slice(t * 128, t * 128 + 128)
        planes = lambda buffer: layers_of([buffer[p, :, lanes] for p in range(PLANES)])
        add_layers(
            out,
            vel,
            t,
            lambda d: pl.ds(d * 16, 16),
            lambda d: pl.ds((15 - d) * 16, 16),
            planes(gy_first),
            planes(gy_second),
            up_y,
            (iy == 0) | (iy == 15),
        )
        add_layers(
            out,
            vel,
            t,
            lambda d: pl.ds(d, 16, stride=16),
            lambda d: pl.ds(15 - d, 16, stride=16),
            planes(gx_first),
            planes(gx_second),
            up_x,
            (ix == 0) | (ix == 7),
        )


def add_receiver(out, vel, at, gx_second, gy_second, gx_first, gy_first):
    ix, iy = lax.axis_index("gx"), lax.axis_index("gy")
    up_x, up_y = sides()
    for t in range(4):
        lanes = slice(t * 128, t * 128 + 128)
        half, col = divmod(t, 2)
        planes = lambda buffer: layers_of([buffer[at + p, :, lanes] for p in range(PLANES)])
        add_layers(
            out,
            vel,
            col,
            lambda d: pl.ds(d * 32 + half * 16, 16),
            lambda d: pl.ds((15 - d) * 32 + half * 16, 16),
            planes(gx_first),
            planes(gx_second),
            up_x,
            (ix == 0) | (ix == 7),
        )
    for col in range(2):
        lane = [(p % 2) * 256 + col * 128 for p in range(PLANES)]
        planes = lambda buffer: layers_of(
            [buffer[at + p // 2, :, lane[p] : lane[p] + 128] for p in range(PLANES)]
        )
        add_layers(
            out,
            vel,
            col,
            lambda d: pl.ds(d, 16, stride=32),
            lambda d: pl.ds(31 - d, 16, stride=32),
            planes(gy_first),
            planes(gy_second),
            up_y,
            (iy == 0) | (iy == 15),
        )


def band(rows, cols, offset=0, block=None):
    i = lax.broadcasted_iota(jnp.int32, (rows, cols), 0)
    j = lax.broadcasted_iota(jnp.int32, (rows, cols), 1)
    distance = jnp.abs(i - j + offset)
    matrix = jnp.zeros((rows, cols), F32)
    for k, entry in ((1, 8064.0), (2, -1008.0), (3, 128.0), (4, -9.0)):
        matrix = jnp.where(distance == k, entry, matrix)
    if block is not None:
        matrix = jnp.where(i // block == j // block, matrix, 0.0)
    return matrix.astype(BF16)


def parts_of(value):
    parts = []
    for _ in range(3):
        parts.append(value.astype(BF16))
        value = value - parts[-1].astype(F32)
    return parts


def local_laplacian(f, now, store):
    lead, rows, tiles = f["lead"], f["rows"], f["lanes"] // 128
    dot = lambda x, y: jnp.dot(x, y, preferred_element_type=F32)
    along_lanes, along_rows = band(256, 256), band(256, 256, block=rows)
    if tiles > 2:
        from_above, from_below = band(128, 128, offset=128), band(128, 128, offset=-128)
    for c in range(lead * rows // 256):
        here = [now[t, c * 256 : c * 256 + 256, :] for t in range(tiles)]
        parts = [parts_of(x) for x in here]
        sums = []
        for t in range(0, tiles, 2):
            both = None
            for one, other in zip(parts[t], parts[t + 1]):
                pair = jnp.concatenate([one, other], axis=1)
                term = dot(pair, along_lanes) + dot(along_rows, pair)
                both = term if both is None else both + term
            sums += [both[:, :128], both[:, 128:]]
        for t in range(2, tiles, 2):
            for below, above in zip(parts[t - 1], parts[t]):
                sums[t - 1] = sums[t - 1] + dot(above, from_above)
                sums[t] = sums[t] + dot(below, from_below)
        for t in range(tiles):
            for i in range(256 // rows):
                a = c * (256 // rows) + i
                part = slice(i * rows, i * rows + rows)
                total = (3.0 * C0) * here[t][part] + sums[t][part] * (1.0 / 5040.0)
                for k in range(1, 5):
                    others = [
                        now[t, other * rows : other * rows + rows, :] for other in (a - k, a + k) if 0 <= other < lead
                    ]
                    total = total + COEFFS[k] * sum(others[1:], others[0])
                store(t, a, slice(a * rows, a * rows + rows), here[t][part], total)


def pack_brick(src, out, columns=range(4)):
    group = lax.broadcasted_iota(jnp.int32, (16, 128), 1) // 32
    for t in columns:
        for xg in range(4):
            rows = [src[t, pl.ds(xg * 4 + xl, 16, stride=16), :] for xl in range(4)]
            for g in range(4):
                piece = None
                for xl in range(4):
                    turned = rows[xl] if xl == g else pltpu.roll(rows[xl], ((xl - g) % 4) * 32, 1)
                    piece = turned if piece is None else jnp.where(group == xl, turned, piece)
                out[t * 4 + g, :, xg * 128 : xg * 128 + 128] = piece.astype(BF16)


def unpack_velocity(pieces, out):
    group = lax.broadcasted_iota(jnp.int32, (16, 128), 1) // 32
    for t in range(4):
        for xg in range(4):
            parts = [pieces[t * 4 + g, :, xg * 128 : xg * 128 + 128] for g in range(4)]
            for xl in range(4):
                row = None
                for g in range(4):
                    turned = parts[g] if xl == g else pltpu.roll(parts[g], ((g - xl) % 4) * 32, 1)
                    row = turned if row is None else jnp.where(group == g, turned, row)
                out[t, pl.ds(xg * 4 + xl, 16, stride=16), :] = row


SRC_PLANES, RCV_PLANES = (PLANES, PLANES), (PLANES, 3)


def halo_buffers(*fields):
    shapes = [(sum(f[axis] for f in fields), 16, 512) for axis in (0, 1, 0, 1)]
    return [jax.ShapeDtypeStruct(shape, BF16) for shape in shapes]


SRC_COLS = jax.ShapeDtypeStruct((4, 256, 128), F32)
RCV_COLS = jax.ShapeDtypeStruct((2, 512, 128), F32)
BRICK = jax.ShapeDtypeStruct((16, 16, 512), BF16)
VM = pl.BlockSpec(memory_space=pltpu.VMEM)
SM = pl.BlockSpec(memory_space=pltpu.SMEM)
HB = pl.BlockSpec(memory_space=pltpu.HBM)


def in_hbm(*arrays):
    return [pltpu.with_memory_space_constraint(x, pltpu.HBM) for x in arrays]


def params():
    return pltpu.CompilerParams(vmem_limit_bytes=VMEM_LIMIT)


def hint(microseconds):
    return pl.CostEstimate(flops=0, bytes_accessed=int(microseconds * 3.6e6), transcendentals=0)


def column_copies(block, cols, sem):
    return [
        pltpu.make_async_copy(
            block.at[pl.ds(a, 8), :, pl.ds(t * 128, 128)], cols.at[t, pl.ds(a, 8), :, :], sem
        )
        for a in (0, 8)
        for t in range(cols.shape[0])
    ]


def start(copies):
    for copy in copies:
        copy.start()


def wait(copies):
    for copy in copies:
        copy.wait()


def turn_velocity(vel):
    def kernel(vel, cols, turned_out, turned, sems):
        pieces = [
            pltpu.make_async_copy(
                vel.at[pl.ds(q * 4, 4), :, pl.ds(t * 128, 128)], cols.at[t, pl.ds(q * 4, 4), :, :], sems.at[q]
            )
            for q in range(4)
            for t in range(2)
        ]
        start(pieces)
        flat_cols = flat(cols)
        outs = []
        for q in range(4):
            wait(pieces[2 * q : 2 * q + 2])
            lanes = pl.ds(q * 128, 128)
            for t in range(2):
                turned[t * 128 : t * 128 + 128, lanes] = flat_cols[t, q * 128 : q * 128 + 128, :].T
            outs.append(pltpu.make_async_copy(turned.at[:, lanes], turned_out.at[:, lanes], sems.at[4]))
            outs[-1].start()
        wait(outs)

    return pl.pallas_call(
        kernel,
        out_shape=[jax.ShapeDtypeStruct((2, 16, 32, 128), F32), pltpu.HBM((256, 512), F32)],
        in_specs=[HB],
        out_specs=[VM, HB],
        scratch_shapes=[pltpu.VMEM((256, 512), F32), pltpu.SemaphoreType.DMA((5,))],
        compiler_params=params(),
        name="turn_velocity",
    )(*in_hbm(vel))


def first_halos(src, rcv):
    def kernel(src, rcv, src_cols, *refs):
        rcv_cols, sems = refs[4:]
        get_src, get_rcv = column_copies(src, src_cols, sems.at[0]), column_copies(rcv, rcv_cols, sems.at[1])
        start(get_src + get_rcv)
        wait(get_src)
        pack_source(flat(src_cols), *refs[:4])
        wait(get_rcv)
        pack_receiver(flat(rcv_cols), PLANES, *refs[:4])

    return pl.pallas_call(
        kernel,
        out_shape=[jax.ShapeDtypeStruct((4, 16, 16, 128), F32), *halo_buffers(SRC_PLANES, RCV_PLANES)],
        in_specs=[HB] * 2,
        out_specs=[VM] * 5,
        scratch_shapes=[pltpu.VMEM((2, 16, 32, 128), F32), pltpu.SemaphoreType.DMA((2,))],
        compiler_params=params(),
        name="first_halos",
    )(*in_hbm(src, rcv))


def source_velocity(pieces):
    return pl.pallas_call(
        unpack_velocity,
        out_shape=SRC_COLS,
        in_specs=[VM],
        out_specs=VM,
        compiler_params=params(),
        name="source_velocity",
    )(pieces)


def injections(traces, receiver_x, receiver_y):
    def kernel(traces_hbm, rx_hbm, ry_hbm, out, traces, rx, ry, sem):
        inputs = [
            pltpu.make_async_copy(traces_hbm, traces, sem),
            pltpu.make_async_copy(rx_hbm, rx, sem),
            pltpu.make_async_copy(ry_hbm, ry, sem),
        ]
        start(inputs)
        wait(inputs)
        xs = lax.axis_index("gx") * 16 + lax.broadcasted_iota(jnp.int32, (16, 512), 0)
        ys = lax.axis_index("gy") * 32 + lax.broadcasted_iota(jnp.int32, (32, 512), 0)
        total = jnp.zeros((32, 128), F32)
        for c in range(8):
            cols = slice(c * 512, c * 512 + 512)
            at_x = rx[:, cols] == xs
            at_y = jnp.where(ry[:, cols] == ys, 1.0, 0.0).astype(BF16)
            weighted = [jnp.where(at_x, traces[s : s + 1, cols], 0.0) for s in range(STEPS)]
            for part in parts_of(jnp.concatenate(weighted, axis=0)):
                part = jnp.concatenate([part, jnp.zeros((64, 512), BF16)], axis=0)
                total = total + lax.dot_general(
                    at_y, part, (((1,), (1,)), ((), ())), preferred_element_type=F32
                )
        out[...] = total

    return pl.pallas_call(
        kernel,
        out_shape=jax.ShapeDtypeStruct((32, 128), F32),
        in_specs=[HB] * 3,
        out_specs=VM,
        scratch_shapes=[
            pltpu.VMEM((4, 4096), F32),
            pltpu.VMEM((1, 4096), jnp.int32),
            pltpu.VMEM((1, 4096), jnp.int32),
            pltpu.SemaphoreType.DMA,
        ],
        compiler_params=params(),
        cost_estimate=hint(2),
        name="injections",
    )(*in_hbm(traces, receiver_x.reshape(1, -1), receiver_y.reshape(1, -1)))


def subtract(cols, block):
    for t in range(cols.shape[0]):
        cols[t] = cols[t] - block[:, t * 128 : t * 128 + 128]


def local_source(now, nxt, vel, out, lap_out=None):
    def store(t, a, rows, here, lap):
        value = 2.0 * here
        if nxt is not None:
            value = value - nxt[t, rows, :]
        if vel is None:
            lap_out[t, rows, :] = lap
        else:
            value = value + vel[t, rows, :] * lap
        out[t, rows, :] = value

    local_laplacian(SRC, now, store)


def local_receiver(step, now, nxt, vel, inject, out):
    lane = lax.broadcasted_iota(jnp.int32, (32, 128), 1)

    def store(t, a, rows, here, lap):
        value = 2.0 * here + vel[t, rows, :] * lap
        if nxt is not None:
            value = value - nxt[t, rows, :]
        if t == 0:
            turn = (RECEIVER_PLANE - step * 16 - a) % 128
            value = value + jnp.where(lane == RECEIVER_PLANE, pltpu.roll(inject[...], turn, 1), 0.0)
        out[t, rows, :] = value

    local_laplacian(RCV, now, store)


def add_wavelet(step, cell, wavelet, out):
    z = cell[2] - lax.axis_index("gy") * 16
    x = cell[0] - lax.axis_index("gx") * 16

    @pl.when((z >= 0) & (z < 16) & (x >= 0) & (x < 16))
    def _():
        at = pl.ds(z * 16 + x, 1)
        lanes = lax.broadcasted_iota(jnp.int32, (1, 128), 1)
        for t in range(4):
            out[t, at, :] = out[t, at, :] + jnp.where(lanes + t * 128 == cell[1], wavelet[step], 0.0)


def local_first(src, src_next, rcv, rcv_next, vel, inject, wavelet, cell, saved, plane_index):
    def kernel(src, src_next, rcv, rcv_next, vel, inject, wavelet_hbm, cell_hbm, saved, index_hbm, *refs):
        base, lap, rcv_out, planes, next_src, rcv_cols, next_rcv, wavelet, cell, index, sems = refs
        ix, iy = lax.axis_index("gx"), lax.axis_index("gy")
        get_index = pltpu.make_async_copy(index_hbm, index, sems.at[0])
        get_index.start()
        later = [
            pltpu.make_async_copy(wavelet_hbm, wavelet, sems.at[1]),
            pltpu.make_async_copy(cell_hbm, cell, sems.at[2]),
            pltpu.make_async_copy(src_next, next_src, sems.at[3]),
            pltpu.make_async_copy(rcv_next, next_rcv, sems.at[4]),
        ]
        get_rcv = column_copies(rcv, rcv_cols, sems.at[6])
        start(get_rcv + later)
        local_source(src, None, None, base, lap)
        get_index.wait()
        edge = (ix == 0) | (ix == 7)
        side = jnp.where(ix == 0, 0, 1)
        restores = [
            pltpu.make_async_copy(
                saved.at[index[step], side, pl.ds(pl.multiple_of(iy * 16, 16), 16), pl.ds(t * 128, 128)],
                planes.at[step, t],
                sems.at[5],
            )
            for step in range(STEPS)
            for t in range(4)
        ]

        @pl.when(edge)
        def _():
            start(restores)

        wait(get_rcv)
        local_receiver(0, flat(rcv_cols), None, vel, inject, rcv_out)
        wait(later)
        subtract(base, next_src)
        subtract(rcv_out, next_rcv)
        add_wavelet(0, cell, wavelet, base)

        @pl.when(edge)
        def _():
            wait(restores)

    return pl.pallas_call(
        kernel,
        out_shape=[SRC_COLS, SRC_COLS, RCV_COLS, jax.ShapeDtypeStruct((STEPS, 4, 16, 128), F32)],
        in_specs=[VM, HB, HB, HB, VM, VM] + [HB] * 4,
        out_specs=[VM] * 4,
        scratch_shapes=[
            pltpu.VMEM((256, 512), F32),
            pltpu.VMEM((2, 16, 32, 128), F32),
            pltpu.VMEM((512, 256), F32),
            pltpu.SMEM((4,), F32),
            pltpu.SMEM((3,), jnp.int32),
            pltpu.SMEM((4,), jnp.int32),
            pltpu.SemaphoreType.DMA((7,)),
        ],
        compiler_params=params(),
        cost_estimate=hint(3),
        name="local_first",
    )(
        src,
        *in_hbm(src_next, rcv, rcv_next),
        vel,
        inject,
        *in_hbm(wavelet, cell, saved, plane_index),
    )


def local_step(step, src, src_next, rcv, rcv_next, vel_src, vel, inject, wavelet, cell):
    from_hbm, keep, last = step == 1, step == 2, step == STEPS - 1

    def kernel(src, src_next, rcv, rcv_next, vel_src, vel, inject, wavelet_hbm, cell_hbm, src_out, rcv_out, *refs):
        brick = refs[0] if last else None
        wavelet, cell, next_src, next_rcv, sems = refs[-5:]
        copies = [
            pltpu.make_async_copy(wavelet_hbm, wavelet, sems.at[0]),
            pltpu.make_async_copy(cell_hbm, cell, sems.at[1]),
        ]
        if from_hbm:
            copies.append(pltpu.make_async_copy(src_next, next_src, sems.at[2]))
            copies.append(pltpu.make_async_copy(rcv_next, next_rcv, sems.at[3]))
        if keep:
            copies.append(pltpu.make_async_copy(rcv, refs[0], sems.at[2]))
        start(copies)
        local_source(src, None if from_hbm else src_next, vel_src, src_out)
        local_receiver(step, rcv, None if from_hbm else rcv_next, vel, inject, rcv_out)
        if last:
            pack_brick(src_next, brick)
        wait(copies)
        if from_hbm:
            subtract(src_out, next_src)
            subtract(rcv_out, next_rcv)
        add_wavelet(step, cell, wavelet, src_out)

    if from_hbm:
        src_next, rcv_next = in_hbm(src_next, rcv_next)
    next_spec = HB if from_hbm else VM
    out_shape = [SRC_COLS, RCV_COLS] + ([BRICK] if last else [])
    if keep:
        out_shape.append(pltpu.HBM(RCV_COLS.shape, F32))
    return pl.pallas_call(
        kernel,
        out_shape=out_shape,
        in_specs=[VM, next_spec, VM, next_spec] + [VM] * 3 + [HB] * 2,
        out_specs=[VM, VM] + [HB if keep else VM] * (len(out_shape) - 2),
        scratch_shapes=[
            pltpu.SMEM((4,), F32),
            pltpu.SMEM((3,), jnp.int32),
            pltpu.VMEM((256, 512) if from_hbm else (8, 128), F32),
            pltpu.VMEM((512, 256) if from_hbm else (8, 128), F32),
            pltpu.SemaphoreType.DMA((4,)),
        ],
        compiler_params=params(),
        cost_estimate=hint(3),
        name=f"local_step{step}",
    )(src, src_next, rcv, rcv_next, vel_src, vel, inject, *in_hbm(wavelet, cell))


def restore_planes(step, src, planes):
    ix = lax.axis_index("gx")

    @pl.when(ix == 0)
    def _():
        for t in range(4):
            src[t, pl.ds(0, 16, stride=16), :] = planes[step, t]

    @pl.when(ix == 7)
    def _():
        for t in range(4):
            src[t, pl.ds(15, 16, stride=16), :] = planes[step, t]


def halo_step(step, local, vel_src, vel, halos, planes):
    first = step == 0

    def kernel(*refs):
        refs = list(refs)
        local_src = refs.pop(0)
        lap = refs.pop(0) if first else None
        local_rcv, vel_src, vel = refs[:3]
        halos, planes, src, rcv, packed = refs[3:7], refs[7], refs[8], refs[9], refs[10:]
        src[...] = local_src[...] + vel_src[...] * lap[...] if first else local_src[...]
        rcv[...] = local_rcv[...]
        add_source(src, vel_src, *halos)
        restore_planes(step, src, planes)
        pack_source(src, *packed)
        add_receiver(rcv, vel, PLANES, *halos)
        pack_receiver(rcv, PLANES, *packed)

    args = [*local, vel_src, vel, *halos, planes]
    out_shape = [SRC_COLS, RCV_COLS, *halo_buffers(SRC_PLANES, RCV_PLANES)]
    return pl.pallas_call(
        kernel,
        out_shape=out_shape,
        in_specs=[VM] * len(args),
        out_specs=[VM] * len(out_shape),
        compiler_params=params(),
        name=f"halo_step{step}",
    )(*args)


def last_source(local, early, vel_src, halos, planes):
    def kernel(local, early, vel_src, *refs):
        halos, planes, src, bricks, late, sems = refs[:4], *refs[4:]
        copies = [pltpu.make_async_copy(early, bricks.at[:, 0], sems.at[0])]
        copies[0].start()
        src[...] = local[...]
        add_source(src, vel_src, *halos)
        restore_planes(STEPS - 1, src, planes)
        for t in range(4):
            pack_brick(src, late, (t,))
            part = pl.ds(t * 4, 4)
            copies.append(pltpu.make_async_copy(late.at[part], bricks.at[part, 1], sems.at[1]))
            copies[-1].start()
        wait(copies)

    return pl.pallas_call(
        kernel,
        out_shape=[SRC_COLS, pltpu.HBM((16, 2, 16, 512), BF16)],
        in_specs=[VM] * 8,
        out_specs=[VM, HB],
        scratch_shapes=[pltpu.VMEM((16, 16, 512), BF16), pltpu.SemaphoreType.DMA((2,))],
        compiler_params=params(),
        name="last_source",
    )(local, early, vel_src, *halos, planes)


def last_receiver(local, vel, halos, src, kept):
    def kernel(local, vel, *refs):
        halos, src, kept, rcv, early, src_out, rcv_out, sem = refs[:4], *refs[4:]
        copies = [pltpu.make_async_copy(src.at[t], src_out.at[:, pl.ds(t * 128, 128)], sem) for t in range(4)]
        copies += [pltpu.make_async_copy(kept.at[t], early.at[t], sem) for t in range(2)]
        start(copies)
        rcv[...] = local[...]
        add_receiver(rcv, vel, PLANES, *halos)
        more = [pltpu.make_async_copy(rcv.at[t], rcv_out.at[:, pl.ds(t * 128, 128)], sem) for t in range(2)]
        start(more)
        wait(copies + more)

    return pl.pallas_call(
        kernel,
        out_shape=[RCV_COLS] * 2 + [jax.ShapeDtypeStruct(shape, F32) for shape in ((256, 512), (512, 256))],
        in_specs=[VM] * 7 + [HB],
        out_specs=[VM, VM, HB, HB],
        scratch_shapes=[pltpu.SemaphoreType.DMA],
        compiler_params=params(),
        cost_estimate=hint(2),
        name="last_receiver",
    )(local, vel, *halos, src, *in_hbm(kept))


def make_image(bricks, rcv_early, rcv_late):
    def kernel(bricks, rcv_early, rcv_late, out, held, sem):
        copies = []
        for q in range(4):
            rows = slice(q * 128, q * 128 + 128)
            early = bricks[:, 0, :, rows].reshape(256, 128).astype(F32).T
            late = bricks[:, 1, :, rows].reshape(256, 128).astype(F32).T
            for t in range(2):
                lanes = slice(t * 128, t * 128 + 128)
                held[rows, lanes] = early[:, lanes] * rcv_early[t, rows, :] + late[:, lanes] * rcv_late[t, rows, :]
            copies.append(pltpu.make_async_copy(held.at[rows, :], out.at[rows, :], sem))
            copies[-1].start()
        wait(copies)

    return pl.pallas_call(
        kernel,
        out_shape=jax.ShapeDtypeStruct((512, 256), F32),
        in_specs=[VM] * 3,
        out_specs=HB,
        scratch_shapes=[pltpu.VMEM((512, 256), F32), pltpu.SemaphoreType.DMA],
        compiler_params=params(),
        name="make_image",
    )(bricks, rcv_early, rcv_late)


def exchange(buffers):
    gx_second, gy_second, gx_first, gy_first = buffers
    inner = lambda n: [(i, i ^ 1) for i in range(n)]
    outer = lambda n: [(i, (((i + 1) ^ 1) - 1) % n) for i in range(n)]
    return (
        lax.ppermute(gx_second, "gx", outer(8)),
        lax.ppermute(gy_second, "gy", outer(16)),
        lax.ppermute(gx_first, "gx", inner(8)),
        lax.ppermute(gy_first, "gy", inner(16)),
    )


def on_device(
    source_now,
    source_next,
    receiver_now,
    receiver_next,
    velocity,
    saved_planes,
    plane_index,
    wavelet,
    source_cell,
    traces,
    receiver_x,
    receiver_y,
):
    vel, turned = turn_velocity(velocity)
    pieces = lax.all_to_all(turned.reshape(16, 16, 512), "gy", split_axis=0, concat_axis=0, tiled=True)
    src, *to_send = first_halos(source_now, receiver_now)
    halos = exchange(to_send)
    src, vel = src.reshape(4, 256, 128), vel.reshape(2, 512, 128)
    inject = injections(traces, receiver_x, receiver_y)
    src_next, rcv_next = source_next.reshape(256, 512), receiver_next.reshape(512, 256)
    *local, planes = local_first(
        src, src_next, receiver_now, rcv_next, vel, inject, wavelet, source_cell, saved_planes, plane_index
    )
    vel_src = source_velocity(pieces)
    src_next, rcv_next = source_now.reshape(256, 512), receiver_now.reshape(512, 256)
    more = []
    for step in range(STEPS - 1):
        src, rcv, *to_send = halo_step(step, local, vel_src, vel, halos, planes)
        halos = exchange(to_send)
        local = local_step(step + 1, src, src_next, rcv, rcv_next, vel_src, vel, inject, wavelet, source_cell)
        more += local[2:]
        local = local[:2]
        src_next, rcv_next = src, rcv
    kept, early = more
    src, bricks = last_source(local[0], early, vel_src, halos, planes)
    bricks = lax.all_to_all(bricks, "gy", split_axis=0, concat_axis=0, tiled=True)
    rcv, rcv_early, source_field, receiver_field = last_receiver(local[1], vel, halos, src, kept)
    image = make_image(bricks, rcv_early, rcv)
    return (image.reshape(16, 32, 256), receiver_field.reshape(16, 32, 256), source_field.reshape(16, 16, 512))


def solution(mesh):
    field, turned = P("gx", "gy", None), P("gy", "gx", None)
    return jax.shard_map(
        on_device,
        mesh=mesh,
        in_specs=(turned, turned, field, field, field, P(), P(), P(), P(), P(), P(), P()),
        out_specs=(field, field, turned),
        check_vma=False,
    )
```

time: 84.4 us -> 81.6 us (0.967)
  waiting for transfers between devices: 10.8 us -> 19.8 us
  starting transfers between devices: 44.2 us -> 37.2 us
  Pallas kernels: 27.8 us -> 21.2 us
  local copies, waits for them, and re-layouts: 0 us -> 1.81 us
    all_to_all x1, waiting for transfers between devices: 0.01 us -> 8.09 us  [on_device(): lax.all_to_all(bricks, 'gy', split_axis=0, concat_axis=0, tiled=True)]
    ppermute x20 -> x16, starting transfers between devices: 31.1 us -> 24.7 us  [the longest x4 12.6 us: exchange(): lax.ppermute(gy_second, 'gy', outer(16))]
    pallas_call x10 -> x8, Pallas kernels: 20.4 us -> 14.3 us  [the longest x3 6.66 us: local_step(): pl.pallas_call(kernel, out_shape=out_shape, in_specs=[VM, next_spec, VM,...]
    unnamed x0 -> x8, local copies, waits for them, and re-layouts: none -> 1.81 us
    pallas_call x3, Pallas kernels: 3.95 us -> 2.93 us  [halo_step(): pl.pallas_call(kernel, out_shape=out_shape, in_specs=[VM] * len(args), ou...]
    ppermute x20 -> x16, waiting for transfers between devices: 10.8 us -> 11.7 us  [the longest x4 11.7 us: exchange(): lax.ppermute(gy_second, 'gy', outer(16))]
    pallas_call x1, Pallas kernels: 1.23 us -> 2.15 us  [first_halos(): pl.pallas_call(kernel, out_shape=[jax.ShapeDtypeStruct((4, 16, 16, 128),...]
  transfers between devices with their start and end apart: 22 -> 18, of which waited for: 6 -> 5; matrix products, arithmetic and copies ran while one was open for 0% -> 0% of each run, Pallas kernels for 24% -> 17%
where the time goes in v5:
time: 81.6 us; the launch traced here: 81 us
  starting transfers between devices  37.2 us (46%)
  Pallas kernels  21.2 us (26%)
  waiting for transfers between devices  19.8 us (24%)
  local copies, waits for them, and re-layouts  1.81 us (2%)
  between operations  0.96 us (1%)
    ppermute x4, starting transfers between devices, exchange(): lax.ppermute(gy_second, 'gy', outer(16))  12.6 us
    ppermute x4, waiting for transfers between devices, exchange(): lax.ppermute(gy_second, 'gy', outer(16))  11.7 us
    ppermute x4, starting transfers between devices, exchange(): lax.ppermute(gx_second, 'gx', outer(8))  9.71 us
    all_to_all x1, starting transfers between devices, on_device(): lax.all_to_all(turned.reshape(16, 16, 512), 'gy', split_axis=0, concat_ax...  8.46 us
    all_to_all x1, waiting for transfers between devices, on_device(): lax.all_to_all(bricks, 'gy', split_axis=0, concat_axis=0, tiled=True)  8.09 us
    pallas_call x3, Pallas kernels, local_step(): pl.pallas_call(kernel, out_shape=out_shape, in_specs=[VM, next_spec, VM,...  6.66 us
    all_to_all x1, starting transfers between devices, on_device(): lax.all_to_all(bricks, 'gy', split_axis=0, concat_axis=0, tiled=True)  4.01 us
    pallas_call x3, Pallas kernels, halo_step(): pl.pallas_call(kernel, out_shape=out_shape, in_specs=[VM] * len(args), ou...  2.93 us
  transfers between devices with their start and end apart: 18, of which 5 were waited for; matrix products, arithmetic and copies ran while one was open for 0% of the time, Pallas kernels for 17%

profile of v5, /device:TPU:1, one launch (start us, length us, event | category | flops | bytes accessed | tf_op | source)
XLA Modules:
  0.0 81.0 jit_solution(5938217450213713014)
XLA Ops:
  0.6 2.0 %turn_velocity.1 = (f32[2,16,32,128]{3,2,1,0:T(8,128)S(1)}, f32[256,512]{1,0:T(8,128)}) custom-call(f32[16,32,256]{2,1,0:T(8,128)} %vel.1), custom_call_target="tpu_custom_call" | custom-call | tf_op jit(solution)/shard_map/turn_velocity/pallas_call | solution.py:309
  2.6 8.5 %all-to-all-start = ((f32[16,16,512]{2,1,0:T(8,128)}), f32[16,16,512]{2,1,0:T(8,128)S(1)}, u32[]{:S(2)}, u32[]{:S(2)}) async-start(f32[16,16,512]{2,1,0:T(8,128)} %bitcast.25), calls=%async_computation | async-start | bytes 1048576 | tf_op jit(solution)/shard_map/all_to_all | solution.py:703
  11.1 2.1 %first_halos.1 = (f32[4,16,16,128]{3,2,1,0:T(8,128)S(1)}, bf16[10,16,512]{2,1,0:T(8,128)(2,1)}, bf16[8,16,512]{2,1,0:T(8,128)(2,1)}, bf16[10,16,512]{2,1,0:T(8,128)(2,1)S(1)}, bf16[8,16,512]{2,1,0:T(8,128)(2,1)}) custom-call(f32[16,16,512]{2,1,0:T(8,128)} %src.1, f32[16,32,256]{2,1,0:T(8,128)} %rcv.3), custom_call_target="tpu_custom_call" | custom-call | tf_op jit(solution)/shard_map/first_halos/pallas_call | solution.py:330
  13.2 4.0 %collective-permute-start = (bf16[10,16,512]{2,1,0:T(8,128)(2,1)}, bf16[10,16,512]{2,1,0:T(8,128)(2,1)S(1)}, u32[]{:S(2)}, u32[]{:S(2)}) collective-permute-start(bf16[10,16,512]{2,1,0:T(8,128)(2,1)} %get-tuple-element.52), channel_id=1, source_target_pairs={{0,112},{16,32},{32,16},{48,64},{64,48},{80,96},{96,80},{112,0},{1... | collective-permute-start | bytes 491528 | tf_op jit(solution)/shard_map/ppermute | solution.py:681
  17.2 0.0 collective-permute-start.2
  17.2 4.0 %collective-permute-start.1 = (bf16[8,16,512]{2,1,0:T(8,128)(2,1)}, bf16[8,16,512]{2,1,0:T(8,128)(2,1)S(1)}, u32[]{:S(2)}, u32[]{:S(2)}) collective-permute-start(bf16[8,16,512]{2,1,0:T(8,128)(2,1)} %get-tuple-element.53), channel_id=1, source_target_pairs={{0,15},{1,2},{2,1},{3,4},{4,3},{5,6},{6,5},{7,8},{8,7},{9,10},{10,... | collective-permute-start | bytes 393224 | tf_op jit(solution)/shard_map/ppermute | solution.py:682
  21.2 2.0 %collective-permute-start.3 = (bf16[8,16,512]{2,1,0:T(8,128)(2,1)}, bf16[8,16,512]{2,1,0:T(8,128)(2,1)S(1)}, u32[]{:S(2)}, u32[]{:S(2)}) collective-permute-start(bf16[8,16,512]{2,1,0:T(8,128)(2,1)} %get-tuple-element.55), channel_id=1, source_target_pairs={{0,1},{1,0},{2,3},{3,2},{4,5},{5,4},{6,7},{7,6},{8,9},{9,8},{10,11... | collective-permute-start | bytes 393224 | tf_op jit(solution)/shard_map/ppermute | solution.py:684
  23.2 1.4 %injections.1.inject = f32[32,128]{1,0:T(8,128)S(1)} custom-call(f32[4,4096]{1,0:T(4,128)} %traces_hbm.1, s32[1,4096]{1,0:T(1,128)} %bitcast.27, s32[1,4096]{1,0:T(1,128)} %bitcast.28), custom_call_target="tpu_custom_call" | custom-call | bytes 7200000 | tf_op jit(solution)/shard_map/injections/pallas_call | solution.py:376
  24.6 2.2 %local_first.1 = (f32[4,256,128]{2,1,0:T(8,128)S(1)}, f32[4,256,128]{2,1,0:T(8,128)S(1)}, f32[2,512,128]{2,1,0:T(8,128)S(1)}, f32[4,4,16,128]{3,2,1,0:T(8,128)S(1)}) custom-call(f32[4,256,128]{2,1,0:T(8,128)S(1)} %bitcast.20, f32[256,512]{1,0:T(8,128)} %bitcast.23, f32[16,32,256]{2,1,0:T(8,128)} %rcv.3, f32[512,256]{1,0:T(8,128)} %bitcast.24, ...), custom_call_target="tpu_custom_call" | custom-call | bytes 10800000 | tf_op jit(solution)/shard_map/local_first/pallas_call | solution.py:482
  26.8 0.0 all-to-all-done.pieces
  26.8 0.5 source_velocity.1.refs_3_.vel_src.refs_2_
  27.3 1.4 %collective-permute-done.1.refs_6_ = bf16[8,16,512]{2,1,0:T(8,128)(2,1)S(1)} collective-permute-done((bf16[8,16,512]{2,1,0:T(8,128)(2,1)}, bf16[8,16,512]{2,1,0:T(8,128)(2,1)S(1)}, u32[]{:S(2)}, u32[]{:S(2)}) %collective-permute-start.1) | collective-permute-done | bytes 131104 | tf_op jit(solution)/shard_map/ppermute | solution.py:682
  28.7 0.0 collective-permute-done.3.refs_8_
  28.7 0.0 collective-permute-done.refs_5_
  28.7 1.0 %halo_step0.1 = (f32[4,256,128]{2,1,0:T(8,128)S(1)}, f32[2,512,128]{2,1,0:T(8,128)S(1)}, bf16[10,16,512]{2,1,0:T(8,128)(2,1)S(1)}, bf16[8,16,512]{2,1,0:T(8,128)...) custom-call(f32[4,256,128]{2,1,0:T(8,128)S(1)} %get-tuple-element.48.refs_0_, ...), custom_call_target="tpu_custom_call" | custom-call | tf_op jit(solution)/shard_map/halo_step0/pallas_call | solution.py:591
  29.7 2.9 %collective-permute-start.4 = (bf16[10,16,512]{2,1,0:T(8,128)(2,1)S(1)}, bf16[10,16,512]{2,1,0:T(8,128)(2,1)S(1)}, u32[]{:S(2)}, u32[]{:S(2)}) collective-permute-start(bf16[10,16,512]{2,1,0:T(8,128)(2,1)S(1)} %get-tuple-element.61), channel_id=1, source_target_pairs={{0,112},{16,32},{32,16},{48,64},{64,48},{80,96},{96,80},{112,0},{1... | collective-permute-start | bytes 491528 | tf_op jit(solution)/shard_map/ppermute | solution.py:681
  32.7 1.7 %collective-permute-start.5 = (bf16[8,16,512]{2,1,0:T(8,128)(2,1)S(1)}, bf16[8,16,512]{2,1,0:T(8,128)(2,1)S(1)}, u32[]{:S(2)}, u32[]{:S(2)}) collective-permute-start(bf16[8,16,512]{2,1,0:T(8,128)(2,1)S(1)} %get-tuple-element.62), channel_id=1, source_target_pairs={{0,15},{1,2},{2,1},{3,4},{4,3},{5,6},{6,5},{7,8},{8,7},{9,10},{10,... | collective-permute-start | bytes 393224 | tf_op jit(solution)/shard_map/ppermute | solution.py:682
  34.4 0.0 collective-permute-start.7
  34.4 2.5 %local_step1.1 = (f32[4,256,128]{2,1,0:T(8,128)S(1)}, f32[2,512,128]{2,1,0:T(8,128)S(1)}) custom-call(f32[4,256,128]{2,1,0:T(8,128)S(1)} %get-tuple-element.57.src.src_next, f32[256,512]{1,0:T(8,128)} %bitcast.22, f32[2,512,128]{2,1,0:T(8,128)S(1)} %get-tuple-element.58.rcv.rcv_next, f32[512,256]{1,0:T(8,128)} %bitcast.21, ...), custom_call_target="tpu_custom_call" | custom-call | bytes 10800000 | tf_op jit(solution)/shard_map/local_step1/pallas_call | solution.py:540
  37.0 3.2 %collective-permute-done.5.refs_5_ = bf16[8,16,512]{2,1,0:T(8,128)(2,1)S(1)} collective-permute-done((bf16[8,16,512]{2,1,0:T(8,128)(2,1)S(1)}, bf16[8,16,512]{2,1,0:T(8,128)(2,1)S(1)}, u32[]{:S(2)}, u32[]{:S(2)}) %collective-permute-start.5) | collective-permute-done | bytes 131104 | tf_op jit(solution)/shard_map/ppermute | solution.py:682
  40.2 0.0 collective-permute-done.7.refs_7_
  40.2 0.0 collective-permute-done.4.refs_4_
  40.2 0.0 collective-permute-done.6.refs_6_
  40.2 1.0 %halo_step1.1 = (f32[4,256,128]{2,1,0:T(8,128)S(1)}, f32[2,512,128]{2,1,0:T(8,128)S(1)}, bf16[10,16,512]{2,1,0:T(8,128)(2,1)S(1)}, bf16[8,16,512]{2,1,0:T(8,128)...) custom-call(f32[4,256,128]{2,1,0:T(8,128)S(1)} %get-tuple-element.59.refs_0_, ...), custom_call_target="tpu_custom_call" | custom-call | tf_op jit(solution)/shard_map/halo_step1/pallas_call | solution.py:591
  41.2 2.0 %collective-permute-start.8 = (bf16[10,16,512]{2,1,0:T(8,128)(2,1)S(1)}, bf16[10,16,512]{2,1,0:T(8,128)(2,1)S(1)}, u32[]{:S(2)}, u32[]{:S(2)}) collective-permute-start(bf16[10,16,512]{2,1,0:T(8,128)(2,1)S(1)} %get-tuple-element.69), channel_id=1, source_target_pairs={{0,112},{16,32},{32,16},{48,64},{64,48},{80,96},{96,80},{112,0},{1... | collective-permute-start | bytes 491528 | tf_op jit(solution)/shard_map/ppermute | solution.py:681
  43.3 0.0 collective-permute-start.10
  43.3 2.9 %collective-permute-start.9 = (bf16[8,16,512]{2,1,0:T(8,128)(2,1)S(1)}, bf16[8,16,512]{2,1,0:T(8,128)(2,1)S(1)}, u32[]{:S(2)}, u32[]{:S(2)}) collective-permute-start(bf16[8,16,512]{2,1,0:T(8,128)(2,1)S(1)} %get-tuple-element.70), channel_id=1, source_target_pairs={{0,15},{1,2},{2,1},{3,4},{4,3},{5,6},{6,5},{7,8},{8,7},{9,10},{10,... | collective-permute-start | bytes 393224 | tf_op jit(solution)/shard_map/ppermute | solution.py:682
  46.2 0.4 collective-permute-start.11
  46.6 2.1 %local_step2.1 = (f32[4,256,128]{2,1,0:T(8,128)S(1)}, f32[2,512,128]{2,1,0:T(8,128)S(1)}, f32[2,512,128]{2,1,0:T(8,128)}) custom-call(f32[4,256,128]{2,1,0:T(8,128)S(1)} %get-tuple-element.65.src.src_next, f32[4,256,128]{2,1,0:T(8,128)S(1)} %get-tuple-element.57.src.src_next, f32[2,512,128]{2,1,0:T(8,128)S(1)} %get-tuple-element.66.rcv.rcv_next, ...), custom_call_target="tpu_custom_call" | custom-call | bytes 10800000 | tf_op jit(solution)/shard_map/local_step2/pallas_call | solution.py:540
  48.7 3.3 %collective-permute-done.9.refs_5_ = bf16[8,16,512]{2,1,0:T(8,128)(2,1)S(1)} collective-permute-done((bf16[8,16,512]{2,1,0:T(8,128)(2,1)S(1)}, bf16[8,16,512]{2,1,0:T(8,128)(2,1)S(1)}, u32[]{:S(2)}, u32[]{:S(2)}) %collective-permute-start.9) | collective-permute-done | bytes 131104 | tf_op jit(solution)/shard_map/ppermute | solution.py:682
  52.0 0.0 collective-permute-done.8.refs_4_
  52.0 0.0 collective-permute-done.10.refs_6_
  52.0 1.0 %halo_step2.1 = (f32[4,256,128]{2,1,0:T(8,128)S(1)}, f32[2,512,128]{2,1,0:T(8,128)S(1)}, bf16[10,16,512]{2,1,0:T(8,128)(2,1)S(1)}, bf16[8,16,512]{2,1,0:T(8,128)...) custom-call(f32[4,256,128]{2,1,0:T(8,128)S(1)} %get-tuple-element.67.refs_0_, ...), custom_call_target="tpu_custom_call" | custom-call | tf_op jit(solution)/shard_map/halo_step2/pallas_call | solution.py:591
  52.9 0.8 collective-permute-start.12
  53.7 0.0 collective-permute-start.14
  53.7 3.9 %collective-permute-start.13 = (bf16[8,16,512]{2,1,0:T(8,128)(2,1)S(1)}, bf16[8,16,512]{2,1,0:T(8,128)(2,1)S(1)}, u32[]{:S(2)}, u32[]{:S(2)}) collective-permute-start(bf16[8,16,512]{2,1,0:T(8,128)(2,1)S(1)} %get-tuple-element.78), channel_id=1, source_target_pairs={{0,15},{1,2},{2,1},{3,4},{4,3},{5,6},{6,5},{7,8},{8,7},{9,10},{10,... | collective-permute-start | bytes 393224 | tf_op jit(solution)/shard_map/ppermute | solution.py:682
  57.6 0.0 collective-permute-start.15
  57.6 2.1 %local_step3.1 = (f32[4,256,128]{2,1,0:T(8,128)S(1)}, f32[2,512,128]{2,1,0:T(8,128)S(1)}, bf16[16,16,512]{2,1,0:T(8,128)(2,1)S(1)}) custom-call(f32[4,256,128]{2,1,0:T(8,128)S(1)} %get-tuple-element.73.src, f32[4,256,128]{2,1,0:T(8,128)S(1)} %get-tuple-element.65.src.src_next, f32[2,512,128]{2,1,0:T(8,128)S(1)} %get-tuple-element.74.rcv, ...), custom_call_target="tpu_custom_call" | custom-call | bytes 10800000 | tf_op jit(solution)/shard_map/local_step3/pallas_call | solution.py:540
  59.7 3.7 %collective-permute-done.13.refs_1_ = bf16[8,16,512]{2,1,0:T(8,128)(2,1)S(1)} collective-permute-done((bf16[8,16,512]{2,1,0:T(8,128)(2,1)S(1)}, bf16[8,16,512]{2,1,0:T(8,128)(2,1)S(1)}, u32[]{:S(2)}, u32[]{:S(2)}) %collective-permute-start.13) | collective-permute-done | bytes 131104 | tf_op jit(solution)/shard_map/ppermute | solution.py:682
  63.4 0.0 collective-permute-done.15.refs_3_
  63.4 0.0 collective-permute-done.14.refs_2_
  63.5 1.3 %last_source.1 = (f32[4,256,128]{2,1,0:T(8,128)S(1)}, bf16[16,2,16,512]{3,2,1,0:T(8,128)(2,1)}) custom-call(f32[4,256,128]{2,1,0:T(8,128)S(1)} %get-tuple-element.75.local, bf16[16,16,512]{2,1,0:T(8,128)(2,1)S(1)} %get-tuple-element.76.early, f32[4,256,128]{2,1,0:T(8,128)S(1)} %source_velocity.1.refs_3_.vel_src.refs_2_, ...), custom_call_target="tpu_custom_call" | custom-call | tf_op jit(solution)/shard_map/last_source/pallas_call | solution.py:616
  64.8 4.0 %all-to-all-start.1 = ((bf16[16,2,16,512]{3,2,1,0:T(8,128)(2,1)}), bf16[16,2,16,512]{3,2,1,0:T(8,128)(2,1)S(1)}, u32[]{:S(2)}, u32[]{:S(2)}) async-start(bf16[16,2,16,512]{3,2,1,0:T(8,128)(2,1)} %get-tuple-element.81), calls=%async_computation.1 | async-start | bytes 1048576 | tf_op jit(solution)/shard_map/all_to_all | solution.py:724
  68.8 0.9 %copy-done.1 = bf16[8,16,512]{2,1,0:T(8,128)(2,1)S(1)} copy-done((bf16[8,16,512]{2,1,0:T(8,128)(2,1)S(1)}, bf16[8,16,512]{2,1,0:T(8,128)(2,1)}, u32[]{:S(2)}) %copy-start.1) | copy-done | bytes 131096
  69.7 0.9 %copy-done.3 = bf16[8,16,512]{2,1,0:T(8,128)(2,1)S(1)} copy-done((bf16[8,16,512]{2,1,0:T(8,128)(2,1)S(1)}, bf16[8,16,512]{2,1,0:T(8,128)(2,1)}, u32[]{:S(2)}) %copy-start.3) | copy-done | bytes 131096
  70.6 1.2 %last_receiver.1 = (f32[2,512,128]{2,1,0:T(8,128)S(1)}, f32[2,512,128]{2,1,0:T(8,128)S(1)}, f32[256,512]{1,0:T(8,128)}, f32[512,256]{1,0:T(8,128)}) custom-call(f32[2,512,128]{2,1,0:T(8,128)S(1)} %get-tuple-element.82.local, f32[2,512,128]{2,1,0:T(8,128)S(1)} %bitcast.19, bf16[10,16,512]{2,1,0:T(8,128)(2,1)S(1)} %collective-permute-done.12.refs_0_, ...), custom_call_target="tpu_custom_call" | custom-call | bytes 7200000 | tf_op jit(solution)/shard_map/last_receiver/pallas_call | solution.py:639
  71.9 8.1 %all-to-all-done.1.bricks = bf16[16,2,16,512]{3,2,1,0:T(8,128)(2,1)S(1)} async-done(((bf16[16,2,16,512]{3,2,1,0:T(8,128)(2,1)}), bf16[16,2,16,512]{3,2,1,0:T(8,128)(2,1)S(1)}, u32[]{:S(2)}, u32[]{:S(2)}) %all-to-all-start.1) | async-done | bytes 524320 | tf_op jit(solution)/shard_map/all_to_all | solution.py:724
  80.0 0.9 %make_image.1 = f32[512,256]{1,0:T(8,128)} custom-call(bf16[16,2,16,512]{3,2,1,0:T(8,128)(2,1)S(1)} %all-to-all-done.1.bricks, f32[2,512,128]{2,1,0:T(8,128)S(1)} %get-tuple-element.85.rcv_early, f32[2,512,128]{2,1,0:T(8,128)S(1)} %get-tuple-element.86.rcv_late), custom_call_target="tpu_custom_call" | custom-call | tf_op jit(solution)/shard_map/make_image/pallas_call | solution.py:665
  (10 shorter events, 0.0 us)
Async XLA Ops:
  2.6 24.2 %all-to-all-start = ((f32[16,16,512]{2,1,0:T(8,128)}), f32[16,16,512]{2,1,0:T(8,128)S(1)}, u32[]{:S(2)}, u32[]{:S(2)}) async-start(f32[16,16,512]{2,1,0:T(8,128)} %bitcast.25), calls=%async_computation | async-start | bytes 1048576 | tf_op jit(solution)/shard_map/all_to_all | solution.py:703
  13.2 15.5 %collective-permute-start = (bf16[10,16,512]{2,1,0:T(8,128)(2,1)}, bf16[10,16,512]{2,1,0:T(8,128)(2,1)S(1)}, u32[]{:S(2)}, u32[]{:S(2)}) collective-permute-start(bf16[10,16,512]{2,1,0:T(8,128)(2,1)} %get-tuple-element.52), channel_id=1, source_target_pairs={{0,112},{16,32},{32,16},{48,64},{64,48},{80,96},{96,80},{112,0},{1... | collective-permute-start | bytes 491528 | tf_op jit(solution)/shard_map/ppermute | solution.py:681
  17.2 11.5 %collective-permute-start.2 = (bf16[10,16,512]{2,1,0:T(8,128)(2,1)S(1)}, bf16[10,16,512]{2,1,0:T(8,128)(2,1)S(1)}, u32[]{:S(2)}, u32[]{:S(2)}) collective-permute-start(bf16[10,16,512]{2,1,0:T(8,128)(2,1)S(1)} %get-tuple-element.54), channel_id=1, source_target_pairs={{0,16},{16,0},{32,48},{48,32},{64,80},{80,64},{96,112},{112,96},{1... | collective-permute-start | bytes 491528 | tf_op jit(solution)/shard_map/ppermute | solution.py:683
  17.2 11.5 %collective-permute-start.1 = (bf16[8,16,512]{2,1,0:T(8,128)(2,1)}, bf16[8,16,512]{2,1,0:T(8,128)(2,1)S(1)}, u32[]{:S(2)}, u32[]{:S(2)}) collective-permute-start(bf16[8,16,512]{2,1,0:T(8,128)(2,1)} %get-tuple-element.53), channel_id=1, source_target_pairs={{0,15},{1,2},{2,1},{3,4},{4,3},{5,6},{6,5},{7,8},{8,7},{9,10},{10,... | collective-permute-start | bytes 393224 | tf_op jit(solution)/shard_map/ppermute | solution.py:682
  21.2 7.5 %collective-permute-start.3 = (bf16[8,16,512]{2,1,0:T(8,128)(2,1)}, bf16[8,16,512]{2,1,0:T(8,128)(2,1)S(1)}, u32[]{:S(2)}, u32[]{:S(2)}) collective-permute-start(bf16[8,16,512]{2,1,0:T(8,128)(2,1)} %get-tuple-element.55), channel_id=1, source_target_pairs={{0,1},{1,0},{2,3},{3,2},{4,5},{5,4},{6,7},{7,6},{8,9},{9,8},{10,11... | collective-permute-start | bytes 393224 | tf_op jit(solution)/shard_map/ppermute | solution.py:684
  29.7 10.5 %collective-permute-start.4 = (bf16[10,16,512]{2,1,0:T(8,128)(2,1)S(1)}, bf16[10,16,512]{2,1,0:T(8,128)(2,1)S(1)}, u32[]{:S(2)}, u32[]{:S(2)}) collective-permute-start(bf16[10,16,512]{2,1,0:T(8,128)(2,1)S(1)} %get-tuple-element.61), channel_id=1, source_target_pairs={{0,112},{16,32},{32,16},{48,64},{64,48},{80,96},{96,80},{112,0},{1... | collective-permute-start | bytes 491528 | tf_op jit(solution)/shard_map/ppermute | solution.py:681
  32.7 7.6 %collective-permute-start.6 = (bf16[10,16,512]{2,1,0:T(8,128)(2,1)S(1)}, bf16[10,16,512]{2,1,0:T(8,128)(2,1)S(1)}, u32[]{:S(2)}, u32[]{:S(2)}) collective-permute-start(bf16[10,16,512]{2,1,0:T(8,128)(2,1)S(1)} %get-tuple-element.63), channel_id=1, source_target_pairs={{0,16},{16,0},{32,48},{48,32},{64,80},{80,64},{96,112},{112,96},{1... | collective-permute-start | bytes 491528 | tf_op jit(solution)/shard_map/ppermute | solution.py:683
  32.7 7.5 %collective-permute-start.5 = (bf16[8,16,512]{2,1,0:T(8,128)(2,1)S(1)}, bf16[8,16,512]{2,1,0:T(8,128)(2,1)S(1)}, u32[]{:S(2)}, u32[]{:S(2)}) collective-permute-start(bf16[8,16,512]{2,1,0:T(8,128)(2,1)S(1)} %get-tuple-element.62), channel_id=1, source_target_pairs={{0,15},{1,2},{2,1},{3,4},{4,3},{5,6},{6,5},{7,8},{8,7},{9,10},{10,... | collective-permute-start | bytes 393224 | tf_op jit(solution)/shard_map/ppermute | solution.py:682
  34.4 5.8 %collective-permute-start.7 = (bf16[8,16,512]{2,1,0:T(8,128)(2,1)S(1)}, bf16[8,16,512]{2,1,0:T(8,128)(2,1)S(1)}, u32[]{:S(2)}, u32[]{:S(2)}) collective-permute-start(bf16[8,16,512]{2,1,0:T(8,128)(2,1)S(1)} %get-tuple-element.64), channel_id=1, source_target_pairs={{0,1},{1,0},{2,3},{3,2},{4,5},{5,4},{6,7},{7,6},{8,9},{9,8},{10,11... | collective-permute-start | bytes 393224 | tf_op jit(solution)/shard_map/ppermute | solution.py:684
  41.2 10.8 %collective-permute-start.8 = (bf16[10,16,512]{2,1,0:T(8,128)(2,1)S(1)}, bf16[10,16,512]{2,1,0:T(8,128)(2,1)S(1)}, u32[]{:S(2)}, u32[]{:S(2)}) collective-permute-start(bf16[10,16,512]{2,1,0:T(8,128)(2,1)S(1)} %get-tuple-element.69), channel_id=1, source_target_pairs={{0,112},{16,32},{32,16},{48,64},{64,48},{80,96},{96,80},{112,0},{1... | collective-permute-start | bytes 491528 | tf_op jit(solution)/shard_map/ppermute | solution.py:681
  43.3 8.7 %collective-permute-start.10 = (bf16[10,16,512]{2,1,0:T(8,128)(2,1)S(1)}, bf16[10,16,512]{2,1,0:T(8,128)(2,1)S(1)}, u32[]{:S(2)}, u32[]{:S(2)}) collective-permute-start(bf16[10,16,512]{2,1,0:T(8,128)(2,1)S(1)} %get-tuple-element.71), channel_id=1, source_target_pairs={{0,16},{16,0},{32,48},{48,32},{64,80},{80,64},{96,112},{112,96},{1... | collective-permute-start | bytes 491528 | tf_op jit(solution)/shard_map/ppermute | solution.py:683
  43.3 8.7 %collective-permute-start.9 = (bf16[8,16,512]{2,1,0:T(8,128)(2,1)S(1)}, bf16[8,16,512]{2,1,0:T(8,128)(2,1)S(1)}, u32[]{:S(2)}, u32[]{:S(2)}) collective-permute-start(bf16[8,16,512]{2,1,0:T(8,128)(2,1)S(1)} %get-tuple-element.70), channel_id=1, source_target_pairs={{0,15},{1,2},{2,1},{3,4},{4,3},{5,6},{6,5},{7,8},{8,7},{9,10},{10,... | collective-permute-start | bytes 393224 | tf_op jit(solution)/shard_map/ppermute | solution.py:682
  46.2 5.8 %collective-permute-start.11 = (bf16[8,16,512]{2,1,0:T(8,128)(2,1)S(1)}, bf16[8,16,512]{2,1,0:T(8,128)(2,1)S(1)}, u32[]{:S(2)}, u32[]{:S(2)}) collective-permute-start(bf16[8,16,512]{2,1,0:T(8,128)(2,1)S(1)} %get-tuple-element.72), channel_id=1, source_target_pairs={{0,1},{1,0},{2,3},{3,2},{4,5},{5,4},{6,7},{7,6},{8,9},{9,8},{10,11... | collective-permute-start | bytes 393224 | tf_op jit(solution)/shard_map/ppermute | solution.py:684
  52.9 10.5 %collective-permute-start.12 = (bf16[10,16,512]{2,1,0:T(8,128)(2,1)S(1)}, bf16[10,16,512]{2,1,0:T(8,128)(2,1)S(1)}, u32[]{:S(2)}, u32[]{:S(2)}) collective-permute-start(bf16[10,16,512]{2,1,0:T(8,128)(2,1)S(1)} %get-tuple-element.77), channel_id=1, source_target_pairs={{0,112},{16,32},{32,16},{48,64},{64,48},{80,96},{96,80},{112,0},{1... | collective-permute-start | bytes 491528 | tf_op jit(solution)/shard_map/ppermute | solution.py:681
  53.7 9.7 %collective-permute-start.14 = (bf16[10,16,512]{2,1,0:T(8,128)(2,1)S(1)}, bf16[10,16,512]{2,1,0:T(8,128)(2,1)S(1)}, u32[]{:S(2)}, u32[]{:S(2)}) collective-permute-start(bf16[10,16,512]{2,1,0:T(8,128)(2,1)S(1)} %get-tuple-element.79), channel_id=1, source_target_pairs={{0,16},{16,0},{32,48},{48,32},{64,80},{80,64},{96,112},{112,96},{1... | collective-permute-start | bytes 491528 | tf_op jit(solution)/shard_map/ppermute | solution.py:683
  53.7 9.7 %collective-permute-start.13 = (bf16[8,16,512]{2,1,0:T(8,128)(2,1)S(1)}, bf16[8,16,512]{2,1,0:T(8,128)(2,1)S(1)}, u32[]{:S(2)}, u32[]{:S(2)}) collective-permute-start(bf16[8,16,512]{2,1,0:T(8,128)(2,1)S(1)} %get-tuple-element.78), channel_id=1, source_target_pairs={{0,15},{1,2},{2,1},{3,4},{4,3},{5,6},{6,5},{7,8},{8,7},{9,10},{10,... | collective-permute-start | bytes 393224 | tf_op jit(solution)/shard_map/ppermute | solution.py:682
  57.6 5.8 %collective-permute-start.15 = (bf16[8,16,512]{2,1,0:T(8,128)(2,1)S(1)}, bf16[8,16,512]{2,1,0:T(8,128)(2,1)S(1)}, u32[]{:S(2)}, u32[]{:S(2)}) collective-permute-start(bf16[8,16,512]{2,1,0:T(8,128)(2,1)S(1)} %get-tuple-element.80), channel_id=1, source_target_pairs={{0,1},{1,0},{2,3},{3,2},{4,5},{5,4},{6,7},{7,6},{8,9},{9,8},{10,11... | collective-permute-start | bytes 393224 | tf_op jit(solution)/shard_map/ppermute | solution.py:684
  63.4 1.3 %copy-start = (bf16[8,16,512]{2,1,0:T(8,128)(2,1)}, bf16[8,16,512]{2,1,0:T(8,128)(2,1)S(1)}, u32[]{:S(2)}) copy-start(bf16[8,16,512]{2,1,0:T(8,128)(2,1)S(1)} %collective-permute-done.13.refs_1_) | copy-start | bytes 393220
  63.4 1.4 %copy-start.2 = (bf16[8,16,512]{2,1,0:T(8,128)(2,1)}, bf16[8,16,512]{2,1,0:T(8,128)(2,1)S(1)}, u32[]{:S(2)}) copy-start(bf16[8,16,512]{2,1,0:T(8,128)(2,1)S(1)} %collective-permute-done.15.refs_3_) | copy-start | bytes 393220
  64.8 15.2 %all-to-all-start.1 = ((bf16[16,2,16,512]{3,2,1,0:T(8,128)(2,1)}), bf16[16,2,16,512]{3,2,1,0:T(8,128)(2,1)S(1)}, u32[]{:S(2)}, u32[]{:S(2)}) async-start(bf16[16,2,16,512]{3,2,1,0:T(8,128)(2,1)} %get-tuple-element.81), calls=%async_computation.1 | async-start | bytes 1048576 | tf_op jit(solution)/shard_map/all_to_all | solution.py:724
  68.8 0.9 %copy-start.1 = (bf16[8,16,512]{2,1,0:T(8,128)(2,1)S(1)}, bf16[8,16,512]{2,1,0:T(8,128)(2,1)}, u32[]{:S(2)}) copy-start(bf16[8,16,512]{2,1,0:T(8,128)(2,1)} %copy-done) | copy-start | bytes 393220
  69.7 0.9 %copy-start.3 = (bf16[8,16,512]{2,1,0:T(8,128)(2,1)S(1)}, bf16[8,16,512]{2,1,0:T(8,128)(2,1)}, u32[]{:S(2)}) copy-start(bf16[8,16,512]{2,1,0:T(8,128)(2,1)} %copy-done.2) | copy-start | bytes 393220

commit v6 on v5

--- a/solution.py
+++ b/solution.py
@@ -10,7 +10,8 @@
 COEFFS = (C0, C1, C2, C3, C4)
 RECEIVER_PLANE = 2
 PLANES = 5
-F32, BF16 = jnp.float32, jnp.bfloat16
+F32, BF16, I16 = jnp.float32, jnp.bfloat16, jnp.int16
+VELOCITY_MIDDLE, VELOCITY_STEP = 0.115, 0.0651 / 32767
 VMEM_LIMIT = 24 * 1024 * 1024
 
 RCV = dict(lead=16, rows=32, lanes=256)
@@ -228,7 +229,8 @@
     group = lax.broadcasted_iota(jnp.int32, (16, 128), 1) // 32
     for t in range(4):
         for xg in range(4):
-            parts = [pieces[t * 4 + g, :, xg * 128 : xg * 128 + 128] for g in range(4)]
+            codes = [pieces[t * 4 + g, :, xg * 128 : xg * 128 + 128] for g in range(4)]
+            parts = [code.astype(jnp.int32).astype(F32) * VELOCITY_STEP + VELOCITY_MIDDLE for code in codes]
             for xl in range(4):
                 row = None
                 for g in range(4):
@@ -301,17 +303,19 @@
             wait(pieces[2 * q : 2 * q + 2])
             lanes = pl.ds(q * 128, 128)
             for t in range(2):
-                turned[t * 128 : t * 128 + 128, lanes] = flat_cols[t, q * 128 : q * 128 + 128, :].T
+                rows = flat_cols[t, q * 128 : q * 128 + 128, :].T
+                code = jnp.round((rows - VELOCITY_MIDDLE) * (1.0 / VELOCITY_STEP)).astype(jnp.int32)
+                turned[t * 128 : t * 128 + 128, lanes] = code.astype(I16)
             outs.append(pltpu.make_async_copy(turned.at[:, lanes], turned_out.at[:, lanes], sems.at[4]))
             outs[-1].start()
         wait(outs)
 
     return pl.pallas_call(
         kernel,
-        out_shape=[jax.ShapeDtypeStruct((2, 16, 32, 128), F32), pltpu.HBM((256, 512), F32)],
+        out_shape=[jax.ShapeDtypeStruct((2, 16, 32, 128), F32), pltpu.HBM((256, 512), I16)],
         in_specs=[HB],
         out_specs=[VM, HB],
-        scratch_shapes=[pltpu.VMEM((256, 512), F32), pltpu.SemaphoreType.DMA((5,))],
+        scratch_shapes=[pltpu.VMEM((256, 512), I16), pltpu.SemaphoreType.DMA((5,))],
         compiler_params=params(),
         name="turn_velocity",
     )(*in_hbm(vel))

time: 81.6 us -> 79.9 us (0.979)
  waiting for transfers between devices: 19.8 us -> 17.8 us
    ppermute x4, starting transfers between devices: 9.71 us -> 7.01 us  [exchange(): lax.ppermute(gx_second, 'gx', outer(8))]
    ppermute x4, waiting for transfers between devices: 11.7 us -> 9.47 us  [exchange(): lax.ppermute(gy_second, 'gy', outer(16))]
    ppermute x4, starting transfers between devices: 2.42 us -> 4.28 us  [exchange(): lax.ppermute(gy_first, 'gy', inner(16))]
    ppermute x4, starting transfers between devices: 12.6 us -> 13.6 us  [exchange(): lax.ppermute(gy_second, 'gy', outer(16))]
  transfers between devices with their start and end apart: 18 -> 18, of which waited for: 5 -> 6; matrix products, arithmetic and copies ran while one was open for 0% -> 0% of each run, Pallas kernels for 17% -> 18%
where the time goes in v6:
time: 79.9 us; the launch traced here: 79.4 us
  starting transfers between devices  37.6 us (47%)
  Pallas kernels  21.1 us (26%)
  waiting for transfers between devices  17.8 us (22%)
  local copies, waits for them, and re-layouts  1.81 us (2%)
  between operations  0.96 us (1%)
    ppermute x4, starting transfers between devices, exchange(): lax.ppermute(gy_second, 'gy', outer(16))  13.6 us
    ppermute x4, waiting for transfers between devices, exchange(): lax.ppermute(gy_second, 'gy', outer(16))  9.47 us
    all_to_all x1, starting transfers between devices, on_device(): lax.all_to_all(turned.reshape(16, 16, 512), 'gy', split_axis=0, concat_ax...  8.46 us
    all_to_all x1, waiting for transfers between devices, on_device(): lax.all_to_all(bricks, 'gy', split_axis=0, concat_axis=0, tiled=True)  8.09 us
    ppermute x4, starting transfers between devices, exchange(): lax.ppermute(gx_second, 'gx', outer(8))  7.01 us
    pallas_call x3, Pallas kernels, local_step(): pl.pallas_call(kernel, out_shape=out_shape, in_specs=[VM, next_spec, VM,...  6.66 us
    ppermute x4, starting transfers between devices, exchange(): lax.ppermute(gy_first, 'gy', inner(16))  4.28 us
    all_to_all x1, starting transfers between devices, on_device(): lax.all_to_all(bricks, 'gy', split_axis=0, concat_axis=0, tiled=True)  4.21 us
  transfers between devices with their start and end apart: 18, of which 6 were waited for; matrix products, arithmetic and copies ran while one was open for 0% of the time, Pallas kernels for 18%

profile of v6, /device:TPU:1, one launch (start us, length us, event | category | flops | bytes accessed | tf_op | source)
XLA Modules:
  0.0 79.4 jit_solution(3430443889521306078)
XLA Ops:
  0.6 2.0 %turn_velocity.1 = (f32[2,16,32,128]{3,2,1,0:T(8,128)S(1)}, s16[256,512]{1,0:T(8,128)(2,1)}) custom-call(f32[16,32,256]{2,1,0:T(8,128)} %vel.1), custom_call_target="tpu_custom_call" | custom-call | tf_op jit(solution)/shard_map/turn_velocity/pallas_call | solution.py:313
  2.6 8.5 %all-to-all-start = ((s16[16,16,512]{2,1,0:T(8,128)(2,1)}), s16[16,16,512]{2,1,0:T(8,128)(2,1)S(1)}, u32[]{:S(2)}, u32[]{:S(2)}) async-start(s16[16,16,512]{2,1,0:T(8,128)(2,1)} %bitcast.26), calls=%async_computation | async-start | bytes 524288 | tf_op jit(solution)/shard_map/all_to_all | solution.py:707
  11.1 2.0 %first_halos.1 = (f32[4,16,16,128]{3,2,1,0:T(8,128)S(1)}, bf16[10,16,512]{2,1,0:T(8,128)(2,1)S(1)}, bf16[8,16,512]{2,1,0:T(8,128)(2,1)}, bf16[10,16,512]{2,1,0:T(8,128)(2,1)S(1)}, bf16[8,16,512]{2,1,0:T(8,128)(2,1)S(1)}) custom-call(f32[16,16,512]{2,1,0:T(8,128)} %src.1, f32[16,32,256]{2,1,0:T(8,128)} %rcv.3), custom_call_target="tpu_custom_call" | custom-call | tf_op jit(solution)/shard_map/first_halos/pallas_call | solution.py:334
  13.1 4.0 %collective-permute-start = (bf16[10,16,512]{2,1,0:T(8,128)(2,1)S(1)}, bf16[10,16,512]{2,1,0:T(8,128)(2,1)S(1)}, u32[]{:S(2)}, u32[]{:S(2)}) collective-permute-start(bf16[10,16,512]{2,1,0:T(8,128)(2,1)S(1)} %get-tuple-element.52), channel_id=1, source_target_pairs={{0,112},{16,32},{32,16},{48,64},{64,48},{80,96},{96,80},{112,0},{1... | collective-permute-start | bytes 491528 | tf_op jit(solution)/shard_map/ppermute | solution.py:685
  17.1 0.0 collective-permute-start.2
  17.1 4.0 %collective-permute-start.1 = (bf16[8,16,512]{2,1,0:T(8,128)(2,1)}, bf16[8,16,512]{2,1,0:T(8,128)(2,1)S(1)}, u32[]{:S(2)}, u32[]{:S(2)}) collective-permute-start(bf16[8,16,512]{2,1,0:T(8,128)(2,1)} %get-tuple-element.53), channel_id=1, source_target_pairs={{0,15},{1,2},{2,1},{3,4},{4,3},{5,6},{6,5},{7,8},{8,7},{9,10},{10,... | collective-permute-start | bytes 393224 | tf_op jit(solution)/shard_map/ppermute | solution.py:686
  21.1 2.0 %collective-permute-start.3 = (bf16[8,16,512]{2,1,0:T(8,128)(2,1)S(1)}, bf16[8,16,512]{2,1,0:T(8,128)(2,1)S(1)}, u32[]{:S(2)}, u32[]{:S(2)}) collective-permute-start(bf16[8,16,512]{2,1,0:T(8,128)(2,1)S(1)} %get-tuple-element.55), channel_id=1, source_target_pairs={{0,1},{1,0},{2,3},{3,2},{4,5},{5,4},{6,7},{7,6},{8,9},{9,8},{10,11... | collective-permute-start | bytes 393224 | tf_op jit(solution)/shard_map/ppermute | solution.py:688
  23.1 1.4 %injections.1.inject = f32[32,128]{1,0:T(8,128)S(1)} custom-call(f32[4,4096]{1,0:T(4,128)} %traces_hbm.1, s32[1,4096]{1,0:T(1,128)} %bitcast.27, s32[1,4096]{1,0:T(1,128)} %bitcast.28), custom_call_target="tpu_custom_call" | custom-call | bytes 7200000 | tf_op jit(solution)/shard_map/injections/pallas_call | solution.py:380
  24.5 2.2 %local_first.1 = (f32[4,256,128]{2,1,0:T(8,128)S(1)}, f32[4,256,128]{2,1,0:T(8,128)S(1)}, f32[2,512,128]{2,1,0:T(8,128)S(1)}, f32[4,4,16,128]{3,2,1,0:T(8,128)S(1)}) custom-call(f32[4,256,128]{2,1,0:T(8,128)S(1)} %bitcast.20, f32[256,512]{1,0:T(8,128)} %bitcast.23, f32[16,32,256]{2,1,0:T(8,128)} %rcv.3, f32[512,256]{1,0:T(8,128)} %bitcast.24, ...), custom_call_target="tpu_custom_call" | custom-call | bytes 10800000 | tf_op jit(solution)/shard_map/local_first/pallas_call | solution.py:486
  26.7 0.0 all-to-all-done.pieces
  26.7 0.5 source_velocity.1.refs_3_.vel_src.refs_2_
  27.2 0.6 collective-permute-done.1.refs_6_
  27.8 0.0 collective-permute-done.2.refs_7_
  27.8 1.0 %halo_step0.1 = (f32[4,256,128]{2,1,0:T(8,128)S(1)}, f32[2,512,128]{2,1,0:T(8,128)S(1)}, bf16[10,16,512]{2,1,0:T(8,128)(2,1)S(1)}, bf16[8,16,512]{2,1,0:T(8,128)...) custom-call(f32[4,256,128]{2,1,0:T(8,128)S(1)} %get-tuple-element.48.refs_0_, ...), custom_call_target="tpu_custom_call" | custom-call | tf_op jit(solution)/shard_map/halo_step0/pallas_call | solution.py:595
  28.9 1.4 %collective-permute-start.4 = (bf16[10,16,512]{2,1,0:T(8,128)(2,1)S(1)}, bf16[10,16,512]{2,1,0:T(8,128)(2,1)S(1)}, u32[]{:S(2)}, u32[]{:S(2)}) collective-permute-start(bf16[10,16,512]{2,1,0:T(8,128)(2,1)S(1)} %get-tuple-element.61), channel_id=1, source_target_pairs={{0,112},{16,32},{32,16},{48,64},{64,48},{80,96},{96,80},{112,0},{1... | collective-permute-start | bytes 491528 | tf_op jit(solution)/shard_map/ppermute | solution.py:685
  30.3 0.0 collective-permute-start.6
  30.3 1.7 %collective-permute-start.5 = (bf16[8,16,512]{2,1,0:T(8,128)(2,1)S(1)}, bf16[8,16,512]{2,1,0:T(8,128)(2,1)S(1)}, u32[]{:S(2)}, u32[]{:S(2)}) collective-permute-start(bf16[8,16,512]{2,1,0:T(8,128)(2,1)S(1)} %get-tuple-element.62), channel_id=1, source_target_pairs={{0,15},{1,2},{2,1},{3,4},{4,3},{5,6},{6,5},{7,8},{8,7},{9,10},{10,... | collective-permute-start | bytes 393224 | tf_op jit(solution)/shard_map/ppermute | solution.py:686
  32.0 2.0 %collective-permute-start.7 = (bf16[8,16,512]{2,1,0:T(8,128)(2,1)S(1)}, bf16[8,16,512]{2,1,0:T(8,128)(2,1)S(1)}, u32[]{:S(2)}, u32[]{:S(2)}) collective-permute-start(bf16[8,16,512]{2,1,0:T(8,128)(2,1)S(1)} %get-tuple-element.64), channel_id=1, source_target_pairs={{0,1},{1,0},{2,3},{3,2},{4,5},{5,4},{6,7},{7,6},{8,9},{9,8},{10,11... | collective-permute-start | bytes 393224 | tf_op jit(solution)/shard_map/ppermute | solution.py:688
  34.0 2.5 %local_step1.1 = (f32[4,256,128]{2,1,0:T(8,128)S(1)}, f32[2,512,128]{2,1,0:T(8,128)S(1)}) custom-call(f32[4,256,128]{2,1,0:T(8,128)S(1)} %get-tuple-element.57.src.src_next, f32[256,512]{1,0:T(8,128)} %bitcast.22, f32[2,512,128]{2,1,0:T(8,128)S(1)} %get-tuple-element.58.rcv.rcv_next, f32[512,256]{1,0:T(8,128)} %bitcast.21, ...), custom_call_target="tpu_custom_call" | custom-call | bytes 10800000 | tf_op jit(solution)/shard_map/local_step1/pallas_call | solution.py:544
  36.5 1.7 %collective-permute-done.5.refs_5_ = bf16[8,16,512]{2,1,0:T(8,128)(2,1)S(1)} collective-permute-done((bf16[8,16,512]{2,1,0:T(8,128)(2,1)S(1)}, bf16[8,16,512]{2,1,0:T(8,128)(2,1)S(1)}, u32[]{:S(2)}, u32[]{:S(2)}) %collective-permute-start.5) | collective-permute-done | bytes 131104 | tf_op jit(solution)/shard_map/ppermute | solution.py:686
  38.2 0.0 collective-permute-done.7.refs_7_
  38.2 0.2 collective-permute-done.4.refs_4_
  38.4 0.0 collective-permute-done.6.refs_6_
  38.4 1.0 %halo_step1.1 = (f32[4,256,128]{2,1,0:T(8,128)S(1)}, f32[2,512,128]{2,1,0:T(8,128)S(1)}, bf16[10,16,512]{2,1,0:T(8,128)(2,1)S(1)}, bf16[8,16,512]{2,1,0:T(8,128)...) custom-call(f32[4,256,128]{2,1,0:T(8,128)S(1)} %get-tuple-element.59.refs_0_, ...), custom_call_target="tpu_custom_call" | custom-call | tf_op jit(solution)/shard_map/halo_step1/pallas_call | solution.py:595
  39.4 1.5 %collective-permute-start.8 = (bf16[10,16,512]{2,1,0:T(8,128)(2,1)S(1)}, bf16[10,16,512]{2,1,0:T(8,128)(2,1)S(1)}, u32[]{:S(2)}, u32[]{:S(2)}) collective-permute-start(bf16[10,16,512]{2,1,0:T(8,128)(2,1)S(1)} %get-tuple-element.69), channel_id=1, source_target_pairs={{0,112},{16,32},{32,16},{48,64},{64,48},{80,96},{96,80},{112,0},{1... | collective-permute-start | bytes 491528 | tf_op jit(solution)/shard_map/ppermute | solution.py:685
  40.9 0.0 collective-permute-start.10
  40.9 4.2 %collective-permute-start.9 = (bf16[8,16,512]{2,1,0:T(8,128)(2,1)S(1)}, bf16[8,16,512]{2,1,0:T(8,128)(2,1)S(1)}, u32[]{:S(2)}, u32[]{:S(2)}) collective-permute-start(bf16[8,16,512]{2,1,0:T(8,128)(2,1)S(1)} %get-tuple-element.70), channel_id=1, source_target_pairs={{0,15},{1,2},{2,1},{3,4},{4,3},{5,6},{6,5},{7,8},{8,7},{9,10},{10,... | collective-permute-start | bytes 393224 | tf_op jit(solution)/shard_map/ppermute | solution.py:686
  45.1 0.1 collective-permute-start.11
  45.3 2.1 %local_step2.1 = (f32[4,256,128]{2,1,0:T(8,128)S(1)}, f32[2,512,128]{2,1,0:T(8,128)S(1)}, f32[2,512,128]{2,1,0:T(8,128)}) custom-call(f32[4,256,128]{2,1,0:T(8,128)S(1)} %get-tuple-element.65.src.src_next, f32[4,256,128]{2,1,0:T(8,128)S(1)} %get-tuple-element.57.src.src_next, f32[2,512,128]{2,1,0:T(8,128)S(1)} %get-tuple-element.66.rcv.rcv_next, ...), custom_call_target="tpu_custom_call" | custom-call | bytes 10800000 | tf_op jit(solution)/shard_map/local_step2/pallas_call | solution.py:544
  47.4 3.6 %collective-permute-done.9.refs_5_ = bf16[8,16,512]{2,1,0:T(8,128)(2,1)S(1)} collective-permute-done((bf16[8,16,512]{2,1,0:T(8,128)(2,1)S(1)}, bf16[8,16,512]{2,1,0:T(8,128)(2,1)S(1)}, u32[]{:S(2)}, u32[]{:S(2)}) %collective-permute-start.9) | collective-permute-done | bytes 131104 | tf_op jit(solution)/shard_map/ppermute | solution.py:686
  51.0 0.0 collective-permute-done.8.refs_4_
  51.0 0.0 collective-permute-done.10.refs_6_
  51.0 1.0 %halo_step2.1 = (f32[4,256,128]{2,1,0:T(8,128)S(1)}, f32[2,512,128]{2,1,0:T(8,128)S(1)}, bf16[10,16,512]{2,1,0:T(8,128)(2,1)S(1)}, bf16[8,16,512]{2,1,0:T(8,128)...) custom-call(f32[4,256,128]{2,1,0:T(8,128)S(1)} %get-tuple-element.67.refs_0_, ...), custom_call_target="tpu_custom_call" | custom-call | tf_op jit(solution)/shard_map/halo_step2/pallas_call | solution.py:595
  51.9 0.1 collective-permute-start.12
  52.0 0.1 collective-permute-start.14
  52.2 3.6 %collective-permute-start.13 = (bf16[8,16,512]{2,1,0:T(8,128)(2,1)S(1)}, bf16[8,16,512]{2,1,0:T(8,128)(2,1)S(1)}, u32[]{:S(2)}, u32[]{:S(2)}) collective-permute-start(bf16[8,16,512]{2,1,0:T(8,128)(2,1)S(1)} %get-tuple-element.78), channel_id=1, source_target_pairs={{0,15},{1,2},{2,1},{3,4},{4,3},{5,6},{6,5},{7,8},{8,7},{9,10},{10,... | collective-permute-start | bytes 393224 | tf_op jit(solution)/shard_map/ppermute | solution.py:686
  55.8 0.2 collective-permute-start.15
  55.9 2.1 %local_step3.1 = (f32[4,256,128]{2,1,0:T(8,128)S(1)}, f32[2,512,128]{2,1,0:T(8,128)S(1)}, bf16[16,16,512]{2,1,0:T(8,128)(2,1)S(1)}) custom-call(f32[4,256,128]{2,1,0:T(8,128)S(1)} %get-tuple-element.73.src, f32[4,256,128]{2,1,0:T(8,128)S(1)} %get-tuple-element.65.src.src_next, f32[2,512,128]{2,1,0:T(8,128)S(1)} %get-tuple-element.74.rcv, ...), custom_call_target="tpu_custom_call" | custom-call | bytes 10800000 | tf_op jit(solution)/shard_map/local_step3/pallas_call | solution.py:544
  58.0 3.6 %collective-permute-done.13.refs_1_ = bf16[8,16,512]{2,1,0:T(8,128)(2,1)S(1)} collective-permute-done((bf16[8,16,512]{2,1,0:T(8,128)(2,1)S(1)}, bf16[8,16,512]{2,1,0:T(8,128)(2,1)S(1)}, u32[]{:S(2)}, u32[]{:S(2)}) %collective-permute-start.13) | collective-permute-done | bytes 131104 | tf_op jit(solution)/shard_map/ppermute | solution.py:686
  61.6 0.0 collective-permute-done.15.refs_3_
  61.6 0.0 collective-permute-done.12.refs_0_
  61.6 1.3 %last_source.1 = (f32[4,256,128]{2,1,0:T(8,128)S(1)}, bf16[16,2,16,512]{3,2,1,0:T(8,128)(2,1)}) custom-call(f32[4,256,128]{2,1,0:T(8,128)S(1)} %get-tuple-element.75.local, bf16[16,16,512]{2,1,0:T(8,128)(2,1)S(1)} %get-tuple-element.76.early, f32[4,256,128]{2,1,0:T(8,128)S(1)} %source_velocity.1.refs_3_.vel_src.refs_2_, ...), custom_call_target="tpu_custom_call" | custom-call | tf_op jit(solution)/shard_map/last_source/pallas_call | solution.py:620
  62.9 4.2 %all-to-all-start.1 = ((bf16[16,2,16,512]{3,2,1,0:T(8,128)(2,1)}), bf16[16,2,16,512]{3,2,1,0:T(8,128)(2,1)S(1)}, u32[]{:S(2)}, u32[]{:S(2)}) async-start(bf16[16,2,16,512]{3,2,1,0:T(8,128)(2,1)} %get-tuple-element.81), calls=%async_computation.1 | async-start | bytes 1048576 | tf_op jit(solution)/shard_map/all_to_all | solution.py:728
  67.2 0.9 %copy-done.1 = bf16[8,16,512]{2,1,0:T(8,128)(2,1)S(1)} copy-done((bf16[8,16,512]{2,1,0:T(8,128)(2,1)S(1)}, bf16[8,16,512]{2,1,0:T(8,128)(2,1)}, u32[]{:S(2)}) %copy-start.1) | copy-done | bytes 131096
  68.1 0.9 %copy-done.3 = bf16[8,16,512]{2,1,0:T(8,128)(2,1)S(1)} copy-done((bf16[8,16,512]{2,1,0:T(8,128)(2,1)S(1)}, bf16[8,16,512]{2,1,0:T(8,128)(2,1)}, u32[]{:S(2)}) %copy-start.3) | copy-done | bytes 131096
  69.0 1.2 %last_receiver.1 = (f32[2,512,128]{2,1,0:T(8,128)S(1)}, f32[2,512,128]{2,1,0:T(8,128)S(1)}, f32[256,512]{1,0:T(8,128)}, f32[512,256]{1,0:T(8,128)}) custom-call(f32[2,512,128]{2,1,0:T(8,128)S(1)} %get-tuple-element.82.local, f32[2,512,128]{2,1,0:T(8,128)S(1)} %bitcast.19, bf16[10,16,512]{2,1,0:T(8,128)(2,1)S(1)} %collective-permute-done.12.refs_0_, ...), custom_call_target="tpu_custom_call" | custom-call | bytes 7200000 | tf_op jit(solution)/shard_map/last_receiver/pallas_call | solution.py:643
  70.2 8.1 %all-to-all-done.1.bricks = bf16[16,2,16,512]{3,2,1,0:T(8,128)(2,1)S(1)} async-done(((bf16[16,2,16,512]{3,2,1,0:T(8,128)(2,1)}), bf16[16,2,16,512]{3,2,1,0:T(8,128)(2,1)S(1)}, u32[]{:S(2)}, u32[]{:S(2)}) %all-to-all-start.1) | async-done | bytes 524320 | tf_op jit(solution)/shard_map/all_to_all | solution.py:728
  78.3 0.9 %make_image.1 = f32[512,256]{1,0:T(8,128)} custom-call(bf16[16,2,16,512]{3,2,1,0:T(8,128)(2,1)S(1)} %all-to-all-done.1.bricks, f32[2,512,128]{2,1,0:T(8,128)S(1)} %get-tuple-element.85.rcv_early, f32[2,512,128]{2,1,0:T(8,128)S(1)} %get-tuple-element.86.rcv_late), custom_call_target="tpu_custom_call" | custom-call | tf_op jit(solution)/shard_map/make_image/pallas_call | solution.py:669
  (10 shorter events, 0.0 us)
Async XLA Ops:
  2.6 24.1 %all-to-all-start = ((s16[16,16,512]{2,1,0:T(8,128)(2,1)}), s16[16,16,512]{2,1,0:T(8,128)(2,1)S(1)}, u32[]{:S(2)}, u32[]{:S(2)}) async-start(s16[16,16,512]{2,1,0:T(8,128)(2,1)} %bitcast.26), calls=%async_computation | async-start | bytes 524288 | tf_op jit(solution)/shard_map/all_to_all | solution.py:707
  13.1 14.7 %collective-permute-start = (bf16[10,16,512]{2,1,0:T(8,128)(2,1)S(1)}, bf16[10,16,512]{2,1,0:T(8,128)(2,1)S(1)}, u32[]{:S(2)}, u32[]{:S(2)}) collective-permute-start(bf16[10,16,512]{2,1,0:T(8,128)(2,1)S(1)} %get-tuple-element.52), channel_id=1, source_target_pairs={{0,112},{16,32},{32,16},{48,64},{64,48},{80,96},{96,80},{112,0},{1... | collective-permute-start | bytes 491528 | tf_op jit(solution)/shard_map/ppermute | solution.py:685
  17.1 10.7 %collective-permute-start.2 = (bf16[10,16,512]{2,1,0:T(8,128)(2,1)S(1)}, bf16[10,16,512]{2,1,0:T(8,128)(2,1)S(1)}, u32[]{:S(2)}, u32[]{:S(2)}) collective-permute-start(bf16[10,16,512]{2,1,0:T(8,128)(2,1)S(1)} %get-tuple-element.54), channel_id=1, source_target_pairs={{0,16},{16,0},{32,48},{48,32},{64,80},{80,64},{96,112},{112,96},{1... | collective-permute-start | bytes 491528 | tf_op jit(solution)/shard_map/ppermute | solution.py:687
  17.1 10.7 %collective-permute-start.1 = (bf16[8,16,512]{2,1,0:T(8,128)(2,1)}, bf16[8,16,512]{2,1,0:T(8,128)(2,1)S(1)}, u32[]{:S(2)}, u32[]{:S(2)}) collective-permute-start(bf16[8,16,512]{2,1,0:T(8,128)(2,1)} %get-tuple-element.53), channel_id=1, source_target_pairs={{0,15},{1,2},{2,1},{3,4},{4,3},{5,6},{6,5},{7,8},{8,7},{9,10},{10,... | collective-permute-start | bytes 393224 | tf_op jit(solution)/shard_map/ppermute | solution.py:686
  21.1 6.7 %collective-permute-start.3 = (bf16[8,16,512]{2,1,0:T(8,128)(2,1)S(1)}, bf16[8,16,512]{2,1,0:T(8,128)(2,1)S(1)}, u32[]{:S(2)}, u32[]{:S(2)}) collective-permute-start(bf16[8,16,512]{2,1,0:T(8,128)(2,1)S(1)} %get-tuple-element.55), channel_id=1, source_target_pairs={{0,1},{1,0},{2,3},{3,2},{4,5},{5,4},{6,7},{7,6},{8,9},{9,8},{10,11... | collective-permute-start | bytes 393224 | tf_op jit(solution)/shard_map/ppermute | solution.py:688
  28.9 9.5 %collective-permute-start.4 = (bf16[10,16,512]{2,1,0:T(8,128)(2,1)S(1)}, bf16[10,16,512]{2,1,0:T(8,128)(2,1)S(1)}, u32[]{:S(2)}, u32[]{:S(2)}) collective-permute-start(bf16[10,16,512]{2,1,0:T(8,128)(2,1)S(1)} %get-tuple-element.61), channel_id=1, source_target_pairs={{0,112},{16,32},{32,16},{48,64},{64,48},{80,96},{96,80},{112,0},{1... | collective-permute-start | bytes 491528 | tf_op jit(solution)/shard_map/ppermute | solution.py:685
  30.3 8.1 %collective-permute-start.6 = (bf16[10,16,512]{2,1,0:T(8,128)(2,1)S(1)}, bf16[10,16,512]{2,1,0:T(8,128)(2,1)S(1)}, u32[]{:S(2)}, u32[]{:S(2)}) collective-permute-start(bf16[10,16,512]{2,1,0:T(8,128)(2,1)S(1)} %get-tuple-element.63), channel_id=1, source_target_pairs={{0,16},{16,0},{32,48},{48,32},{64,80},{80,64},{96,112},{112,96},{1... | collective-permute-start | bytes 491528 | tf_op jit(solution)/shard_map/ppermute | solution.py:687
  30.3 7.9 %collective-permute-start.5 = (bf16[8,16,512]{2,1,0:T(8,128)(2,1)S(1)}, bf16[8,16,512]{2,1,0:T(8,128)(2,1)S(1)}, u32[]{:S(2)}, u32[]{:S(2)}) collective-permute-start(bf16[8,16,512]{2,1,0:T(8,128)(2,1)S(1)} %get-tuple-element.62), channel_id=1, source_target_pairs={{0,15},{1,2},{2,1},{3,4},{4,3},{5,6},{6,5},{7,8},{8,7},{9,10},{10,... | collective-permute-start | bytes 393224 | tf_op jit(solution)/shard_map/ppermute | solution.py:686
  32.0 6.2 %collective-permute-start.7 = (bf16[8,16,512]{2,1,0:T(8,128)(2,1)S(1)}, bf16[8,16,512]{2,1,0:T(8,128)(2,1)S(1)}, u32[]{:S(2)}, u32[]{:S(2)}) collective-permute-start(bf16[8,16,512]{2,1,0:T(8,128)(2,1)S(1)} %get-tuple-element.64), channel_id=1, source_target_pairs={{0,1},{1,0},{2,3},{3,2},{4,5},{5,4},{6,7},{7,6},{8,9},{9,8},{10,11... | collective-permute-start | bytes 393224 | tf_op jit(solution)/shard_map/ppermute | solution.py:688
  39.4 11.6 %collective-permute-start.8 = (bf16[10,16,512]{2,1,0:T(8,128)(2,1)S(1)}, bf16[10,16,512]{2,1,0:T(8,128)(2,1)S(1)}, u32[]{:S(2)}, u32[]{:S(2)}) collective-permute-start(bf16[10,16,512]{2,1,0:T(8,128)(2,1)S(1)} %get-tuple-element.69), channel_id=1, source_target_pairs={{0,112},{16,32},{32,16},{48,64},{64,48},{80,96},{96,80},{112,0},{1... | collective-permute-start | bytes 491528 | tf_op jit(solution)/shard_map/ppermute | solution.py:685
  40.9 10.1 %collective-permute-start.10 = (bf16[10,16,512]{2,1,0:T(8,128)(2,1)S(1)}, bf16[10,16,512]{2,1,0:T(8,128)(2,1)S(1)}, u32[]{:S(2)}, u32[]{:S(2)}) collective-permute-start(bf16[10,16,512]{2,1,0:T(8,128)(2,1)S(1)} %get-tuple-element.71), channel_id=1, source_target_pairs={{0,16},{16,0},{32,48},{48,32},{64,80},{80,64},{96,112},{112,96},{1... | collective-permute-start | bytes 491528 | tf_op jit(solution)/shard_map/ppermute | solution.py:687
  40.9 10.1 %collective-permute-start.9 = (bf16[8,16,512]{2,1,0:T(8,128)(2,1)S(1)}, bf16[8,16,512]{2,1,0:T(8,128)(2,1)S(1)}, u32[]{:S(2)}, u32[]{:S(2)}) collective-permute-start(bf16[8,16,512]{2,1,0:T(8,128)(2,1)S(1)} %get-tuple-element.70), channel_id=1, source_target_pairs={{0,15},{1,2},{2,1},{3,4},{4,3},{5,6},{6,5},{7,8},{8,7},{9,10},{10,... | collective-permute-start | bytes 393224 | tf_op jit(solution)/shard_map/ppermute | solution.py:686
  45.1 5.8 %collective-permute-start.11 = (bf16[8,16,512]{2,1,0:T(8,128)(2,1)S(1)}, bf16[8,16,512]{2,1,0:T(8,128)(2,1)S(1)}, u32[]{:S(2)}, u32[]{:S(2)}) collective-permute-start(bf16[8,16,512]{2,1,0:T(8,128)(2,1)S(1)} %get-tuple-element.72), channel_id=1, source_target_pairs={{0,1},{1,0},{2,3},{3,2},{4,5},{5,4},{6,7},{7,6},{8,9},{9,8},{10,11... | collective-permute-start | bytes 393224 | tf_op jit(solution)/shard_map/ppermute | solution.py:688
  51.9 9.7 %collective-permute-start.12 = (bf16[10,16,512]{2,1,0:T(8,128)(2,1)S(1)}, bf16[10,16,512]{2,1,0:T(8,128)(2,1)S(1)}, u32[]{:S(2)}, u32[]{:S(2)}) collective-permute-start(bf16[10,16,512]{2,1,0:T(8,128)(2,1)S(1)} %get-tuple-element.77), channel_id=1, source_target_pairs={{0,112},{16,32},{32,16},{48,64},{64,48},{80,96},{96,80},{112,0},{1... | collective-permute-start | bytes 491528 | tf_op jit(solution)/shard_map/ppermute | solution.py:685
  52.0 9.6 %collective-permute-start.14 = (bf16[10,16,512]{2,1,0:T(8,128)(2,1)S(1)}, bf16[10,16,512]{2,1,0:T(8,128)(2,1)S(1)}, u32[]{:S(2)}, u32[]{:S(2)}) collective-permute-start(bf16[10,16,512]{2,1,0:T(8,128)(2,1)S(1)} %get-tuple-element.79), channel_id=1, source_target_pairs={{0,16},{16,0},{32,48},{48,32},{64,80},{80,64},{96,112},{112,96},{1... | collective-permute-start | bytes 491528 | tf_op jit(solution)/shard_map/ppermute | solution.py:687
  52.2 9.4 %collective-permute-start.13 = (bf16[8,16,512]{2,1,0:T(8,128)(2,1)S(1)}, bf16[8,16,512]{2,1,0:T(8,128)(2,1)S(1)}, u32[]{:S(2)}, u32[]{:S(2)}) collective-permute-start(bf16[8,16,512]{2,1,0:T(8,128)(2,1)S(1)} %get-tuple-element.78), channel_id=1, source_target_pairs={{0,15},{1,2},{2,1},{3,4},{4,3},{5,6},{6,5},{7,8},{8,7},{9,10},{10,... | collective-permute-start | bytes 393224 | tf_op jit(solution)/shard_map/ppermute | solution.py:686
  55.8 5.8 %collective-permute-start.15 = (bf16[8,16,512]{2,1,0:T(8,128)(2,1)S(1)}, bf16[8,16,512]{2,1,0:T(8,128)(2,1)S(1)}, u32[]{:S(2)}, u32[]{:S(2)}) collective-permute-start(bf16[8,16,512]{2,1,0:T(8,128)(2,1)S(1)} %get-tuple-element.80), channel_id=1, source_target_pairs={{0,1},{1,0},{2,3},{3,2},{4,5},{5,4},{6,7},{7,6},{8,9},{9,8},{10,11... | collective-permute-start | bytes 393224 | tf_op jit(solution)/shard_map/ppermute | solution.py:688
  61.6 1.3 %copy-start = (bf16[8,16,512]{2,1,0:T(8,128)(2,1)}, bf16[8,16,512]{2,1,0:T(8,128)(2,1)S(1)}, u32[]{:S(2)}) copy-start(bf16[8,16,512]{2,1,0:T(8,128)(2,1)S(1)} %collective-permute-done.13.refs_1_) | copy-start | bytes 393220
  61.6 1.4 %copy-start.2 = (bf16[8,16,512]{2,1,0:T(8,128)(2,1)}, bf16[8,16,512]{2,1,0:T(8,128)(2,1)S(1)}, u32[]{:S(2)}) copy-start(bf16[8,16,512]{2,1,0:T(8,128)(2,1)S(1)} %collective-permute-done.15.refs_3_) | copy-start | bytes 393220
  62.9 15.3 %all-to-all-start.1 = ((bf16[16,2,16,512]{3,2,1,0:T(8,128)(2,1)}), bf16[16,2,16,512]{3,2,1,0:T(8,128)(2,1)S(1)}, u32[]{:S(2)}, u32[]{:S(2)}) async-start(bf16[16,2,16,512]{3,2,1,0:T(8,128)(2,1)} %get-tuple-element.81), calls=%async_computation.1 | async-start | bytes 1048576 | tf_op jit(solution)/shard_map/all_to_all | solution.py:728
  67.2 0.9 %copy-start.1 = (bf16[8,16,512]{2,1,0:T(8,128)(2,1)S(1)}, bf16[8,16,512]{2,1,0:T(8,128)(2,1)}, u32[]{:S(2)}) copy-start(bf16[8,16,512]{2,1,0:T(8,128)(2,1)} %copy-done) | copy-start | bytes 393220
  68.1 0.9 %copy-start.3 = (bf16[8,16,512]{2,1,0:T(8,128)(2,1)S(1)}, bf16[8,16,512]{2,1,0:T(8,128)(2,1)}, u32[]{:S(2)}) copy-start(bf16[8,16,512]{2,1,0:T(8,128)(2,1)} %copy-done.2) | copy-start | bytes 393220

commit v7 on v6

--- a/solution.py
+++ b/solution.py
@@ -92,10 +92,10 @@
             out[t, rows, :] = out[t, rows, :] + vel[t, rows, :] * term
 
 
-def add_source(out, vel, gx_second, gy_second, gx_first, gy_first):
+def add_source(out, vel, gx_second, gy_second, gx_first, gy_first, columns=range(4)):
     ix, iy = lax.axis_index("gx"), lax.axis_index("gy")
     up_x, up_y = sides()
-    for t in range(4):
+    for t in columns:
         lanes = slice(t * 128, t * 128 + 128)
         planes = lambda buffer: layers_of([buffer[p, :, lanes] for p in range(PLANES)])
         add_layers(
@@ -249,7 +249,7 @@
 
 SRC_COLS = jax.ShapeDtypeStruct((4, 256, 128), F32)
 RCV_COLS = jax.ShapeDtypeStruct((2, 512, 128), F32)
-BRICK = jax.ShapeDtypeStruct((16, 16, 512), BF16)
+BRICKS = (16, 2, 16, 512)
 VM = pl.BlockSpec(memory_space=pltpu.VMEM)
 SM = pl.BlockSpec(memory_space=pltpu.SMEM)
 HB = pl.BlockSpec(memory_space=pltpu.HBM)
@@ -287,8 +287,8 @@
         copy.wait()
 
 
-def turn_velocity(vel):
-    def kernel(vel, cols, turned_out, turned, sems):
+def turn_velocity(vel, src, rcv):
+    def kernel(vel, src, rcv, cols, src_cols, rcv_cols, turned_out, turned, sems):
         pieces = [
             pltpu.make_async_copy(
                 vel.at[pl.ds(q * 4, 4), :, pl.ds(t * 128, 128)], cols.at[t, pl.ds(q * 4, 4), :, :], sems.at[q]
@@ -297,6 +297,8 @@
             for t in range(2)
         ]
         start(pieces)
+        fields = column_copies(src, src_cols, sems.at[5]) + column_copies(rcv, rcv_cols, sems.at[5])
+        start(fields)
         flat_cols = flat(cols)
         outs = []
         for q in range(4):
@@ -309,37 +311,37 @@
             outs.append(pltpu.make_async_copy(turned.at[:, lanes], turned_out.at[:, lanes], sems.at[4]))
             outs[-1].start()
         wait(outs)
+        wait(fields)
 
     return pl.pallas_call(
         kernel,
-        out_shape=[jax.ShapeDtypeStruct((2, 16, 32, 128), F32), pltpu.HBM((256, 512), I16)],
-        in_specs=[HB],
-        out_specs=[VM, HB],
-        scratch_shapes=[pltpu.VMEM((256, 512), I16), pltpu.SemaphoreType.DMA((5,))],
+        out_shape=[
+            jax.ShapeDtypeStruct((2, 16, 32, 128), F32),
+            jax.ShapeDtypeStruct((4, 16, 16, 128), F32),
+            jax.ShapeDtypeStruct((2, 16, 32, 128), F32),
+            pltpu.HBM((256, 512), I16),
+        ],
+        in_specs=[HB] * 3,
+        out_specs=[VM] * 3 + [HB],
+        scratch_shapes=[pltpu.VMEM((256, 512), I16), pltpu.SemaphoreType.DMA((6,))],
         compiler_params=params(),
         name="turn_velocity",
-    )(*in_hbm(vel))
+    )(*in_hbm(vel, src, rcv))
 
 
 def first_halos(src, rcv):
-    def kernel(src, rcv, src_cols, *refs):
-        rcv_cols, sems = refs[4:]
-        get_src, get_rcv = column_copies(src, src_cols, sems.at[0]), column_copies(rcv, rcv_cols, sems.at[1])
-        start(get_src + get_rcv)
-        wait(get_src)
-        pack_source(flat(src_cols), *refs[:4])
-        wait(get_rcv)
-        pack_receiver(flat(rcv_cols), PLANES, *refs[:4])
+    def kernel(src, rcv, *packed):
+        pack_source(src, *packed)
+        pack_receiver(rcv, PLANES, *packed)
 
     return pl.pallas_call(
         kernel,
-        out_shape=[jax.ShapeDtypeStruct((4, 16, 16, 128), F32), *halo_buffers(SRC_PLANES, RCV_PLANES)],
-        in_specs=[HB] * 2,
-        out_specs=[VM] * 5,
-        scratch_shapes=[pltpu.VMEM((2, 16, 32, 128), F32), pltpu.SemaphoreType.DMA((2,))],
+        out_shape=halo_buffers(SRC_PLANES, RCV_PLANES),
+        in_specs=[VM] * 2,
+        out_specs=[VM] * 4,
         compiler_params=params(),
         name="first_halos",
-    )(*in_hbm(src, rcv))
+    )(src, rcv)
 
 
 def source_velocity(pieces):
@@ -353,45 +355,19 @@
     )(pieces)
 
 
-def injections(traces, receiver_x, receiver_y):
-    def kernel(traces_hbm, rx_hbm, ry_hbm, out, traces, rx, ry, sem):
-        inputs = [
-            pltpu.make_async_copy(traces_hbm, traces, sem),
-            pltpu.make_async_copy(rx_hbm, rx, sem),
-            pltpu.make_async_copy(ry_hbm, ry, sem),
-        ]
-        start(inputs)
-        wait(inputs)
-        xs = lax.axis_index("gx") * 16 + lax.broadcasted_iota(jnp.int32, (16, 512), 0)
-        ys = lax.axis_index("gy") * 32 + lax.broadcasted_iota(jnp.int32, (32, 512), 0)
-        total = jnp.zeros((32, 128), F32)
-        for c in range(8):
-            cols = slice(c * 512, c * 512 + 512)
-            at_x = rx[:, cols] == xs
-            at_y = jnp.where(ry[:, cols] == ys, 1.0, 0.0).astype(BF16)
-            weighted = [jnp.where(at_x, traces[s : s + 1, cols], 0.0) for s in range(STEPS)]
-            for part in parts_of(jnp.concatenate(weighted, axis=0)):
-                part = jnp.concatenate([part, jnp.zeros((64, 512), BF16)], axis=0)
-                total = total + lax.dot_general(
-                    at_y, part, (((1,), (1,)), ((), ())), preferred_element_type=F32
-                )
-        out[...] = total
-
-    return pl.pallas_call(
-        kernel,
-        out_shape=jax.ShapeDtypeStruct((32, 128), F32),
-        in_specs=[HB] * 3,
-        out_specs=VM,
-        scratch_shapes=[
-            pltpu.VMEM((4, 4096), F32),
-            pltpu.VMEM((1, 4096), jnp.int32),
-            pltpu.VMEM((1, 4096), jnp.int32),
-            pltpu.SemaphoreType.DMA,
-        ],
-        compiler_params=params(),
-        cost_estimate=hint(2),
-        name="injections",
-    )(*in_hbm(traces, receiver_x.reshape(1, -1), receiver_y.reshape(1, -1)))
+def injections(traces, rx, ry):
+    xs = lax.axis_index("gx") * 16 + lax.broadcasted_iota(jnp.int32, (16, 512), 0)
+    ys = lax.axis_index("gy") * 32 + lax.broadcasted_iota(jnp.int32, (32, 512), 0)
+    total = jnp.zeros((32, 128), F32)
+    for c in range(8):
+        cols = slice(c * 512, c * 512 + 512)
+        at_x = rx[:, cols] == xs
+        at_y = jnp.where(ry[:, cols] == ys, 1.0, 0.0).astype(BF16)
+        weighted = [jnp.where(at_x, traces[s : s + 1, cols], 0.0) for s in range(STEPS)]
+        for part in parts_of(jnp.concatenate(weighted, axis=0)):
+            part = jnp.concatenate([part, jnp.zeros((64, 512), BF16)], axis=0)
+            total = total + lax.dot_general(at_y, part, (((1,), (1,)), ((), ())), preferred_element_type=F32)
+    return total
 
 
 def subtract(cols, block):
@@ -440,21 +416,29 @@
             out[t, at, :] = out[t, at, :] + jnp.where(lanes + t * 128 == cell[1], wavelet[step], 0.0)
 
 
-def local_first(src, src_next, rcv, rcv_next, vel, inject, wavelet, cell, saved, plane_index):
-    def kernel(src, src_next, rcv, rcv_next, vel, inject, wavelet_hbm, cell_hbm, saved, index_hbm, *refs):
-        base, lap, rcv_out, planes, next_src, rcv_cols, next_rcv, wavelet, cell, index, sems = refs
+def local_first(src, src_next, rcv, rcv_next, vel, wavelet, cell, saved, plane_index, traces, receiver_x, receiver_y):
+    def kernel(vel, *refs):
+        hbm, (base, lap, rcv_out, planes, inject), refs = refs[:11], refs[11:16], refs[16:]
+        src, src_next, rcv, rcv_next, wavelet_hbm, cell_hbm, saved, index_hbm, traces_hbm, rx_hbm, ry_hbm = hbm
+        src_cols, next_src, rcv_cols, next_rcv, traces, rx, ry, wavelet, cell, index, sems = refs
         ix, iy = lax.axis_index("gx"), lax.axis_index("gy")
         get_index = pltpu.make_async_copy(index_hbm, index, sems.at[0])
         get_index.start()
+        receivers = [
+            pltpu.make_async_copy(traces_hbm, traces, sems.at[7]),
+            pltpu.make_async_copy(rx_hbm, rx, sems.at[7]),
+            pltpu.make_async_copy(ry_hbm, ry, sems.at[7]),
+        ]
+        get_src, get_rcv = column_copies(src, src_cols, sems.at[5]), column_copies(rcv, rcv_cols, sems.at[6])
         later = [
             pltpu.make_async_copy(wavelet_hbm, wavelet, sems.at[1]),
             pltpu.make_async_copy(cell_hbm, cell, sems.at[2]),
             pltpu.make_async_copy(src_next, next_src, sems.at[3]),
             pltpu.make_async_copy(rcv_next, next_rcv, sems.at[4]),
         ]
-        get_rcv = column_copies(rcv, rcv_cols, sems.at[6])
-        start(get_rcv + later)
-        local_source(src, None, None, base, lap)
+        start(receivers + get_src + get_rcv + later)
+        wait(receivers)
+        inject[...] = injections(traces, rx, ry)
         get_index.wait()
         edge = (ix == 0) | (ix == 7)
         side = jnp.where(ix == 0, 0, 1)
@@ -462,7 +446,7 @@
             pltpu.make_async_copy(
                 saved.at[index[step], side, pl.ds(pl.multiple_of(iy * 16, 16), 16), pl.ds(t * 128, 128)],
                 planes.at[step, t],
-                sems.at[5],
+                sems.at[8],
             )
             for step in range(STEPS)
             for t in range(4)
@@ -472,6 +456,8 @@
         def _():
             start(restores)
 
+        wait(get_src)
+        local_source(flat(src_cols), None, None, base, lap)
         wait(get_rcv)
         local_receiver(0, flat(rcv_cols), None, vel, inject, rcv_out)
         wait(later)
@@ -485,27 +471,46 @@
 
     return pl.pallas_call(
         kernel,
-        out_shape=[SRC_COLS, SRC_COLS, RCV_COLS, jax.ShapeDtypeStruct((STEPS, 4, 16, 128), F32)],
-        in_specs=[VM, HB, HB, HB, VM, VM] + [HB] * 4,
-        out_specs=[VM] * 4,
+        out_shape=[
+            SRC_COLS,
+            SRC_COLS,
+            RCV_COLS,
+            jax.ShapeDtypeStruct((STEPS, 4, 16, 128), F32),
+            jax.ShapeDtypeStruct((32, 128), F32),
+        ],
+        in_specs=[VM] + [HB] * 11,
+        out_specs=[VM] * 5,
         scratch_shapes=[
+            pltpu.VMEM((4, 16, 16, 128), F32),
             pltpu.VMEM((256, 512), F32),
             pltpu.VMEM((2, 16, 32, 128), F32),
             pltpu.VMEM((512, 256), F32),
+            pltpu.VMEM((4, 4096), F32),
+            pltpu.VMEM((1, 4096), jnp.int32),
+            pltpu.VMEM((1, 4096), jnp.int32),
             pltpu.SMEM((4,), F32),
             pltpu.SMEM((3,), jnp.int32),
             pltpu.SMEM((4,), jnp.int32),
-            pltpu.SemaphoreType.DMA((7,)),
+            pltpu.SemaphoreType.DMA((9,)),
         ],
         compiler_params=params(),
-        cost_estimate=hint(3),
+        cost_estimate=hint(4),
         name="local_first",
     )(
-        src,
-        *in_hbm(src_next, rcv, rcv_next),
         vel,
-        inject,
-        *in_hbm(wavelet, cell, saved, plane_index),
+        *in_hbm(
+            src,
+            src_next,
+            rcv,
+            rcv_next,
+            wavelet,
+            cell,
+            saved,
+            plane_index,
+            traces,
+            receiver_x.reshape(1, -1),
+            receiver_y.reshape(1, -1),
+        ),
     )
 
 
@@ -513,7 +518,7 @@
     from_hbm, keep, last = step == 1, step == 2, step == STEPS - 1
 
     def kernel(src, src_next, rcv, rcv_next, vel_src, vel, inject, wavelet_hbm, cell_hbm, src_out, rcv_out, *refs):
-        brick = refs[0] if last else None
+        bricks, brick = (refs[0], refs[1]) if last else (None, None)
         wavelet, cell, next_src, next_rcv, sems = refs[-5:]
         copies = [
             pltpu.make_async_copy(wavelet_hbm, wavelet, sems.at[0]),
@@ -525,10 +530,12 @@
         if keep:
             copies.append(pltpu.make_async_copy(rcv, refs[0], sems.at[2]))
         start(copies)
+        if last:
+            pack_brick(src_next, brick)
+            copies.append(pltpu.make_async_copy(brick, bricks.at[:, 0], sems.at[2]))
+            copies[-1].start()
         local_source(src, None if from_hbm else src_next, vel_src, src_out)
         local_receiver(step, rcv, None if from_hbm else rcv_next, vel, inject, rcv_out)
-        if last:
-            pack_brick(src_next, brick)
         wait(copies)
         if from_hbm:
             subtract(src_out, next_src)
@@ -538,15 +545,18 @@
     if from_hbm:
         src_next, rcv_next = in_hbm(src_next, rcv_next)
     next_spec = HB if from_hbm else VM
-    out_shape = [SRC_COLS, RCV_COLS] + ([BRICK] if last else [])
+    out_shape = [SRC_COLS, RCV_COLS]
     if keep:
         out_shape.append(pltpu.HBM(RCV_COLS.shape, F32))
+    if last:
+        out_shape.append(pltpu.HBM(BRICKS, BF16))
     return pl.pallas_call(
         kernel,
         out_shape=out_shape,
         in_specs=[VM, next_spec, VM, next_spec] + [VM] * 3 + [HB] * 2,
-        out_specs=[VM, VM] + [HB if keep else VM] * (len(out_shape) - 2),
-        scratch_shapes=[
+        out_specs=[VM, VM] + [HB] * (len(out_shape) - 2),
+        scratch_shapes=([pltpu.VMEM((16, 16, 512), BF16)] if last else [])
+        + [
             pltpu.SMEM((4,), F32),
             pltpu.SMEM((3,), jnp.int32),
             pltpu.VMEM((256, 512) if from_hbm else (8, 128), F32),
@@ -559,17 +569,17 @@
     )(src, src_next, rcv, rcv_next, vel_src, vel, inject, *in_hbm(wavelet, cell))
 
 
-def restore_planes(step, src, planes):
+def restore_planes(step, src, planes, columns=range(4)):
     ix = lax.axis_index("gx")
 
     @pl.when(ix == 0)
     def _():
-        for t in range(4):
+        for t in columns:
             src[t, pl.ds(0, 16, stride=16), :] = planes[step, t]
 
     @pl.when(ix == 7)
     def _():
-        for t in range(4):
+        for t in columns:
             src[t, pl.ds(15, 16, stride=16), :] = planes[step, t]
 
 
@@ -602,30 +612,30 @@
     )(*args)
 
 
-def last_source(local, early, vel_src, halos, planes):
-    def kernel(local, early, vel_src, *refs):
-        halos, planes, src, bricks, late, sems = refs[:4], *refs[4:]
-        copies = [pltpu.make_async_copy(early, bricks.at[:, 0], sems.at[0])]
-        copies[0].start()
+def last_source(local, bricks, vel_src, halos, planes):
+    def kernel(local, _, vel_src, *refs):
+        halos, planes, src, bricks, late, sem = refs[:4], *refs[4:]
+        copies = []
         src[...] = local[...]
         add_source(src, vel_src, *halos)
         restore_planes(STEPS - 1, src, planes)
         for t in range(4):
             pack_brick(src, late, (t,))
             part = pl.ds(t * 4, 4)
-            copies.append(pltpu.make_async_copy(late.at[part], bricks.at[part, 1], sems.at[1]))
+            copies.append(pltpu.make_async_copy(late.at[part], bricks.at[part, 1], sem))
             copies[-1].start()
         wait(copies)
 
     return pl.pallas_call(
         kernel,
-        out_shape=[SRC_COLS, pltpu.HBM((16, 2, 16, 512), BF16)],
-        in_specs=[VM] * 8,
+        out_shape=[SRC_COLS, pltpu.HBM(BRICKS, BF16)],
+        in_specs=[VM, HB] + [VM] * 6,
         out_specs=[VM, HB],
-        scratch_shapes=[pltpu.VMEM((16, 16, 512), BF16), pltpu.SemaphoreType.DMA((2,))],
+        input_output_aliases={1: 1},
+        scratch_shapes=[pltpu.VMEM((16, 16, 512), BF16), pltpu.SemaphoreType.DMA],
         compiler_params=params(),
         name="last_source",
-    )(local, early, vel_src, *halos, planes)
+    )(local, *in_hbm(bricks), vel_src, *halos, planes)
 
 
 def last_receiver(local, vel, halos, src, kept):
@@ -703,15 +713,23 @@
     receiver_x,
     receiver_y,
 ):
-    vel, turned = turn_velocity(velocity)
+    vel, src, rcv, turned = turn_velocity(velocity, source_now, receiver_now)
     pieces = lax.all_to_all(turned.reshape(16, 16, 512), "gy", split_axis=0, concat_axis=0, tiled=True)
-    src, *to_send = first_halos(source_now, receiver_now)
-    halos = exchange(to_send)
-    src, vel = src.reshape(4, 256, 128), vel.reshape(2, 512, 128)
-    inject = injections(traces, receiver_x, receiver_y)
-    src_next, rcv_next = source_next.reshape(256, 512), receiver_next.reshape(512, 256)
-    *local, planes = local_first(
-        src, src_next, receiver_now, rcv_next, vel, inject, wavelet, source_cell, saved_planes, plane_index
+    src, rcv, vel = (x.reshape(x.shape[0], -1, 128) for x in (src, rcv, vel))
+    halos = exchange(first_halos(src, rcv))
+    *local, planes, inject = local_first(
+        source_now,
+        source_next.reshape(256, 512),
+        receiver_now,
+        receiver_next.reshape(512, 256),
+        vel,
+        wavelet,
+        source_cell,
+        saved_planes,
+        plane_index,
+        traces,
+        receiver_x,
+        receiver_y,
     )
     vel_src = source_velocity(pieces)
     src_next, rcv_next = source_now.reshape(256, 512), receiver_now.reshape(512, 256)

time: 79.9 us -> 78.8 us (0.986)
    pallas_call x3 -> x2, Pallas kernels: 4.77 us -> 2.16 us  [the longest x1 1.3 us: last_source(): pl.pallas_call(kernel, out_shape=[SRC_COLS, pltpu.HBM(BRICKS, BF16)], in_...]
    pallas_call x1, Pallas kernels: 2.2 us -> 4.05 us  [local_first(): pl.pallas_call(kernel, out_shape=[SRC_COLS, SRC_COLS, RCV_COLS, jax.Shape...]
    ppermute x4, waiting for transfers between devices: 9.47 us -> 7.74 us  [exchange(): lax.ppermute(gy_second, 'gy', outer(16))]
    ppermute x4, waiting for transfers between devices: 0.23 us -> 1.5 us  [exchange(): lax.ppermute(gx_second, 'gx', outer(8))]
  transfers between devices with their start and end apart: 18 -> 18, of which waited for: 6 -> 6; matrix products, arithmetic and copies ran while one was open for 0% -> 0% of each run, Pallas kernels for 18% -> 17%
where the time goes in v7:
time: 78.8 us; the launch traced here: 78.4 us
  starting transfers between devices  37.8 us (48%)
  Pallas kernels  20.5 us (26%)
  waiting for transfers between devices  17.3 us (22%)
  local copies, waits for them, and re-layouts  1.81 us (2%)
  between operations  0.96 us (1%)
    ppermute x4, starting transfers between devices, exchange(): lax.ppermute(gy_second, 'gy', outer(16))  12.8 us
    all_to_all x1, starting transfers between devices, on_device(): lax.all_to_all(turned.reshape(16, 16, 512), 'gy', split_axis=0, concat_ax...  8.46 us
    all_to_all x1, waiting for transfers between devices, on_device(): lax.all_to_all(bricks, 'gy', split_axis=0, concat_axis=0, tiled=True)  8.09 us
    ppermute x4, starting transfers between devices, exchange(): lax.ppermute(gx_second, 'gx', outer(8))  7.76 us
    ppermute x4, waiting for transfers between devices, exchange(): lax.ppermute(gy_second, 'gy', outer(16))  7.74 us
    pallas_call x3, Pallas kernels, local_step(): pl.pallas_call(kernel, out_shape=out_shape, in_specs=[VM, next_spec, VM,...  6.76 us
    all_to_all x1, starting transfers between devices, on_device(): lax.all_to_all(bricks, 'gy', split_axis=0, concat_axis=0, tiled=True)  4.51 us
    ppermute x4, starting transfers between devices, exchange(): lax.ppermute(gy_first, 'gy', inner(16))  4.12 us
  transfers between devices with their start and end apart: 18, of which 6 were waited for; matrix products, arithmetic and copies ran while one was open for 0% of the time, Pallas kernels for 17%

profile of v7, /device:TPU:1, one launch (start us, length us, event | category | flops | bytes accessed | tf_op | source)
XLA Modules:
  0.0 78.4 jit_solution(13831847228463953774)
XLA Ops:
  0.6 2.0 %turn_velocity.1 = (f32[2,16,32,128]{3,2,1,0:T(8,128)S(1)}, f32[4,16,16,128]{3,2,1,0:T(8,128)S(1)}, f32[2,16,32,128]{3,2,1,0:T(8,128)S(1)}, s16[256,512]{1,0:T(8,128)(2,1)}) custom-call(f32[16,32,256]{2,1,0:T(8,128)} %vel.1, f32[16,16,512]{2,1,0:T(8,128)} %refs_0_.1, f32[16,32,256]{2,1,0:T(8,128)} %refs_2_.1), custom_call_target="tpu_custom_call" | custom-call | tf_op jit(solution)/shard_map/turn_velocity/pallas_call | solution.py:316
  2.6 8.5 %all-to-all-start = ((s16[16,16,512]{2,1,0:T(8,128)(2,1)}), s16[16,16,512]{2,1,0:T(8,128)(2,1)S(1)}, u32[]{:S(2)}, u32[]{:S(2)}) async-start(s16[16,16,512]{2,1,0:T(8,128)(2,1)} %bitcast.28), calls=%async_computation | async-start | bytes 524288 | tf_op jit(solution)/shard_map/all_to_all | solution.py:717
  11.1 0.9 %first_halos.1 = (bf16[10,16,512]{2,1,0:T(8,128)(2,1)S(1)}, bf16[8,16,512]{2,1,0:T(8,128)(2,1)}, bf16[10,16,512]{2,1,0:T(8,128)(2,1)S(1)}, bf16[8,16,512]{2,1,0:T(8,128)(2,1)S(1)}) custom-call(f32[4,256,128]{2,1,0:T(8,128)S(1)} %bitcast.21, f32[2,512,128]{2,1,0:T(8,128)S(1)} %bitcast.22), custom_call_target="tpu_custom_call" | custom-call | tf_op jit(solution)/shard_map/first_halos/pallas_call | solution.py:337
  11.9 3.9 %collective-permute-start = (bf16[10,16,512]{2,1,0:T(8,128)(2,1)S(1)}, bf16[10,16,512]{2,1,0:T(8,128)(2,1)S(1)}, u32[]{:S(2)}, u32[]{:S(2)}) collective-permute-start(bf16[10,16,512]{2,1,0:T(8,128)(2,1)S(1)} %get-tuple-element.55), channel_id=1, source_target_pairs={{0,112},{16,32},{32,16},{48,64},{64,48},{80,96},{96,80},{112,0},{1... | collective-permute-start | bytes 491528 | tf_op jit(solution)/shard_map/ppermute | solution.py:695
  15.8 0.0 collective-permute-start.2
  15.8 4.0 %collective-permute-start.1 = (bf16[8,16,512]{2,1,0:T(8,128)(2,1)}, bf16[8,16,512]{2,1,0:T(8,128)(2,1)S(1)}, u32[]{:S(2)}, u32[]{:S(2)}) collective-permute-start(bf16[8,16,512]{2,1,0:T(8,128)(2,1)} %get-tuple-element.56), channel_id=1, source_target_pairs={{0,15},{1,2},{2,1},{3,4},{4,3},{5,6},{6,5},{7,8},{8,7},{9,10},{10,... | collective-permute-start | bytes 393224 | tf_op jit(solution)/shard_map/ppermute | solution.py:696
  19.8 2.0 %collective-permute-start.3 = (bf16[8,16,512]{2,1,0:T(8,128)(2,1)S(1)}, bf16[8,16,512]{2,1,0:T(8,128)(2,1)S(1)}, u32[]{:S(2)}, u32[]{:S(2)}) collective-permute-start(bf16[8,16,512]{2,1,0:T(8,128)(2,1)S(1)} %get-tuple-element.58), channel_id=1, source_target_pairs={{0,1},{1,0},{2,3},{3,2},{4,5},{5,4},{6,7},{7,6},{8,9},{9,8},{10,11... | collective-permute-start | bytes 393224 | tf_op jit(solution)/shard_map/ppermute | solution.py:698
  21.8 4.0 %local_first.1 = (f32[4,256,128]{2,1,0:T(8,128)S(1)}, f32[4,256,128]{2,1,0:T(8,128)S(1)}, f32[2,512,128]{2,1,0:T(8,128)S(1)}, f32[4,4,16,128]{3,2,1,0:T(8,128)S(1)}, f32[32,128]{1,0:T(8,128)S(1)}) custom-call(f32[2,512,128]{2,1,0:T(8,128)S(1)} %bitcast.13, f32[16,16,512]{2,1,0:T(8,128)} %refs_0_.1, f32[256,512]{1,0:T(8,128)} %bitcast.25, ...), custom_call_target="tpu_custom_call" | custom-call | bytes 14400000 | tf_op jit(solution)/shard_map/local_first/pallas_call | solution.py:472
  25.9 0.0 all-to-all-done.pieces
  25.9 0.5 source_velocity.1.refs_3_.vel_src.refs_2_
  26.4 0.2 collective-permute-done.1.refs_6_
  26.6 0.0 collective-permute-done.3.refs_8_
  26.6 0.0 collective-permute-done.refs_5_
  26.6 0.0 collective-permute-done.2.refs_7_
  26.6 1.0 %halo_step0.1 = (f32[4,256,128]{2,1,0:T(8,128)S(1)}, f32[2,512,128]{2,1,0:T(8,128)S(1)}, bf16[10,16,512]{2,1,0:T(8,128)(2,1)S(1)}, bf16[8,16,512]{2,1,0:T(8,128)...) custom-call(f32[4,256,128]{2,1,0:T(8,128)S(1)} %get-tuple-element.49.refs_0_, ...), custom_call_target="tpu_custom_call" | custom-call | tf_op jit(solution)/shard_map/halo_step0/pallas_call | solution.py:605
  27.6 1.8 %collective-permute-start.4 = (bf16[10,16,512]{2,1,0:T(8,128)(2,1)S(1)}, bf16[10,16,512]{2,1,0:T(8,128)(2,1)S(1)}, u32[]{:S(2)}, u32[]{:S(2)}) collective-permute-start(bf16[10,16,512]{2,1,0:T(8,128)(2,1)S(1)} %get-tuple-element.65), channel_id=1, source_target_pairs={{0,112},{16,32},{32,16},{48,64},{64,48},{80,96},{96,80},{112,0},{1... | collective-permute-start | bytes 491528 | tf_op jit(solution)/shard_map/ppermute | solution.py:695
  29.4 0.0 collective-permute-start.6
  29.4 1.4 %collective-permute-start.5 = (bf16[8,16,512]{2,1,0:T(8,128)(2,1)S(1)}, bf16[8,16,512]{2,1,0:T(8,128)(2,1)S(1)}, u32[]{:S(2)}, u32[]{:S(2)}) collective-permute-start(bf16[8,16,512]{2,1,0:T(8,128)(2,1)S(1)} %get-tuple-element.66), channel_id=1, source_target_pairs={{0,15},{1,2},{2,1},{3,4},{4,3},{5,6},{6,5},{7,8},{8,7},{9,10},{10,... | collective-permute-start | bytes 393224 | tf_op jit(solution)/shard_map/ppermute | solution.py:696
  30.8 1.9 %collective-permute-start.7 = (bf16[8,16,512]{2,1,0:T(8,128)(2,1)S(1)}, bf16[8,16,512]{2,1,0:T(8,128)(2,1)S(1)}, u32[]{:S(2)}, u32[]{:S(2)}) collective-permute-start(bf16[8,16,512]{2,1,0:T(8,128)(2,1)S(1)} %get-tuple-element.68), channel_id=1, source_target_pairs={{0,1},{1,0},{2,3},{3,2},{4,5},{5,4},{6,7},{7,6},{8,9},{9,8},{10,11... | collective-permute-start | bytes 393224 | tf_op jit(solution)/shard_map/ppermute | solution.py:698
  32.7 2.5 %local_step1.1 = (f32[4,256,128]{2,1,0:T(8,128)S(1)}, f32[2,512,128]{2,1,0:T(8,128)S(1)}) custom-call(f32[4,256,128]{2,1,0:T(8,128)S(1)} %get-tuple-element.60.src.src_next, f32[256,512]{1,0:T(8,128)} %bitcast.23, f32[2,512,128]{2,1,0:T(8,128)S(1)} %get-tuple-element.61.rcv.rcv_next, f32[512,256]{1,0:T(8,128)} %bitcast.24, ...), custom_call_target="tpu_custom_call" | custom-call | bytes 10800000 | tf_op jit(solution)/shard_map/local_step1/pallas_call | solution.py:553
  35.2 0.4 collective-permute-done.5.refs_5_
  35.6 0.0 collective-permute-done.7.refs_7_
  35.6 1.5 %collective-permute-done.4.refs_4_ = bf16[10,16,512]{2,1,0:T(8,128)(2,1)S(1)} collective-permute-done((bf16[10,16,512]{2,1,0:T(8,128)(2,1)S(1)}, bf16[10,16,512]{2,1,0:T(8,128)(2,1)S(1)}, u32[]{:S(2)}, u32[]{:S(2)}) %collective-permute-start.4) | collective-permute-done | bytes 163872 | tf_op jit(solution)/shard_map/ppermute | solution.py:695
  37.1 0.0 collective-permute-done.6.refs_6_
  37.1 1.0 %halo_step1.1 = (f32[4,256,128]{2,1,0:T(8,128)S(1)}, f32[2,512,128]{2,1,0:T(8,128)S(1)}, bf16[10,16,512]{2,1,0:T(8,128)(2,1)S(1)}, bf16[8,16,512]{2,1,0:T(8,128)...) custom-call(f32[4,256,128]{2,1,0:T(8,128)S(1)} %get-tuple-element.63.refs_0_, ...), custom_call_target="tpu_custom_call" | custom-call | tf_op jit(solution)/shard_map/halo_step1/pallas_call | solution.py:605
  38.1 2.0 %collective-permute-start.8 = (bf16[10,16,512]{2,1,0:T(8,128)(2,1)S(1)}, bf16[10,16,512]{2,1,0:T(8,128)(2,1)S(1)}, u32[]{:S(2)}, u32[]{:S(2)}) collective-permute-start(bf16[10,16,512]{2,1,0:T(8,128)(2,1)S(1)} %get-tuple-element.73), channel_id=1, source_target_pairs={{0,112},{16,32},{32,16},{48,64},{64,48},{80,96},{96,80},{112,0},{1... | collective-permute-start | bytes 491528 | tf_op jit(solution)/shard_map/ppermute | solution.py:695
  40.0 0.0 collective-permute-start.10
  40.0 4.0 %collective-permute-start.9 = (bf16[8,16,512]{2,1,0:T(8,128)(2,1)S(1)}, bf16[8,16,512]{2,1,0:T(8,128)(2,1)S(1)}, u32[]{:S(2)}, u32[]{:S(2)}) collective-permute-start(bf16[8,16,512]{2,1,0:T(8,128)(2,1)S(1)} %get-tuple-element.74), channel_id=1, source_target_pairs={{0,15},{1,2},{2,1},{3,4},{4,3},{5,6},{6,5},{7,8},{8,7},{9,10},{10,... | collective-permute-start | bytes 393224 | tf_op jit(solution)/shard_map/ppermute | solution.py:696
  44.0 0.0 collective-permute-start.11
  44.0 2.1 %local_step2.1 = (f32[4,256,128]{2,1,0:T(8,128)S(1)}, f32[2,512,128]{2,1,0:T(8,128)S(1)}, f32[2,512,128]{2,1,0:T(8,128)}) custom-call(f32[4,256,128]{2,1,0:T(8,128)S(1)} %get-tuple-element.69.src.src_next, f32[4,256,128]{2,1,0:T(8,128)S(1)} %get-tuple-element.60.src.src_next, f32[2,512,128]{2,1,0:T(8,128)S(1)} %get-tuple-element.70.rcv.rcv_next, ...), custom_call_target="tpu_custom_call" | custom-call | bytes 10800000 | tf_op jit(solution)/shard_map/local_step2/pallas_call | solution.py:553
  46.1 3.7 %collective-permute-done.9.refs_5_ = bf16[8,16,512]{2,1,0:T(8,128)(2,1)S(1)} collective-permute-done((bf16[8,16,512]{2,1,0:T(8,128)(2,1)S(1)}, bf16[8,16,512]{2,1,0:T(8,128)(2,1)S(1)}, u32[]{:S(2)}, u32[]{:S(2)}) %collective-permute-start.9) | collective-permute-done | bytes 131104 | tf_op jit(solution)/shard_map/ppermute | solution.py:696
  49.8 0.0 collective-permute-done.11.refs_7_
  49.8 1.0 %halo_step2.1 = (f32[4,256,128]{2,1,0:T(8,128)S(1)}, f32[2,512,128]{2,1,0:T(8,128)S(1)}, bf16[10,16,512]{2,1,0:T(8,128)(2,1)S(1)}, bf16[8,16,512]{2,1,0:T(8,128)...) custom-call(f32[4,256,128]{2,1,0:T(8,128)S(1)} %get-tuple-element.71.refs_0_, ...), custom_call_target="tpu_custom_call" | custom-call | tf_op jit(solution)/shard_map/halo_step2/pallas_call | solution.py:605
  50.8 0.1 collective-permute-start.12
  50.9 0.1 collective-permute-start.14
  51.0 3.5 %collective-permute-start.13 = (bf16[8,16,512]{2,1,0:T(8,128)(2,1)S(1)}, bf16[8,16,512]{2,1,0:T(8,128)(2,1)S(1)}, u32[]{:S(2)}, u32[]{:S(2)}) collective-permute-start(bf16[8,16,512]{2,1,0:T(8,128)(2,1)S(1)} %get-tuple-element.82), channel_id=1, source_target_pairs={{0,15},{1,2},{2,1},{3,4},{4,3},{5,6},{6,5},{7,8},{8,7},{9,10},{10,... | collective-permute-start | bytes 393224 | tf_op jit(solution)/shard_map/ppermute | solution.py:696
  54.5 0.2 collective-permute-start.15
  54.7 2.2 %local_step3.1 = (f32[4,256,128]{2,1,0:T(8,128)S(1)}, f32[2,512,128]{2,1,0:T(8,128)S(1)}, bf16[16,2,16,512]{3,2,1,0:T(8,128)(2,1)}) custom-call(f32[4,256,128]{2,1,0:T(8,128)S(1)} %get-tuple-element.77.src, f32[4,256,128]{2,1,0:T(8,128)S(1)} %get-tuple-element.69.src.src_next, f32[2,512,128]{2,1,0:T(8,128)S(1)} %get-tuple-element.78.rcv, ...), custom_call_target="tpu_custom_call" | custom-call | bytes 10800000 | tf_op jit(solution)/shard_map/local_step3/pallas_call | solution.py:553
  56.9 3.4 %collective-permute-done.13.refs_1_ = bf16[8,16,512]{2,1,0:T(8,128)(2,1)S(1)} collective-permute-done((bf16[8,16,512]{2,1,0:T(8,128)(2,1)S(1)}, bf16[8,16,512]{2,1,0:T(8,128)(2,1)S(1)}, u32[]{:S(2)}, u32[]{:S(2)}) %collective-permute-start.13) | collective-permute-done | bytes 131104 | tf_op jit(solution)/shard_map/ppermute | solution.py:696
  60.3 0.0 collective-permute-done.15.refs_3_
  60.3 0.0 collective-permute-done.14.refs_2_
  60.3 1.3 %last_source.1 = (f32[4,256,128]{2,1,0:T(8,128)S(1)}, bf16[16,2,16,512]{3,2,1,0:T(8,128)(2,1)}) custom-call(f32[4,256,128]{2,1,0:T(8,128)S(1)} %get-tuple-element.79.local, bf16[16,2,16,512]{3,2,1,0:T(8,128)(2,1)} %get-tuple-element.80._, f32[4,256,128]{2,1,0:T(8,128)S(1)} %source_velocity.1.refs_3_.vel_src.refs_2_, ...), custom_call_target="tpu_custom_call", output_to_operand_aliasing={{1}: (1, {})} | custom-call | tf_op jit(solution)/shard_map/last_source/pallas_call | solution.py:629
  61.7 4.5 %all-to-all-start.1 = ((bf16[16,2,16,512]{3,2,1,0:T(8,128)(2,1)}), bf16[16,2,16,512]{3,2,1,0:T(8,128)(2,1)S(1)}, u32[]{:S(2)}, u32[]{:S(2)}) async-start(bf16[16,2,16,512]{3,2,1,0:T(8,128)(2,1)} %get-tuple-element.85), calls=%async_computation.1 | async-start | bytes 1048576 | tf_op jit(solution)/shard_map/all_to_all | solution.py:746
  66.2 0.9 %copy-done.1 = bf16[8,16,512]{2,1,0:T(8,128)(2,1)S(1)} copy-done((bf16[8,16,512]{2,1,0:T(8,128)(2,1)S(1)}, bf16[8,16,512]{2,1,0:T(8,128)(2,1)}, u32[]{:S(2)}) %copy-start.1) | copy-done | bytes 131096
  67.1 0.9 %copy-done.3 = bf16[8,16,512]{2,1,0:T(8,128)(2,1)S(1)} copy-done((bf16[8,16,512]{2,1,0:T(8,128)(2,1)S(1)}, bf16[8,16,512]{2,1,0:T(8,128)(2,1)}, u32[]{:S(2)}) %copy-start.3) | copy-done | bytes 131096
  68.0 1.2 %last_receiver.1 = (f32[2,512,128]{2,1,0:T(8,128)S(1)}, f32[2,512,128]{2,1,0:T(8,128)S(1)}, f32[256,512]{1,0:T(8,128)}, f32[512,256]{1,0:T(8,128)}) custom-call(f32[2,512,128]{2,1,0:T(8,128)S(1)} %get-tuple-element.86.local, f32[2,512,128]{2,1,0:T(8,128)S(1)} %bitcast.20, bf16[10,16,512]{2,1,0:T(8,128)(2,1)S(1)} %collective-permute-done.12.refs_0_, ...), custom_call_target="tpu_custom_call" | custom-call | bytes 7200000 | tf_op jit(solution)/shard_map/last_receiver/pallas_call | solution.py:653
  69.2 8.1 %all-to-all-done.1.bricks = bf16[16,2,16,512]{3,2,1,0:T(8,128)(2,1)S(1)} async-done(((bf16[16,2,16,512]{3,2,1,0:T(8,128)(2,1)}), bf16[16,2,16,512]{3,2,1,0:T(8,128)(2,1)S(1)}, u32[]{:S(2)}, u32[]{:S(2)}) %all-to-all-start.1) | async-done | bytes 524320 | tf_op jit(solution)/shard_map/all_to_all | solution.py:746
  77.3 0.9 %make_image.1 = f32[512,256]{1,0:T(8,128)} custom-call(bf16[16,2,16,512]{3,2,1,0:T(8,128)(2,1)S(1)} %all-to-all-done.1.bricks, f32[2,512,128]{2,1,0:T(8,128)S(1)} %get-tuple-element.89.rcv_early, f32[2,512,128]{2,1,0:T(8,128)S(1)} %get-tuple-element.90.rcv_late), custom_call_target="tpu_custom_call" | custom-call | tf_op jit(solution)/shard_map/make_image/pallas_call | solution.py:679
  (9 shorter events, 0.0 us)
Async XLA Ops:
  2.6 23.3 %all-to-all-start = ((s16[16,16,512]{2,1,0:T(8,128)(2,1)}), s16[16,16,512]{2,1,0:T(8,128)(2,1)S(1)}, u32[]{:S(2)}, u32[]{:S(2)}) async-start(s16[16,16,512]{2,1,0:T(8,128)(2,1)} %bitcast.28), calls=%async_computation | async-start | bytes 524288 | tf_op jit(solution)/shard_map/all_to_all | solution.py:717
  11.9 14.6 %collective-permute-start = (bf16[10,16,512]{2,1,0:T(8,128)(2,1)S(1)}, bf16[10,16,512]{2,1,0:T(8,128)(2,1)S(1)}, u32[]{:S(2)}, u32[]{:S(2)}) collective-permute-start(bf16[10,16,512]{2,1,0:T(8,128)(2,1)S(1)} %get-tuple-element.55), channel_id=1, source_target_pairs={{0,112},{16,32},{32,16},{48,64},{64,48},{80,96},{96,80},{112,0},{1... | collective-permute-start | bytes 491528 | tf_op jit(solution)/shard_map/ppermute | solution.py:695
  15.8 10.7 %collective-permute-start.2 = (bf16[10,16,512]{2,1,0:T(8,128)(2,1)S(1)}, bf16[10,16,512]{2,1,0:T(8,128)(2,1)S(1)}, u32[]{:S(2)}, u32[]{:S(2)}) collective-permute-start(bf16[10,16,512]{2,1,0:T(8,128)(2,1)S(1)} %get-tuple-element.57), channel_id=1, source_target_pairs={{0,16},{16,0},{32,48},{48,32},{64,80},{80,64},{96,112},{112,96},{1... | collective-permute-start | bytes 491528 | tf_op jit(solution)/shard_map/ppermute | solution.py:697
  15.8 10.7 %collective-permute-start.1 = (bf16[8,16,512]{2,1,0:T(8,128)(2,1)}, bf16[8,16,512]{2,1,0:T(8,128)(2,1)S(1)}, u32[]{:S(2)}, u32[]{:S(2)}) collective-permute-start(bf16[8,16,512]{2,1,0:T(8,128)(2,1)} %get-tuple-element.56), channel_id=1, source_target_pairs={{0,15},{1,2},{2,1},{3,4},{4,3},{5,6},{6,5},{7,8},{8,7},{9,10},{10,... | collective-permute-start | bytes 393224 | tf_op jit(solution)/shard_map/ppermute | solution.py:696
  19.8 6.7 %collective-permute-start.3 = (bf16[8,16,512]{2,1,0:T(8,128)(2,1)S(1)}, bf16[8,16,512]{2,1,0:T(8,128)(2,1)S(1)}, u32[]{:S(2)}, u32[]{:S(2)}) collective-permute-start(bf16[8,16,512]{2,1,0:T(8,128)(2,1)S(1)} %get-tuple-element.58), channel_id=1, source_target_pairs={{0,1},{1,0},{2,3},{3,2},{4,5},{5,4},{6,7},{7,6},{8,9},{9,8},{10,11... | collective-permute-start | bytes 393224 | tf_op jit(solution)/shard_map/ppermute | solution.py:698
  27.6 9.5 %collective-permute-start.4 = (bf16[10,16,512]{2,1,0:T(8,128)(2,1)S(1)}, bf16[10,16,512]{2,1,0:T(8,128)(2,1)S(1)}, u32[]{:S(2)}, u32[]{:S(2)}) collective-permute-start(bf16[10,16,512]{2,1,0:T(8,128)(2,1)S(1)} %get-tuple-element.65), channel_id=1, source_target_pairs={{0,112},{16,32},{32,16},{48,64},{64,48},{80,96},{96,80},{112,0},{1... | collective-permute-start | bytes 491528 | tf_op jit(solution)/shard_map/ppermute | solution.py:695
  29.4 7.7 %collective-permute-start.6 = (bf16[10,16,512]{2,1,0:T(8,128)(2,1)S(1)}, bf16[10,16,512]{2,1,0:T(8,128)(2,1)S(1)}, u32[]{:S(2)}, u32[]{:S(2)}) collective-permute-start(bf16[10,16,512]{2,1,0:T(8,128)(2,1)S(1)} %get-tuple-element.67), channel_id=1, source_target_pairs={{0,16},{16,0},{32,48},{48,32},{64,80},{80,64},{96,112},{112,96},{1... | collective-permute-start | bytes 491528 | tf_op jit(solution)/shard_map/ppermute | solution.py:697
  29.4 6.2 %collective-permute-start.5 = (bf16[8,16,512]{2,1,0:T(8,128)(2,1)S(1)}, bf16[8,16,512]{2,1,0:T(8,128)(2,1)S(1)}, u32[]{:S(2)}, u32[]{:S(2)}) collective-permute-start(bf16[8,16,512]{2,1,0:T(8,128)(2,1)S(1)} %get-tuple-element.66), channel_id=1, source_target_pairs={{0,15},{1,2},{2,1},{3,4},{4,3},{5,6},{6,5},{7,8},{8,7},{9,10},{10,... | collective-permute-start | bytes 393224 | tf_op jit(solution)/shard_map/ppermute | solution.py:696
  30.8 4.9 %collective-permute-start.7 = (bf16[8,16,512]{2,1,0:T(8,128)(2,1)S(1)}, bf16[8,16,512]{2,1,0:T(8,128)(2,1)S(1)}, u32[]{:S(2)}, u32[]{:S(2)}) collective-permute-start(bf16[8,16,512]{2,1,0:T(8,128)(2,1)S(1)} %get-tuple-element.68), channel_id=1, source_target_pairs={{0,1},{1,0},{2,3},{3,2},{4,5},{5,4},{6,7},{7,6},{8,9},{9,8},{10,11... | collective-permute-start | bytes 393224 | tf_op jit(solution)/shard_map/ppermute | solution.py:698
  38.1 11.7 %collective-permute-start.8 = (bf16[10,16,512]{2,1,0:T(8,128)(2,1)S(1)}, bf16[10,16,512]{2,1,0:T(8,128)(2,1)S(1)}, u32[]{:S(2)}, u32[]{:S(2)}) collective-permute-start(bf16[10,16,512]{2,1,0:T(8,128)(2,1)S(1)} %get-tuple-element.73), channel_id=1, source_target_pairs={{0,112},{16,32},{32,16},{48,64},{64,48},{80,96},{96,80},{112,0},{1... | collective-permute-start | bytes 491528 | tf_op jit(solution)/shard_map/ppermute | solution.py:695
  40.0 9.8 %collective-permute-start.10 = (bf16[10,16,512]{2,1,0:T(8,128)(2,1)S(1)}, bf16[10,16,512]{2,1,0:T(8,128)(2,1)S(1)}, u32[]{:S(2)}, u32[]{:S(2)}) collective-permute-start(bf16[10,16,512]{2,1,0:T(8,128)(2,1)S(1)} %get-tuple-element.75), channel_id=1, source_target_pairs={{0,16},{16,0},{32,48},{48,32},{64,80},{80,64},{96,112},{112,96},{1... | collective-permute-start | bytes 491528 | tf_op jit(solution)/shard_map/ppermute | solution.py:697
  40.0 9.8 %collective-permute-start.9 = (bf16[8,16,512]{2,1,0:T(8,128)(2,1)S(1)}, bf16[8,16,512]{2,1,0:T(8,128)(2,1)S(1)}, u32[]{:S(2)}, u32[]{:S(2)}) collective-permute-start(bf16[8,16,512]{2,1,0:T(8,128)(2,1)S(1)} %get-tuple-element.74), channel_id=1, source_target_pairs={{0,15},{1,2},{2,1},{3,4},{4,3},{5,6},{6,5},{7,8},{8,7},{9,10},{10,... | collective-permute-start | bytes 393224 | tf_op jit(solution)/shard_map/ppermute | solution.py:696
  44.0 5.8 %collective-permute-start.11 = (bf16[8,16,512]{2,1,0:T(8,128)(2,1)S(1)}, bf16[8,16,512]{2,1,0:T(8,128)(2,1)S(1)}, u32[]{:S(2)}, u32[]{:S(2)}) collective-permute-start(bf16[8,16,512]{2,1,0:T(8,128)(2,1)S(1)} %get-tuple-element.76), channel_id=1, source_target_pairs={{0,1},{1,0},{2,3},{3,2},{4,5},{5,4},{6,7},{7,6},{8,9},{9,8},{10,11... | collective-permute-start | bytes 393224 | tf_op jit(solution)/shard_map/ppermute | solution.py:698
  50.8 9.5 %collective-permute-start.12 = (bf16[10,16,512]{2,1,0:T(8,128)(2,1)S(1)}, bf16[10,16,512]{2,1,0:T(8,128)(2,1)S(1)}, u32[]{:S(2)}, u32[]{:S(2)}) collective-permute-start(bf16[10,16,512]{2,1,0:T(8,128)(2,1)S(1)} %get-tuple-element.81), channel_id=1, source_target_pairs={{0,112},{16,32},{32,16},{48,64},{64,48},{80,96},{96,80},{112,0},{1... | collective-permute-start | bytes 491528 | tf_op jit(solution)/shard_map/ppermute | solution.py:695
  50.9 9.4 %collective-permute-start.14 = (bf16[10,16,512]{2,1,0:T(8,128)(2,1)S(1)}, bf16[10,16,512]{2,1,0:T(8,128)(2,1)S(1)}, u32[]{:S(2)}, u32[]{:S(2)}) collective-permute-start(bf16[10,16,512]{2,1,0:T(8,128)(2,1)S(1)} %get-tuple-element.83), channel_id=1, source_target_pairs={{0,16},{16,0},{32,48},{48,32},{64,80},{80,64},{96,112},{112,96},{1... | collective-permute-start | bytes 491528 | tf_op jit(solution)/shard_map/ppermute | solution.py:697
  51.0 9.3 %collective-permute-start.13 = (bf16[8,16,512]{2,1,0:T(8,128)(2,1)S(1)}, bf16[8,16,512]{2,1,0:T(8,128)(2,1)S(1)}, u32[]{:S(2)}, u32[]{:S(2)}) collective-permute-start(bf16[8,16,512]{2,1,0:T(8,128)(2,1)S(1)} %get-tuple-element.82), channel_id=1, source_target_pairs={{0,15},{1,2},{2,1},{3,4},{4,3},{5,6},{6,5},{7,8},{8,7},{9,10},{10,... | collective-permute-start | bytes 393224 | tf_op jit(solution)/shard_map/ppermute | solution.py:696
  54.5 5.8 %collective-permute-start.15 = (bf16[8,16,512]{2,1,0:T(8,128)(2,1)S(1)}, bf16[8,16,512]{2,1,0:T(8,128)(2,1)S(1)}, u32[]{:S(2)}, u32[]{:S(2)}) collective-permute-start(bf16[8,16,512]{2,1,0:T(8,128)(2,1)S(1)} %get-tuple-element.84), channel_id=1, source_target_pairs={{0,1},{1,0},{2,3},{3,2},{4,5},{5,4},{6,7},{7,6},{8,9},{9,8},{10,11... | collective-permute-start | bytes 393224 | tf_op jit(solution)/shard_map/ppermute | solution.py:698
  60.3 1.3 %copy-start = (bf16[8,16,512]{2,1,0:T(8,128)(2,1)}, bf16[8,16,512]{2,1,0:T(8,128)(2,1)S(1)}, u32[]{:S(2)}) copy-start(bf16[8,16,512]{2,1,0:T(8,128)(2,1)S(1)} %collective-permute-done.13.refs_1_) | copy-start | bytes 393220
  60.3 1.3 %copy-start.2 = (bf16[8,16,512]{2,1,0:T(8,128)(2,1)}, bf16[8,16,512]{2,1,0:T(8,128)(2,1)S(1)}, u32[]{:S(2)}) copy-start(bf16[8,16,512]{2,1,0:T(8,128)(2,1)S(1)} %collective-permute-done.15.refs_3_) | copy-start | bytes 393220
  61.7 15.7 %all-to-all-start.1 = ((bf16[16,2,16,512]{3,2,1,0:T(8,128)(2,1)}), bf16[16,2,16,512]{3,2,1,0:T(8,128)(2,1)S(1)}, u32[]{:S(2)}, u32[]{:S(2)}) async-start(bf16[16,2,16,512]{3,2,1,0:T(8,128)(2,1)} %get-tuple-element.85), calls=%async_computation.1 | async-start | bytes 1048576 | tf_op jit(solution)/shard_map/all_to_all | solution.py:746
  66.2 0.9 %copy-start.1 = (bf16[8,16,512]{2,1,0:T(8,128)(2,1)S(1)}, bf16[8,16,512]{2,1,0:T(8,128)(2,1)}, u32[]{:S(2)}) copy-start(bf16[8,16,512]{2,1,0:T(8,128)(2,1)} %copy-done) | copy-start | bytes 393220
  67.1 0.9 %copy-start.3 = (bf16[8,16,512]{2,1,0:T(8,128)(2,1)S(1)}, bf16[8,16,512]{2,1,0:T(8,128)(2,1)}, u32[]{:S(2)}) copy-start(bf16[8,16,512]{2,1,0:T(8,128)(2,1)} %copy-done.2) | copy-start | bytes 393220

commit v8 on v7

--- a/solution.py
+++ b/solution.py
@@ -217,11 +217,11 @@
     for t in columns:
         for xg in range(4):
             rows = [src[t, pl.ds(xg * 4 + xl, 16, stride=16), :] for xl in range(4)]
+            rows = [rows[0]] + [pltpu.roll(rows[xl], xl * 32, 1) for xl in range(1, 4)]
             for g in range(4):
-                piece = None
-                for xl in range(4):
-                    turned = rows[xl] if xl == g else pltpu.roll(rows[xl], ((xl - g) % 4) * 32, 1)
-                    piece = turned if piece is None else jnp.where(group == xl, turned, piece)
+                piece = rows[(0 - g) % 4]
+                for p in range(1, 4):
+                    piece = jnp.where(group == p, rows[(p - g) % 4], piece)
                 out[t * 4 + g, :, xg * 128 : xg * 128 + 128] = piece.astype(BF16)
 
 
@@ -665,13 +665,17 @@
 def make_image(bricks, rcv_early, rcv_late):
     def kernel(bricks, rcv_early, rcv_late, out, held, sem):
         copies = []
+        turn = lax.axis_index("gy") % 4
         for q in range(4):
             rows = slice(q * 128, q * 128 + 128)
             early = bricks[:, 0, :, rows].reshape(256, 128).astype(F32).T
             late = bricks[:, 1, :, rows].reshape(256, 128).astype(F32).T
-            for t in range(2):
-                lanes = slice(t * 128, t * 128 + 128)
-                held[rows, lanes] = early[:, lanes] * rcv_early[t, rows, :] + late[:, lanes] * rcv_late[t, rows, :]
+            for place in range(4):
+                part = slice(place * 32, place * 32 + 32)
+                at = pl.ds(pl.multiple_of(q * 128 + lax.rem(place + 4 - turn, 4) * 32, 32), 32)
+                for t in range(2):
+                    lanes = slice(t * 128, t * 128 + 128)
+                    held[at, lanes] = early[part, lanes] * rcv_early[t, at, :] + late[part, lanes] * rcv_late[t, at, :]
             copies.append(pltpu.make_async_copy(held.at[rows, :], out.at[rows, :], sem))
             copies[-1].start()
         wait(copies)

time: 78.8 us -> 78.8 us (level)
  no operation moved by 1% of the time
where the time goes in v8:
time: 78.8 us; the launch traced here: 78.3 us
  starting transfers between devices  37.8 us (48%)
  Pallas kernels  20.4 us (26%)
  waiting for transfers between devices  17.4 us (22%)
  local copies, waits for them, and re-layouts  1.81 us (2%)
  between operations  0.96 us (1%)
    ppermute x4, starting transfers between devices, exchange(): lax.ppermute(gy_second, 'gy', outer(16))  12.8 us
    all_to_all x1, starting transfers between devices, on_device(): lax.all_to_all(turned.reshape(16, 16, 512), 'gy', split_axis=0, concat_ax...  8.46 us
    all_to_all x1, waiting for transfers between devices, on_device(): lax.all_to_all(bricks, 'gy', split_axis=0, concat_axis=0, tiled=True)  8.09 us
    ppermute x4, starting transfers between devices, exchange(): lax.ppermute(gx_second, 'gx', outer(8))  7.76 us
    ppermute x4, waiting for transfers between devices, exchange(): lax.ppermute(gy_second, 'gy', outer(16))  7.76 us
    pallas_call x3, Pallas kernels, local_step(): pl.pallas_call(kernel, out_shape=out_shape, in_specs=[VM, next_spec, VM,...  6.74 us
    all_to_all x1, starting transfers between devices, on_device(): lax.all_to_all(bricks, 'gy', split_axis=0, concat_axis=0, tiled=True)  4.51 us
    ppermute x4, starting transfers between devices, exchange(): lax.ppermute(gy_first, 'gy', inner(16))  4.12 us
  transfers between devices with their start and end apart: 18, of which 6 were waited for; matrix products, arithmetic and copies ran while one was open for 0% of the time, Pallas kernels for 17%

profile of v8, /device:TPU:1, one launch (start us, length us, event | category | flops | bytes accessed | tf_op | source)
XLA Modules:
  0.0 78.3 jit_solution(7811232278674523611)
XLA Ops:
  0.6 2.0 %turn_velocity.1 = (f32[2,16,32,128]{3,2,1,0:T(8,128)S(1)}, f32[4,16,16,128]{3,2,1,0:T(8,128)S(1)}, f32[2,16,32,128]{3,2,1,0:T(8,128)S(1)}, s16[256,512]{1,0:T(8,128)(2,1)}) custom-call(f32[16,32,256]{2,1,0:T(8,128)} %vel.1, f32[16,16,512]{2,1,0:T(8,128)} %refs_0_.1, f32[16,32,256]{2,1,0:T(8,128)} %refs_2_.1), custom_call_target="tpu_custom_call" | custom-call | tf_op jit(solution)/shard_map/turn_velocity/pallas_call | solution.py:316
  2.6 8.5 %all-to-all-start = ((s16[16,16,512]{2,1,0:T(8,128)(2,1)}), s16[16,16,512]{2,1,0:T(8,128)(2,1)S(1)}, u32[]{:S(2)}, u32[]{:S(2)}) async-start(s16[16,16,512]{2,1,0:T(8,128)(2,1)} %bitcast.28), calls=%async_computation | async-start | bytes 524288 | tf_op jit(solution)/shard_map/all_to_all | solution.py:721
  11.1 0.9 %first_halos.1 = (bf16[10,16,512]{2,1,0:T(8,128)(2,1)S(1)}, bf16[8,16,512]{2,1,0:T(8,128)(2,1)}, bf16[10,16,512]{2,1,0:T(8,128)(2,1)S(1)}, bf16[8,16,512]{2,1,0:T(8,128)(2,1)S(1)}) custom-call(f32[4,256,128]{2,1,0:T(8,128)S(1)} %bitcast.21, f32[2,512,128]{2,1,0:T(8,128)S(1)} %bitcast.22), custom_call_target="tpu_custom_call" | custom-call | tf_op jit(solution)/shard_map/first_halos/pallas_call | solution.py:337
  11.9 3.9 %collective-permute-start = (bf16[10,16,512]{2,1,0:T(8,128)(2,1)S(1)}, bf16[10,16,512]{2,1,0:T(8,128)(2,1)S(1)}, u32[]{:S(2)}, u32[]{:S(2)}) collective-permute-start(bf16[10,16,512]{2,1,0:T(8,128)(2,1)S(1)} %get-tuple-element.55), channel_id=1, source_target_pairs={{0,112},{16,32},{32,16},{48,64},{64,48},{80,96},{96,80},{112,0},{1... | collective-permute-start | bytes 491528 | tf_op jit(solution)/shard_map/ppermute | solution.py:699
  15.8 0.0 collective-permute-start.2
  15.8 4.0 %collective-permute-start.1 = (bf16[8,16,512]{2,1,0:T(8,128)(2,1)}, bf16[8,16,512]{2,1,0:T(8,128)(2,1)S(1)}, u32[]{:S(2)}, u32[]{:S(2)}) collective-permute-start(bf16[8,16,512]{2,1,0:T(8,128)(2,1)} %get-tuple-element.56), channel_id=1, source_target_pairs={{0,15},{1,2},{2,1},{3,4},{4,3},{5,6},{6,5},{7,8},{8,7},{9,10},{10,... | collective-permute-start | bytes 393224 | tf_op jit(solution)/shard_map/ppermute | solution.py:700
  19.8 2.0 %collective-permute-start.3 = (bf16[8,16,512]{2,1,0:T(8,128)(2,1)S(1)}, bf16[8,16,512]{2,1,0:T(8,128)(2,1)S(1)}, u32[]{:S(2)}, u32[]{:S(2)}) collective-permute-start(bf16[8,16,512]{2,1,0:T(8,128)(2,1)S(1)} %get-tuple-element.58), channel_id=1, source_target_pairs={{0,1},{1,0},{2,3},{3,2},{4,5},{5,4},{6,7},{7,6},{8,9},{9,8},{10,11... | collective-permute-start | bytes 393224 | tf_op jit(solution)/shard_map/ppermute | solution.py:702
  21.8 4.0 %local_first.1 = (f32[4,256,128]{2,1,0:T(8,128)S(1)}, f32[4,256,128]{2,1,0:T(8,128)S(1)}, f32[2,512,128]{2,1,0:T(8,128)S(1)}, f32[4,4,16,128]{3,2,1,0:T(8,128)S(1)}, f32[32,128]{1,0:T(8,128)S(1)}) custom-call(f32[2,512,128]{2,1,0:T(8,128)S(1)} %bitcast.13, f32[16,16,512]{2,1,0:T(8,128)} %refs_0_.1, f32[256,512]{1,0:T(8,128)} %bitcast.25, ...), custom_call_target="tpu_custom_call" | custom-call | bytes 14400000 | tf_op jit(solution)/shard_map/local_first/pallas_call | solution.py:472
  25.9 0.0 all-to-all-done.pieces
  25.9 0.5 source_velocity.1.refs_3_.vel_src.refs_2_
  26.4 0.2 collective-permute-done.1.refs_6_
  26.6 0.0 collective-permute-done.3.refs_8_
  26.6 0.0 collective-permute-done.refs_5_
  26.6 0.0 collective-permute-done.2.refs_7_
  26.6 1.0 %halo_step0.1 = (f32[4,256,128]{2,1,0:T(8,128)S(1)}, f32[2,512,128]{2,1,0:T(8,128)S(1)}, bf16[10,16,512]{2,1,0:T(8,128)(2,1)S(1)}, bf16[8,16,512]{2,1,0:T(8,128)...) custom-call(f32[4,256,128]{2,1,0:T(8,128)S(1)} %get-tuple-element.49.refs_0_, ...), custom_call_target="tpu_custom_call" | custom-call | tf_op jit(solution)/shard_map/halo_step0/pallas_call | solution.py:605
  27.6 1.8 %collective-permute-start.4 = (bf16[10,16,512]{2,1,0:T(8,128)(2,1)S(1)}, bf16[10,16,512]{2,1,0:T(8,128)(2,1)S(1)}, u32[]{:S(2)}, u32[]{:S(2)}) collective-permute-start(bf16[10,16,512]{2,1,0:T(8,128)(2,1)S(1)} %get-tuple-element.65), channel_id=1, source_target_pairs={{0,112},{16,32},{32,16},{48,64},{64,48},{80,96},{96,80},{112,0},{1... | collective-permute-start | bytes 491528 | tf_op jit(solution)/shard_map/ppermute | solution.py:699
  29.4 0.0 collective-permute-start.6
  29.4 1.4 %collective-permute-start.5 = (bf16[8,16,512]{2,1,0:T(8,128)(2,1)S(1)}, bf16[8,16,512]{2,1,0:T(8,128)(2,1)S(1)}, u32[]{:S(2)}, u32[]{:S(2)}) collective-permute-start(bf16[8,16,512]{2,1,0:T(8,128)(2,1)S(1)} %get-tuple-element.66), channel_id=1, source_target_pairs={{0,15},{1,2},{2,1},{3,4},{4,3},{5,6},{6,5},{7,8},{8,7},{9,10},{10,... | collective-permute-start | bytes 393224 | tf_op jit(solution)/shard_map/ppermute | solution.py:700
  30.8 1.9 %collective-permute-start.7 = (bf16[8,16,512]{2,1,0:T(8,128)(2,1)S(1)}, bf16[8,16,512]{2,1,0:T(8,128)(2,1)S(1)}, u32[]{:S(2)}, u32[]{:S(2)}) collective-permute-start(bf16[8,16,512]{2,1,0:T(8,128)(2,1)S(1)} %get-tuple-element.68), channel_id=1, source_target_pairs={{0,1},{1,0},{2,3},{3,2},{4,5},{5,4},{6,7},{7,6},{8,9},{9,8},{10,11... | collective-permute-start | bytes 393224 | tf_op jit(solution)/shard_map/ppermute | solution.py:702
  32.7 2.5 %local_step1.1 = (f32[4,256,128]{2,1,0:T(8,128)S(1)}, f32[2,512,128]{2,1,0:T(8,128)S(1)}) custom-call(f32[4,256,128]{2,1,0:T(8,128)S(1)} %get-tuple-element.60.src.src_next, f32[256,512]{1,0:T(8,128)} %bitcast.23, f32[2,512,128]{2,1,0:T(8,128)S(1)} %get-tuple-element.61.rcv.rcv_next, f32[512,256]{1,0:T(8,128)} %bitcast.24, ...), custom_call_target="tpu_custom_call" | custom-call | bytes 10800000 | tf_op jit(solution)/shard_map/local_step1/pallas_call | solution.py:553
  35.2 0.4 collective-permute-done.5.refs_5_
  35.6 0.0 collective-permute-done.7.refs_7_
  35.6 1.5 %collective-permute-done.4.refs_4_ = bf16[10,16,512]{2,1,0:T(8,128)(2,1)S(1)} collective-permute-done((bf16[10,16,512]{2,1,0:T(8,128)(2,1)S(1)}, bf16[10,16,512]{2,1,0:T(8,128)(2,1)S(1)}, u32[]{:S(2)}, u32[]{:S(2)}) %collective-permute-start.4) | collective-permute-done | bytes 163872 | tf_op jit(solution)/shard_map/ppermute | solution.py:699
  37.1 0.0 collective-permute-done.6.refs_6_
  37.1 1.0 %halo_step1.1 = (f32[4,256,128]{2,1,0:T(8,128)S(1)}, f32[2,512,128]{2,1,0:T(8,128)S(1)}, bf16[10,16,512]{2,1,0:T(8,128)(2,1)S(1)}, bf16[8,16,512]{2,1,0:T(8,128)...) custom-call(f32[4,256,128]{2,1,0:T(8,128)S(1)} %get-tuple-element.63.refs_0_, ...), custom_call_target="tpu_custom_call" | custom-call | tf_op jit(solution)/shard_map/halo_step1/pallas_call | solution.py:605
  38.1 2.0 %collective-permute-start.8 = (bf16[10,16,512]{2,1,0:T(8,128)(2,1)S(1)}, bf16[10,16,512]{2,1,0:T(8,128)(2,1)S(1)}, u32[]{:S(2)}, u32[]{:S(2)}) collective-permute-start(bf16[10,16,512]{2,1,0:T(8,128)(2,1)S(1)} %get-tuple-element.73), channel_id=1, source_target_pairs={{0,112},{16,32},{32,16},{48,64},{64,48},{80,96},{96,80},{112,0},{1... | collective-permute-start | bytes 491528 | tf_op jit(solution)/shard_map/ppermute | solution.py:699
  40.0 0.0 collective-permute-start.10
  40.0 4.0 %collective-permute-start.9 = (bf16[8,16,512]{2,1,0:T(8,128)(2,1)S(1)}, bf16[8,16,512]{2,1,0:T(8,128)(2,1)S(1)}, u32[]{:S(2)}, u32[]{:S(2)}) collective-permute-start(bf16[8,16,512]{2,1,0:T(8,128)(2,1)S(1)} %get-tuple-element.74), channel_id=1, source_target_pairs={{0,15},{1,2},{2,1},{3,4},{4,3},{5,6},{6,5},{7,8},{8,7},{9,10},{10,... | collective-permute-start | bytes 393224 | tf_op jit(solution)/shard_map/ppermute | solution.py:700
  44.0 0.0 collective-permute-start.11
  44.0 2.1 %local_step2.1 = (f32[4,256,128]{2,1,0:T(8,128)S(1)}, f32[2,512,128]{2,1,0:T(8,128)S(1)}, f32[2,512,128]{2,1,0:T(8,128)}) custom-call(f32[4,256,128]{2,1,0:T(8,128)S(1)} %get-tuple-element.69.src.src_next, f32[4,256,128]{2,1,0:T(8,128)S(1)} %get-tuple-element.60.src.src_next, f32[2,512,128]{2,1,0:T(8,128)S(1)} %get-tuple-element.70.rcv.rcv_next, ...), custom_call_target="tpu_custom_call" | custom-call | bytes 10800000 | tf_op jit(solution)/shard_map/local_step2/pallas_call | solution.py:553
  46.1 3.7 %collective-permute-done.9.refs_5_ = bf16[8,16,512]{2,1,0:T(8,128)(2,1)S(1)} collective-permute-done((bf16[8,16,512]{2,1,0:T(8,128)(2,1)S(1)}, bf16[8,16,512]{2,1,0:T(8,128)(2,1)S(1)}, u32[]{:S(2)}, u32[]{:S(2)}) %collective-permute-start.9) | collective-permute-done | bytes 131104 | tf_op jit(solution)/shard_map/ppermute | solution.py:700
  49.8 0.0 collective-permute-done.11.refs_7_
  49.8 1.0 %halo_step2.1 = (f32[4,256,128]{2,1,0:T(8,128)S(1)}, f32[2,512,128]{2,1,0:T(8,128)S(1)}, bf16[10,16,512]{2,1,0:T(8,128)(2,1)S(1)}, bf16[8,16,512]{2,1,0:T(8,128)...) custom-call(f32[4,256,128]{2,1,0:T(8,128)S(1)} %get-tuple-element.71.refs_0_, ...), custom_call_target="tpu_custom_call" | custom-call | tf_op jit(solution)/shard_map/halo_step2/pallas_call | solution.py:605
  50.8 0.1 collective-permute-start.12
  50.9 0.1 collective-permute-start.14
  51.0 3.5 %collective-permute-start.13 = (bf16[8,16,512]{2,1,0:T(8,128)(2,1)S(1)}, bf16[8,16,512]{2,1,0:T(8,128)(2,1)S(1)}, u32[]{:S(2)}, u32[]{:S(2)}) collective-permute-start(bf16[8,16,512]{2,1,0:T(8,128)(2,1)S(1)} %get-tuple-element.82), channel_id=1, source_target_pairs={{0,15},{1,2},{2,1},{3,4},{4,3},{5,6},{6,5},{7,8},{8,7},{9,10},{10,... | collective-permute-start | bytes 393224 | tf_op jit(solution)/shard_map/ppermute | solution.py:700
  54.5 0.2 collective-permute-start.15
  54.7 2.1 %local_step3.1 = (f32[4,256,128]{2,1,0:T(8,128)S(1)}, f32[2,512,128]{2,1,0:T(8,128)S(1)}, bf16[16,2,16,512]{3,2,1,0:T(8,128)(2,1)}) custom-call(f32[4,256,128]{2,1,0:T(8,128)S(1)} %get-tuple-element.77.src, f32[4,256,128]{2,1,0:T(8,128)S(1)} %get-tuple-element.69.src.src_next, f32[2,512,128]{2,1,0:T(8,128)S(1)} %get-tuple-element.78.rcv, ...), custom_call_target="tpu_custom_call" | custom-call | bytes 10800000 | tf_op jit(solution)/shard_map/local_step3/pallas_call | solution.py:553
  56.9 3.4 %collective-permute-done.13.refs_1_ = bf16[8,16,512]{2,1,0:T(8,128)(2,1)S(1)} collective-permute-done((bf16[8,16,512]{2,1,0:T(8,128)(2,1)S(1)}, bf16[8,16,512]{2,1,0:T(8,128)(2,1)S(1)}, u32[]{:S(2)}, u32[]{:S(2)}) %collective-permute-start.13) | collective-permute-done | bytes 131104 | tf_op jit(solution)/shard_map/ppermute | solution.py:700
  60.3 0.0 collective-permute-done.15.refs_3_
  60.3 0.0 collective-permute-done.14.refs_2_
  60.3 1.2 %last_source.1 = (f32[4,256,128]{2,1,0:T(8,128)S(1)}, bf16[16,2,16,512]{3,2,1,0:T(8,128)(2,1)}) custom-call(f32[4,256,128]{2,1,0:T(8,128)S(1)} %get-tuple-element.79.local, bf16[16,2,16,512]{3,2,1,0:T(8,128)(2,1)} %get-tuple-element.80._, f32[4,256,128]{2,1,0:T(8,128)S(1)} %source_velocity.1.refs_3_.vel_src.refs_2_, ...), custom_call_target="tpu_custom_call", output_to_operand_aliasing={{1}: (1, {})} | custom-call | tf_op jit(solution)/shard_map/last_source/pallas_call | solution.py:629
  61.6 4.5 %all-to-all-start.1 = ((bf16[16,2,16,512]{3,2,1,0:T(8,128)(2,1)}), bf16[16,2,16,512]{3,2,1,0:T(8,128)(2,1)S(1)}, u32[]{:S(2)}, u32[]{:S(2)}) async-start(bf16[16,2,16,512]{3,2,1,0:T(8,128)(2,1)} %get-tuple-element.85), calls=%async_computation.1 | async-start | bytes 1048576 | tf_op jit(solution)/shard_map/all_to_all | solution.py:750
  66.1 0.9 %copy-done.1 = bf16[8,16,512]{2,1,0:T(8,128)(2,1)S(1)} copy-done((bf16[8,16,512]{2,1,0:T(8,128)(2,1)S(1)}, bf16[8,16,512]{2,1,0:T(8,128)(2,1)}, u32[]{:S(2)}) %copy-start.1) | copy-done | bytes 131096
  67.0 0.9 %copy-done.3 = bf16[8,16,512]{2,1,0:T(8,128)(2,1)S(1)} copy-done((bf16[8,16,512]{2,1,0:T(8,128)(2,1)S(1)}, bf16[8,16,512]{2,1,0:T(8,128)(2,1)}, u32[]{:S(2)}) %copy-start.3) | copy-done | bytes 131096
  67.9 1.2 %last_receiver.1 = (f32[2,512,128]{2,1,0:T(8,128)S(1)}, f32[2,512,128]{2,1,0:T(8,128)S(1)}, f32[256,512]{1,0:T(8,128)}, f32[512,256]{1,0:T(8,128)}) custom-call(f32[2,512,128]{2,1,0:T(8,128)S(1)} %get-tuple-element.86.local, f32[2,512,128]{2,1,0:T(8,128)S(1)} %bitcast.20, bf16[10,16,512]{2,1,0:T(8,128)(2,1)S(1)} %collective-permute-done.12.refs_0_, ...), custom_call_target="tpu_custom_call" | custom-call | bytes 7200000 | tf_op jit(solution)/shard_map/last_receiver/pallas_call | solution.py:653
  69.2 8.1 %all-to-all-done.1.bricks = bf16[16,2,16,512]{3,2,1,0:T(8,128)(2,1)S(1)} async-done(((bf16[16,2,16,512]{3,2,1,0:T(8,128)(2,1)}), bf16[16,2,16,512]{3,2,1,0:T(8,128)(2,1)S(1)}, u32[]{:S(2)}, u32[]{:S(2)}) %all-to-all-start.1) | async-done | bytes 524320 | tf_op jit(solution)/shard_map/all_to_all | solution.py:750
  77.3 0.9 %make_image.1 = f32[512,256]{1,0:T(8,128)} custom-call(bf16[16,2,16,512]{3,2,1,0:T(8,128)(2,1)S(1)} %all-to-all-done.1.bricks, f32[2,512,128]{2,1,0:T(8,128)S(1)} %get-tuple-element.89.rcv_early, f32[2,512,128]{2,1,0:T(8,128)S(1)} %get-tuple-element.90.rcv_late), custom_call_target="tpu_custom_call" | custom-call | tf_op jit(solution)/shard_map/make_image/pallas_call | solution.py:683
  (9 shorter events, 0.0 us)
Async XLA Ops:
  2.6 23.3 %all-to-all-start = ((s16[16,16,512]{2,1,0:T(8,128)(2,1)}), s16[16,16,512]{2,1,0:T(8,128)(2,1)S(1)}, u32[]{:S(2)}, u32[]{:S(2)}) async-start(s16[16,16,512]{2,1,0:T(8,128)(2,1)} %bitcast.28), calls=%async_computation | async-start | bytes 524288 | tf_op jit(solution)/shard_map/all_to_all | solution.py:721
  11.9 14.6 %collective-permute-start = (bf16[10,16,512]{2,1,0:T(8,128)(2,1)S(1)}, bf16[10,16,512]{2,1,0:T(8,128)(2,1)S(1)}, u32[]{:S(2)}, u32[]{:S(2)}) collective-permute-start(bf16[10,16,512]{2,1,0:T(8,128)(2,1)S(1)} %get-tuple-element.55), channel_id=1, source_target_pairs={{0,112},{16,32},{32,16},{48,64},{64,48},{80,96},{96,80},{112,0},{1... | collective-permute-start | bytes 491528 | tf_op jit(solution)/shard_map/ppermute | solution.py:699
  15.8 10.7 %collective-permute-start.2 = (bf16[10,16,512]{2,1,0:T(8,128)(2,1)S(1)}, bf16[10,16,512]{2,1,0:T(8,128)(2,1)S(1)}, u32[]{:S(2)}, u32[]{:S(2)}) collective-permute-start(bf16[10,16,512]{2,1,0:T(8,128)(2,1)S(1)} %get-tuple-element.57), channel_id=1, source_target_pairs={{0,16},{16,0},{32,48},{48,32},{64,80},{80,64},{96,112},{112,96},{1... | collective-permute-start | bytes 491528 | tf_op jit(solution)/shard_map/ppermute | solution.py:701
  15.8 10.7 %collective-permute-start.1 = (bf16[8,16,512]{2,1,0:T(8,128)(2,1)}, bf16[8,16,512]{2,1,0:T(8,128)(2,1)S(1)}, u32[]{:S(2)}, u32[]{:S(2)}) collective-permute-start(bf16[8,16,512]{2,1,0:T(8,128)(2,1)} %get-tuple-element.56), channel_id=1, source_target_pairs={{0,15},{1,2},{2,1},{3,4},{4,3},{5,6},{6,5},{7,8},{8,7},{9,10},{10,... | collective-permute-start | bytes 393224 | tf_op jit(solution)/shard_map/ppermute | solution.py:700
  19.8 6.7 %collective-permute-start.3 = (bf16[8,16,512]{2,1,0:T(8,128)(2,1)S(1)}, bf16[8,16,512]{2,1,0:T(8,128)(2,1)S(1)}, u32[]{:S(2)}, u32[]{:S(2)}) collective-permute-start(bf16[8,16,512]{2,1,0:T(8,128)(2,1)S(1)} %get-tuple-element.58), channel_id=1, source_target_pairs={{0,1},{1,0},{2,3},{3,2},{4,5},{5,4},{6,7},{7,6},{8,9},{9,8},{10,11... | collective-permute-start | bytes 393224 | tf_op jit(solution)/shard_map/ppermute | solution.py:702
  27.6 9.5 %collective-permute-start.4 = (bf16[10,16,512]{2,1,0:T(8,128)(2,1)S(1)}, bf16[10,16,512]{2,1,0:T(8,128)(2,1)S(1)}, u32[]{:S(2)}, u32[]{:S(2)}) collective-permute-start(bf16[10,16,512]{2,1,0:T(8,128)(2,1)S(1)} %get-tuple-element.65), channel_id=1, source_target_pairs={{0,112},{16,32},{32,16},{48,64},{64,48},{80,96},{96,80},{112,0},{1... | collective-permute-start | bytes 491528 | tf_op jit(solution)/shard_map/ppermute | solution.py:699
  29.4 7.7 %collective-permute-start.6 = (bf16[10,16,512]{2,1,0:T(8,128)(2,1)S(1)}, bf16[10,16,512]{2,1,0:T(8,128)(2,1)S(1)}, u32[]{:S(2)}, u32[]{:S(2)}) collective-permute-start(bf16[10,16,512]{2,1,0:T(8,128)(2,1)S(1)} %get-tuple-element.67), channel_id=1, source_target_pairs={{0,16},{16,0},{32,48},{48,32},{64,80},{80,64},{96,112},{112,96},{1... | collective-permute-start | bytes 491528 | tf_op jit(solution)/shard_map/ppermute | solution.py:701
  29.4 6.2 %collective-permute-start.5 = (bf16[8,16,512]{2,1,0:T(8,128)(2,1)S(1)}, bf16[8,16,512]{2,1,0:T(8,128)(2,1)S(1)}, u32[]{:S(2)}, u32[]{:S(2)}) collective-permute-start(bf16[8,16,512]{2,1,0:T(8,128)(2,1)S(1)} %get-tuple-element.66), channel_id=1, source_target_pairs={{0,15},{1,2},{2,1},{3,4},{4,3},{5,6},{6,5},{7,8},{8,7},{9,10},{10,... | collective-permute-start | bytes 393224 | tf_op jit(solution)/shard_map/ppermute | solution.py:700
  30.8 4.9 %collective-permute-start.7 = (bf16[8,16,512]{2,1,0:T(8,128)(2,1)S(1)}, bf16[8,16,512]{2,1,0:T(8,128)(2,1)S(1)}, u32[]{:S(2)}, u32[]{:S(2)}) collective-permute-start(bf16[8,16,512]{2,1,0:T(8,128)(2,1)S(1)} %get-tuple-element.68), channel_id=1, source_target_pairs={{0,1},{1,0},{2,3},{3,2},{4,5},{5,4},{6,7},{7,6},{8,9},{9,8},{10,11... | collective-permute-start | bytes 393224 | tf_op jit(solution)/shard_map/ppermute | solution.py:702
  38.1 11.7 %collective-permute-start.8 = (bf16[10,16,512]{2,1,0:T(8,128)(2,1)S(1)}, bf16[10,16,512]{2,1,0:T(8,128)(2,1)S(1)}, u32[]{:S(2)}, u32[]{:S(2)}) collective-permute-start(bf16[10,16,512]{2,1,0:T(8,128)(2,1)S(1)} %get-tuple-element.73), channel_id=1, source_target_pairs={{0,112},{16,32},{32,16},{48,64},{64,48},{80,96},{96,80},{112,0},{1... | collective-permute-start | bytes 491528 | tf_op jit(solution)/shard_map/ppermute | solution.py:699
  40.0 9.8 %collective-permute-start.10 = (bf16[10,16,512]{2,1,0:T(8,128)(2,1)S(1)}, bf16[10,16,512]{2,1,0:T(8,128)(2,1)S(1)}, u32[]{:S(2)}, u32[]{:S(2)}) collective-permute-start(bf16[10,16,512]{2,1,0:T(8,128)(2,1)S(1)} %get-tuple-element.75), channel_id=1, source_target_pairs={{0,16},{16,0},{32,48},{48,32},{64,80},{80,64},{96,112},{112,96},{1... | collective-permute-start | bytes 491528 | tf_op jit(solution)/shard_map/ppermute | solution.py:701
  40.0 9.8 %collective-permute-start.9 = (bf16[8,16,512]{2,1,0:T(8,128)(2,1)S(1)}, bf16[8,16,512]{2,1,0:T(8,128)(2,1)S(1)}, u32[]{:S(2)}, u32[]{:S(2)}) collective-permute-start(bf16[8,16,512]{2,1,0:T(8,128)(2,1)S(1)} %get-tuple-element.74), channel_id=1, source_target_pairs={{0,15},{1,2},{2,1},{3,4},{4,3},{5,6},{6,5},{7,8},{8,7},{9,10},{10,... | collective-permute-start | bytes 393224 | tf_op jit(solution)/shard_map/ppermute | solution.py:700
  44.0 5.8 %collective-permute-start.11 = (bf16[8,16,512]{2,1,0:T(8,128)(2,1)S(1)}, bf16[8,16,512]{2,1,0:T(8,128)(2,1)S(1)}, u32[]{:S(2)}, u32[]{:S(2)}) collective-permute-start(bf16[8,16,512]{2,1,0:T(8,128)(2,1)S(1)} %get-tuple-element.76), channel_id=1, source_target_pairs={{0,1},{1,0},{2,3},{3,2},{4,5},{5,4},{6,7},{7,6},{8,9},{9,8},{10,11... | collective-permute-start | bytes 393224 | tf_op jit(solution)/shard_map/ppermute | solution.py:702
  50.8 9.5 %collective-permute-start.12 = (bf16[10,16,512]{2,1,0:T(8,128)(2,1)S(1)}, bf16[10,16,512]{2,1,0:T(8,128)(2,1)S(1)}, u32[]{:S(2)}, u32[]{:S(2)}) collective-permute-start(bf16[10,16,512]{2,1,0:T(8,128)(2,1)S(1)} %get-tuple-element.81), channel_id=1, source_target_pairs={{0,112},{16,32},{32,16},{48,64},{64,48},{80,96},{96,80},{112,0},{1... | collective-permute-start | bytes 491528 | tf_op jit(solution)/shard_map/ppermute | solution.py:699
  50.9 9.4 %collective-permute-start.14 = (bf16[10,16,512]{2,1,0:T(8,128)(2,1)S(1)}, bf16[10,16,512]{2,1,0:T(8,128)(2,1)S(1)}, u32[]{:S(2)}, u32[]{:S(2)}) collective-permute-start(bf16[10,16,512]{2,1,0:T(8,128)(2,1)S(1)} %get-tuple-element.83), channel_id=1, source_target_pairs={{0,16},{16,0},{32,48},{48,32},{64,80},{80,64},{96,112},{112,96},{1... | collective-permute-start | bytes 491528 | tf_op jit(solution)/shard_map/ppermute | solution.py:701
  51.0 9.3 %collective-permute-start.13 = (bf16[8,16,512]{2,1,0:T(8,128)(2,1)S(1)}, bf16[8,16,512]{2,1,0:T(8,128)(2,1)S(1)}, u32[]{:S(2)}, u32[]{:S(2)}) collective-permute-start(bf16[8,16,512]{2,1,0:T(8,128)(2,1)S(1)} %get-tuple-element.82), channel_id=1, source_target_pairs={{0,15},{1,2},{2,1},{3,4},{4,3},{5,6},{6,5},{7,8},{8,7},{9,10},{10,... | collective-permute-start | bytes 393224 | tf_op jit(solution)/shard_map/ppermute | solution.py:700
  54.5 5.8 %collective-permute-start.15 = (bf16[8,16,512]{2,1,0:T(8,128)(2,1)S(1)}, bf16[8,16,512]{2,1,0:T(8,128)(2,1)S(1)}, u32[]{:S(2)}, u32[]{:S(2)}) collective-permute-start(bf16[8,16,512]{2,1,0:T(8,128)(2,1)S(1)} %get-tuple-element.84), channel_id=1, source_target_pairs={{0,1},{1,0},{2,3},{3,2},{4,5},{5,4},{6,7},{7,6},{8,9},{9,8},{10,11... | collective-permute-start | bytes 393224 | tf_op jit(solution)/shard_map/ppermute | solution.py:702
  60.3 1.3 %copy-start = (bf16[8,16,512]{2,1,0:T(8,128)(2,1)}, bf16[8,16,512]{2,1,0:T(8,128)(2,1)S(1)}, u32[]{:S(2)}) copy-start(bf16[8,16,512]{2,1,0:T(8,128)(2,1)S(1)} %collective-permute-done.13.refs_1_) | copy-start | bytes 393220
  60.3 1.3 %copy-start.2 = (bf16[8,16,512]{2,1,0:T(8,128)(2,1)}, bf16[8,16,512]{2,1,0:T(8,128)(2,1)S(1)}, u32[]{:S(2)}) copy-start(bf16[8,16,512]{2,1,0:T(8,128)(2,1)S(1)} %collective-permute-done.15.refs_3_) | copy-start | bytes 393220
  61.6 15.7 %all-to-all-start.1 = ((bf16[16,2,16,512]{3,2,1,0:T(8,128)(2,1)}), bf16[16,2,16,512]{3,2,1,0:T(8,128)(2,1)S(1)}, u32[]{:S(2)}, u32[]{:S(2)}) async-start(bf16[16,2,16,512]{3,2,1,0:T(8,128)(2,1)} %get-tuple-element.85), calls=%async_computation.1 | async-start | bytes 1048576 | tf_op jit(solution)/shard_map/all_to_all | solution.py:750
  66.1 0.9 %copy-start.1 = (bf16[8,16,512]{2,1,0:T(8,128)(2,1)S(1)}, bf16[8,16,512]{2,1,0:T(8,128)(2,1)}, u32[]{:S(2)}) copy-start(bf16[8,16,512]{2,1,0:T(8,128)(2,1)} %copy-done) | copy-start | bytes 393220
  67.0 0.9 %copy-start.3 = (bf16[8,16,512]{2,1,0:T(8,128)(2,1)S(1)}, bf16[8,16,512]{2,1,0:T(8,128)(2,1)}, u32[]{:S(2)}) copy-start(bf16[8,16,512]{2,1,0:T(8,128)(2,1)} %copy-done.2) | copy-start | bytes 393220

commit v9 on v8

--- a/solution.py
+++ b/solution.py
@@ -232,10 +232,10 @@
             codes = [pieces[t * 4 + g, :, xg * 128 : xg * 128 + 128] for g in range(4)]
             parts = [code.astype(jnp.int32).astype(F32) * VELOCITY_STEP + VELOCITY_MIDDLE for code in codes]
             for xl in range(4):
-                row = None
-                for g in range(4):
-                    turned = parts[g] if xl == g else pltpu.roll(parts[g], ((g - xl) % 4) * 32, 1)
-                    row = turned if row is None else jnp.where(group == g, turned, row)
+                row = parts[-xl % 4]
+                for p in range(1, 4):
+                    row = jnp.where(group == p, parts[(p - xl) % 4], row)
+                row = row if xl == 0 else pltpu.roll(row, 128 - xl * 32, 1)
                 out[t, pl.ds(xg * 4 + xl, 16, stride=16), :] = row
 
 
@@ -305,7 +305,9 @@
             wait(pieces[2 * q : 2 * q + 2])
             lanes = pl.ds(q * 128, 128)
             for t in range(2):
-                rows = flat_cols[t, q * 128 : q * 128 + 128, :].T
+                places = [q * 128 + lax.rem(p + 4 - lax.axis_index("gy") % 4, 4) * 32 for p in range(4)]
+                rows = [flat_cols[t, pl.ds(pl.multiple_of(at, 32), 32), :] for at in places]
+                rows = jnp.concatenate(rows, axis=0).T
                 code = jnp.round((rows - VELOCITY_MIDDLE) * (1.0 / VELOCITY_STEP)).astype(jnp.int32)
                 turned[t * 128 : t * 128 + 128, lanes] = code.astype(I16)
             outs.append(pltpu.make_async_copy(turned.at[:, lanes], turned_out.at[:, lanes], sems.at[4]))

time: 78.8 us -> 78.8 us (level)
    ppermute x4, waiting for transfers between devices: 7.76 us -> 9.64 us  [exchange(): lax.ppermute(gy_second, 'gy', outer(16))]
    ppermute x4, waiting for transfers between devices: 1.5 us -> 0.36 us  [exchange(): lax.ppermute(gx_second, 'gx', outer(8))]
where the time goes in v9:
time: 78.8 us; the launch traced here: 78.3 us
  starting transfers between devices  37.3 us (47%)
  Pallas kernels  20.1 us (26%)
  waiting for transfers between devices  18.1 us (23%)
  local copies, waits for them, and re-layouts  1.81 us (2%)
  between operations  0.94 us (1%)
    ppermute x4, starting transfers between devices, exchange(): lax.ppermute(gy_second, 'gy', outer(16))  13.2 us
    ppermute x4, waiting for transfers between devices, exchange(): lax.ppermute(gy_second, 'gy', outer(16))  9.64 us
    all_to_all x1, starting transfers between devices, on_device(): lax.all_to_all(turned.reshape(16, 16, 512), 'gy', split_axis=0, concat_ax...  8.46 us
    all_to_all x1, waiting for transfers between devices, on_device(): lax.all_to_all(bricks, 'gy', split_axis=0, concat_axis=0, tiled=True)  8.09 us
    ppermute x4, starting transfers between devices, exchange(): lax.ppermute(gx_second, 'gx', outer(8))  7.36 us
    pallas_call x3, Pallas kernels, local_step(): pl.pallas_call(kernel, out_shape=out_shape, in_specs=[VM, next_spec, VM,...  6.74 us
    all_to_all x1, starting transfers between devices, on_device(): lax.all_to_all(bricks, 'gy', split_axis=0, concat_axis=0, tiled=True)  4.26 us
    pallas_call x1, Pallas kernels, local_first(): pl.pallas_call(kernel, out_shape=[SRC_COLS, SRC_COLS, RCV_COLS, jax.Shape...  4.05 us
  transfers between devices with their start and end apart: 18, of which 6 were waited for; matrix products, arithmetic and copies ran while one was open for 0% of the time, Pallas kernels for 17%

profile of v9, /device:TPU:1, one launch (start us, length us, event | category | flops | bytes accessed | tf_op | source)
XLA Modules:
  0.0 78.3 jit_solution(4050733744904067269)
XLA Ops:
  0.6 2.0 %turn_velocity.1 = (f32[2,16,32,128]{3,2,1,0:T(8,128)S(1)}, f32[4,16,16,128]{3,2,1,0:T(8,128)S(1)}, f32[2,16,32,128]{3,2,1,0:T(8,128)S(1)}, s16[256,512]{1,0:T(8,128)(2,1)}) custom-call(f32[16,32,256]{2,1,0:T(8,128)} %vel.1, f32[16,16,512]{2,1,0:T(8,128)} %refs_0_.1, f32[16,32,256]{2,1,0:T(8,128)} %refs_2_.1), custom_call_target="tpu_custom_call" | custom-call | tf_op jit(solution)/shard_map/turn_velocity/pallas_call | solution.py:318
  2.6 8.5 %all-to-all-start = ((s16[16,16,512]{2,1,0:T(8,128)(2,1)}), s16[16,16,512]{2,1,0:T(8,128)(2,1)S(1)}, u32[]{:S(2)}, u32[]{:S(2)}) async-start(s16[16,16,512]{2,1,0:T(8,128)(2,1)} %bitcast.28), calls=%async_computation | async-start | bytes 524288 | tf_op jit(solution)/shard_map/all_to_all | solution.py:723
  11.1 0.9 %first_halos.1 = (bf16[10,16,512]{2,1,0:T(8,128)(2,1)S(1)}, bf16[8,16,512]{2,1,0:T(8,128)(2,1)}, bf16[10,16,512]{2,1,0:T(8,128)(2,1)S(1)}, bf16[8,16,512]{2,1,0:T(8,128)(2,1)S(1)}) custom-call(f32[4,256,128]{2,1,0:T(8,128)S(1)} %bitcast.21, f32[2,512,128]{2,1,0:T(8,128)S(1)} %bitcast.22), custom_call_target="tpu_custom_call" | custom-call | tf_op jit(solution)/shard_map/first_halos/pallas_call | solution.py:339
  11.9 3.9 %collective-permute-start = (bf16[10,16,512]{2,1,0:T(8,128)(2,1)S(1)}, bf16[10,16,512]{2,1,0:T(8,128)(2,1)S(1)}, u32[]{:S(2)}, u32[]{:S(2)}) collective-permute-start(bf16[10,16,512]{2,1,0:T(8,128)(2,1)S(1)} %get-tuple-element.55), channel_id=1, source_target_pairs={{0,112},{16,32},{32,16},{48,64},{64,48},{80,96},{96,80},{112,0},{1... | collective-permute-start | bytes 491528 | tf_op jit(solution)/shard_map/ppermute | solution.py:701
  15.8 0.0 collective-permute-start.2
  15.8 4.0 %collective-permute-start.1 = (bf16[8,16,512]{2,1,0:T(8,128)(2,1)}, bf16[8,16,512]{2,1,0:T(8,128)(2,1)S(1)}, u32[]{:S(2)}, u32[]{:S(2)}) collective-permute-start(bf16[8,16,512]{2,1,0:T(8,128)(2,1)} %get-tuple-element.56), channel_id=1, source_target_pairs={{0,15},{1,2},{2,1},{3,4},{4,3},{5,6},{6,5},{7,8},{8,7},{9,10},{10,... | collective-permute-start | bytes 393224 | tf_op jit(solution)/shard_map/ppermute | solution.py:702
  19.8 2.0 %collective-permute-start.3 = (bf16[8,16,512]{2,1,0:T(8,128)(2,1)S(1)}, bf16[8,16,512]{2,1,0:T(8,128)(2,1)S(1)}, u32[]{:S(2)}, u32[]{:S(2)}) collective-permute-start(bf16[8,16,512]{2,1,0:T(8,128)(2,1)S(1)} %get-tuple-element.58), channel_id=1, source_target_pairs={{0,1},{1,0},{2,3},{3,2},{4,5},{5,4},{6,7},{7,6},{8,9},{9,8},{10,11... | collective-permute-start | bytes 393224 | tf_op jit(solution)/shard_map/ppermute | solution.py:704
  21.8 4.0 %local_first.1 = (f32[4,256,128]{2,1,0:T(8,128)S(1)}, f32[4,256,128]{2,1,0:T(8,128)S(1)}, f32[2,512,128]{2,1,0:T(8,128)S(1)}, f32[4,4,16,128]{3,2,1,0:T(8,128)S(1)}, f32[32,128]{1,0:T(8,128)S(1)}) custom-call(f32[2,512,128]{2,1,0:T(8,128)S(1)} %bitcast.13, f32[16,16,512]{2,1,0:T(8,128)} %refs_0_.1, f32[256,512]{1,0:T(8,128)} %bitcast.25, ...), custom_call_target="tpu_custom_call" | custom-call | bytes 14400000 | tf_op jit(solution)/shard_map/local_first/pallas_call | solution.py:474
  25.9 0.0 all-to-all-done.pieces
  25.9 0.2 source_velocity.1.refs_3_.vel_src.refs_2_
  26.1 0.5 collective-permute-done.1.refs_6_
  26.6 0.0 collective-permute-done.3.refs_8_
  26.6 0.0 collective-permute-done.refs_5_
  26.6 0.0 collective-permute-done.2.refs_7_
  26.6 1.0 %halo_step0.1 = (f32[4,256,128]{2,1,0:T(8,128)S(1)}, f32[2,512,128]{2,1,0:T(8,128)S(1)}, bf16[10,16,512]{2,1,0:T(8,128)(2,1)S(1)}, bf16[8,16,512]{2,1,0:T(8,128)...) custom-call(f32[4,256,128]{2,1,0:T(8,128)S(1)} %get-tuple-element.49.refs_0_, ...), custom_call_target="tpu_custom_call" | custom-call | tf_op jit(solution)/shard_map/halo_step0/pallas_call | solution.py:607
  27.6 1.8 %collective-permute-start.4 = (bf16[10,16,512]{2,1,0:T(8,128)(2,1)S(1)}, bf16[10,16,512]{2,1,0:T(8,128)(2,1)S(1)}, u32[]{:S(2)}, u32[]{:S(2)}) collective-permute-start(bf16[10,16,512]{2,1,0:T(8,128)(2,1)S(1)} %get-tuple-element.65), channel_id=1, source_target_pairs={{0,112},{16,32},{32,16},{48,64},{64,48},{80,96},{96,80},{112,0},{1... | collective-permute-start | bytes 491528 | tf_op jit(solution)/shard_map/ppermute | solution.py:701
  29.4 0.0 collective-permute-start.6
  29.4 1.4 %collective-permute-start.5 = (bf16[8,16,512]{2,1,0:T(8,128)(2,1)S(1)}, bf16[8,16,512]{2,1,0:T(8,128)(2,1)S(1)}, u32[]{:S(2)}, u32[]{:S(2)}) collective-permute-start(bf16[8,16,512]{2,1,0:T(8,128)(2,1)S(1)} %get-tuple-element.66), channel_id=1, source_target_pairs={{0,15},{1,2},{2,1},{3,4},{4,3},{5,6},{6,5},{7,8},{8,7},{9,10},{10,... | collective-permute-start | bytes 393224 | tf_op jit(solution)/shard_map/ppermute | solution.py:702
  30.8 1.9 %collective-permute-start.7 = (bf16[8,16,512]{2,1,0:T(8,128)(2,1)S(1)}, bf16[8,16,512]{2,1,0:T(8,128)(2,1)S(1)}, u32[]{:S(2)}, u32[]{:S(2)}) collective-permute-start(bf16[8,16,512]{2,1,0:T(8,128)(2,1)S(1)} %get-tuple-element.68), channel_id=1, source_target_pairs={{0,1},{1,0},{2,3},{3,2},{4,5},{5,4},{6,7},{7,6},{8,9},{9,8},{10,11... | collective-permute-start | bytes 393224 | tf_op jit(solution)/shard_map/ppermute | solution.py:704
  32.7 2.5 %local_step1.1 = (f32[4,256,128]{2,1,0:T(8,128)S(1)}, f32[2,512,128]{2,1,0:T(8,128)S(1)}) custom-call(f32[4,256,128]{2,1,0:T(8,128)S(1)} %get-tuple-element.60.src.src_next, f32[256,512]{1,0:T(8,128)} %bitcast.23, f32[2,512,128]{2,1,0:T(8,128)S(1)} %get-tuple-element.61.rcv.rcv_next, f32[512,256]{1,0:T(8,128)} %bitcast.24, ...), custom_call_target="tpu_custom_call" | custom-call | bytes 10800000 | tf_op jit(solution)/shard_map/local_step1/pallas_call | solution.py:555
  35.2 1.8 %collective-permute-done.5.refs_5_ = bf16[8,16,512]{2,1,0:T(8,128)(2,1)S(1)} collective-permute-done((bf16[8,16,512]{2,1,0:T(8,128)(2,1)S(1)}, bf16[8,16,512]{2,1,0:T(8,128)(2,1)S(1)}, u32[]{:S(2)}, u32[]{:S(2)}) %collective-permute-start.5) | collective-permute-done | bytes 131104 | tf_op jit(solution)/shard_map/ppermute | solution.py:702
  37.0 0.0 collective-permute-done.7.refs_7_
  37.0 0.4 collective-permute-done.4.refs_4_
  37.4 1.0 %halo_step1.1 = (f32[4,256,128]{2,1,0:T(8,128)S(1)}, f32[2,512,128]{2,1,0:T(8,128)S(1)}, bf16[10,16,512]{2,1,0:T(8,128)(2,1)S(1)}, bf16[8,16,512]{2,1,0:T(8,128)...) custom-call(f32[4,256,128]{2,1,0:T(8,128)S(1)} %get-tuple-element.63.refs_0_, ...), custom_call_target="tpu_custom_call" | custom-call | tf_op jit(solution)/shard_map/halo_step1/pallas_call | solution.py:607
  38.3 1.5 %collective-permute-start.8 = (bf16[10,16,512]{2,1,0:T(8,128)(2,1)S(1)}, bf16[10,16,512]{2,1,0:T(8,128)(2,1)S(1)}, u32[]{:S(2)}, u32[]{:S(2)}) collective-permute-start(bf16[10,16,512]{2,1,0:T(8,128)(2,1)S(1)} %get-tuple-element.73), channel_id=1, source_target_pairs={{0,112},{16,32},{32,16},{48,64},{64,48},{80,96},{96,80},{112,0},{1... | collective-permute-start | bytes 491528 | tf_op jit(solution)/shard_map/ppermute | solution.py:701
  39.9 0.0 collective-permute-start.10
  39.9 4.1 %collective-permute-start.9 = (bf16[8,16,512]{2,1,0:T(8,128)(2,1)S(1)}, bf16[8,16,512]{2,1,0:T(8,128)(2,1)S(1)}, u32[]{:S(2)}, u32[]{:S(2)}) collective-permute-start(bf16[8,16,512]{2,1,0:T(8,128)(2,1)S(1)} %get-tuple-element.74), channel_id=1, source_target_pairs={{0,15},{1,2},{2,1},{3,4},{4,3},{5,6},{6,5},{7,8},{8,7},{9,10},{10,... | collective-permute-start | bytes 393224 | tf_op jit(solution)/shard_map/ppermute | solution.py:702
  44.0 0.0 collective-permute-start.11
  44.0 2.1 %local_step2.1 = (f32[4,256,128]{2,1,0:T(8,128)S(1)}, f32[2,512,128]{2,1,0:T(8,128)S(1)}, f32[2,512,128]{2,1,0:T(8,128)}) custom-call(f32[4,256,128]{2,1,0:T(8,128)S(1)} %get-tuple-element.69.src.src_next, f32[4,256,128]{2,1,0:T(8,128)S(1)} %get-tuple-element.60.src.src_next, f32[2,512,128]{2,1,0:T(8,128)S(1)} %get-tuple-element.70.rcv.rcv_next, ...), custom_call_target="tpu_custom_call" | custom-call | bytes 10800000 | tf_op jit(solution)/shard_map/local_step2/pallas_call | solution.py:555
  46.1 3.7 %collective-permute-done.9.refs_5_ = bf16[8,16,512]{2,1,0:T(8,128)(2,1)S(1)} collective-permute-done((bf16[8,16,512]{2,1,0:T(8,128)(2,1)S(1)}, bf16[8,16,512]{2,1,0:T(8,128)(2,1)S(1)}, u32[]{:S(2)}, u32[]{:S(2)}) %collective-permute-start.9) | collective-permute-done | bytes 131104 | tf_op jit(solution)/shard_map/ppermute | solution.py:702
  49.8 0.0 collective-permute-done.11.refs_7_
  49.8 0.0 collective-permute-done.8.refs_4_
  49.8 0.0 collective-permute-done.10.refs_6_
  49.8 1.0 %halo_step2.1 = (f32[4,256,128]{2,1,0:T(8,128)S(1)}, f32[2,512,128]{2,1,0:T(8,128)S(1)}, bf16[10,16,512]{2,1,0:T(8,128)(2,1)S(1)}, bf16[8,16,512]{2,1,0:T(8,128)...) custom-call(f32[4,256,128]{2,1,0:T(8,128)S(1)} %get-tuple-element.71.refs_0_, ...), custom_call_target="tpu_custom_call" | custom-call | tf_op jit(solution)/shard_map/halo_step2/pallas_call | solution.py:607
  50.8 0.1 collective-permute-start.12
  50.9 0.2 collective-permute-start.14
  51.1 3.7 %collective-permute-start.13 = (bf16[8,16,512]{2,1,0:T(8,128)(2,1)S(1)}, bf16[8,16,512]{2,1,0:T(8,128)(2,1)S(1)}, u32[]{:S(2)}, u32[]{:S(2)}) collective-permute-start(bf16[8,16,512]{2,1,0:T(8,128)(2,1)S(1)} %get-tuple-element.82), channel_id=1, source_target_pairs={{0,15},{1,2},{2,1},{3,4},{4,3},{5,6},{6,5},{7,8},{8,7},{9,10},{10,... | collective-permute-start | bytes 393224 | tf_op jit(solution)/shard_map/ppermute | solution.py:702
  54.8 0.0 collective-permute-start.15
  54.8 2.1 %local_step3.1 = (f32[4,256,128]{2,1,0:T(8,128)S(1)}, f32[2,512,128]{2,1,0:T(8,128)S(1)}, bf16[16,2,16,512]{3,2,1,0:T(8,128)(2,1)}) custom-call(f32[4,256,128]{2,1,0:T(8,128)S(1)} %get-tuple-element.77.src, f32[4,256,128]{2,1,0:T(8,128)S(1)} %get-tuple-element.69.src.src_next, f32[2,512,128]{2,1,0:T(8,128)S(1)} %get-tuple-element.78.rcv, ...), custom_call_target="tpu_custom_call" | custom-call | bytes 10800000 | tf_op jit(solution)/shard_map/local_step3/pallas_call | solution.py:555
  56.9 3.7 %collective-permute-done.13.refs_1_ = bf16[8,16,512]{2,1,0:T(8,128)(2,1)S(1)} collective-permute-done((bf16[8,16,512]{2,1,0:T(8,128)(2,1)S(1)}, bf16[8,16,512]{2,1,0:T(8,128)(2,1)S(1)}, u32[]{:S(2)}, u32[]{:S(2)}) %collective-permute-start.13) | collective-permute-done | bytes 131104 | tf_op jit(solution)/shard_map/ppermute | solution.py:702
  60.6 0.0 collective-permute-done.12.refs_0_
  60.6 1.2 %last_source.1 = (f32[4,256,128]{2,1,0:T(8,128)S(1)}, bf16[16,2,16,512]{3,2,1,0:T(8,128)(2,1)}) custom-call(f32[4,256,128]{2,1,0:T(8,128)S(1)} %get-tuple-element.79.local, bf16[16,2,16,512]{3,2,1,0:T(8,128)(2,1)} %get-tuple-element.80._, f32[4,256,128]{2,1,0:T(8,128)S(1)} %source_velocity.1.refs_3_.vel_src.refs_2_, ...), custom_call_target="tpu_custom_call", output_to_operand_aliasing={{1}: (1, {})} | custom-call | tf_op jit(solution)/shard_map/last_source/pallas_call | solution.py:631
  61.9 4.3 %all-to-all-start.1 = ((bf16[16,2,16,512]{3,2,1,0:T(8,128)(2,1)}), bf16[16,2,16,512]{3,2,1,0:T(8,128)(2,1)S(1)}, u32[]{:S(2)}, u32[]{:S(2)}) async-start(bf16[16,2,16,512]{3,2,1,0:T(8,128)(2,1)} %get-tuple-element.85), calls=%async_computation.1 | async-start | bytes 1048576 | tf_op jit(solution)/shard_map/all_to_all | solution.py:752
  66.1 0.9 %copy-done.1 = bf16[8,16,512]{2,1,0:T(8,128)(2,1)S(1)} copy-done((bf16[8,16,512]{2,1,0:T(8,128)(2,1)S(1)}, bf16[8,16,512]{2,1,0:T(8,128)(2,1)}, u32[]{:S(2)}) %copy-start.1) | copy-done | bytes 131096
  67.0 0.9 %copy-done.3 = bf16[8,16,512]{2,1,0:T(8,128)(2,1)S(1)} copy-done((bf16[8,16,512]{2,1,0:T(8,128)(2,1)S(1)}, bf16[8,16,512]{2,1,0:T(8,128)(2,1)}, u32[]{:S(2)}) %copy-start.3) | copy-done | bytes 131096
  67.9 1.2 %last_receiver.1 = (f32[2,512,128]{2,1,0:T(8,128)S(1)}, f32[2,512,128]{2,1,0:T(8,128)S(1)}, f32[256,512]{1,0:T(8,128)}, f32[512,256]{1,0:T(8,128)}) custom-call(f32[2,512,128]{2,1,0:T(8,128)S(1)} %get-tuple-element.86.local, f32[2,512,128]{2,1,0:T(8,128)S(1)} %bitcast.20, bf16[10,16,512]{2,1,0:T(8,128)(2,1)S(1)} %collective-permute-done.12.refs_0_, ...), custom_call_target="tpu_custom_call" | custom-call | bytes 7200000 | tf_op jit(solution)/shard_map/last_receiver/pallas_call | solution.py:655
  69.2 8.1 %all-to-all-done.1.bricks = bf16[16,2,16,512]{3,2,1,0:T(8,128)(2,1)S(1)} async-done(((bf16[16,2,16,512]{3,2,1,0:T(8,128)(2,1)}), bf16[16,2,16,512]{3,2,1,0:T(8,128)(2,1)S(1)}, u32[]{:S(2)}, u32[]{:S(2)}) %all-to-all-start.1) | async-done | bytes 524320 | tf_op jit(solution)/shard_map/all_to_all | solution.py:752
  77.3 0.9 %make_image.1 = f32[512,256]{1,0:T(8,128)} custom-call(bf16[16,2,16,512]{3,2,1,0:T(8,128)(2,1)S(1)} %all-to-all-done.1.bricks, f32[2,512,128]{2,1,0:T(8,128)S(1)} %get-tuple-element.89.rcv_early, f32[2,512,128]{2,1,0:T(8,128)S(1)} %get-tuple-element.90.rcv_late), custom_call_target="tpu_custom_call" | custom-call | tf_op jit(solution)/shard_map/make_image/pallas_call | solution.py:685
  (9 shorter events, 0.0 us)
Async XLA Ops:
  2.6 23.3 %all-to-all-start = ((s16[16,16,512]{2,1,0:T(8,128)(2,1)}), s16[16,16,512]{2,1,0:T(8,128)(2,1)S(1)}, u32[]{:S(2)}, u32[]{:S(2)}) async-start(s16[16,16,512]{2,1,0:T(8,128)(2,1)} %bitcast.28), calls=%async_computation | async-start | bytes 524288 | tf_op jit(solution)/shard_map/all_to_all | solution.py:723
  11.9 14.6 %collective-permute-start = (bf16[10,16,512]{2,1,0:T(8,128)(2,1)S(1)}, bf16[10,16,512]{2,1,0:T(8,128)(2,1)S(1)}, u32[]{:S(2)}, u32[]{:S(2)}) collective-permute-start(bf16[10,16,512]{2,1,0:T(8,128)(2,1)S(1)} %get-tuple-element.55), channel_id=1, source_target_pairs={{0,112},{16,32},{32,16},{48,64},{64,48},{80,96},{96,80},{112,0},{1... | collective-permute-start | bytes 491528 | tf_op jit(solution)/shard_map/ppermute | solution.py:701
  15.8 10.7 %collective-permute-start.2 = (bf16[10,16,512]{2,1,0:T(8,128)(2,1)S(1)}, bf16[10,16,512]{2,1,0:T(8,128)(2,1)S(1)}, u32[]{:S(2)}, u32[]{:S(2)}) collective-permute-start(bf16[10,16,512]{2,1,0:T(8,128)(2,1)S(1)} %get-tuple-element.57), channel_id=1, source_target_pairs={{0,16},{16,0},{32,48},{48,32},{64,80},{80,64},{96,112},{112,96},{1... | collective-permute-start | bytes 491528 | tf_op jit(solution)/shard_map/ppermute | solution.py:703
  15.8 10.7 %collective-permute-start.1 = (bf16[8,16,512]{2,1,0:T(8,128)(2,1)}, bf16[8,16,512]{2,1,0:T(8,128)(2,1)S(1)}, u32[]{:S(2)}, u32[]{:S(2)}) collective-permute-start(bf16[8,16,512]{2,1,0:T(8,128)(2,1)} %get-tuple-element.56), channel_id=1, source_target_pairs={{0,15},{1,2},{2,1},{3,4},{4,3},{5,6},{6,5},{7,8},{8,7},{9,10},{10,... | collective-permute-start | bytes 393224 | tf_op jit(solution)/shard_map/ppermute | solution.py:702
  19.8 6.7 %collective-permute-start.3 = (bf16[8,16,512]{2,1,0:T(8,128)(2,1)S(1)}, bf16[8,16,512]{2,1,0:T(8,128)(2,1)S(1)}, u32[]{:S(2)}, u32[]{:S(2)}) collective-permute-start(bf16[8,16,512]{2,1,0:T(8,128)(2,1)S(1)} %get-tuple-element.58), channel_id=1, source_target_pairs={{0,1},{1,0},{2,3},{3,2},{4,5},{5,4},{6,7},{7,6},{8,9},{9,8},{10,11... | collective-permute-start | bytes 393224 | tf_op jit(solution)/shard_map/ppermute | solution.py:704
  27.6 9.8 %collective-permute-start.4 = (bf16[10,16,512]{2,1,0:T(8,128)(2,1)S(1)}, bf16[10,16,512]{2,1,0:T(8,128)(2,1)S(1)}, u32[]{:S(2)}, u32[]{:S(2)}) collective-permute-start(bf16[10,16,512]{2,1,0:T(8,128)(2,1)S(1)} %get-tuple-element.65), channel_id=1, source_target_pairs={{0,112},{16,32},{32,16},{48,64},{64,48},{80,96},{96,80},{112,0},{1... | collective-permute-start | bytes 491528 | tf_op jit(solution)/shard_map/ppermute | solution.py:701
  29.4 8.0 %collective-permute-start.6 = (bf16[10,16,512]{2,1,0:T(8,128)(2,1)S(1)}, bf16[10,16,512]{2,1,0:T(8,128)(2,1)S(1)}, u32[]{:S(2)}, u32[]{:S(2)}) collective-permute-start(bf16[10,16,512]{2,1,0:T(8,128)(2,1)S(1)} %get-tuple-element.67), channel_id=1, source_target_pairs={{0,16},{16,0},{32,48},{48,32},{64,80},{80,64},{96,112},{112,96},{1... | collective-permute-start | bytes 491528 | tf_op jit(solution)/shard_map/ppermute | solution.py:703
  29.4 7.6 %collective-permute-start.5 = (bf16[8,16,512]{2,1,0:T(8,128)(2,1)S(1)}, bf16[8,16,512]{2,1,0:T(8,128)(2,1)S(1)}, u32[]{:S(2)}, u32[]{:S(2)}) collective-permute-start(bf16[8,16,512]{2,1,0:T(8,128)(2,1)S(1)} %get-tuple-element.66), channel_id=1, source_target_pairs={{0,15},{1,2},{2,1},{3,4},{4,3},{5,6},{6,5},{7,8},{8,7},{9,10},{10,... | collective-permute-start | bytes 393224 | tf_op jit(solution)/shard_map/ppermute | solution.py:702
  30.8 6.2 %collective-permute-start.7 = (bf16[8,16,512]{2,1,0:T(8,128)(2,1)S(1)}, bf16[8,16,512]{2,1,0:T(8,128)(2,1)S(1)}, u32[]{:S(2)}, u32[]{:S(2)}) collective-permute-start(bf16[8,16,512]{2,1,0:T(8,128)(2,1)S(1)} %get-tuple-element.68), channel_id=1, source_target_pairs={{0,1},{1,0},{2,3},{3,2},{4,5},{5,4},{6,7},{7,6},{8,9},{9,8},{10,11... | collective-permute-start | bytes 393224 | tf_op jit(solution)/shard_map/ppermute | solution.py:704
  38.3 11.5 %collective-permute-start.8 = (bf16[10,16,512]{2,1,0:T(8,128)(2,1)S(1)}, bf16[10,16,512]{2,1,0:T(8,128)(2,1)S(1)}, u32[]{:S(2)}, u32[]{:S(2)}) collective-permute-start(bf16[10,16,512]{2,1,0:T(8,128)(2,1)S(1)} %get-tuple-element.73), channel_id=1, source_target_pairs={{0,112},{16,32},{32,16},{48,64},{64,48},{80,96},{96,80},{112,0},{1... | collective-permute-start | bytes 491528 | tf_op jit(solution)/shard_map/ppermute | solution.py:701
  39.9 9.9 %collective-permute-start.10 = (bf16[10,16,512]{2,1,0:T(8,128)(2,1)S(1)}, bf16[10,16,512]{2,1,0:T(8,128)(2,1)S(1)}, u32[]{:S(2)}, u32[]{:S(2)}) collective-permute-start(bf16[10,16,512]{2,1,0:T(8,128)(2,1)S(1)} %get-tuple-element.75), channel_id=1, source_target_pairs={{0,16},{16,0},{32,48},{48,32},{64,80},{80,64},{96,112},{112,96},{1... | collective-permute-start | bytes 491528 | tf_op jit(solution)/shard_map/ppermute | solution.py:703
  39.9 9.9 %collective-permute-start.9 = (bf16[8,16,512]{2,1,0:T(8,128)(2,1)S(1)}, bf16[8,16,512]{2,1,0:T(8,128)(2,1)S(1)}, u32[]{:S(2)}, u32[]{:S(2)}) collective-permute-start(bf16[8,16,512]{2,1,0:T(8,128)(2,1)S(1)} %get-tuple-element.74), channel_id=1, source_target_pairs={{0,15},{1,2},{2,1},{3,4},{4,3},{5,6},{6,5},{7,8},{8,7},{9,10},{10,... | collective-permute-start | bytes 393224 | tf_op jit(solution)/shard_map/ppermute | solution.py:702
  44.0 5.8 %collective-permute-start.11 = (bf16[8,16,512]{2,1,0:T(8,128)(2,1)S(1)}, bf16[8,16,512]{2,1,0:T(8,128)(2,1)S(1)}, u32[]{:S(2)}, u32[]{:S(2)}) collective-permute-start(bf16[8,16,512]{2,1,0:T(8,128)(2,1)S(1)} %get-tuple-element.76), channel_id=1, source_target_pairs={{0,1},{1,0},{2,3},{3,2},{4,5},{5,4},{6,7},{7,6},{8,9},{9,8},{10,11... | collective-permute-start | bytes 393224 | tf_op jit(solution)/shard_map/ppermute | solution.py:704
  50.8 9.8 %collective-permute-start.12 = (bf16[10,16,512]{2,1,0:T(8,128)(2,1)S(1)}, bf16[10,16,512]{2,1,0:T(8,128)(2,1)S(1)}, u32[]{:S(2)}, u32[]{:S(2)}) collective-permute-start(bf16[10,16,512]{2,1,0:T(8,128)(2,1)S(1)} %get-tuple-element.81), channel_id=1, source_target_pairs={{0,112},{16,32},{32,16},{48,64},{64,48},{80,96},{96,80},{112,0},{1... | collective-permute-start | bytes 491528 | tf_op jit(solution)/shard_map/ppermute | solution.py:701
  50.9 9.7 %collective-permute-start.14 = (bf16[10,16,512]{2,1,0:T(8,128)(2,1)S(1)}, bf16[10,16,512]{2,1,0:T(8,128)(2,1)S(1)}, u32[]{:S(2)}, u32[]{:S(2)}) collective-permute-start(bf16[10,16,512]{2,1,0:T(8,128)(2,1)S(1)} %get-tuple-element.83), channel_id=1, source_target_pairs={{0,16},{16,0},{32,48},{48,32},{64,80},{80,64},{96,112},{112,96},{1... | collective-permute-start | bytes 491528 | tf_op jit(solution)/shard_map/ppermute | solution.py:703
  51.1 9.5 %collective-permute-start.13 = (bf16[8,16,512]{2,1,0:T(8,128)(2,1)S(1)}, bf16[8,16,512]{2,1,0:T(8,128)(2,1)S(1)}, u32[]{:S(2)}, u32[]{:S(2)}) collective-permute-start(bf16[8,16,512]{2,1,0:T(8,128)(2,1)S(1)} %get-tuple-element.82), channel_id=1, source_target_pairs={{0,15},{1,2},{2,1},{3,4},{4,3},{5,6},{6,5},{7,8},{8,7},{9,10},{10,... | collective-permute-start | bytes 393224 | tf_op jit(solution)/shard_map/ppermute | solution.py:702
  54.8 5.8 %collective-permute-start.15 = (bf16[8,16,512]{2,1,0:T(8,128)(2,1)S(1)}, bf16[8,16,512]{2,1,0:T(8,128)(2,1)S(1)}, u32[]{:S(2)}, u32[]{:S(2)}) collective-permute-start(bf16[8,16,512]{2,1,0:T(8,128)(2,1)S(1)} %get-tuple-element.84), channel_id=1, source_target_pairs={{0,1},{1,0},{2,3},{3,2},{4,5},{5,4},{6,7},{7,6},{8,9},{9,8},{10,11... | collective-permute-start | bytes 393224 | tf_op jit(solution)/shard_map/ppermute | solution.py:704
  60.6 1.3 %copy-start = (bf16[8,16,512]{2,1,0:T(8,128)(2,1)}, bf16[8,16,512]{2,1,0:T(8,128)(2,1)S(1)}, u32[]{:S(2)}) copy-start(bf16[8,16,512]{2,1,0:T(8,128)(2,1)S(1)} %collective-permute-done.13.refs_1_) | copy-start | bytes 393220
  60.6 1.3 %copy-start.2 = (bf16[8,16,512]{2,1,0:T(8,128)(2,1)}, bf16[8,16,512]{2,1,0:T(8,128)(2,1)S(1)}, u32[]{:S(2)}) copy-start(bf16[8,16,512]{2,1,0:T(8,128)(2,1)S(1)} %collective-permute-done.15.refs_3_) | copy-start | bytes 393220
  61.9 15.4 %all-to-all-start.1 = ((bf16[16,2,16,512]{3,2,1,0:T(8,128)(2,1)}), bf16[16,2,16,512]{3,2,1,0:T(8,128)(2,1)S(1)}, u32[]{:S(2)}, u32[]{:S(2)}) async-start(bf16[16,2,16,512]{3,2,1,0:T(8,128)(2,1)} %get-tuple-element.85), calls=%async_computation.1 | async-start | bytes 1048576 | tf_op jit(solution)/shard_map/all_to_all | solution.py:752
  66.1 0.9 %copy-start.1 = (bf16[8,16,512]{2,1,0:T(8,128)(2,1)S(1)}, bf16[8,16,512]{2,1,0:T(8,128)(2,1)}, u32[]{:S(2)}) copy-start(bf16[8,16,512]{2,1,0:T(8,128)(2,1)} %copy-done) | copy-start | bytes 393220
  67.0 0.9 %copy-start.3 = (bf16[8,16,512]{2,1,0:T(8,128)(2,1)S(1)}, bf16[8,16,512]{2,1,0:T(8,128)(2,1)}, u32[]{:S(2)}) copy-start(bf16[8,16,512]{2,1,0:T(8,128)(2,1)} %copy-done.2) | copy-start | bytes 393220
